TPU v7x, 32 devices: a whole 2x2x4 slice. The times are simulated.
32 devices in a mesh: rep: 4 (over z), tok: 4 (over y, core), head: 2 (over x).
Axes of the slice: x: 2, y: 2, z: 4, core: 2. Of those that a mesh axis runs over, the one named last changes fastest.
Arguments:
- image_tokens: bfloat16 [8, 1024, 1536], P('rep', 'tok'), may hold values from -6 to 6
- text_tokens: bfloat16 [8, 152, 1536], P('rep'), may hold values from -6 to 6
- text_owner: int32 [8, 152], P('rep'), may hold values from 0 to 3, as said below
- conditioning: float32 [8, 1536], replicated, may hold values from -6 to 6
- slot_sequence: int32 [8], replicated, may hold values from 0 to 7, each once
- image_w_mod: bfloat16 [1536, 6, 1536], P('tok'), may hold values from -0.15625 to 0.15625
- image_b_mod: bfloat16 [6, 1536], replicated, may hold values from -3 to 3
- image_w_qkv: bfloat16 [1536, 3, 1536], P('tok', None, 'head'), may hold values from -0.15625 to 0.15625
- image_w_proj: bfloat16 [1536, 1536], P('tok', 'head'), may hold values from -2.5 to 2.5
- image_w_up: bfloat16 [1536, 6144], P('tok', 'head'), may hold values from -0.15625 to 0.15625
- image_w_down: bfloat16 [1536, 6144], P('tok', 'head'), may hold values from -0.078125 to 0.078125
- text_w_mod: bfloat16 [1536, 6, 1536], P('tok'), may hold values from -0.15625 to 0.15625
- text_b_mod: bfloat16 [6, 1536], replicated, may hold values from -3 to 3
- text_w_qkv: bfloat16 [1536, 3, 1536], P('tok', None, 'head'), may hold values from -0.15625 to 0.15625
- text_w_proj: bfloat16 [1536, 1536], P('tok', 'head'), may hold values from -2.5 to 2.5
- text_w_up: bfloat16 [1536, 6144], P('tok', 'head'), may hold values from -0.15625 to 0.15625
- text_w_down: bfloat16 [1536, 6144], P('tok', 'head'), may hold values from -0.078125 to 0.078125
- image_cotangent: bfloat16 [8, 1024, 1536], P('rep', 'tok'), may hold values from -6 to 6
- text_cotangent: bfloat16 [8, 152, 1536], P('rep', 'tok'), may hold values from -6 to 6
Outputs:
- image_out: bfloat16 [8, 1024, 1536], P('rep', 'tok')
- text_out: bfloat16 [8, 152, 1536], P('rep', 'tok')
- image_grad: bfloat16 [8, 1024, 1536], P('rep', 'tok')
- text_grad: bfloat16 [8, 152, 1536], P('rep', 'tok')
- cond_grad: float32 [8, 1536], P(None, 'tok')
- image_g_mod: float32 [1536, 6, 1536], P('tok')
- image_g_bmod: float32 [6, 1536], replicated
- image_g_qkv: float32 [1536, 3, 1536], P('tok', None, 'head')
- image_g_proj: float32 [1536, 1536], P('tok', 'head')
- image_g_up: float32 [1536, 6144], P('tok', 'head')
- image_g_down: float32 [1536, 6144], P('tok', 'head')
- text_g_mod: float32 [1536, 6, 1536], P('tok')
- text_g_bmod: float32 [6, 1536], replicated
- text_g_qkv: float32 [1536, 3, 1536], P('tok', None, 'head')
- text_g_proj: float32 [1536, 1536], P('tok', 'head')
- text_g_up: float32 [1536, 6144], P('tok', 'head')
- text_g_down: float32 [1536, 6144], P('tok', 'head')
- stream_rms: float32 [10], replicated
Inputs may be any that keep to these rules, and one draw needn't show every extreme that they name: `text_owner`: in every row each value occurs exactly 38 times. `slot_sequence`: each sequence number occurs once.
All inputs are finite; a program needn't handle non-finite values.
Results may differ from a plain program's by a relative error of at most 0.02.
Values may be sent and summed in bfloat16 or wider, within the bound.
No kernel may reach another device: no remote copies, remote signals or barrier semaphores. Data moves between devices by JAX's collectives and lax.ppermute only.
A program may use at most 320 MiB of HBM per device.

v0:
```python
import jax
import jax.numpy as jnp
from jax import lax
from jax.sharding import PartitionSpec as P

HD = 64


exact_mode = lax.Precision.HIGHEST


def layer_norm(values):
    centered = values - jnp.mean(values, axis=-1, keepdims=True)
    spread = jnp.mean(centered * centered, axis=-1, keepdims=True)
    return centered * lax.rsqrt(spread + 1e-06)


def modulate(stream, shift_part, scale_part):
    return layer_norm(stream) * (1.0 + scale_part[:, None, :]) + shift_part[:, None, :]


def modulate_back(stream, modul, hidden_grad, shift_index, scale_index):
    unused_value, back_fn = jax.vjp(modulate, stream, modul[:, shift_index], modul[:, scale_index])
    return back_fn(hidden_grad)


def gelu_tanh(values):
    return jax.nn.gelu(values, approximate=True)


def attention_scores(query_rows, key_rows):
    return (
        jnp.einsum("qhe,khe->hqk", query_rows, key_rows, preferred_element_type=jnp.float32) * 0.125
    )


def recompute_probs(scores, row_max, row_total):
    return (
        jnp.exp(scores - jnp.transpose(row_max)[:, :, None]) / jnp.transpose(row_total)[:, :, None]
    )


def attend_one(packed):
    query_rows, key_all, value_all = packed
    scores = attention_scores(query_rows, key_all)
    row_max = jnp.max(scores, axis=-1, keepdims=True)
    expd = jnp.exp(scores - row_max)
    row_total = jnp.sum(expd, axis=-1, keepdims=True)
    attn_probs = (expd / row_total).astype(jnp.bfloat16)
    mixed = jnp.einsum("hqk,khe->qhe", attn_probs, value_all, preferred_element_type=jnp.float32)
    return (
        mixed.astype(jnp.bfloat16),
        jnp.transpose(row_max[..., 0]),
        jnp.transpose(row_total[..., 0]),
    )


def query_side(packed):
    query_rows, key_all, value_all, grad_mixed, row_max, row_total = packed
    attn_probs = recompute_probs(attention_scores(query_rows, key_all), row_max, row_total)
    grad_probs = jnp.einsum(
        "qhe,khe->hqk", grad_mixed, value_all, preferred_element_type=jnp.float32
    )
    row_delta = jnp.sum(attn_probs * grad_probs, axis=-1, keepdims=True)
    grad_scores = (attn_probs * (grad_probs - row_delta)).astype(jnp.bfloat16)
    grad_query = (
        jnp.einsum("hqk,khe->qhe", grad_scores, key_all, preferred_element_type=jnp.float32) * 0.125
    )
    grad_key = (
        jnp.einsum("hqk,qhe->khe", grad_scores, query_rows, preferred_element_type=jnp.float32)
        * 0.125
    )
    grad_value = jnp.einsum(
        "hqk,qhe->khe",
        attn_probs.astype(jnp.bfloat16),
        grad_mixed,
        preferred_element_type=jnp.float32,
    )
    return (grad_query.astype(jnp.bfloat16), grad_key, grad_value)


def mlp_forward(middle, modul, up_full, down_full):
    hidden = modulate(middle, modul[:, 3], modul[:, 4]).astype(jnp.bfloat16)
    upward = jnp.einsum("std,df->stf", hidden, up_full, preferred_element_type=jnp.float32)
    activ = gelu_tanh(upward).astype(jnp.bfloat16)
    partial_sum = jnp.einsum("stf,of->sto", activ, down_full, preferred_element_type=jnp.float32)
    return (hidden, upward, activ, partial_sum)


def mlp_backward(out_grad, modul, branch_two, hidden, upward, activ, up_full, down_full):
    gate_grad = jnp.sum(out_grad * branch_two, axis=1)
    branch_grad = (modul[:, 5][:, None, :] * out_grad).astype(jnp.bfloat16)
    down_grad = jnp.einsum("sto,stf->of", branch_grad, activ, preferred_element_type=jnp.float32)
    activ_grad = jnp.einsum(
        "sto,of->stf", branch_grad, down_full, preferred_element_type=jnp.float32
    )
    unused_value, gelu_back = jax.vjp(gelu_tanh, upward)
    upward_grad = gelu_back(activ_grad)[0].astype(jnp.bfloat16)
    up_grad = jnp.einsum("std,stf->df", hidden, upward_grad, preferred_element_type=jnp.float32)
    hidden_grad = jnp.einsum(
        "stf,df->std", upward_grad, up_full, preferred_element_type=jnp.float32
    )
    return (gate_grad, down_grad, up_grad, hidden_grad)


def proj_backward(mid_grad, modul, branch_one, mixed_rows, proj_full):
    gate_grad = jnp.sum(mid_grad * branch_one, axis=1)
    branch_grad = (modul[:, 2][:, None, :] * mid_grad).astype(jnp.bfloat16)
    proj_grad = jnp.einsum(
        "sqo,sqi->oi", branch_grad, mixed_rows, preferred_element_type=jnp.float32
    )
    mixed_grad = jnp.einsum(
        "sqo,oi->sqi", branch_grad, proj_full, preferred_element_type=jnp.float32
    )
    return (gate_grad, proj_grad, mixed_grad)


def stream_squares(stream, gated_one, middle, gated_two, result):
    return jnp.stack(
        [jnp.sum(member * member) for member in (stream, gated_one, middle, gated_two, result)]
    )


def on_device(
    image_tokens,
    text_tokens,
    text_owner,
    conditioning,
    slot_sequence,
    image_w_mod,
    image_b_mod,
    image_w_qkv,
    image_w_proj,
    image_w_up,
    image_w_down,
    text_w_mod,
    text_b_mod,
    text_w_qkv,
    text_w_proj,
    text_w_up,
    text_w_down,
    image_cotangent,
    text_cotangent,
):
    tok_rank = lax.axis_index("tok")
    rep_rank = lax.axis_index("rep")
    tok_count = lax.axis_size("tok")
    seq_group, image_rows, width = image_tokens.shape
    text_rows = text_cotangent.shape[1]
    slot_total = conditioning.shape[0]
    row_share = image_w_mod.shape[0]
    head_width = image_w_qkv.shape[2]
    head_count = head_width // HD
    local_rows = image_rows + text_rows
    caption_order = jnp.argsort(text_owner, axis=1, stable=True)
    owned_rows = lax.dynamic_slice_in_dim(caption_order, tok_rank * text_rows, text_rows, axis=1)
    text_input = jnp.take_along_axis(text_tokens, owned_rows[:, :, None], axis=1).astype(
        jnp.float32
    )
    image_input = image_tokens.astype(jnp.float32)
    picker = (slot_sequence[:, None] == jnp.arange(slot_total, dtype=jnp.int32)[None, :]).astype(
        jnp.float32
    )
    cond_slots = jnp.dot(picker, conditioning, precision=exact_mode)
    activ_all = jax.nn.silu(cond_slots).astype(jnp.bfloat16)
    activ_group = lax.dynamic_slice_in_dim(activ_all, rep_rank * seq_group, seq_group, axis=0)
    activ_share = lax.dynamic_slice_in_dim(activ_group, tok_rank * row_share, row_share, axis=1)
    image_mod, text_mod = lax.psum(
        (
            jnp.einsum("sd,dke->ske", activ_share, image_w_mod, preferred_element_type=jnp.float32),
            jnp.einsum("sd,dke->ske", activ_share, text_w_mod, preferred_element_type=jnp.float32),
        ),
        "tok",
    )
    image_mod = image_mod + image_b_mod.astype(jnp.float32)[None]
    text_mod = text_mod + text_b_mod.astype(jnp.float32)[None]
    image_qkv, text_qkv, image_proj, text_proj = (
        lax.all_gather(image_w_qkv, "tok", axis=0, tiled=True),
        lax.all_gather(text_w_qkv, "tok", axis=0, tiled=True),
        lax.all_gather(image_w_proj, "tok", axis=0, tiled=True),
        lax.all_gather(text_w_proj, "tok", axis=0, tiled=True),
    )
    image_hid_one = modulate(image_input, image_mod[:, 0], image_mod[:, 1]).astype(jnp.bfloat16)
    text_hid_one = modulate(text_input, text_mod[:, 0], text_mod[:, 1]).astype(jnp.bfloat16)
    projected = jnp.concatenate(
        [
            jnp.einsum(
                "std,dke->stke", image_hid_one, image_qkv, preferred_element_type=jnp.float32
            ),
            jnp.einsum("std,dke->stke", text_hid_one, text_qkv, preferred_element_type=jnp.float32),
        ],
        axis=1,
    ).astype(jnp.bfloat16)
    key_all, value_all = (
        lax.all_gather(projected[:, :, 1], "tok", axis=1, tiled=True),
        lax.all_gather(projected[:, :, 2], "tok", axis=1, tiled=True),
    )
    key_total = key_all.shape[1]
    query_heads = projected[:, :, 0].reshape(seq_group, local_rows, head_count, HD)
    key_heads = key_all.reshape(seq_group, key_total, head_count, HD)
    value_heads = value_all.reshape(seq_group, key_total, head_count, HD)
    mixed_heads, row_max, row_total = lax.map(attend_one, (query_heads, key_heads, value_heads))
    mixed = mixed_heads.reshape(seq_group, local_rows, head_width)
    image_branch, text_branch = (
        lax.psum(
            jnp.einsum(
                "sqi,oi->sqo", mixed[:, :image_rows], image_proj, preferred_element_type=jnp.float32
            ).astype(jnp.bfloat16),
            "head",
        ).astype(jnp.float32),
        lax.psum(
            jnp.einsum(
                "sqi,oi->sqo", mixed[:, image_rows:], text_proj, preferred_element_type=jnp.float32
            ).astype(jnp.bfloat16),
            "head",
        ).astype(jnp.float32),
    )
    image_middle = image_input + image_mod[:, 2][:, None, :] * image_branch
    text_middle = text_input + text_mod[:, 2][:, None, :] * text_branch
    image_up, text_up, image_down, text_down = (
        lax.all_gather(image_w_up, "tok", axis=0, tiled=True),
        lax.all_gather(text_w_up, "tok", axis=0, tiled=True),
        lax.all_gather(image_w_down, "tok", axis=0, tiled=True),
        lax.all_gather(text_w_down, "tok", axis=0, tiled=True),
    )
    image_hid_two, image_upward, image_activ, image_part = mlp_forward(
        image_middle, image_mod, image_up, image_down
    )
    text_hid_two, text_upward, text_activ, text_part = mlp_forward(
        text_middle, text_mod, text_up, text_down
    )
    image_branch_two, text_branch_two = (
        lax.psum(image_part.astype(jnp.bfloat16), "head").astype(jnp.float32),
        lax.psum(text_part.astype(jnp.bfloat16), "head").astype(jnp.float32),
    )
    image_result = image_middle + image_mod[:, 5][:, None, :] * image_branch_two
    text_result = text_middle + text_mod[:, 5][:, None, :] * text_branch_two
    square_partial = jnp.concatenate(
        [
            stream_squares(
                image_input,
                image_mod[:, 2][:, None, :] * image_branch,
                image_middle,
                image_mod[:, 5][:, None, :] * image_branch_two,
                image_result,
            ),
            stream_squares(
                text_input,
                text_mod[:, 2][:, None, :] * text_branch,
                text_middle,
                text_mod[:, 5][:, None, :] * text_branch_two,
                text_result,
            ),
        ]
    )
    image_cot = image_cotangent.astype(jnp.float32)
    text_cot = text_cotangent.astype(jnp.float32)
    image_gate_two, image_g_down, image_g_up, image_hid_part = mlp_backward(
        image_cot,
        image_mod,
        image_branch_two,
        image_hid_two,
        image_upward,
        image_activ,
        image_up,
        image_down,
    )
    text_gate_two, text_g_down, text_g_up, text_hid_part = mlp_backward(
        text_cot,
        text_mod,
        text_branch_two,
        text_hid_two,
        text_upward,
        text_activ,
        text_up,
        text_down,
    )
    image_hid_grad, text_hid_grad = (
        lax.psum(image_hid_part.astype(jnp.bfloat16), "head").astype(jnp.float32),
        lax.psum(text_hid_part.astype(jnp.bfloat16), "head").astype(jnp.float32),
    )
    image_ln_grad, image_shift_two, image_scale_two = modulate_back(
        image_middle, image_mod, image_hid_grad, 3, 4
    )
    text_ln_grad, text_shift_two, text_scale_two = modulate_back(
        text_middle, text_mod, text_hid_grad, 3, 4
    )
    image_mid_grad = image_cot + image_ln_grad
    text_mid_grad = text_cot + text_ln_grad
    image_gate_one, image_g_proj, image_mixed_grad = proj_backward(
        image_mid_grad, image_mod, image_branch, mixed[:, :image_rows], image_proj
    )
    text_gate_one, text_g_proj, text_mixed_grad = proj_backward(
        text_mid_grad, text_mod, text_branch, mixed[:, image_rows:], text_proj
    )
    mixed_grad = jnp.concatenate([image_mixed_grad, text_mixed_grad], axis=1).astype(jnp.bfloat16)
    grad_heads = mixed_grad.reshape(seq_group, local_rows, head_count, HD)
    query_grad, key_grad_all, value_grad_all = lax.map(
        query_side, (query_heads, key_heads, value_heads, grad_heads, row_max, row_total)
    )
    key_grad, value_grad = (
        lax.psum_scatter(
            key_grad_all.reshape(seq_group, key_total, head_width).astype(jnp.bfloat16),
            "tok",
            scatter_dimension=1,
            tiled=True,
        ).astype(jnp.float32),
        lax.psum_scatter(
            value_grad_all.reshape(seq_group, key_total, head_width).astype(jnp.bfloat16),
            "tok",
            scatter_dimension=1,
            tiled=True,
        ).astype(jnp.float32),
    )
    qkv_grad = jnp.stack(
        [
            query_grad.reshape(seq_group, local_rows, head_width),
            key_grad.astype(jnp.bfloat16),
            value_grad.astype(jnp.bfloat16),
        ],
        axis=2,
    )
    image_g_qkv = jnp.einsum(
        "std,stke->dke", image_hid_one, qkv_grad[:, :image_rows], preferred_element_type=jnp.float32
    )
    text_g_qkv = jnp.einsum(
        "std,stke->dke", text_hid_one, qkv_grad[:, image_rows:], preferred_element_type=jnp.float32
    )
    image_in_part = jnp.einsum(
        "stke,dke->std", qkv_grad[:, :image_rows], image_qkv, preferred_element_type=jnp.float32
    )
    text_in_part = jnp.einsum(
        "stke,dke->std", qkv_grad[:, image_rows:], text_qkv, preferred_element_type=jnp.float32
    )
    image_in_grad, text_in_grad = (
        lax.psum(image_in_part.astype(jnp.bfloat16), "head").astype(jnp.float32),
        lax.psum(text_in_part.astype(jnp.bfloat16), "head").astype(jnp.float32),
    )
    image_ln_one, image_shift_one, image_scale_one = modulate_back(
        image_input, image_mod, image_in_grad, 0, 1
    )
    text_ln_one, text_shift_one, text_scale_one = modulate_back(
        text_input, text_mod, text_in_grad, 0, 1
    )
    image_grad = (image_mid_grad + image_ln_one).astype(jnp.bfloat16)
    text_grad = (text_mid_grad + text_ln_one).astype(jnp.bfloat16)
    mod_partial = jnp.stack(
        [
            jnp.stack(
                [
                    image_shift_one,
                    image_scale_one,
                    image_gate_one,
                    image_shift_two,
                    image_scale_two,
                    image_gate_two,
                ],
                axis=1,
            ),
            jnp.stack(
                [
                    text_shift_one,
                    text_scale_one,
                    text_gate_one,
                    text_shift_two,
                    text_scale_two,
                    text_gate_two,
                ],
                axis=1,
            ),
        ]
    )
    mod_copies = jnp.broadcast_to(mod_partial[None], (tok_count,) + mod_partial.shape)
    square_copies = jnp.broadcast_to(square_partial[None], (tok_count, 10))
    scattered = (
        lax.psum_scatter(
            image_g_qkv.astype(jnp.bfloat16), "tok", scatter_dimension=0, tiled=True
        ).astype(jnp.float32),
        lax.psum_scatter(
            text_g_qkv.astype(jnp.bfloat16), "tok", scatter_dimension=0, tiled=True
        ).astype(jnp.float32),
        lax.psum_scatter(
            image_g_proj.astype(jnp.bfloat16), "tok", scatter_dimension=0, tiled=True
        ).astype(jnp.float32),
        lax.psum_scatter(
            text_g_proj.astype(jnp.bfloat16), "tok", scatter_dimension=0, tiled=True
        ).astype(jnp.float32),
        lax.psum_scatter(
            image_g_up.astype(jnp.bfloat16), "tok", scatter_dimension=0, tiled=True
        ).astype(jnp.float32),
        lax.psum_scatter(
            text_g_up.astype(jnp.bfloat16), "tok", scatter_dimension=0, tiled=True
        ).astype(jnp.float32),
        lax.psum_scatter(
            image_g_down.astype(jnp.bfloat16), "tok", scatter_dimension=0, tiled=True
        ).astype(jnp.float32),
        lax.psum_scatter(
            text_g_down.astype(jnp.bfloat16), "tok", scatter_dimension=0, tiled=True
        ).astype(jnp.float32),
        lax.psum_scatter(
            mod_copies.astype(jnp.bfloat16), "tok", scatter_dimension=0, tiled=True
        ).astype(jnp.float32),
        lax.psum_scatter(
            square_copies.astype(jnp.bfloat16), "tok", scatter_dimension=0, tiled=True
        ).astype(jnp.float32),
    )
    mod_table = lax.dynamic_update_slice_in_dim(
        jnp.zeros((2, slot_total, 6, width), jnp.float32),
        scattered[8][0],
        rep_rank * seq_group,
        axis=1,
    )
    reduced = (
        lax.psum(scattered[0].astype(jnp.bfloat16), "rep").astype(jnp.float32),
        lax.psum(scattered[1].astype(jnp.bfloat16), "rep").astype(jnp.float32),
        lax.psum(scattered[2].astype(jnp.bfloat16), "rep").astype(jnp.float32),
        lax.psum(scattered[3].astype(jnp.bfloat16), "rep").astype(jnp.float32),
        lax.psum(scattered[4].astype(jnp.bfloat16), "rep").astype(jnp.float32),
        lax.psum(scattered[5].astype(jnp.bfloat16), "rep").astype(jnp.float32),
        lax.psum(scattered[6].astype(jnp.bfloat16), "rep").astype(jnp.float32),
        lax.psum(scattered[7].astype(jnp.bfloat16), "rep").astype(jnp.float32),
        lax.psum(mod_table.astype(jnp.bfloat16), "rep").astype(jnp.float32),
        lax.psum(scattered[9][0].astype(jnp.bfloat16), "rep").astype(jnp.float32),
    )
    weight_sums = reduced[:8]
    mod_sum = reduced[8]
    square_total = reduced[9]
    activ_rows = lax.dynamic_slice_in_dim(
        activ_all, tok_rank * row_share, row_share, axis=1
    ).astype(jnp.float32)
    image_g_mod = jnp.einsum("sd,ske->dke", activ_rows, mod_sum[0], precision=exact_mode)
    text_g_mod = jnp.einsum("sd,ske->dke", activ_rows, mod_sum[1], precision=exact_mode)
    image_g_bmod = jnp.sum(mod_sum[0], axis=0)
    text_g_bmod = jnp.sum(mod_sum[1], axis=0)
    activ_grad = jnp.einsum(
        "ske,dke->sd", mod_sum[0], image_w_mod.astype(jnp.float32), precision=exact_mode
    ) + jnp.einsum("ske,dke->sd", mod_sum[1], text_w_mod.astype(jnp.float32), precision=exact_mode)
    cond_rows = lax.dynamic_slice_in_dim(cond_slots, tok_rank * row_share, row_share, axis=1)
    unused_value, silu_back = jax.vjp(jax.nn.silu, cond_rows)
    slot_grad = silu_back(activ_grad)[0]
    cond_grad = jnp.dot(jnp.transpose(picker), slot_grad, precision=exact_mode)
    image_count = float(slot_total * image_rows * tok_count * width)
    text_count = float(slot_total * text_rows * tok_count * width)
    count_table = jnp.concatenate(
        [jnp.full((5,), image_count, jnp.float32), jnp.full((5,), text_count, jnp.float32)]
    )
    stream_rms = jnp.sqrt(square_total / count_table)
    return (
        image_result.astype(jnp.bfloat16),
        text_result.astype(jnp.bfloat16),
        image_grad,
        text_grad,
        cond_grad,
        image_g_mod,
        image_g_bmod,
        weight_sums[0],
        weight_sums[2],
        weight_sums[4],
        weight_sums[6],
        text_g_mod,
        text_g_bmod,
        weight_sums[1],
        weight_sums[3],
        weight_sums[5],
        weight_sums[7],
        stream_rms,
    )


def solution(mesh):
    in_specs = (
        P("rep", "tok", None),
        P("rep", None, None),
        P("rep", None),
        P(),
        P(),
        P("tok", None, None),
        P(),
        P("tok", None, "head"),
        P("tok", "head"),
        P("tok", "head"),
        P("tok", "head"),
        P("tok", None, None),
        P(),
        P("tok", None, "head"),
        P("tok", "head"),
        P("tok", "head"),
        P("tok", "head"),
        P("rep", "tok", None),
        P("rep", "tok", None),
    )
    out_specs = (
        P("rep", "tok", None),
        P("rep", "tok", None),
        P("rep", "tok", None),
        P("rep", "tok", None),
        P(None, "tok"),
        P("tok", None, None),
        P(),
        P("tok", None, "head"),
        P("tok", "head"),
        P("tok", "head"),
        P("tok", "head"),
        P("tok", None, None),
        P(),
        P("tok", None, "head"),
        P("tok", "head"),
        P("tok", "head"),
        P("tok", "head"),
        P(),
    )
    return jax.shard_map(
        on_device, mesh=mesh, in_specs=in_specs, out_specs=out_specs, check_vma=False
    )
```

profile of v0, /device:TPU:0, one launch (start us, length us, event | category | flops | bytes accessed | tf_op | source)
XLA Modules:
  0.0 2236.2 jit_solution(11141889025247617126)
XLA Ops:
  24.7 24.7 %all-reduce.20.cloned.1.call-done = (f32[2,6,1536]{2,0,1:T(2,128)}, f32[2,6,1536]{2,0,1:T(2,128)}) async-done(((f32[2,6,1536]{2,0,1:T(2,128)}, f32[2,6,1536]{2,0,1:T(2,128)}), (f32[2,6,1536]{2,0,1:T(2,128)}, f32[2,6,1536]{2,0,1:T(2,128)})) %all-reduce.20.cloned.1.call-update) | async-done | bytes 147472 | tf_op jit(solution)/shard_map/psum | solution.py:168
  51.7 51.1 %all-gather.15.cloned.1.call-done = bf16[1536,3,768]{2,0,1:T(8,128)(2,1)} async-done(((bf16[384,3,768]{2,0,1:T(8,128)(2,1)}), bf16[1536,3,768]{2,0,1:T(8,128)(2,1)}) %all-gather.15.cloned.1.call-update) | async-done | bytes 7077904 | tf_op jit(solution)/shard_map/all_gather | solution.py:179
  107.3 48.0 %all-gather.13.cloned.1.call-done = bf16[1536,3,768]{2,0,1:T(8,128)(2,1)} async-done(((bf16[384,3,768]{2,0,1:T(8,128)(2,1)}), bf16[1536,3,768]{2,0,1:T(8,128)(2,1)}) %all-gather.13.cloned.1.call-update) | async-done | bytes 7077904 | tf_op jit(solution)/shard_map/all_gather | solution.py:178
  155.3 7.4 fusion.151
  168.6 27.3 %all-gather.31.cloned.1.call-done = bf16[2,1176,1,768]{3,0,2,1:T(2,128)(2,1)} async-done(((bf16[2,294,1,768]{3,0,2,1:T(2,128)(2,1)}), bf16[2,1176,1,768]{3,0,2,1:T(2,128)(2,1)}) %all-gather.31.cloned.1.call-update) | async-done | bytes 3612688 | tf_op jit(solution)/shard_map/all_gather | solution.py:195
  195.9 10.4 copy.81
  206.3 22.8 %all-gather.29.cloned.1.call-done = bf16[2,1176,1,768]{3,0,2,1:T(2,128)(2,1)} async-done(((bf16[2,294,1,768]{3,0,2,1:T(2,128)(2,1)}), bf16[2,1176,1,768]{3,0,2,1:T(2,128)(2,1)}) %all-gather.29.cloned.1.call-update) | async-done | bytes 3612688 | tf_op jit(solution)/shard_map/all_gather | solution.py:196
  229.2 10.4 copy.78
  239.7 56.6 %while.28 = (s32[]{:T(128)}, bf16[2,294,12,64]{1,3,2,0:T(8,128)(2,1)S(1)}, f32[2,294,12]{1,2,0:T(8,128)S(1)}, f32[2,294,12]{1,2,0:T(8,128)S(1)}, bf16[2,1176,12,...) while((s32[]{:T(128)}, ...), condition=%wide.region_10.11_spmd, body=%wide.region_7.10_spmd.sunk | while | flops 1091386880 | bytes 56681408 | solution.py:202
  239.7 10.3 fusion.291
  250.1 8.9 fusion.292
  259.0 9.4 fusion.293
  268.4 10.3 fusion.291
  278.8 8.9 fusion.292
  287.7 8.6 fusion.293
  307.9 54.0 %all-reduce.30.cloned.1.call-done = (bf16[2,256,1536]{2,1,0:T(8,128)(2,1)}, bf16[2,38,1536]{2,1,0:T(8,128)(2,1)}) async-done(((bf16[2,256,1536]{2,1,0:T(8,128)(2,1)}, bf16[2,38,1536]{2,1,0:T(8,128)(2,1)}), (bf16[2,256,1536]{2,1,0:T(8,128)(2,1)}, bf16[2,38,1536]{2,1,0:T(8,128)(2,1)})) %all-reduce.30.cloned.1.call-update) | async-done | bytes 1806352 | tf_op jit(solution)/shard_map/psum | solution.py:205
  367.4 60.4 %all-gather.25.cloned.1.call-done = bf16[1536,3072]{1,0:T(8,128)(2,1)} async-done(((bf16[384,3072]{1,0:T(8,128)(2,1)}), bf16[1536,3072]{1,0:T(8,128)(2,1)}) %all-gather.25.cloned.1.call-update) | async-done | bytes 9437200 | tf_op jit(solution)/shard_map/all_gather | solution.py:222
  427.9 5.6 fusion.63
  433.6 60.1 %all-gather.27.cloned.1.call-done = bf16[1536,3072]{1,0:T(8,128)(2,1)} async-done(((bf16[384,3072]{1,0:T(8,128)(2,1)}), bf16[1536,3072]{1,0:T(8,128)(2,1)}) %all-gather.27.cloned.1.call-update) | async-done | bytes 9437200 | tf_op jit(solution)/shard_map/all_gather | solution.py:224
  493.7 6.1 fusion.175
  507.4 52.1 %all-gather.19.cloned.1.call-done = bf16[1536,3072]{1,0:T(8,128)(2,1)} async-done(((bf16[384,3072]{1,0:T(8,128)(2,1)}), bf16[1536,3072]{1,0:T(8,128)(2,1)}) %all-gather.19.cloned.1.call-update) | async-done | bytes 9437200 | tf_op jit(solution)/shard_map/all_gather | solution.py:221
  559.6 11.3 fusion.71
  570.9 54.5 %all-gather.21.cloned.1.call-done = bf16[1536,3072]{1,0:T(8,128)(2,1)} async-done(((bf16[384,3072]{1,0:T(8,128)(2,1)}), bf16[1536,3072]{1,0:T(8,128)(2,1)}) %all-gather.21.cloned.1.call-update) | async-done | bytes 9437200 | tf_op jit(solution)/shard_map/all_gather | solution.py:223
  625.3 11.5 fusion.123
  636.9 11.6 fusion.87
  650.2 6.3 fusion.120
  656.8 96.9 %all-reduce.28.cloned.1.call-done = (bf16[2,256,1536]{2,1,0:T(8,128)(2,1)}, bf16[2,38,1536]{2,1,0:T(8,128)(2,1)}, bf16[2,256,1536]{2,1,0:T(8,128)(2,1)}, bf16[2,38,1536]{2,1,0:T(8,128)(2,1)}) async-done(((bf16[2,256,1536]{2,1,0:T(8,128)(2,1)}, bf16[2,38,1536]{2,1,0:T(8,128)(2,1)}, bf16[2,256,1536]{2,1,0:T(8,128)(2,1)}, bf16[2,38,1536]{2,1,0:T(8,128)(2,1)}), (bf16[2,256,1536]{2,1,0:T(8,128)(2,1)}, ...) | async-done | bytes 3612688 | tf_op jit(solution)/shard_map/psum | solution.py:233
  760.3 5.9 multiply_reduce_fusion.1
  779.7 110.5 %while.29 = (s32[]{:T(128)}, bf16[2,294,12,64]{1,3,2,0:T(8,128)(2,1)}, bf16[2,1176,12,64]{1,3,2,0:T(8,128)(2,1)}, bf16[2,1176,12,64]{1,3,2,0:T(8,128)(2,1)}, bf1...) while((s32[]{:T(128)}, ...), condition=%wide.region_27.28_spmd, body=%wide.region_25.27_spmd.sunk | while | flops 2694005504 | bytes 165536784 | solution.py:298
  780.2 10.5 fusion.302
  790.7 16.0 multiply_reduce_fusion.8
  806.7 12.1 multiply_convert_fusion.15
  818.9 9.8 bitcast_dynamic-update-slice_fusion.9
  835.2 10.5 fusion.302
  845.7 16.0 multiply_reduce_fusion.8
  861.8 12.1 multiply_convert_fusion.15
  873.9 9.8 bitcast_dynamic-update-slice_fusion.9
  890.3 10.5 copy.89
  900.8 10.5 copy.87
  913.9 132.7 %all-reduce.22.cloned.1.call-done = (bf16[2,1176,768]{2,0,1:T(2,128)(2,1)}, bf16[2,1176,768]{2,0,1:T(2,128)(2,1)}) async-done(((bf16[2,1176,768]{2,0,1:T(2,128)(2,1)}, bf16[2,1176,768]{2,0,1:T(2,128)(2,1)}), (bf16[2,1176,768]{2,0,1:T(2,128)(2,1)}, bf16[2,1176,768]{2,0,1:T(2,128)(2,1)})) %all-reduce.22.cloned.1.call-update) | async-done | bytes 7225360
  1055.7 4.9 fusion.117
  1062.7 55.3 %all-reduce.26.cloned.1.call-done = (bf16[2,256,1536]{2,1,0:T(8,128)(2,1)}, bf16[2,38,1536]{2,1,0:T(8,128)(2,1)}) async-done(((bf16[2,256,1536]{2,1,0:T(8,128)(2,1)}, bf16[2,38,1536]{2,1,0:T(8,128)(2,1)}), (bf16[2,256,1536]{2,1,0:T(8,128)(2,1)}, bf16[2,38,1536]{2,1,0:T(8,128)(2,1)})) %all-reduce.26.cloned.1.call-update) | async-done | bytes 1806352 | tf_op jit(solution)/shard_map/psum | solution.py:336
  1128.0 5.0 bitcast_convert_fusion.7
  1136.4 10.4 bitcast_convert_fusion.2
  1147.6 10.1 bitcast_convert_fusion.3
  1158.9 5.3 bitcast_convert_fusion.1
  1165.4 5.3 bitcast_convert_fusion
  1171.4 8.0 bitcast_convert_fusion.5
  1180.4 5.0 bitcast_convert_fusion.4
  1187.2 9.1 reduce-scatter.11.cloned.1.call-done
  1196.4 36.2 %reduce-scatter.19.cloned.1.call-done = bf16[384,768]{1,0:T(8,128)(2,1)} async-done(((bf16[1536,768]{1,0:T(8,128)(2,1)}), bf16[384,768]{1,0:T(8,128)(2,1)}) %reduce-scatter.19.cloned.1.call-update) | async-done | bytes 589840 | tf_op jit(solution)/shard_map/reduce_scatter | solution.py:385
  1232.6 81.5 %reduce-scatter.15.cloned.1.call-done = bf16[384,3072]{1,0:T(8,128)(2,1)} async-done(((bf16[1536,3072]{1,0:T(8,128)(2,1)}), bf16[384,3072]{1,0:T(8,128)(2,1)}) %reduce-scatter.15.cloned.1.call-update) | async-done | bytes 2359312 | tf_op jit(solution)/shard_map/reduce_scatter | solution.py:394
  1314.1 81.5 %reduce-scatter.13.cloned.1.call-done = bf16[384,3072]{1,0:T(8,128)(2,1)} async-done(((bf16[1536,3072]{1,0:T(8,128)(2,1)}), bf16[384,3072]{1,0:T(8,128)(2,1)}) %reduce-scatter.13.cloned.1.call-update) | async-done | bytes 2359312 | tf_op jit(solution)/shard_map/reduce_scatter | solution.py:388
  1395.6 81.1 %reduce-scatter.21.cloned.1.call-done = bf16[384,3072]{1,0:T(8,128)(2,1)} async-done(((bf16[1536,3072]{1,0:T(8,128)(2,1)}), bf16[384,3072]{1,0:T(8,128)(2,1)}) %reduce-scatter.21.cloned.1.call-update) | async-done | bytes 2359312 | tf_op jit(solution)/shard_map/reduce_scatter | solution.py:391
  1476.7 81.0 %reduce-scatter.23.cloned.1.call-done = bf16[384,3072]{1,0:T(8,128)(2,1)} async-done(((bf16[1536,3072]{1,0:T(8,128)(2,1)}), bf16[384,3072]{1,0:T(8,128)(2,1)}) %reduce-scatter.23.cloned.1.call-update) | async-done | bytes 2359312 | tf_op jit(solution)/shard_map/reduce_scatter | solution.py:397
  1557.7 66.3 %reduce-scatter.9.cloned.1.call-done = bf16[384,3,768]{2,0,1:T(8,128)(2,1)} async-done(((bf16[1536,3,768]{2,0,1:T(8,128)(2,1)}), bf16[384,3,768]{2,0,1:T(8,128)(2,1)}) %reduce-scatter.9.cloned.1.call-update) | async-done | bytes 1769488 | tf_op jit(solution)/shard_map/reduce_scatter | solution.py:376
  1624.0 66.3 %reduce-scatter.17.cloned.1.call-done = bf16[384,3,768]{2,0,1:T(8,128)(2,1)} async-done(((bf16[1536,3,768]{2,0,1:T(8,128)(2,1)}), bf16[384,3,768]{2,0,1:T(8,128)(2,1)}) %reduce-scatter.17.cloned.1.call-update) | async-done | bytes 1769488 | tf_op jit(solution)/shard_map/reduce_scatter | solution.py:379
  1690.3 6.4 concatenate.21
  1696.8 5.8 all-reduce.3
  1703.2 13.1 psum.159
  1723.4 463.7 %all-reduce.24.cloned.1.call-done = (bf16[2,8,6,1536]{3,1,2,0:T(8,128)(2,1)}, bf16[384,3,768]{2,0,1:T(8,128)(2,1)}, bf16[384,768]{1,0:T(8,128)(2,1)}, bf16[384,3...) async-done(((bf16[2,8,6,1536]{3,1,2,0:T(8,128)(2,1)}, ...) | async-done | bytes 14450704 | tf_op jit(solution)/shard_map/psum | solution.py:422
  2187.2 5.1 convolution_bitcast_fusion.1
  2192.3 7.3 fusion.219
  2199.7 7.3 fusion.218
  (455 shorter events, 152.6 us)
Async XLA Ops:
  7.2 42.2 %all-reduce.20.cloned.1.call-start = ((), (), s32[]{:S(2)}) async-start(), calls=%async_computation.27 | async-start | bytes 294912 | tf_op jit(solution)/shard_map/psum | solution.py:168
  15.8 87.0 %all-gather.15.cloned.1.call-start = ((), (), s32[]{:S(2)}) async-start(), calls=%async_computation.9 | async-start | bytes 8847360 | tf_op jit(solution)/shard_map/all_gather | solution.py:179
  16.5 138.8 %all-gather.13.cloned.1.call-start = ((), (), s32[]{:S(2)}) async-start(), calls=%async_computation.8 | async-start | bytes 8847360 | tf_op jit(solution)/shard_map/all_gather | solution.py:178
  17.2 178.6 %all-gather.31.cloned.1.call-start = ((), (), s32[]{:S(2)}) async-start(), calls=%async_computation.25 | async-start | bytes 4515840 | tf_op jit(solution)/shard_map/all_gather | solution.py:195
  23.0 84.2 %copy-start.7 = (bf16[2,38,1536]{2,1,0:T(8,128)(2,1)}, bf16[2,38,1536]{2,1,0:T(8,128)(2,1)S(1)}, u32[]{:S(2)}) copy-start(bf16[2,38,1536]{2,1,0:T(8,128)(2,1)S(1)} %reshape.224) | copy-start | bytes 700420
  23.1 84.1 %copy-start.72 = (pred[2,38]{1,0:T(4,128)(4,1)}, pred[2,38]{1,0:T(4,128)(4,1)S(1)}, u32[]{:S(2)}) copy-start(pred[2,38]{1,0:T(4,128)(4,1)S(1)} %compare_and_fusion) | copy-start | bytes 232
  23.3 83.9 %copy-start.87 = (f32[2,38]{1,0:T(2,128)}, f32[2,38]{1,0:T(2,128)S(1)}, u32[]{:S(2)}) copy-start(f32[2,38]{1,0:T(2,128)S(1)} %broadcast_multiply_fusion.3) | copy-start | bytes 916
  24.1 83.1 %copy-start.91 = (f32[2,38]{1,0:T(2,128)}, f32[2,38]{1,0:T(2,128)S(1)}, u32[]{:S(2)}) copy-start(f32[2,38]{1,0:T(2,128)S(1)} %fusion.254) | copy-start | bytes 916
  24.1 131.2 %copy-start.85 = (f32[2,256]{1,0:T(2,128)}, f32[2,256]{1,0:T(2,128)S(1)}, u32[]{:S(2)}) copy-start(f32[2,256]{1,0:T(2,128)S(1)} %broadcast_multiply_fusion.1) | copy-start | bytes 6148
  24.7 130.6 %copy-start.105 = (f32[2,256]{1,0:T(2,128)}, f32[2,256]{1,0:T(2,128)S(1)}, u32[]{:S(2)}) copy-start(f32[2,256]{1,0:T(2,128)S(1)} %fusion.249) | copy-start | bytes 6148
  51.0 56.3 %copy-start.59 = (f32[2,1536]{1,0:T(2,128)}, f32[2,1536]{1,0:T(2,128)S(1)}, u32[]{:S(2)}) copy-start(f32[2,1536]{1,0:T(2,128)S(1)} %get-tuple-element.293) | copy-start | bytes 36868
  51.0 56.3 %copy-start.77 = (f32[2,1536]{1,0:T(2,128)}, f32[2,1536]{1,0:T(2,128)S(1)}, u32[]{:S(2)}) copy-start(f32[2,1536]{1,0:T(2,128)S(1)} %get-tuple-element.292) | copy-start | bytes 36868
  51.7 103.6 %copy-start.66 = (f32[2,1536]{1,0:T(2,128)}, f32[2,1536]{1,0:T(2,128)S(1)}, u32[]{:S(2)}) copy-start(f32[2,1536]{1,0:T(2,128)S(1)} %get-tuple-element.298) | copy-start | bytes 36868
  51.7 103.6 %copy-start.107 = (f32[2,1536]{1,0:T(2,128)}, f32[2,1536]{1,0:T(2,128)S(1)}, u32[]{:S(2)}) copy-start(f32[2,1536]{1,0:T(2,128)S(1)} %get-tuple-element.297) | copy-start | bytes 36868
  164.5 64.6 %all-gather.29.cloned.1.call-start = ((), (), s32[]{:S(2)}) async-start(), calls=%async_computation.24 | async-start | bytes 4515840 | tf_op jit(solution)/shard_map/all_gather | solution.py:196
  166.2 130.2 %all-gather.23.cloned.1.call-start = ((), (), s32[]{:S(2)}) async-start(), calls=%async_computation.13 | async-start | bytes 2949120 | tf_op jit(solution)/shard_map/all_gather | solution.py:181
  166.8 133.7 %all-gather.17.cloned.1.call-start = ((), (), s32[]{:S(2)}) async-start(), calls=%async_computation.10 | async-start | bytes 2949120 | tf_op jit(solution)/shard_map/all_gather | solution.py:180
  167.5 194.4 %all-reduce.30.cloned.1.call-start = ((), (), s32[]{:S(2)}) async-start(), calls=%async_computation.32 | async-start | bytes 3637248 | tf_op jit(solution)/shard_map/psum | solution.py:205
  304.8 123.1 %all-gather.25.cloned.1.call-start = ((), (), s32[]{:S(2)}) async-start(), calls=%async_computation.14 | async-start | bytes 11796480 | tf_op jit(solution)/shard_map/all_gather | solution.py:222
  305.5 56.4 %copy-start.8 = (bf16[2,38,1536]{2,1,0:T(8,128)(2,1)S(1)}, bf16[2,38,1536]{2,1,0:T(8,128)(2,1)}, u32[]{:S(2)}) copy-start(bf16[2,38,1536]{2,1,0:T(8,128)(2,1)} %copy-done.7) | copy-start | bytes 700420
  305.5 56.4 %copy-start.51 = (f32[2,1536]{1,0:T(2,128)S(1)}, f32[2,1536]{1,0:T(2,128)}, u32[]{:S(2)}) copy-start(f32[2,1536]{1,0:T(2,128)} %get-tuple-element.291) | copy-start | bytes 36868
  305.6 56.4 %copy-start.73 = (pred[2,38]{1,0:T(4,128)(4,1)S(1)}, pred[2,38]{1,0:T(4,128)(4,1)}, u32[]{:S(2)}) copy-start(pred[2,38]{1,0:T(4,128)(4,1)} %copy-done.72) | copy-start | bytes 232
  305.6 188.1 %all-gather.27.cloned.1.call-start = ((), (), s32[]{:S(2)}) async-start(), calls=%async_computation.15 | async-start | bytes 11796480 | tf_op jit(solution)/shard_map/all_gather | solution.py:224
  306.2 58.3 %copy-start.3 = (bf16[2,256,1536]{2,1,0:T(8,128)(2,1)S(1)}, bf16[2,256,1536]{2,1,0:T(8,128)(2,1)}, u32[]{:S(2)}) copy-start(bf16[2,256,1536]{2,1,0:T(8,128)(2,1)} %param.23) | copy-start | bytes 4718596
  306.2 58.3 %copy-start.61 = (f32[2,1536]{1,0:T(2,128)S(1)}, f32[2,1536]{1,0:T(2,128)}, u32[]{:S(2)}) copy-start(f32[2,1536]{1,0:T(2,128)} %get-tuple-element.299) | copy-start | bytes 36868
  306.2 253.4 %all-gather.19.cloned.1.call-start = ((), (), s32[]{:S(2)}) async-start(), calls=%async_computation.11 | async-start | bytes 11796480 | tf_op jit(solution)/shard_map/all_gather | solution.py:221
  306.9 318.4 %all-gather.21.cloned.1.call-start = ((), (), s32[]{:S(2)}) async-start(), calls=%async_computation.12 | async-start | bytes 11796480 | tf_op jit(solution)/shard_map/all_gather | solution.py:223
  307.5 446.2 %all-reduce.28.cloned.1.call-start = ((), (), s32[]{:S(2)}) async-start(), calls=%async_computation.31 | async-start | bytes 7274496 | tf_op jit(solution)/shard_map/psum | solution.py:233
  363.3 402.9 %copy-start.79 = (f32[2,38]{1,0:T(2,128)}, f32[2,38]{1,0:T(2,128)S(1)}, u32[]{:S(2)}) copy-start(f32[2,38]{1,0:T(2,128)S(1)} %broadcast_multiply_fusion.2) | copy-start | bytes 916
  364.5 401.7 %copy-start.81 = (f32[2,38]{1,0:T(2,128)}, f32[2,38]{1,0:T(2,128)S(1)}, u32[]{:S(2)}) copy-start(f32[2,38]{1,0:T(2,128)S(1)} %fusion.255) | copy-start | bytes 916
  364.5 63.4 %copy-start.16 = (bf16[2,38,1536]{2,1,0:T(8,128)(2,1)S(1)}, bf16[2,38,1536]{2,1,0:T(8,128)(2,1)}, u32[]{:S(2)}) copy-start(bf16[2,38,1536]{2,1,0:T(8,128)(2,1)} %get-tuple-element.270) | copy-start | bytes 700420
  364.5 63.4 %copy-start.57 = (f32[2,1536]{1,0:T(2,128)S(1)}, f32[2,1536]{1,0:T(2,128)}, u32[]{:S(2)}) copy-start(f32[2,1536]{1,0:T(2,128)} %get-tuple-element.290) | copy-start | bytes 36868
  364.5 63.4 %copy-start.70 = (f32[2,1536]{1,0:T(2,128)S(1)}, f32[2,1536]{1,0:T(2,128)}, u32[]{:S(2)}) copy-start(f32[2,1536]{1,0:T(2,128)} %get-tuple-element.289) | copy-start | bytes 36868
  366.6 402.9 %copy-start.83 = (f32[2,256]{1,0:T(2,128)}, f32[2,256]{1,0:T(2,128)S(1)}, u32[]{:S(2)}) copy-start(f32[2,256]{1,0:T(2,128)S(1)} %broadcast_multiply_fusion) | copy-start | bytes 6148
  367.4 402.0 %copy-start.101 = (f32[2,256]{1,0:T(2,128)}, f32[2,256]{1,0:T(2,128)S(1)}, u32[]{:S(2)}) copy-start(f32[2,256]{1,0:T(2,128)S(1)} %fusion.250) | copy-start | bytes 6148
  427.9 65.8 %copy-start.38 = (bf16[2,38,1536]{2,0,1:T(2,128)(2,1)S(1)}, bf16[2,38,1536]{2,0,1:T(2,128)(2,1)}, u32[]{:S(2)}) copy-start(bf16[2,38,1536]{2,0,1:T(2,128)(2,1)} %param.41) | copy-start | bytes 700420
  427.9 65.7 %copy-start.75 = (f32[2,1536]{1,0:T(2,128)S(1)}, f32[2,1536]{1,0:T(2,128)}, u32[]{:S(2)}) copy-start(f32[2,1536]{1,0:T(2,128)} %get-tuple-element.288) | copy-start | bytes 36868
  433.6 70.2 %copy-start.19 = (f32[2,38,3072]{2,1,0:T(8,128)}, f32[2,38,3072]{2,1,0:T(8,128)S(1)}, u32[]{:S(2)}) copy-start(f32[2,38,3072]{2,1,0:T(8,128)S(1)} %fusion.63) | copy-start | bytes 2801668
  570.9 66.0 %copy-start.89 = (f32[2,1536]{1,0:T(2,128)S(1)}, f32[2,1536]{1,0:T(2,128)}, u32[]{:S(2)}) copy-start(f32[2,1536]{1,0:T(2,128)} %get-tuple-element.294) | copy-start | bytes 36868
  656.5 101.6 %copy-start.39 = (bf16[2,38,1536]{2,0,1:T(2,128)(2,1)S(1)}, bf16[2,38,1536]{2,0,1:T(2,128)(2,1)}, u32[]{:S(2)}) copy-start(bf16[2,38,1536]{2,0,1:T(2,128)(2,1)} %param.41) | copy-start | bytes 700420
  656.5 390.1 %all-reduce.22.cloned.1.call-start = ((), (), s32[]{:S(2)}) async-start(), calls=%async_computation.28 | async-start | bytes 14450688
  911.3 206.7 %all-reduce.26.cloned.1.call-start = ((), (), s32[]{:S(2)}) async-start(), calls=%async_computation.30 | async-start | bytes 3637248 | tf_op jit(solution)/shard_map/psum | solution.py:336
  1060.6 57.4 %copy-start.9 = (bf16[2,38,1536]{2,1,0:T(8,128)(2,1)S(1)}, bf16[2,38,1536]{2,1,0:T(8,128)(2,1)}, u32[]{:S(2)}) copy-start(bf16[2,38,1536]{2,1,0:T(8,128)(2,1)} %copy-done.7) | copy-start | bytes 700420
  1060.6 57.4 %copy-start.60 = (f32[2,1536]{1,0:T(2,128)S(1)}, f32[2,1536]{1,0:T(2,128)}, u32[]{:S(2)}) copy-start(f32[2,1536]{1,0:T(2,128)} %copy-done.59) | copy-start | bytes 36868
  1060.6 57.4 %copy-start.74 = (pred[2,38]{1,0:T(4,128)(4,1)S(1)}, pred[2,38]{1,0:T(4,128)(4,1)}, u32[]{:S(2)}) copy-start(pred[2,38]{1,0:T(4,128)(4,1)} %copy-done.72) | copy-start | bytes 232
  1060.6 57.4 %copy-start.88 = (f32[2,38]{1,0:T(2,128)S(1)}, f32[2,38]{1,0:T(2,128)}, u32[]{:S(2)}) copy-start(f32[2,38]{1,0:T(2,128)} %copy-done.87) | copy-start | bytes 916
  1060.6 58.6 %copy-start.114 = (f32[2,38]{1,0:T(2,128)S(1)}, f32[2,38]{1,0:T(2,128)}, u32[]{:S(2)}) copy-start(f32[2,38]{1,0:T(2,128)} %copy-done.113) | copy-start | bytes 916
  1060.6 58.6 %copy-start.4 = (bf16[2,256,1536]{2,1,0:T(8,128)(2,1)S(1)}, bf16[2,256,1536]{2,1,0:T(8,128)(2,1)}, u32[]{:S(2)}) copy-start(bf16[2,256,1536]{2,1,0:T(8,128)(2,1)} %param.23) | copy-start | bytes 4718596
  1060.7 58.6 %copy-start.67 = (f32[2,1536]{1,0:T(2,128)S(1)}, f32[2,1536]{1,0:T(2,128)}, u32[]{:S(2)}) copy-start(f32[2,1536]{1,0:T(2,128)} %copy-done.66) | copy-start | bytes 36868
  1060.7 58.6 %copy-start.86 = (f32[2,256]{1,0:T(2,128)S(1)}, f32[2,256]{1,0:T(2,128)}, u32[]{:S(2)}) copy-start(f32[2,256]{1,0:T(2,128)} %copy-done.85) | copy-start | bytes 6148
  1060.7 60.8 %copy-start.104 = (f32[2,256]{1,0:T(2,128)S(1)}, f32[2,256]{1,0:T(2,128)}, u32[]{:S(2)}) copy-start(f32[2,256]{1,0:T(2,128)} %copy-done.103) | copy-start | bytes 6148
  1060.7 124.8 %all-reduce.18.cloned.1.call-start = ((), (), s32[]{:S(2)}) async-start(), calls=%async_computation.26 | async-start | bytes 589824
  1062.6 60.7 %copy-start.92 = (f32[2,38]{1,0:T(2,128)S(1)}, f32[2,38]{1,0:T(2,128)}, u32[]{:S(2)}) copy-start(f32[2,38]{1,0:T(2,128)} %copy-done.91) | copy-start | bytes 916
  1062.6 61.1 %copy-start.106 = (f32[2,256]{1,0:T(2,128)S(1)}, f32[2,256]{1,0:T(2,128)}, u32[]{:S(2)}) copy-start(f32[2,256]{1,0:T(2,128)} %copy-done.105) | copy-start | bytes 6148
  1127.9 68.4 %reduce-scatter.11.cloned.1.call-start = ((), (), s32[]{:S(2)}) async-start(), calls=%async_computation.17 | async-start | bytes 2949120 | tf_op jit(solution)/shard_map/reduce_scatter | solution.py:382
  1133.0 99.6 %reduce-scatter.19.cloned.1.call-start = ((), (), s32[]{:S(2)}) async-start(), calls=%async_computation.21 | async-start | bytes 2949120 | tf_op jit(solution)/shard_map/reduce_scatter | solution.py:385
  1136.4 177.8 %reduce-scatter.15.cloned.1.call-start = ((), (), s32[]{:S(2)}) async-start(), calls=%async_computation.19 | async-start | bytes 11796480 | tf_op jit(solution)/shard_map/reduce_scatter | solution.py:394
  1146.9 248.7 %reduce-scatter.13.cloned.1.call-start = ((), (), s32[]{:S(2)}) async-start(), calls=%async_computation.18 | async-start | bytes 11796480 | tf_op jit(solution)/shard_map/reduce_scatter | solution.py:388
  1157.7 318.9 %reduce-scatter.21.cloned.1.call-start = ((), (), s32[]{:S(2)}) async-start(), calls=%async_computation.22 | async-start | bytes 11796480 | tf_op jit(solution)/shard_map/reduce_scatter | solution.py:391
  1164.2 393.5 %reduce-scatter.23.cloned.1.call-start = ((), (), s32[]{:S(2)}) async-start(), calls=%async_computation.23 | async-start | bytes 11796480 | tf_op jit(solution)/shard_map/reduce_scatter | solution.py:397
  1170.7 453.3 %reduce-scatter.9.cloned.1.call-start = ((), (), s32[]{:S(2)}) async-start(), calls=%async_computation.16 | async-start | bytes 8847360 | tf_op jit(solution)/shard_map/reduce_scatter | solution.py:376
  1179.4 510.8 %reduce-scatter.17.cloned.1.call-start = ((), (), s32[]{:S(2)}) async-start(), calls=%async_computation.20 | async-start | bytes 8847360 | tf_op jit(solution)/shard_map/reduce_scatter | solution.py:379
  1185.5 1001.7 %all-reduce.24.cloned.1.call-start = ((), (), s32[]{:S(2)}) async-start(), calls=%async_computation.29 | async-start | bytes 28901376 | tf_op jit(solution)/shard_map/psum | solution.py:422
  1187.2 503.1 %copy-start.53 = (bf16[2,8,6,1536]{3,1,2,0:T(8,128)(2,1)}, bf16[2,8,6,1536]{3,1,2,0:T(8,128)(2,1)S(1)}, u32[]{:S(2)}) copy-start(bf16[2,8,6,1536]{3,1,2,0:T(8,128)(2,1)S(1)} %convert_dynamic-update-slice_fusion) | copy-start | bytes 884740
  (97 other events, 686.9 us)
Sparse Core Ops, SparseCore 0:
  15.9 33.4 all-reduce.19
  51.0 51.6 all-gather.14
  104.4 50.8 all-gather.12
  164.7 31.1 all-gather.30
  197.9 31.1 all-gather.28
  230.6 24.0 all-gather.22
  256.4 24.0 all-gather.16
  304.9 56.9 all-reduce.29
  363.6 64.2 all-gather.24
  429.4 64.2 all-gather.26
  495.3 64.2 all-gather.18
  561.1 64.2 all-gather.20
  656.6 96.9 all-reduce.27
  911.4 135.1 all-reduce.21
  1060.8 57.1 all-reduce.25
  1128.0 32.2 all-reduce.17
  1163.3 33.0 reduce-scatter.10
  1199.5 33.0 reduce-scatter.18
  1235.8 78.3 reduce-scatter.14
  1317.2 78.4 reduce-scatter.12
  1398.2 78.4 reduce-scatter.20
  1479.3 78.3 reduce-scatter.22
  1560.2 63.7 reduce-scatter.8
  1626.5 63.7 reduce-scatter.16
  1694.6 492.4 all-reduce.23
where the time goes:
time: 2250 us; the launch traced here: 2240 us
  waiting for transfers between devices  1710 us (76%)
  matrix products  298 us (13%)
  other arithmetic  110 us (5%)
  local copies, waits for them, and re-layouts  78.3 us (3%)
    psum x1, waiting for transfers between devices, on_device(): lax.psum(mod_table.astype(jnp.bfloat16), 'rep').astype(jnp.float32)  464 us
    unnamed x27, waiting for transfers between devices  138 us
    psum x1, waiting for transfers between devices, on_device(): lax.psum(image_part.astype(jnp.bfloat16), 'head').astype(jnp.float32)  96.9 us
    reduce_scatter x1, waiting for transfers between devices, on_device(): lax.psum_scatter(image_g_down.astype(jnp.bfloat16), 'tok', scatter_dimens...  81.5 us
    reduce_scatter x1, waiting for transfers between devices, on_device(): lax.psum_scatter(image_g_up.astype(jnp.bfloat16), 'tok', scatter_dimensio...  81.5 us
    reduce_scatter x1, waiting for transfers between devices, on_device(): lax.psum_scatter(text_g_up.astype(jnp.bfloat16), 'tok', scatter_dimension...  81.1 us
    reduce_scatter x1, waiting for transfers between devices, on_device(): lax.psum_scatter(text_g_down.astype(jnp.bfloat16), 'tok', scatter_dimensi...  81 us
    reduce_scatter x1, waiting for transfers between devices, on_device(): lax.psum_scatter(image_g_qkv.astype(jnp.bfloat16), 'tok', scatter_dimensi...  66.3 us
  transfers between devices with their start and end apart: 25, of which 22 were waited for; matrix products, arithmetic and copies ran while one was open for 9% of the time, Pallas kernels for 0%

commit v1 on v0

--- a/solution.py
+++ b/solution.py
@@ -118,6 +118,131 @@
 def stream_squares(stream, gated_one, middle, gated_two, result):
     return jnp.stack(
         [jnp.sum(member * member) for member in (stream, gated_one, middle, gated_two, result)]
+    )
+
+
+def flip(values, axis, bit):
+    return lax.ppermute(
+        values, axis, [(place, place ^ bit) for place in range(lax.axis_size(axis))]
+    )
+
+
+def head_sum(partial):
+    if lax.axis_size("head") != 2:
+        return lax.psum(partial, "head").astype(jnp.float32)
+    return partial.astype(jnp.float32) + flip(partial, "head", 1).astype(jnp.float32)
+
+
+def gather_pair(first, second):
+    count = lax.axis_size("tok")
+    rank = lax.axis_index("tok")
+    parity = lax.rem(lax.axis_index("rep"), 2)
+    rows = first.shape[0]
+    entries = [(0, 0, first), (0, 1, second)]
+    fetched = [(0, jnp.where(parity == 0, first, second))]
+    bit = count // 2
+    while bit > 1:
+        fetched = fetched + [(away ^ bit, flip(part, "tok", bit)) for away, part in fetched]
+        bit //= 2
+    for away, part in fetched[1:]:
+        entries.append((away, parity, part))
+        entries.append((away, 1 - parity, flip(part, "rep", 1)))
+    entries = entries + [(away ^ 1, which, flip(part, "tok", 1)) for away, which, part in entries]
+    whole = jnp.zeros((2, rows * count) + first.shape[1:], first.dtype)
+    rest = (0,) * (first.ndim - 1)
+    for away, which, part in entries:
+        whole = lax.dynamic_update_slice(
+            whole, part[None], (which, jnp.bitwise_xor(rank, away) * rows) + rest
+        )
+    return whole[0], whole[1]
+
+
+def gather_rows(values, axis):
+    pieces = [values]
+    bit = lax.axis_size("tok") // 2
+    order = [0]
+    while bit > 0:
+        pieces = pieces + [flip(piece, "tok", bit) for piece in pieces]
+        order = order + [place ^ bit for place in order]
+        bit //= 2
+    by_distance = [pieces[order.index(away)] for away in range(len(order))]
+    return jnp.concatenate(by_distance, axis=axis)
+
+
+def halve(pieces):
+    bit = 1
+    while bit < lax.axis_size("tok"):
+        pieces = {
+            away: part.astype(jnp.float32)
+            + flip(pieces[away | bit].astype(jnp.bfloat16), "tok", bit).astype(jnp.float32)
+            for away, part in pieces.items()
+            if not away & bit
+        }
+        bit *= 2
+    return pieces[0]
+
+
+def scatter_tok(grad):
+    count = lax.axis_size("tok")
+    rank = lax.axis_index("tok")
+    rows = grad.shape[0] // count
+    return halve(
+        {
+            away: lax.dynamic_slice_in_dim(grad, jnp.bitwise_xor(rank, away) * rows, rows, axis=0)
+            for away in range(count)
+        }
+    )
+
+
+def line_sum(chunks):
+    if lax.axis_size("rep") != 4:
+        return [lax.psum(part.astype(jnp.bfloat16), "rep").astype(jnp.float32) for part in chunks]
+    rank = lax.axis_index("rep")
+    inner = (rank == 1) | (rank == 2)
+    chunks = [part.astype(jnp.bfloat16) for part in chunks]
+    outer_pairs = [(0, 1), (1, 0), (2, 3), (3, 2)]
+    total, moved = {}, {}
+    count = len(chunks)
+    for step in range(count + 2):
+        if step < count and step >= 2:
+            load = jnp.where(inner, total[step - 2], chunks[step])
+            pairs = outer_pairs
+        elif step < count:
+            load, pairs = chunks[step], [(0, 1), (3, 2)]
+        else:
+            load, pairs = total[step - 2], [(1, 0), (2, 3)]
+        moved[step] = lax.ppermute(load, "rep", pairs)
+        if step < count:
+            pair = chunks[step].astype(jnp.float32) + moved[step].astype(jnp.float32)
+            pair = pair.astype(jnp.bfloat16)
+            over = lax.ppermute(pair, "rep", [(1, 2), (2, 1)])
+            total[step] = (pair.astype(jnp.float32) + over.astype(jnp.float32)).astype(jnp.bfloat16)
+    return [
+        jnp.where(inner, total[step], moved[step + 2]).astype(jnp.float32) for step in range(count)
+    ]
+
+
+def tok_total(values):
+    bit = 1
+    while bit < lax.axis_size("tok"):
+        values = values + flip(values, "tok", bit)
+        bit *= 2
+    return values
+
+
+def rep_gather(values):
+    count = lax.axis_size("rep")
+    rank = lax.axis_index("rep")
+    pieces = values[None]
+    bit = 1
+    while bit < count:
+        pieces = jnp.concatenate([pieces, flip(pieces, "rep", bit)], axis=0)
+        bit *= 2
+    return jnp.stack(
+        [
+            lax.dynamic_index_in_dim(pieces, jnp.bitwise_xor(rank, place), 0, keepdims=False)
+            for place in range(count)
+        ]
     )
 
 
@@ -165,21 +290,21 @@
     activ_all = jax.nn.silu(cond_slots).astype(jnp.bfloat16)
     activ_group = lax.dynamic_slice_in_dim(activ_all, rep_rank * seq_group, seq_group, axis=0)
     activ_share = lax.dynamic_slice_in_dim(activ_group, tok_rank * row_share, row_share, axis=1)
-    image_mod, text_mod = lax.psum(
-        (
-            jnp.einsum("sd,dke->ske", activ_share, image_w_mod, preferred_element_type=jnp.float32),
-            jnp.einsum("sd,dke->ske", activ_share, text_w_mod, preferred_element_type=jnp.float32),
-        ),
-        "tok",
-    )
+    both_mod = tok_total(
+        jnp.stack(
+            [
+                jnp.einsum("sd,dke->ske", activ_share, weight, preferred_element_type=jnp.float32)
+                for weight in (image_w_mod, text_w_mod)
+            ]
+        )
+    )
+    image_mod, text_mod = both_mod[0], both_mod[1]
     image_mod = image_mod + image_b_mod.astype(jnp.float32)[None]
     text_mod = text_mod + text_b_mod.astype(jnp.float32)[None]
-    image_qkv, text_qkv, image_proj, text_proj = (
-        lax.all_gather(image_w_qkv, "tok", axis=0, tiled=True),
-        lax.all_gather(text_w_qkv, "tok", axis=0, tiled=True),
-        lax.all_gather(image_w_proj, "tok", axis=0, tiled=True),
-        lax.all_gather(text_w_proj, "tok", axis=0, tiled=True),
-    )
+    image_qkv, text_qkv = gather_pair(image_w_qkv, text_w_qkv)
+    image_proj, text_proj = gather_pair(image_w_proj, text_w_proj)
+    text_up, text_down = gather_pair(text_w_up, text_w_down)
+    image_up, image_down = gather_pair(image_w_up, image_w_down)
     image_hid_one = modulate(image_input, image_mod[:, 0], image_mod[:, 1]).astype(jnp.bfloat16)
     text_hid_one = modulate(text_input, text_mod[:, 0], text_mod[:, 1]).astype(jnp.bfloat16)
     projected = jnp.concatenate(
@@ -191,38 +316,26 @@
         ],
         axis=1,
     ).astype(jnp.bfloat16)
-    key_all, value_all = (
-        lax.all_gather(projected[:, :, 1], "tok", axis=1, tiled=True),
-        lax.all_gather(projected[:, :, 2], "tok", axis=1, tiled=True),
-    )
+    key_all = gather_rows(projected[:, :, 1], 1)
+    value_all = gather_rows(projected[:, :, 2], 1)
     key_total = key_all.shape[1]
     query_heads = projected[:, :, 0].reshape(seq_group, local_rows, head_count, HD)
     key_heads = key_all.reshape(seq_group, key_total, head_count, HD)
     value_heads = value_all.reshape(seq_group, key_total, head_count, HD)
     mixed_heads, row_max, row_total = lax.map(attend_one, (query_heads, key_heads, value_heads))
     mixed = mixed_heads.reshape(seq_group, local_rows, head_width)
-    image_branch, text_branch = (
-        lax.psum(
-            jnp.einsum(
-                "sqi,oi->sqo", mixed[:, :image_rows], image_proj, preferred_element_type=jnp.float32
-            ).astype(jnp.bfloat16),
-            "head",
-        ).astype(jnp.float32),
-        lax.psum(
-            jnp.einsum(
-                "sqi,oi->sqo", mixed[:, image_rows:], text_proj, preferred_element_type=jnp.float32
-            ).astype(jnp.bfloat16),
-            "head",
-        ).astype(jnp.float32),
+    image_branch = head_sum(
+        jnp.einsum(
+            "sqi,oi->sqo", mixed[:, :image_rows], image_proj, preferred_element_type=jnp.float32
+        ).astype(jnp.bfloat16)
+    )
+    text_branch = head_sum(
+        jnp.einsum(
+            "sqi,oi->sqo", mixed[:, image_rows:], text_proj, preferred_element_type=jnp.float32
+        ).astype(jnp.bfloat16)
     )
     image_middle = image_input + image_mod[:, 2][:, None, :] * image_branch
     text_middle = text_input + text_mod[:, 2][:, None, :] * text_branch
-    image_up, text_up, image_down, text_down = (
-        lax.all_gather(image_w_up, "tok", axis=0, tiled=True),
-        lax.all_gather(text_w_up, "tok", axis=0, tiled=True),
-        lax.all_gather(image_w_down, "tok", axis=0, tiled=True),
-        lax.all_gather(text_w_down, "tok", axis=0, tiled=True),
-    )
     image_hid_two, image_upward, image_activ, image_part = mlp_forward(
         image_middle, image_mod, image_up, image_down
     )
@@ -230,8 +343,8 @@
         text_middle, text_mod, text_up, text_down
     )
     image_branch_two, text_branch_two = (
-        lax.psum(image_part.astype(jnp.bfloat16), "head").astype(jnp.float32),
-        lax.psum(text_part.astype(jnp.bfloat16), "head").astype(jnp.float32),
+        head_sum(image_part.astype(jnp.bfloat16)),
+        head_sum(text_part.astype(jnp.bfloat16)),
     )
     image_result = image_middle + image_mod[:, 5][:, None, :] * image_branch_two
     text_result = text_middle + text_mod[:, 5][:, None, :] * text_branch_two
@@ -276,8 +389,8 @@
         text_down,
     )
     image_hid_grad, text_hid_grad = (
-        lax.psum(image_hid_part.astype(jnp.bfloat16), "head").astype(jnp.float32),
-        lax.psum(text_hid_part.astype(jnp.bfloat16), "head").astype(jnp.float32),
+        head_sum(image_hid_part.astype(jnp.bfloat16)),
+        head_sum(text_hid_part.astype(jnp.bfloat16)),
     )
     image_ln_grad, image_shift_two, image_scale_two = modulate_back(
         image_middle, image_mod, image_hid_grad, 3, 4
@@ -298,20 +411,17 @@
     query_grad, key_grad_all, value_grad_all = lax.map(
         query_side, (query_heads, key_heads, value_heads, grad_heads, row_max, row_total)
     )
-    key_grad, value_grad = (
-        lax.psum_scatter(
-            key_grad_all.reshape(seq_group, key_total, head_width).astype(jnp.bfloat16),
-            "tok",
-            scatter_dimension=1,
-            tiled=True,
-        ).astype(jnp.float32),
-        lax.psum_scatter(
-            value_grad_all.reshape(seq_group, key_total, head_width).astype(jnp.bfloat16),
-            "tok",
-            scatter_dimension=1,
-            tiled=True,
-        ).astype(jnp.float32),
-    )
+    key_grad, value_grad = [
+        halve(
+            {
+                away: whole.reshape(seq_group, key_total, head_width)[
+                    :, away * local_rows : (away + 1) * local_rows
+                ]
+                for away in range(tok_count)
+            }
+        )
+        for whole in (key_grad_all, value_grad_all)
+    ]
     qkv_grad = jnp.stack(
         [
             query_grad.reshape(seq_group, local_rows, head_width),
@@ -333,8 +443,8 @@
         "stke,dke->std", qkv_grad[:, image_rows:], text_qkv, preferred_element_type=jnp.float32
     )
     image_in_grad, text_in_grad = (
-        lax.psum(image_in_part.astype(jnp.bfloat16), "head").astype(jnp.float32),
-        lax.psum(text_in_part.astype(jnp.bfloat16), "head").astype(jnp.float32),
+        head_sum(image_in_part.astype(jnp.bfloat16)),
+        head_sum(text_in_part.astype(jnp.bfloat16)),
     )
     image_ln_one, image_shift_one, image_scale_one = modulate_back(
         image_input, image_mod, image_in_grad, 0, 1
@@ -344,87 +454,46 @@
     )
     image_grad = (image_mid_grad + image_ln_one).astype(jnp.bfloat16)
     text_grad = (text_mid_grad + text_ln_one).astype(jnp.bfloat16)
-    mod_partial = jnp.stack(
+    early = jnp.stack(
         [
-            jnp.stack(
-                [
-                    image_shift_one,
-                    image_scale_one,
-                    image_gate_one,
-                    image_shift_two,
-                    image_scale_two,
-                    image_gate_two,
-                ],
-                axis=1,
-            ),
-            jnp.stack(
-                [
-                    text_shift_one,
-                    text_scale_one,
-                    text_gate_one,
-                    text_shift_two,
-                    text_scale_two,
-                    text_gate_two,
-                ],
-                axis=1,
-            ),
+            jnp.stack([image_gate_one, image_shift_two, image_scale_two, image_gate_two], axis=1),
+            jnp.stack([text_gate_one, text_shift_two, text_scale_two, text_gate_two], axis=1),
         ]
     )
-    mod_copies = jnp.broadcast_to(mod_partial[None], (tok_count,) + mod_partial.shape)
-    square_copies = jnp.broadcast_to(square_partial[None], (tok_count, 10))
-    scattered = (
-        lax.psum_scatter(
-            image_g_qkv.astype(jnp.bfloat16), "tok", scatter_dimension=0, tiled=True
-        ).astype(jnp.float32),
-        lax.psum_scatter(
-            text_g_qkv.astype(jnp.bfloat16), "tok", scatter_dimension=0, tiled=True
-        ).astype(jnp.float32),
-        lax.psum_scatter(
-            image_g_proj.astype(jnp.bfloat16), "tok", scatter_dimension=0, tiled=True
-        ).astype(jnp.float32),
-        lax.psum_scatter(
-            text_g_proj.astype(jnp.bfloat16), "tok", scatter_dimension=0, tiled=True
-        ).astype(jnp.float32),
-        lax.psum_scatter(
-            image_g_up.astype(jnp.bfloat16), "tok", scatter_dimension=0, tiled=True
-        ).astype(jnp.float32),
-        lax.psum_scatter(
-            text_g_up.astype(jnp.bfloat16), "tok", scatter_dimension=0, tiled=True
-        ).astype(jnp.float32),
-        lax.psum_scatter(
-            image_g_down.astype(jnp.bfloat16), "tok", scatter_dimension=0, tiled=True
-        ).astype(jnp.float32),
-        lax.psum_scatter(
-            text_g_down.astype(jnp.bfloat16), "tok", scatter_dimension=0, tiled=True
-        ).astype(jnp.float32),
-        lax.psum_scatter(
-            mod_copies.astype(jnp.bfloat16), "tok", scatter_dimension=0, tiled=True
-        ).astype(jnp.float32),
-        lax.psum_scatter(
-            square_copies.astype(jnp.bfloat16), "tok", scatter_dimension=0, tiled=True
-        ).astype(jnp.float32),
-    )
-    mod_table = lax.dynamic_update_slice_in_dim(
-        jnp.zeros((2, slot_total, 6, width), jnp.float32),
-        scattered[8][0],
-        rep_rank * seq_group,
-        axis=1,
-    )
-    reduced = (
-        lax.psum(scattered[0].astype(jnp.bfloat16), "rep").astype(jnp.float32),
-        lax.psum(scattered[1].astype(jnp.bfloat16), "rep").astype(jnp.float32),
-        lax.psum(scattered[2].astype(jnp.bfloat16), "rep").astype(jnp.float32),
-        lax.psum(scattered[3].astype(jnp.bfloat16), "rep").astype(jnp.float32),
-        lax.psum(scattered[4].astype(jnp.bfloat16), "rep").astype(jnp.float32),
-        lax.psum(scattered[5].astype(jnp.bfloat16), "rep").astype(jnp.float32),
-        lax.psum(scattered[6].astype(jnp.bfloat16), "rep").astype(jnp.float32),
-        lax.psum(scattered[7].astype(jnp.bfloat16), "rep").astype(jnp.float32),
-        lax.psum(mod_table.astype(jnp.bfloat16), "rep").astype(jnp.float32),
-        lax.psum(scattered[9][0].astype(jnp.bfloat16), "rep").astype(jnp.float32),
-    )
-    weight_sums = reduced[:8]
-    mod_sum = reduced[8]
-    square_total = reduced[9]
+    late = jnp.stack(
+        [
+            jnp.stack([image_shift_one, image_scale_one], axis=1),
+            jnp.stack([text_shift_one, text_scale_one], axis=1),
+        ]
+    )
+    square_row = jnp.pad(square_partial, (0, width - 10))[None]
+    early_flat = jnp.concatenate([early.reshape(-1, width), square_row], axis=0)
+    early_all = rep_gather(tok_total(early_flat))
+    late_all = rep_gather(tok_total(late))
+    rep_count = lax.axis_size("rep")
+    square_total = jnp.sum(early_all[:, -1, :10], axis=0)
+    early_table = jnp.moveaxis(
+        early_all[:, :-1].reshape(rep_count, 2, seq_group, 4, width), 0, 1
+    ).reshape(2, slot_total, 4, width)
+    late_table = jnp.moveaxis(late_all, 0, 1).reshape(2, slot_total, 2, width)
+    mod_sum = jnp.concatenate([late_table, early_table], axis=2)
+    mlp_shares = [
+        scatter_tok(grad) for grad in (text_g_down, text_g_up, image_g_down, image_g_up)
+    ]
+    half = mlp_shares[0].shape[1] // 2
+    mlp_sums = line_sum(
+        [part for share in mlp_shares for part in (share[:, :half], share[:, half:])]
+    )
+    text_down_sum, text_up_sum, image_down_sum, image_up_sum = [
+        jnp.concatenate(mlp_sums[place : place + 2], axis=1) for place in (0, 2, 4, 6)
+    ]
+    text_proj_sum, image_proj_sum = line_sum(
+        [scatter_tok(text_g_proj), scatter_tok(image_g_proj)]
+    )
+    qkv_shares = [scatter_tok(text_g_qkv), scatter_tok(image_g_qkv)]
+    qkv_sums = line_sum([share[:, place] for share in qkv_shares for place in range(3)])
+    text_qkv_sum = jnp.stack(qkv_sums[:3], axis=1)
+    image_qkv_sum = jnp.stack(qkv_sums[3:], axis=1)
     activ_rows = lax.dynamic_slice_in_dim(
         activ_all, tok_rank * row_share, row_share, axis=1
     ).astype(jnp.float32)
@@ -453,16 +522,16 @@
         cond_grad,
         image_g_mod,
         image_g_bmod,
-        weight_sums[0],
-        weight_sums[2],
-        weight_sums[4],
-        weight_sums[6],
+        image_qkv_sum,
+        image_proj_sum,
+        image_up_sum,
+        image_down_sum,
         text_g_mod,
         text_g_bmod,
-        weight_sums[1],
-        weight_sums[3],
-        weight_sums[5],
-        weight_sums[7],
+        text_qkv_sum,
+        text_proj_sum,
+        text_up_sum,
+        text_down_sum,
         stream_rms,
     )
 

time: 2250 us -> 1650 us (0.73)
  waiting for transfers between devices: 1710 us -> 648 us
  starting transfers between devices: 2.09 us -> 216 us
  local copies, waits for them, and re-layouts: 78.3 us -> 255 us
  other arithmetic: 110 us -> 220 us
    psum x5 -> x0, waiting for transfers between devices: 695 us -> none  [the longest x1 464 us: on_device(): lax.psum(mod_table.astype(jnp.bfloat16), 'rep').astype(jnp.float32)]
    ppermute x0 -> x116, waiting for transfers between devices: none -> 648 us  [the longest x78 414 us: flip(): lax.ppermute(values, axis, [(place, place ^ bit) for place in range(lax.a...]
    reduce_scatter x8 -> x0, waiting for transfers between devices: 503 us -> none  [the longest x1 81.5 us: on_device(): lax.psum_scatter(image_g_down.astype(jnp.bfloat16), 'tok', scatter_dimens...]
    all_gather x10 -> x0, waiting for transfers between devices: 376 us -> none  [the longest x1 60.4 us: on_device(): lax.all_gather(text_w_up, 'tok', axis=0, tiled=True)]
    ppermute x0 -> x116, starting transfers between devices: none -> 216 us  [the longest x22 149 us: line_sum(): moved[step] = lax.ppermute(load, 'rep', pairs)]
    unnamed x27 -> x0, waiting for transfers between devices: 138 us -> none
    dynamic_update_slice x0 -> x32, local copies, waits for them, and re-layouts: none -> 64.2 us  [gather_pair(): lax.dynamic_update_slice(whole, part[None], (which, jnp.bitwise_xor(rank,...]
    another operation x5 -> x26, other arithmetic: 0.11 us -> 43.8 us  [the longest x1 0.1 us: on_device(): jnp.stack([jnp.stack([image_shift_one, image_scale_one, image_gate_one, i...]
  transfers between devices with their start and end apart: 25 -> 116, of which waited for: 22 -> 38; matrix products, arithmetic and copies ran while one was open for 9% -> 42% of each run, Pallas kernels for 0% -> 0%
where the time goes in v1:
time: 1650 us; the launch traced here: 1640 us
  waiting for transfers between devices  648 us (39%)
  matrix products  300 us (18%)
  local copies, waits for them, and re-layouts  255 us (15%)
  other arithmetic  220 us (13%)
  starting transfers between devices  216 us (13%)
    ppermute x78, waiting for transfers between devices, flip(): lax.ppermute(values, axis, [(place, place ^ bit) for place in range(lax.a...  414 us
    ppermute x22, waiting for transfers between devices, line_sum(): moved[step] = lax.ppermute(load, 'rep', pairs)  234 us
    ppermute x22, starting transfers between devices, line_sum(): moved[step] = lax.ppermute(load, 'rep', pairs)  149 us
    dynamic_update_slice x32, local copies, waits for them, and re-layouts, gather_pair(): lax.dynamic_update_slice(whole, part[None], (which, jnp.bitwise_xor(rank,...  64.2 us
    ppermute x78, starting transfers between devices, flip(): lax.ppermute(values, axis, [(place, place ^ bit) for place in range(lax.a...  54.9 us
    dot_general x4, matrix products, attention_scores(): jnp.einsum('qhe,khe->hqk', query_rows, key_rows, preferred_element_type=j...  52.7 us
    convert_element_type x10, other arithmetic, halve(): pieces[away | bit].astype(jnp.bfloat16)  43.1 us
    convert_element_type x10, local copies, waits for them, and re-layouts, halve(): pieces[away | bit].astype(jnp.bfloat16)  38.9 us
  transfers between devices with their start and end apart: 116, of which 38 were waited for; matrix products, arithmetic and copies ran while one was open for 42% of the time, Pallas kernels for 0%

profile of v1, /device:TPU:0, one launch (start us, length us, event | category | flops | bytes accessed | tf_op | source)
XLA Modules:
  0.0 1643.9 jit_solution(9750261139281470123)
XLA Ops:
  39.6 7.0 broadcast.232.clone
  52.3 6.8 broadcast.232.clone.1
  79.5 10.2 collective-permute-done.15
  114.9 11.6 collective-permute-done.21
  126.6 49.5 %collective-permute-done.29 = bf16[384,3072]{1,0:T(8,128)(2,1)} collective-permute-done((bf16[384,3072]{1,0:T(8,128)(2,1)}, bf16[384,3072]{1,0:T(8,128)(2,1)}, u32[]{:S(2)}, u32[]{:S(2)}) %collective-permute-start.29) | collective-permute-done | bytes 2359328 | tf_op jit(solution)/shard_map/ppermute | solution.py:125
  195.6 32.9 %collective-permute-done.22 = bf16[384,3072]{1,0:T(8,128)(2,1)} collective-permute-done((bf16[384,3072]{1,0:T(8,128)(2,1)}, bf16[384,3072]{1,0:T(8,128)(2,1)}, u32[]{:S(2)}, u32[]{:S(2)}) %collective-permute-start.22) | collective-permute-done | bytes 2359328 | tf_op jit(solution)/shard_map/ppermute | solution.py:125
  248.7 38.7 %collective-permute-done.30 = bf16[384,3072]{1,0:T(8,128)(2,1)} collective-permute-done((bf16[384,3072]{1,0:T(8,128)(2,1)}, bf16[384,3072]{1,0:T(8,128)(2,1)}, u32[]{:S(2)}, u32[]{:S(2)}) %collective-permute-start.30) | collective-permute-done | bytes 2359328 | tf_op jit(solution)/shard_map/ppermute | solution.py:125
  295.9 12.9 collective-permute-done.9
  320.4 8.9 collective-permute-done.12
  353.9 8.2 concatenate.85
  366.7 8.0 concatenate.90
  374.9 56.4 %while.28 = (s32[]{:T(128)}, bf16[2,294,12,64]{1,3,2,0:T(8,128)(2,1)S(1)}, f32[2,294,12]{1,2,0:T(8,128)S(1)}, f32[2,294,12]{1,2,0:T(8,128)S(1)}, bf16[2,1176,12,...) while((s32[]{:T(128)}, ...), condition=%wide.region_8.9_spmd, body=%wide.region_5.8_spmd.sunk | while | flops 1091386880 | bytes 56681408 | solution.py:325
  375.3 10.4 fusion.258
  385.7 8.9 fusion.259
  394.5 8.6 fusion.260
  403.2 10.4 fusion.258
  413.6 8.9 fusion.259
  422.4 8.6 fusion.260
  476.6 8.0 convolution_bitcast_fusion
  493.6 6.8 dynamic-slice_convert_fusion.1
  513.2 11.5 fusion.58
  524.7 12.3 fusion.92
  537.0 11.5 fusion.71
  548.5 7.8 fusion.93
  556.4 9.6 convolution_bitcast_fusion.3
  566.0 7.6 convolution_bitcast_fusion.2
  611.2 32.9 %collective-permute-done.36 = bf16[2,256,1536]{2,1,0:T(8,128)(2,1)} collective-permute-done((bf16[2,256,1536]{2,1,0:T(8,128)(2,1)S(1)}, bf16[2,256,1536]{2,1,0:T(8,128)(2,1)}, u32[]{:S(2)}, u32[]{:S(2)}) %collective-permute-start.36) | collective-permute-done | bytes 1572896 | tf_op jit(solution)/shard_map/ppermute | solution.py:125
  661.1 112.9 %while.29 = (s32[]{:T(128)}, bf16[2,294,12,64]{1,3,2,0:T(8,128)(2,1)}, f32[2,1176,12,64]{1,3,2,0:T(8,128)}, f32[2,1176,12,64]{1,3,2,0:T(8,128)}, bf16[2,1176,12,...) while((s32[]{:T(128)}, ...), condition=%wide.region_19.20_spmd, body=%wide.region_17.19_spmd.sunk | while | flops 2694005504 | bytes 166175760 | solution.py:411
  661.5 10.5 fusion.269
  672.0 16.0 multiply_reduce_fusion.18
  688.0 12.2 multiply_convert_fusion.13
  707.5 10.3 bitcast_dynamic-update-slice_fusion.41
  717.8 10.4 fusion.269
  728.2 16.0 multiply_reduce_fusion.18
  744.2 12.2 multiply_convert_fusion.13
  763.7 10.3 bitcast_dynamic-update-slice_fusion.41
  774.0 9.4 bitcast_convert_fusion
  876.8 15.1 collective-permute-done.40
  908.1 9.0 convolution_bitcast_fusion.5
  928.8 64.3 %collective-permute-done.91 = bf16[384,3072]{1,0:T(8,128)(2,1)} collective-permute-done((bf16[384,3072]{1,0:T(8,128)(2,1)}, bf16[384,3072]{1,0:T(8,128)(2,1)}, u32[]{:S(2)}, u32[]{:S(2)}) %collective-permute-start.91) | collective-permute-done | bytes 2359328 | tf_op jit(solution)/shard_map/ppermute | solution.py:125
  1018.8 13.1 collective-permute-done.79
  1034.0 22.2 %collective-permute-done.101 = bf16[384,1536]{1,0:T(8,128)(2,1)S(1)} collective-permute-done((bf16[384,1536]{1,0:T(8,128)(2,1)S(1)}, bf16[384,1536]{1,0:T(8,128)(2,1)S(1)}, u32[]{:S(2)}, u32[]{:S(2)}) %collective-permute-start.101) | collective-permute-done | bytes 1179680 | tf_op jit(solution)/shard_map/ppermute | solution.py:214
  1070.7 36.6 %collective-permute-done.85 = bf16[384,3072]{1,0:T(8,128)(2,1)S(1)} collective-permute-done((bf16[384,3072]{1,0:T(8,128)(2,1)S(1)}, bf16[384,3072]{1,0:T(8,128)(2,1)S(1)}, u32[]{:S(2)}, u32[]{:S(2)}) %collective-permute-start.85) | collective-permute-done | bytes 2359328 | tf_op jit(solution)/shard_map/ppermute | solution.py:125
  1144.1 43.5 %collective-permute-done.49 = f32[2,2,2,2,1536]{4,2,0,3,1:T(2,128)S(1)} collective-permute-done((f32[2,2,2,2,1536]{4,2,0,3,1:T(2,128)S(1)}, f32[2,2,2,2,1536]{4,2,0,3,1:T(2,128)S(1)}, u32[]{:S(2)}, u32[]{:S(2)}) %collective-permute-start.49) | collective-permute-done | bytes 98336 | tf_op jit(solution)/shard_map/ppermute | solution.py:125
  1192.9 13.8 collective-permute-done.53
  1212.2 7.8 convolution_bitcast_fusion.11
  1220.1 8.9 fusion.167
  1235.4 8.9 fusion.164
  1260.1 25.3 %collective-permute-done.56 = bf16[384,3,768]{2,0,1:T(8,128)(2,1)S(1)} collective-permute-done((bf16[384,3,768]{2,0,1:T(8,128)(2,1)S(1)}, bf16[384,3,768]{2,0,1:T(8,128)(2,1)S(1)}, u32[]{:S(2)}, u32[]{:S(2)}) %collective-permute-start.56) | collective-permute-done | bytes 1769504 | tf_op jit(solution)/shard_map/ppermute | solution.py:125
  1288.5 14.3 collective-permute-done.103
  1306.7 7.8 collective-permute-done.65
  1317.3 53.3 %collective-permute-start.67 = (bf16[384,768]{1,0:T(8,128)(2,1)S(1)}, bf16[384,768]{1,0:T(8,128)(2,1)S(1)}, u32[]{:S(2)}, u32[]{:S(2)}) collective-permute-start(bf16[384,768]{1,0:T(8,128)(2,1)S(1)} %broadcast_select_fusion.18), channel_id=1, source_target_pairs={{0,8},{8,0},{16,24},{24,16},{1,9},{9,1},{17,25},{25,17},{2,10},{10... | collective-permute-start | bytes 1769480 | tf_op jit(solution)/shard_map/ppermute | solution.py:214
  1373.7 11.1 collective-permute-done.67
  1389.8 12.5 collective-permute-start.62
  1402.3 7.8 collective-permute-done.96
  1410.1 25.3 %collective-permute-done.105 = bf16[384,1536]{1,0:T(8,128)(2,1)S(1)} collective-permute-done((bf16[384,1536]{1,0:T(8,128)(2,1)S(1)}, bf16[384,1536]{1,0:T(8,128)(2,1)S(1)}, u32[]{:S(2)}, u32[]{:S(2)}) %collective-permute-start.105) | collective-permute-done | bytes 1179680 | tf_op jit(solution)/shard_map/ppermute | solution.py:214
  1448.3 49.3 %collective-permute-start.69 = (bf16[384,768]{1,0:T(8,128)(2,1)S(1)}, bf16[384,768]{1,0:T(8,128)(2,1)S(1)}, u32[]{:S(2)}, u32[]{:S(2)}) collective-permute-start(bf16[384,768]{1,0:T(8,128)(2,1)S(1)} %get-tuple-element.337), channel_id=1, source_target_pairs={{0,8},{8,0},{16,24},{24,16},{1,9},{9,1},{17,25},{25,17},{2,10},{10... | collective-permute-start | bytes 1769480 | tf_op jit(solution)/shard_map/ppermute | solution.py:214
  1500.8 11.1 collective-permute-done.69
  1511.9 12.6 collective-permute-done.64
  1531.9 17.9 %collective-permute-done.98 = bf16[384,1536]{1,0:T(8,128)(2,1)S(1)} collective-permute-done((bf16[384,1536]{1,0:T(8,128)(2,1)S(1)}, bf16[384,1536]{1,0:T(8,128)(2,1)S(1)}, u32[]{:S(2)}, u32[]{:S(2)}) %collective-permute-start.98) | collective-permute-done | bytes 1179680 | tf_op jit(solution)/shard_map/ppermute | solution.py:214
  1549.8 25.3 %collective-permute-done.107 = bf16[384,1536]{1,0:T(8,128)(2,1)S(1)} collective-permute-done((bf16[384,1536]{1,0:T(8,128)(2,1)S(1)}, bf16[384,1536]{1,0:T(8,128)(2,1)S(1)}, u32[]{:S(2)}, u32[]{:S(2)}) %collective-permute-start.107) | collective-permute-done | bytes 1179680 | tf_op jit(solution)/shard_map/ppermute | solution.py:214
  1587.8 12.6 collective-permute-done.71
  1602.5 25.0 %collective-permute-done.109 = bf16[384,1536]{1,0:T(8,128)(2,1)S(1)} collective-permute-done((bf16[384,1536]{1,0:T(8,128)(2,1)S(1)}, bf16[384,1536]{1,0:T(8,128)(2,1)S(1)}, u32[]{:S(2)}, u32[]{:S(2)}) %collective-permute-start.109) | collective-permute-done | bytes 1179680 | tf_op jit(solution)/shard_map/ppermute | solution.py:214
  1627.7 13.0 collective-permute-done.100
  (721 shorter events, 606.4 us)
Async XLA Ops:
  0.7 76.3 %collective-permute-start.16 = (bf16[384,768]{1,0:T(8,128)(2,1)}, bf16[384,768]{1,0:T(8,128)(2,1)}, u32[]{:S(2)}, u32[]{:S(2)}) collective-permute-start(bf16[384,768]{1,0:T(8,128)(2,1)} %param.31), channel_id=1, source_target_pairs={{0,2},{2,0},{4,6},{6,4},{1,3},{3,1},{5,7},{7,5},{8,10},{10,8},{12,... | collective-permute-start | bytes 1769480 | tf_op jit(solution)/shard_map/ppermute | solution.py:125
  1.2 89.4 %collective-permute-start.17 = (bf16[384,768]{1,0:T(8,128)(2,1)}, bf16[384,768]{1,0:T(8,128)(2,1)}, u32[]{:S(2)}, u32[]{:S(2)}) collective-permute-start(bf16[384,768]{1,0:T(8,128)(2,1)} %param.37), channel_id=1, source_target_pairs={{0,2},{2,0},{4,6},{6,4},{1,3},{3,1},{5,7},{7,5},{8,10},{10,8},{12,... | collective-permute-start | bytes 1769480 | tf_op jit(solution)/shard_map/ppermute | solution.py:125
  3.2 71.5 %collective-permute-start.14 = (bf16[384,768]{1,0:T(8,128)(2,1)}, bf16[384,768]{1,0:T(8,128)(2,1)}, u32[]{:S(2)}, u32[]{:S(2)}) collective-permute-start(bf16[384,768]{1,0:T(8,128)(2,1)} %broadcast_select_fusion.21), channel_id=1, source_target_pairs={{0,4},{2,6},{4,0},{6,2},{1,5},{3,7},{5,1},{7,3},{8,12},{10,14},{12... | collective-permute-start | bytes 1769480 | tf_op jit(solution)/shard_map/ppermute | solution.py:125
  9.0 87.2 %collective-permute-start.2 = (bf16[384,3,768]{2,0,1:T(8,128)(2,1)}, bf16[384,3,768]{2,0,1:T(8,128)(2,1)}, u32[]{:S(2)}, u32[]{:S(2)}) collective-permute-start(bf16[384,3,768]{2,0,1:T(8,128)(2,1)} %broadcast_select_fusion.2), channel_id=1, source_target_pairs={{0,4},{2,6},{4,0},{6,2},{1,5},{3,7},{5,1},{7,3},{8,12},{10,14},{12... | collective-permute-start | bytes 5308424 | tf_op jit(solution)/shard_map/ppermute | solution.py:125
  16.7 48.7 %collective-permute-start = (f32[2,2,6,1536]{3,1,2,0:T(2,128)}, f32[2,2,6,1536]{3,1,2,0:T(2,128)S(1)}, u32[]{:S(2)}, u32[]{:S(2)}) collective-permute-start(f32[2,2,6,1536]{3,1,2,0:T(2,128)} %pad_maximum_fusion.8), channel_id=1, source_target_pairs={{0,2},{2,0},{4,6},{6,4},{1,3},{3,1},{5,7},{7,5},{8,10},{10,8},{12,... | collective-permute-start | bytes 442376 | tf_op jit(solution)/shard_map/ppermute | solution.py:125
  72.1 54.4 %collective-permute-start.21 = (bf16[384,3072]{1,0:T(8,128)(2,1)}, bf16[384,3072]{1,0:T(8,128)(2,1)}, u32[]{:S(2)}, u32[]{:S(2)}) collective-permute-start(bf16[384,3072]{1,0:T(8,128)(2,1)} %broadcast_select_fusion.1), channel_id=1, source_target_pairs={{0,4},{2,6},{4,0},{6,2},{1,5},{3,7},{5,1},{7,3},{8,12},{10,14},{12... | collective-permute-start | bytes 7077896 | tf_op jit(solution)/shard_map/ppermute | solution.py:125
  77.0 99.0 %collective-permute-start.29 = (bf16[384,3072]{1,0:T(8,128)(2,1)}, bf16[384,3072]{1,0:T(8,128)(2,1)}, u32[]{:S(2)}, u32[]{:S(2)}) collective-permute-start(bf16[384,3072]{1,0:T(8,128)(2,1)} %broadcast_select_fusion), channel_id=1, source_target_pairs={{0,4},{2,6},{4,0},{6,2},{1,5},{3,7},{5,1},{7,3},{8,12},{10,14},{12... | collective-permute-start | bytes 7077896 | tf_op jit(solution)/shard_map/ppermute | solution.py:125
  94.9 92.4 %collective-permute-start.4 = (bf16[384,3,768]{2,0,1:T(8,128)(2,1)}, bf16[384,3,768]{2,0,1:T(8,128)(2,1)}, u32[]{:S(2)}, u32[]{:S(2)}) collective-permute-start(bf16[384,3,768]{2,0,1:T(8,128)(2,1)} %param.30), channel_id=1, source_target_pairs={{0,2},{2,0},{4,6},{6,4},{1,3},{3,1},{5,7},{7,5},{8,10},{10,8},{12,... | collective-permute-start | bytes 5308424 | tf_op jit(solution)/shard_map/ppermute | solution.py:125
  95.8 95.0 %collective-permute-start.5 = (bf16[384,3,768]{2,0,1:T(8,128)(2,1)}, bf16[384,3,768]{2,0,1:T(8,128)(2,1)}, u32[]{:S(2)}, u32[]{:S(2)}) collective-permute-start(bf16[384,3,768]{2,0,1:T(8,128)(2,1)} %param.36), channel_id=1, source_target_pairs={{0,2},{2,0},{4,6},{6,4},{1,3},{3,1},{5,7},{7,5},{8,10},{10,8},{12,... | collective-permute-start | bytes 5308424 | tf_op jit(solution)/shard_map/ppermute | solution.py:125
  96.3 84.7 %collective-permute-start.3 = (bf16[384,3,768]{2,0,1:T(8,128)(2,1)}, bf16[384,3,768]{2,0,1:T(8,128)(2,1)}, u32[]{:S(2)}, u32[]{:S(2)}) collective-permute-start(bf16[384,3,768]{2,0,1:T(8,128)(2,1)} %collective-permute-done.2), channel_id=1, source_target_pairs={{0,8},{8,0},{16,24},{24,16},{1,9},{9,1},{17,25},{25,17},{2,10},{10... | collective-permute-start | bytes 5308424 | tf_op jit(solution)/shard_map/ppermute | solution.py:125
  126.6 67.3 %collective-permute-start.6 = (bf16[384,3,768]{2,0,1:T(8,128)(2,1)}, bf16[384,3,768]{2,0,1:T(8,128)(2,1)S(1)}, u32[]{:S(2)}, u32[]{:S(2)}) collective-permute-start(bf16[384,3,768]{2,0,1:T(8,128)(2,1)} %collective-permute-done.2), channel_id=1, source_target_pairs={{0,2},{2,0},{4,6},{6,4},{1,3},{3,1},{5,7},{7,5},{8,10},{10,8},{12,... | collective-permute-start | bytes 5308424 | tf_op jit(solution)/shard_map/ppermute | solution.py:125
  176.0 52.5 %collective-permute-start.22 = (bf16[384,3072]{1,0:T(8,128)(2,1)}, bf16[384,3072]{1,0:T(8,128)(2,1)}, u32[]{:S(2)}, u32[]{:S(2)}) collective-permute-start(bf16[384,3072]{1,0:T(8,128)(2,1)} %collective-permute-done.21), channel_id=1, source_target_pairs={{0,8},{8,0},{16,24},{24,16},{1,9},{9,1},{17,25},{25,17},{2,10},{10... | collective-permute-start | bytes 7077896 | tf_op jit(solution)/shard_map/ppermute | solution.py:125
  181.0 50.7 %collective-permute-start.23 = (bf16[384,3072]{1,0:T(8,128)(2,1)S(1)}, bf16[384,3072]{1,0:T(8,128)(2,1)S(1)}, u32[]{:S(2)}, u32[]{:S(2)}) collective-permute-start(bf16[384,3072]{1,0:T(8,128)(2,1)S(1)} %copy-done.28), channel_id=1, source_target_pairs={{0,2},{2,0},{4,6},{6,4},{1,3},{3,1},{5,7},{7,5},{8,10},{10,8},{12,... | collective-permute-start | bytes 7077896 | tf_op jit(solution)/shard_map/ppermute | solution.py:125
  187.3 46.6 %collective-permute-start.24 = (bf16[384,3072]{1,0:T(8,128)(2,1)S(1)}, bf16[384,3072]{1,0:T(8,128)(2,1)S(1)}, u32[]{:S(2)}, u32[]{:S(2)}) collective-permute-start(bf16[384,3072]{1,0:T(8,128)(2,1)S(1)} %copy-done.30), channel_id=1, source_target_pairs={{0,2},{2,0},{4,6},{6,4},{1,3},{3,1},{5,7},{7,5},{8,10},{10,8},{12,... | collective-permute-start | bytes 7077896 | tf_op jit(solution)/shard_map/ppermute | solution.py:125
  190.8 101.3 %collective-permute-start.31 = (bf16[384,3072]{1,0:T(8,128)(2,1)S(1)}, bf16[384,3072]{1,0:T(8,128)(2,1)S(1)}, u32[]{:S(2)}, u32[]{:S(2)}) collective-permute-start(bf16[384,3072]{1,0:T(8,128)(2,1)S(1)} %copy-done.32), channel_id=1, source_target_pairs={{0,2},{2,0},{4,6},{6,4},{1,3},{3,1},{5,7},{7,5},{8,10},{10,8},{12,... | collective-permute-start | bytes 7077896 | tf_op jit(solution)/shard_map/ppermute | solution.py:125
  193.8 101.5 %collective-permute-start.32 = (bf16[384,3072]{1,0:T(8,128)(2,1)S(1)}, bf16[384,3072]{1,0:T(8,128)(2,1)S(1)}, u32[]{:S(2)}, u32[]{:S(2)}) collective-permute-start(bf16[384,3072]{1,0:T(8,128)(2,1)S(1)} %copy-done.34), channel_id=1, source_target_pairs={{0,2},{2,0},{4,6},{6,4},{1,3},{3,1},{5,7},{7,5},{8,10},{10,8},{12,... | collective-permute-start | bytes 7077896 | tf_op jit(solution)/shard_map/ppermute | solution.py:125
  233.9 53.5 %collective-permute-start.30 = (bf16[384,3072]{1,0:T(8,128)(2,1)}, bf16[384,3072]{1,0:T(8,128)(2,1)}, u32[]{:S(2)}, u32[]{:S(2)}) collective-permute-start(bf16[384,3072]{1,0:T(8,128)(2,1)} %collective-permute-done.29), channel_id=1, source_target_pairs={{0,8},{8,0},{16,24},{24,16},{1,9},{9,1},{17,25},{25,17},{2,10},{10... | collective-permute-start | bytes 7077896 | tf_op jit(solution)/shard_map/ppermute | solution.py:125
  236.9 58.9 %collective-permute-start.33 = (bf16[384,3072]{1,0:T(8,128)(2,1)}, bf16[384,3072]{1,0:T(8,128)(2,1)S(1)}, u32[]{:S(2)}, u32[]{:S(2)}) collective-permute-start(bf16[384,3072]{1,0:T(8,128)(2,1)} %collective-permute-done.29), channel_id=1, source_target_pairs={{0,2},{2,0},{4,6},{6,4},{1,3},{3,1},{5,7},{7,5},{8,10},{10,8},{12,... | collective-permute-start | bytes 7077896 | tf_op jit(solution)/shard_map/ppermute | solution.py:125
  238.4 104.3 %collective-permute-start.26 = (bf16[384,3072]{1,0:T(8,128)(2,1)}, bf16[384,3072]{1,0:T(8,128)(2,1)}, u32[]{:S(2)}, u32[]{:S(2)}) collective-permute-start(bf16[384,3072]{1,0:T(8,128)(2,1)} %collective-permute-done.22), channel_id=1, source_target_pairs={{0,2},{2,0},{4,6},{6,4},{1,3},{3,1},{5,7},{7,5},{8,10},{10,8},{12,... | collective-permute-start | bytes 7077896 | tf_op jit(solution)/shard_map/ppermute | solution.py:125
  292.1 53.9 %collective-permute-start.34 = (bf16[384,3072]{1,0:T(8,128)(2,1)}, bf16[384,3072]{1,0:T(8,128)(2,1)}, u32[]{:S(2)}, u32[]{:S(2)}) collective-permute-start(bf16[384,3072]{1,0:T(8,128)(2,1)} %collective-permute-done.30), channel_id=1, source_target_pairs={{0,2},{2,0},{4,6},{6,4},{1,3},{3,1},{5,7},{7,5},{8,10},{10,8},{12,... | collective-permute-start | bytes 7077896 | tf_op jit(solution)/shard_map/ppermute | solution.py:125
  440.5 69.3 %collective-permute-start.20 = (bf16[2,256,1536]{2,1,0:T(8,128)(2,1)}, bf16[2,256,1536]{2,1,0:T(8,128)(2,1)}, u32[]{:S(2)}, u32[]{:S(2)}) collective-permute-start(bf16[2,256,1536]{2,1,0:T(8,128)(2,1)} %convolution_convert_fusion), channel_id=1, source_target_pairs={{0,1},{1,0},{2,3},{3,2},{4,5},{5,4},{6,7},{7,6},{8,9},{9,8},{10,11... | collective-permute-start | bytes 4718600 | tf_op jit(solution)/shard_map/ppermute | solution.py:125
  476.6 118.1 %collective-permute-start.87 = (bf16[384,3072]{1,0:T(8,128)(2,1)}, bf16[384,3072]{1,0:T(8,128)(2,1)}, u32[]{:S(2)}, u32[]{:S(2)}) collective-permute-start(bf16[384,3072]{1,0:T(8,128)(2,1)} %get-tuple-element.291), channel_id=1, source_target_pairs={{0,2},{2,0},{4,6},{6,4},{1,3},{3,1},{5,7},{7,5},{8,10},{10,8},{12,... | collective-permute-start | bytes 7077896 | tf_op jit(solution)/shard_map/ppermute | solution.py:125
  500.4 100.0 %collective-permute-start.90 = (bf16[384,3072]{1,0:T(8,128)(2,1)}, bf16[384,3072]{1,0:T(8,128)(2,1)}, u32[]{:S(2)}, u32[]{:S(2)}) collective-permute-start(bf16[384,3072]{1,0:T(8,128)(2,1)} %get-tuple-element.289), channel_id=1, source_target_pairs={{0,2},{2,0},{4,6},{6,4},{1,3},{3,1},{5,7},{7,5},{8,10},{10,8},{12,... | collective-permute-start | bytes 7077896 | tf_op jit(solution)/shard_map/ppermute | solution.py:125
  506.3 68.4 %collective-permute-start.110 = (bf16[384,768]{1,0:T(8,128)(2,1)}, bf16[384,768]{1,0:T(8,128)(2,1)}, u32[]{:S(2)}, u32[]{:S(2)}) collective-permute-start(bf16[384,768]{1,0:T(8,128)(2,1)} %get-tuple-element.306), channel_id=1, source_target_pairs={{0,2},{2,0},{4,6},{6,4},{1,3},{3,1},{5,7},{7,5},{8,10},{10,8},{12,... | collective-permute-start | bytes 1769480 | tf_op jit(solution)/shard_map/ppermute | solution.py:125
  507.9 67.8 %collective-permute-start.112 = (bf16[384,768]{1,0:T(8,128)(2,1)S(1)}, bf16[384,768]{1,0:T(8,128)(2,1)S(1)}, u32[]{:S(2)}, u32[]{:S(2)}) collective-permute-start(bf16[384,768]{1,0:T(8,128)(2,1)S(1)} %add_convert_fusion.35), channel_id=1, source_target_pairs={{0,4},{2,6},{4,0},{6,2},{1,5},{3,7},{5,1},{7,3},{8,12},{10,14},{12... | collective-permute-start | bytes 1769480 | tf_op jit(solution)/shard_map/ppermute | solution.py:125
  574.7 69.3 %collective-permute-start.36 = (bf16[2,256,1536]{2,1,0:T(8,128)(2,1)S(1)}, bf16[2,256,1536]{2,1,0:T(8,128)(2,1)}, u32[]{:S(2)}, u32[]{:S(2)}) collective-permute-start(bf16[2,256,1536]{2,1,0:T(8,128)(2,1)S(1)} %fusion.93), channel_id=1, source_target_pairs={{0,1},{1,0},{2,3},{3,2},{4,5},{5,4},{6,7},{7,6},{8,9},{9,8},{10,11... | collective-permute-start | bytes 4718600 | tf_op jit(solution)/shard_map/ppermute | solution.py:125
  594.5 220.1 %collective-permute-start.81 = (bf16[384,3072]{1,0:T(8,128)(2,1)}, bf16[384,3072]{1,0:T(8,128)(2,1)}, u32[]{:S(2)}, u32[]{:S(2)}) collective-permute-start(bf16[384,3072]{1,0:T(8,128)(2,1)} %get-tuple-element.295), channel_id=1, source_target_pairs={{0,2},{2,0},{4,6},{6,4},{1,3},{3,1},{5,7},{7,5},{8,10},{10,8},{12,... | collective-permute-start | bytes 7077896 | tf_op jit(solution)/shard_map/ppermute | solution.py:125
  594.7 259.4 %collective-permute-start.84 = (bf16[384,3072]{1,0:T(8,128)(2,1)}, bf16[384,3072]{1,0:T(8,128)(2,1)}, u32[]{:S(2)}, u32[]{:S(2)}) collective-permute-start(bf16[384,3072]{1,0:T(8,128)(2,1)} %get-tuple-element.293), channel_id=1, source_target_pairs={{0,2},{2,0},{4,6},{6,4},{1,3},{3,1},{5,7},{7,5},{8,10},{10,8},{12,... | collective-permute-start | bytes 7077896 | tf_op jit(solution)/shard_map/ppermute | solution.py:125
  607.6 201.8 %collective-permute-start.115 = (bf16[384,768]{1,0:T(8,128)(2,1)}, bf16[384,768]{1,0:T(8,128)(2,1)}, u32[]{:S(2)}, u32[]{:S(2)}) collective-permute-start(bf16[384,768]{1,0:T(8,128)(2,1)} %add_convert_fusion.32), channel_id=1, source_target_pairs={{8,0},{16,24},{9,1},{17,25},{10,2},{18,26},{11,3},{19,27},{12,4},{... | collective-permute-start | bytes 1769480 | tf_op jit(solution)/shard_map/ppermute | solution.py:214
  809.3 63.0 %collective-permute-start.41 = (bf16[2,294,768]{2,0,1:T(2,128)(2,1)}, bf16[2,294,768]{2,0,1:T(2,128)(2,1)}, u32[]{:S(2)}, u32[]{:S(2)}) collective-permute-start(bf16[2,294,768]{2,0,1:T(2,128)(2,1)} %copy.167), channel_id=1, source_target_pairs={{0,2},{2,0},{4,6},{6,4},{1,3},{3,1},{5,7},{7,5},{8,10},{10,8},{12,... | collective-permute-start | bytes 2709512 | tf_op jit(solution)/shard_map/ppermute | solution.py:125
  870.9 128.3 %collective-permute-start.86 = (bf16[384,3072]{1,0:T(8,128)(2,1)}, bf16[384,3072]{1,0:T(8,128)(2,1)}, u32[]{:S(2)}, u32[]{:S(2)}) collective-permute-start(bf16[384,3072]{1,0:T(8,128)(2,1)} %get-tuple-element.290), channel_id=1, source_target_pairs={{0,2},{2,0},{4,6},{6,4},{1,3},{3,1},{5,7},{7,5},{8,10},{10,8},{12,... | collective-permute-start | bytes 7077896 | tf_op jit(solution)/shard_map/ppermute | solution.py:125
  872.3 56.1 %collective-permute-start.89 = (bf16[384,3072]{1,0:T(8,128)(2,1)}, bf16[384,3072]{1,0:T(8,128)(2,1)}, u32[]{:S(2)}, u32[]{:S(2)}) collective-permute-start(bf16[384,3072]{1,0:T(8,128)(2,1)} %get-tuple-element.288), channel_id=1, source_target_pairs={{0,2},{2,0},{4,6},{6,4},{1,3},{3,1},{5,7},{7,5},{8,10},{10,8},{12,... | collective-permute-start | bytes 7077896 | tf_op jit(solution)/shard_map/ppermute | solution.py:125
  872.9 187.2 %collective-permute-start.80 = (bf16[384,3072]{1,0:T(8,128)(2,1)}, bf16[384,3072]{1,0:T(8,128)(2,1)}, u32[]{:S(2)}, u32[]{:S(2)}) collective-permute-start(bf16[384,3072]{1,0:T(8,128)(2,1)} %get-tuple-element.294), channel_id=1, source_target_pairs={{0,2},{2,0},{4,6},{6,4},{1,3},{3,1},{5,7},{7,5},{8,10},{10,8},{12,... | collective-permute-start | bytes 7077896 | tf_op jit(solution)/shard_map/ppermute | solution.py:125
  875.3 125.1 %collective-permute-start.88 = (bf16[384,3072]{1,0:T(8,128)(2,1)S(1)}, bf16[384,3072]{1,0:T(8,128)(2,1)}, u32[]{:S(2)}, u32[]{:S(2)}) collective-permute-start(bf16[384,3072]{1,0:T(8,128)(2,1)S(1)} %copy-done.49), channel_id=1, source_target_pairs={{0,4},{2,6},{4,0},{6,2},{1,5},{3,7},{5,1},{7,3},{8,12},{10,14},{12... | collective-permute-start | bytes 7077896 | tf_op jit(solution)/shard_map/ppermute | solution.py:125
  892.0 101.1 %collective-permute-start.91 = (bf16[384,3072]{1,0:T(8,128)(2,1)}, bf16[384,3072]{1,0:T(8,128)(2,1)}, u32[]{:S(2)}, u32[]{:S(2)}) collective-permute-start(bf16[384,3072]{1,0:T(8,128)(2,1)} %add_convert_fusion.1), channel_id=1, source_target_pairs={{0,4},{2,6},{4,0},{6,2},{1,5},{3,7},{5,1},{7,3},{8,12},{10,14},{12... | collective-permute-start | bytes 7077896 | tf_op jit(solution)/shard_map/ppermute | solution.py:125
  928.4 131.6 %collective-permute-start.82 = (bf16[384,3072]{1,0:T(8,128)(2,1)}, bf16[384,3072]{1,0:T(8,128)(2,1)S(1)}, u32[]{:S(2)}, u32[]{:S(2)}) collective-permute-start(bf16[384,3072]{1,0:T(8,128)(2,1)} %add_convert_fusion.7), channel_id=1, source_target_pairs={{0,4},{2,6},{4,0},{6,2},{1,5},{3,7},{5,1},{7,3},{8,12},{10,14},{12... | collective-permute-start | bytes 7077896 | tf_op jit(solution)/shard_map/ppermute | solution.py:125
  1013.1 43.1 %collective-permute-start.101 = (bf16[384,1536]{1,0:T(8,128)(2,1)S(1)}, bf16[384,1536]{1,0:T(8,128)(2,1)S(1)}, u32[]{:S(2)}, u32[]{:S(2)}) collective-permute-start(bf16[384,1536]{1,0:T(8,128)(2,1)S(1)} %get-tuple-element.334), channel_id=1, source_target_pairs={{0,8},{24,16},{1,9},{25,17},{2,10},{26,18},{3,11},{27,19},{4,12},{... | collective-permute-start | bytes 3538952 | tf_op jit(solution)/shard_map/ppermute | solution.py:214
  1056.2 51.0 %collective-permute-start.85 = (bf16[384,3072]{1,0:T(8,128)(2,1)S(1)}, bf16[384,3072]{1,0:T(8,128)(2,1)S(1)}, u32[]{:S(2)}, u32[]{:S(2)}) collective-permute-start(bf16[384,3072]{1,0:T(8,128)(2,1)S(1)} %copy-done.50), channel_id=1, source_target_pairs={{0,4},{2,6},{4,0},{6,2},{1,5},{3,7},{5,1},{7,3},{8,12},{10,14},{12... | collective-permute-start | bytes 7077896 | tf_op jit(solution)/shard_map/ppermute | solution.py:125
  1060.0 69.1 %collective-permute-start.55 = (bf16[384,3,768]{2,0,1:T(8,128)(2,1)}, bf16[384,3,768]{2,0,1:T(8,128)(2,1)}, u32[]{:S(2)}, u32[]{:S(2)}) collective-permute-start(bf16[384,3,768]{2,0,1:T(8,128)(2,1)} %get-tuple-element.299), channel_id=1, source_target_pairs={{0,2},{2,0},{4,6},{6,4},{1,3},{3,1},{5,7},{7,5},{8,10},{10,8},{12,... | collective-permute-start | bytes 5308424 | tf_op jit(solution)/shard_map/ppermute | solution.py:125
  1060.1 198.5 %collective-permute-start.54 = (bf16[384,3,768]{2,0,1:T(8,128)(2,1)}, bf16[384,3,768]{2,0,1:T(8,128)(2,1)}, u32[]{:S(2)}, u32[]{:S(2)}) collective-permute-start(bf16[384,3,768]{2,0,1:T(8,128)(2,1)} %get-tuple-element.298), channel_id=1, source_target_pairs={{0,2},{2,0},{4,6},{6,4},{1,3},{3,1},{5,7},{7,5},{8,10},{10,8},{12,... | collective-permute-start | bytes 5308424 | tf_op jit(solution)/shard_map/ppermute | solution.py:125
  1066.1 68.1 %collective-permute-start.58 = (bf16[384,3,768]{2,0,1:T(8,128)(2,1)}, bf16[384,3,768]{2,0,1:T(8,128)(2,1)}, u32[]{:S(2)}, u32[]{:S(2)}) collective-permute-start(bf16[384,3,768]{2,0,1:T(8,128)(2,1)} %get-tuple-element.297), channel_id=1, source_target_pairs={{0,2},{2,0},{4,6},{6,4},{1,3},{3,1},{5,7},{7,5},{8,10},{10,8},{12,... | collective-permute-start | bytes 5308424 | tf_op jit(solution)/shard_map/ppermute | solution.py:125
  1128.1 122.1 %collective-permute-start.57 = (bf16[384,3,768]{2,0,1:T(8,128)(2,1)}, bf16[384,3,768]{2,0,1:T(8,128)(2,1)}, u32[]{:S(2)}, u32[]{:S(2)}) collective-permute-start(bf16[384,3,768]{2,0,1:T(8,128)(2,1)} %get-tuple-element.296), channel_id=1, source_target_pairs={{0,2},{2,0},{4,6},{6,4},{1,3},{3,1},{5,7},{7,5},{8,10},{10,8},{12,... | collective-permute-start | bytes 5308424 | tf_op jit(solution)/shard_map/ppermute | solution.py:125
  1128.3 116.0 %collective-permute-start.93 = (bf16[384,1536]{1,0:T(8,128)(2,1)}, bf16[384,1536]{1,0:T(8,128)(2,1)S(1)}, u32[]{:S(2)}, u32[]{:S(2)}) collective-permute-start(bf16[384,1536]{1,0:T(8,128)(2,1)} %get-tuple-element.331), channel_id=1, source_target_pairs={{8,16},{16,8},{9,17},{17,9},{10,18},{18,10},{11,19},{19,11},{12,20... | collective-permute-start | bytes 3538952 | tf_op jit(solution)/shard_map/ppermute | solution.py:218
  1129.2 118.4 %collective-permute-start.102 = (bf16[384,1536]{1,0:T(8,128)(2,1)}, bf16[384,1536]{1,0:T(8,128)(2,1)S(1)}, u32[]{:S(2)}, u32[]{:S(2)}) collective-permute-start(bf16[384,1536]{1,0:T(8,128)(2,1)} %get-tuple-element.332), channel_id=1, source_target_pairs={{8,16},{16,8},{9,17},{17,9},{10,18},{18,10},{11,19},{19,11},{12,20... | collective-permute-start | bytes 3538952 | tf_op jit(solution)/shard_map/ppermute | solution.py:218
  1140.3 47.3 %collective-permute-start.49 = (f32[2,2,2,2,1536]{4,2,0,3,1:T(2,128)S(1)}, f32[2,2,2,2,1536]{4,2,0,3,1:T(2,128)S(1)}, u32[]{:S(2)}, u32[]{:S(2)}) collective-permute-start(f32[2,2,2,2,1536]{4,2,0,3,1:T(2,128)S(1)} %pad_maximum_fusion.9), channel_id=1, source_target_pairs={{0,16},{8,24},{16,0},{24,8},{1,17},{9,25},{17,1},{25,9},{2,18},{10... | collective-permute-start | bytes 294920 | tf_op jit(solution)/shard_map/ppermute | solution.py:125
  1206.7 46.1 %collective-permute-start.59 = (bf16[384,3,768]{2,0,1:T(8,128)(2,1)}, bf16[384,3,768]{2,0,1:T(8,128)(2,1)}, u32[]{:S(2)}, u32[]{:S(2)}) collective-permute-start(bf16[384,3,768]{2,0,1:T(8,128)(2,1)} %add_convert_fusion.9), channel_id=1, source_target_pairs={{0,4},{2,6},{4,0},{6,2},{1,5},{3,7},{5,1},{7,3},{8,12},{10,14},{12... | collective-permute-start | bytes 5308424 | tf_op jit(solution)/shard_map/ppermute | solution.py:125
  1250.2 52.6 %collective-permute-start.103 = (bf16[384,1536]{1,0:T(8,128)(2,1)S(1)}, bf16[384,1536]{1,0:T(8,128)(2,1)S(1)}, u32[]{:S(2)}, u32[]{:S(2)}) collective-permute-start(bf16[384,1536]{1,0:T(8,128)(2,1)S(1)} %get-tuple-element.330), channel_id=1, source_target_pairs={{0,8},{8,0},{16,24},{24,16},{1,9},{9,1},{17,25},{25,17},{2,10},{10... | collective-permute-start | bytes 3538952 | tf_op jit(solution)/shard_map/ppermute | solution.py:214
  1256.5 58.0 %collective-permute-start.65 = (bf16[384,768]{1,0:T(8,128)(2,1)S(1)}, bf16[384,768]{1,0:T(8,128)(2,1)S(1)}, u32[]{:S(2)}, u32[]{:S(2)}) collective-permute-start(bf16[384,768]{1,0:T(8,128)(2,1)S(1)} %get-tuple-element.341), channel_id=1, source_target_pairs={{0,8},{24,16},{1,9},{25,17},{2,10},{26,18},{3,11},{27,19},{4,12},{... | collective-permute-start | bytes 1769480 | tf_op jit(solution)/shard_map/ppermute | solution.py:214
  1258.5 115.2 %collective-permute-start.60 = (bf16[384,768]{1,0:T(8,128)(2,1)S(1)}, bf16[384,768]{1,0:T(8,128)(2,1)S(1)}, u32[]{:S(2)}, u32[]{:S(2)}) collective-permute-start(bf16[384,768]{1,0:T(8,128)(2,1)S(1)} %get-tuple-element.342), channel_id=1, source_target_pairs={{0,8},{24,16},{1,9},{25,17},{2,10},{26,18},{3,11},{27,19},{4,12},{... | collective-permute-start | bytes 1769480 | tf_op jit(solution)/shard_map/ppermute | solution.py:214
  1303.5 67.1 %collective-permute-start.95 = (bf16[384,1536]{1,0:T(8,128)(2,1)S(1)}, bf16[384,1536]{1,0:T(8,128)(2,1)S(1)}, u32[]{:S(2)}, u32[]{:S(2)}) collective-permute-start(bf16[384,1536]{1,0:T(8,128)(2,1)S(1)} %get-tuple-element.327), channel_id=1, source_target_pairs={{8,16},{16,8},{9,17},{17,9},{10,18},{18,10},{11,19},{19,11},{12,20... | collective-permute-start | bytes 3538952 | tf_op jit(solution)/shard_map/ppermute | solution.py:218
  1304.2 66.4 %collective-permute-start.104 = (bf16[384,1536]{1,0:T(8,128)(2,1)S(1)}, bf16[384,1536]{1,0:T(8,128)(2,1)S(1)}, u32[]{:S(2)}, u32[]{:S(2)}) collective-permute-start(bf16[384,1536]{1,0:T(8,128)(2,1)S(1)} %get-tuple-element.328), channel_id=1, source_target_pairs={{8,16},{16,8},{9,17},{17,9},{10,18},{18,10},{11,19},{19,11},{12,20... | collective-permute-start | bytes 3538952 | tf_op jit(solution)/shard_map/ppermute | solution.py:218
  1317.3 67.5 %collective-permute-start.67 = (bf16[384,768]{1,0:T(8,128)(2,1)S(1)}, bf16[384,768]{1,0:T(8,128)(2,1)S(1)}, u32[]{:S(2)}, u32[]{:S(2)}) collective-permute-start(bf16[384,768]{1,0:T(8,128)(2,1)S(1)} %broadcast_select_fusion.18), channel_id=1, source_target_pairs={{0,8},{8,0},{16,24},{24,16},{1,9},{9,1},{17,25},{25,17},{2,10},{10... | collective-permute-start | bytes 1769480 | tf_op jit(solution)/shard_map/ppermute | solution.py:214
  1371.7 63.7 %collective-permute-start.105 = (bf16[384,1536]{1,0:T(8,128)(2,1)S(1)}, bf16[384,1536]{1,0:T(8,128)(2,1)S(1)}, u32[]{:S(2)}, u32[]{:S(2)}) collective-permute-start(bf16[384,1536]{1,0:T(8,128)(2,1)S(1)} %get-tuple-element.326), channel_id=1, source_target_pairs={{0,8},{8,0},{16,24},{24,16},{1,9},{9,1},{17,25},{25,17},{2,10},{10... | collective-permute-start | bytes 3538952 | tf_op jit(solution)/shard_map/ppermute | solution.py:214
  1388.6 59.2 %collective-permute-start.68 = (bf16[384,768]{1,0:T(8,128)(2,1)S(1)}, bf16[384,768]{1,0:T(8,128)(2,1)S(1)}, u32[]{:S(2)}, u32[]{:S(2)}) collective-permute-start(bf16[384,768]{1,0:T(8,128)(2,1)S(1)} %get-tuple-element.339), channel_id=1, source_target_pairs={{8,16},{16,8},{9,17},{17,9},{10,18},{18,10},{11,19},{19,11},{12,20... | collective-permute-start | bytes 1769480 | tf_op jit(solution)/shard_map/ppermute | solution.py:218
  1389.8 54.1 %collective-permute-start.62 = (bf16[384,768]{1,0:T(8,128)(2,1)S(1)}, bf16[384,768]{1,0:T(8,128)(2,1)S(1)}, u32[]{:S(2)}, u32[]{:S(2)}) collective-permute-start(bf16[384,768]{1,0:T(8,128)(2,1)S(1)} %broadcast_select_fusion.20), channel_id=1, source_target_pairs={{0,8},{8,0},{16,24},{24,16},{1,9},{9,1},{17,25},{25,17},{2,10},{10... | collective-permute-start | bytes 1769480 | tf_op jit(solution)/shard_map/ppermute | solution.py:214
  1436.0 61.7 %collective-permute-start.97 = (bf16[384,1536]{1,0:T(8,128)(2,1)S(1)}, bf16[384,1536]{1,0:T(8,128)(2,1)S(1)}, u32[]{:S(2)}, u32[]{:S(2)}) collective-permute-start(bf16[384,1536]{1,0:T(8,128)(2,1)S(1)} %get-tuple-element.323), channel_id=1, source_target_pairs={{8,16},{16,8},{9,17},{17,9},{10,18},{18,10},{11,19},{19,11},{12,20... | collective-permute-start | bytes 3538952 | tf_op jit(solution)/shard_map/ppermute | solution.py:218
  1436.8 60.9 %collective-permute-start.106 = (bf16[384,1536]{1,0:T(8,128)(2,1)S(1)}, bf16[384,1536]{1,0:T(8,128)(2,1)S(1)}, u32[]{:S(2)}, u32[]{:S(2)}) collective-permute-start(bf16[384,1536]{1,0:T(8,128)(2,1)S(1)} %get-tuple-element.324), channel_id=1, source_target_pairs={{8,16},{16,8},{9,17},{17,9},{10,18},{18,10},{11,19},{19,11},{12,20... | collective-permute-start | bytes 3538952 | tf_op jit(solution)/shard_map/ppermute | solution.py:218
  1448.3 63.6 %collective-permute-start.69 = (bf16[384,768]{1,0:T(8,128)(2,1)S(1)}, bf16[384,768]{1,0:T(8,128)(2,1)S(1)}, u32[]{:S(2)}, u32[]{:S(2)}) collective-permute-start(bf16[384,768]{1,0:T(8,128)(2,1)S(1)} %get-tuple-element.337), channel_id=1, source_target_pairs={{0,8},{8,0},{16,24},{24,16},{1,9},{9,1},{17,25},{25,17},{2,10},{10... | collective-permute-start | bytes 1769480 | tf_op jit(solution)/shard_map/ppermute | solution.py:214
  1498.7 51.1 %collective-permute-start.98 = (bf16[384,1536]{1,0:T(8,128)(2,1)S(1)}, bf16[384,1536]{1,0:T(8,128)(2,1)S(1)}, u32[]{:S(2)}, u32[]{:S(2)}) collective-permute-start(bf16[384,1536]{1,0:T(8,128)(2,1)S(1)} %get-tuple-element.321), channel_id=1, source_target_pairs={{0,8},{8,0},{16,24},{24,16},{1,9},{9,1},{17,25},{25,17},{2,10},{10... | collective-permute-start | bytes 3538952 | tf_op jit(solution)/shard_map/ppermute | solution.py:214
  1500.8 74.3 %collective-permute-start.107 = (bf16[384,1536]{1,0:T(8,128)(2,1)S(1)}, bf16[384,1536]{1,0:T(8,128)(2,1)S(1)}, u32[]{:S(2)}, u32[]{:S(2)}) collective-permute-start(bf16[384,1536]{1,0:T(8,128)(2,1)S(1)} %get-tuple-element.322), channel_id=1, source_target_pairs={{0,8},{8,0},{16,24},{24,16},{1,9},{9,1},{17,25},{25,17},{2,10},{10... | collective-permute-start | bytes 3538952 | tf_op jit(solution)/shard_map/ppermute | solution.py:214
  1528.9 58.8 %collective-permute-start.73 = (bf16[384,768]{1,0:T(8,128)(2,1)S(1)}, bf16[384,768]{1,0:T(8,128)(2,1)S(1)}, u32[]{:S(2)}, u32[]{:S(2)}) collective-permute-start(bf16[384,768]{1,0:T(8,128)(2,1)S(1)} %add_convert_fusion.40), channel_id=1, source_target_pairs={{8,0},{16,24},{9,1},{17,25},{10,2},{18,26},{11,3},{19,27},{12,4},{... | collective-permute-start | bytes 1769480 | tf_op jit(solution)/shard_map/ppermute | solution.py:214
  1530.6 69.7 %collective-permute-start.71 = (bf16[384,768]{1,0:T(8,128)(2,1)S(1)}, bf16[384,768]{1,0:T(8,128)(2,1)S(1)}, u32[]{:S(2)}, u32[]{:S(2)}) collective-permute-start(bf16[384,768]{1,0:T(8,128)(2,1)S(1)} %add_convert_fusion.42), channel_id=1, source_target_pairs={{8,0},{16,24},{9,1},{17,25},{10,2},{18,26},{11,3},{19,27},{12,4},{... | collective-permute-start | bytes 1769480 | tf_op jit(solution)/shard_map/ppermute | solution.py:214
  1581.2 46.4 %collective-permute-start.109 = (bf16[384,1536]{1,0:T(8,128)(2,1)S(1)}, bf16[384,1536]{1,0:T(8,128)(2,1)S(1)}, u32[]{:S(2)}, u32[]{:S(2)}) collective-permute-start(bf16[384,1536]{1,0:T(8,128)(2,1)S(1)} %add_convert_fusion.14), channel_id=1, source_target_pairs={{8,0},{16,24},{9,1},{17,25},{10,2},{18,26},{11,3},{19,27},{12,4},{... | collective-permute-start | bytes 3538952 | tf_op jit(solution)/shard_map/ppermute | solution.py:214
  1582.8 57.8 %collective-permute-start.100 = (bf16[384,1536]{1,0:T(8,128)(2,1)S(1)}, bf16[384,1536]{1,0:T(8,128)(2,1)S(1)}, u32[]{:S(2)}, u32[]{:S(2)}) collective-permute-start(bf16[384,1536]{1,0:T(8,128)(2,1)S(1)} %add_convert_fusion.22), channel_id=1, source_target_pairs={{8,0},{16,24},{9,1},{17,25},{10,2},{18,26},{11,3},{19,27},{12,4},{... | collective-permute-start | bytes 3538952 | tf_op jit(solution)/shard_map/ppermute | solution.py:214
  (175 other events, 4146.3 us)

commit v2 on v1

v2 whole, which is shorter than its diff:
```python
import functools

import jax
import jax.numpy as jnp
from jax import lax
from jax.experimental import pallas as pl
from jax.experimental.pallas import tpu as pltpu
from jax.sharding import PartitionSpec as P

HD = 64
LANES = 128
VMEM_LIMIT = 60 * 1024 * 1024

exact_mode = lax.Precision.HIGHEST


def layer_norm(values):
    centered = values - jnp.mean(values, axis=-1, keepdims=True)
    spread = jnp.mean(centered * centered, axis=-1, keepdims=True)
    return centered * lax.rsqrt(spread + 1e-06)


def modulate(stream, shift_part, scale_part):
    return layer_norm(stream) * (1.0 + scale_part[:, None, :]) + shift_part[:, None, :]


def modulate_back(stream, modul, hidden_grad, shift_index, scale_index):
    unused_value, back_fn = jax.vjp(modulate, stream, modul[:, shift_index], modul[:, scale_index])
    return back_fn(hidden_grad)


def stream_squares(stream, gated_one, middle, gated_two, result):
    return jnp.stack(
        [jnp.sum(member * member) for member in (stream, gated_one, middle, gated_two, result)]
    )


def flip(values, axis, bit):
    return lax.ppermute(
        values, axis, [(place, place ^ bit) for place in range(lax.axis_size(axis))]
    )


def head_sum(partial):
    if lax.axis_size("head") != 2:
        return lax.psum(partial, "head").astype(jnp.float32)
    return partial.astype(jnp.float32) + flip(partial, "head", 1).astype(jnp.float32)


def gather_pair(first, second):
    count = lax.axis_size("tok")
    parity = lax.rem(lax.axis_index("rep"), 2)
    fetched = {0: jnp.where(parity == 0, first, second)}
    bit = count // 2
    while bit > 1:
        for away, part in list(fetched.items()):
            fetched[away ^ bit] = flip(part, "tok", bit)
        bit //= 2
    entries = {0: (first, second)}
    for away, part in fetched.items():
        if away:
            entries[away] = (part, flip(part, "rep", 1))
    for away, parts in list(entries.items()):
        entries[away ^ 1] = tuple(flip(part, "tok", 1) for part in parts)
    return entries


def gather_blocks(values):
    pieces = {0: values}
    bit = lax.axis_size("tok") // 2
    while bit > 0:
        for away, part in list(pieces.items()):
            pieces[away ^ bit] = flip(part, "tok", bit)
        bit //= 2
    return [pieces[away] for away in range(len(pieces))]


def halve(pieces):
    bit = 1
    while bit < lax.axis_size("tok"):
        pieces = {
            away: (
                part.astype(jnp.float32)
                + flip(pieces[away | bit], "tok", bit).astype(jnp.float32)
            ).astype(jnp.bfloat16)
            for away, part in pieces.items()
            if not away & bit
        }
        bit *= 2
    return pieces[0]


def scatter_grad(keep, send, rows):
    axis = keep.ndim - 2
    moved = flip(send, "tok", 1)
    pieces = {}
    for place in range(keep.shape[axis] // rows):
        cut = functools.partial(
            lax.slice_in_dim, start_index=place * rows, limit_index=(place + 1) * rows, axis=axis
        )
        pieces[2 * place] = (
            cut(keep).astype(jnp.float32) + cut(moved).astype(jnp.float32)
        ).astype(jnp.bfloat16)
    bit = 2
    while bit < lax.axis_size("tok"):
        pieces = {
            away: (
                part.astype(jnp.float32)
                + flip(pieces[away | bit], "tok", bit).astype(jnp.float32)
            ).astype(jnp.bfloat16)
            for away, part in pieces.items()
            if not away & bit
        }
        bit *= 2
    return pieces[0]


def line_sum(chunks):
    if lax.axis_size("rep") != 4:
        return [lax.psum(part, "rep").astype(jnp.float32) for part in chunks]
    rank = lax.axis_index("rep")
    inner = (rank == 1) | (rank == 2)
    outer_pairs = [(0, 1), (1, 0), (2, 3), (3, 2)]
    total, moved = {}, {}
    count = len(chunks)
    for step in range(count + 2):
        if step < count and step >= 2:
            load = jnp.where(inner, total[step - 2], chunks[step])
            pairs = outer_pairs
        elif step < count:
            load, pairs = chunks[step], [(0, 1), (3, 2)]
        else:
            load, pairs = total[step - 2], [(1, 0), (2, 3)]
        moved[step] = lax.ppermute(load, "rep", pairs)
        if step < count:
            pair = chunks[step].astype(jnp.float32) + moved[step].astype(jnp.float32)
            pair = pair.astype(jnp.bfloat16)
            over = lax.ppermute(pair, "rep", [(1, 2), (2, 1)])
            total[step] = (pair.astype(jnp.float32) + over.astype(jnp.float32)).astype(jnp.bfloat16)
    return [
        jnp.where(inner, total[step], moved[step + 2]).astype(jnp.float32) for step in range(count)
    ]


def tok_total(values):
    bit = 1
    while bit < lax.axis_size("tok"):
        values = values + flip(values, "tok", bit)
        bit *= 2
    return values


def rep_gather(values):
    count = lax.axis_size("rep")
    rank = lax.axis_index("rep")
    pieces = values[None]
    bit = 1
    while bit < count:
        pieces = jnp.concatenate([pieces, flip(pieces, "rep", bit)], axis=0)
        bit *= 2
    return jnp.stack(
        [
            lax.dynamic_index_in_dim(pieces, jnp.bitwise_xor(rank, place), 0, keepdims=False)
            for place in range(count)
        ]
    )


def product(left, right):
    return jnp.dot(left, right, preferred_element_type=jnp.float32)


def product_back(left, right):
    return lax.dot_general(
        left, right, (((1,), (1,)), ((), ())), preferred_element_type=jnp.float32
    )


def weight_list(entries, which):
    arrays = []
    for away in range(len(entries)):
        if which is None or away > 1:
            arrays.extend(entries[away])
        else:
            arrays.append(entries[away][which])
    return arrays


def tile_spec(rank, rows, columns):
    if rank == 3:
        return pl.BlockSpec((1, rows, columns), lambda step: (step, 0, 0))
    return pl.BlockSpec((rows, columns), lambda step: (0, step))


def whole_spec(array):
    zeros = (0,) * array.ndim
    return pl.BlockSpec(array.shape, lambda step: zeros, pipeline_mode=pl.Buffered(1))


def tile_of(ref):
    return ref[0] if len(ref.shape) == 3 else ref[...]


def fill(scratch, spot, refs, which, rows, count):
    rank, parity = spot[0], spot[1]
    refs = list(refs)
    for away in range(count):
        at = pl.ds(pl.multiple_of(jnp.bitwise_xor(rank, away) * rows, rows), rows)
        if away < 2:
            scratch[at, :] = tile_of(refs.pop(0))
        else:
            fetched, swapped = refs.pop(0), refs.pop(0)

            @pl.when(parity == which)
            def use_fetched():
                scratch[at, :] = tile_of(fetched)

            @pl.when(parity != which)
            def use_swapped():
                scratch[at, :] = tile_of(swapped)


def fill_both(scratch_one, scratch_two, spot, refs, rows, count):
    rank, parity = spot[0], spot[1]
    refs = list(refs)
    for away in range(count):
        one, two = refs.pop(0), refs.pop(0)
        at = pl.ds(pl.multiple_of(jnp.bitwise_xor(rank, away) * rows, rows), rows)
        if away < 2:
            scratch_one[at, :] = tile_of(one)
            scratch_two[at, :] = tile_of(two)
        else:

            @pl.when(parity == 0)
            def straight():
                scratch_one[at, :] = tile_of(one)
                scratch_two[at, :] = tile_of(two)

            @pl.when(parity != 0)
            def crossed():
                scratch_one[at, :] = tile_of(two)
                scratch_two[at, :] = tile_of(one)


def put_grad(spot, left_ref, right, keep_ref, send_ref, rows, count):
    rank = spot[0]
    for away in range(count):
        at = pl.ds(pl.multiple_of(jnp.bitwise_xor(rank, away) * rows, rows), rows)
        block = product(left_ref[at, :], right).astype(jnp.bfloat16)
        to = send_ref if away & 1 else keep_ref
        place = (away // 2) * rows
        if len(to.shape) == 3:
            to[0, place : place + rows, :] = block
        else:
            to[place : place + rows, :] = block


def call(kernel, tiles, spot, arrays, specs, outs, out_specs, scratch, flops, moved):
    return pl.pallas_call(
        kernel,
        grid=(tiles,),
        in_specs=[pl.BlockSpec(memory_space=pltpu.SMEM)] + specs,
        out_specs=out_specs,
        out_shape=outs,
        scratch_shapes=scratch,
        compiler_params=pltpu.CompilerParams(
            dimension_semantics=("arbitrary",), vmem_limit_bytes=VMEM_LIMIT
        ),
        cost_estimate=pl.CostEstimate(flops=flops, bytes_accessed=moved, transcendentals=0),
    )(spot, *arrays)


def bf16(*shape):
    return jax.ShapeDtypeStruct(shape, jnp.bfloat16)


def project(spot, rows_in, entries, which, tiles):
    arrays = weight_list(entries, which)
    count = len(entries)
    share, columns = arrays[0].shape[-2], arrays[0].shape[-1]
    if arrays[0].ndim == 2:
        columns //= tiles
    length, width = rows_in.shape

    def kernel(spot_ref, in_ref, *rest):
        refs, out_ref, scratch = rest[:-2], rest[-2], rest[-1]
        fill(scratch, spot_ref, refs, which, share, count)
        out_ref[0] = product(in_ref[...], scratch[...]).astype(jnp.bfloat16)

    return call(
        kernel,
        tiles,
        spot,
        [rows_in] + arrays,
        [whole_spec(rows_in)] + [tile_spec(part.ndim, share, columns) for part in arrays],
        bf16(tiles, length, columns),
        pl.BlockSpec((1, length, columns), lambda step: (step, 0, 0)),
        [pltpu.VMEM((width, columns), jnp.bfloat16)],
        2 * length * width * columns * tiles,
        2 * width * columns * tiles,
    )


def project_back(spot, rows_in, entries, which):
    arrays = weight_list(entries, which)
    count = len(entries)
    share, columns = arrays[0].shape
    length, width = rows_in.shape[0], share * count

    def kernel(spot_ref, in_ref, *rest):
        refs, out_ref, scratch = rest[:-2], rest[-2], rest[-1]
        fill(scratch, spot_ref, refs, which, share, count)
        out_ref[...] = product_back(in_ref[...], scratch[...]).astype(jnp.bfloat16)

    return call(
        kernel,
        1,
        spot,
        [rows_in] + arrays,
        [whole_spec(rows_in)] + [tile_spec(2, share, columns) for part in arrays],
        bf16(length, width),
        pl.BlockSpec((length, width), lambda step: (0, 0)),
        [pltpu.VMEM((width, columns), jnp.bfloat16)],
        2 * length * width * columns,
        2 * width * columns,
    )


def proj_grads(spot, grad_rows, grad_turned, mixed_rows, entries, which):
    arrays = weight_list(entries, which)
    count = len(entries)
    share, columns = arrays[0].shape
    length, width = grad_rows.shape

    def kernel(spot_ref, grad_ref, turned_ref, mixed_ref, *rest):
        refs, (out_ref, keep_ref, send_ref, scratch) = rest[:-4], rest[-4:]
        fill(scratch, spot_ref, refs, which, share, count)
        out_ref[...] = product(grad_ref[...], scratch[...]).astype(jnp.bfloat16)
        put_grad(spot_ref, turned_ref, mixed_ref[...], keep_ref, send_ref, share, count)

    half = width // 2
    return call(
        kernel,
        1,
        spot,
        [grad_rows, grad_turned, mixed_rows] + arrays,
        [whole_spec(grad_rows), whole_spec(grad_turned), whole_spec(mixed_rows)]
        + [tile_spec(2, share, columns) for part in arrays],
        (bf16(length, columns), bf16(half, columns), bf16(half, columns)),
        (
            pl.BlockSpec((length, columns), lambda step: (0, 0)),
            pl.BlockSpec((half, columns), lambda step: (0, 0)),
            pl.BlockSpec((half, columns), lambda step: (0, 0)),
        ),
        [pltpu.VMEM((width, columns), jnp.bfloat16)],
        4 * length * width * columns,
        4 * width * columns,
    )


def qkv_grads(spot, hidden_turned, grads, entries, which):
    arrays = weight_list(entries, which)
    count = len(entries)
    tiles, share, columns = arrays[0].shape
    width, length = hidden_turned.shape

    def kernel(spot_ref, turned_ref, grad_ref, *rest):
        refs, (out_ref, keep_ref, send_ref, scratch, total) = rest[:-5], rest[-5:]
        step = pl.program_id(0)
        fill(scratch, spot_ref, refs, which, share, count)
        part = product_back(grad_ref[0], scratch[...])

        @pl.when(step == 0)
        def begin():
            total[...] = part

        @pl.when(step > 0)
        def add():
            total[...] += part

        @pl.when(step == tiles - 1)
        def finish():
            out_ref[...] = total[...].astype(jnp.bfloat16)

        put_grad(spot_ref, turned_ref, grad_ref[0], keep_ref, send_ref, share, count)

    half = width // 2
    return call(
        kernel,
        tiles,
        spot,
        [hidden_turned, grads] + arrays,
        [whole_spec(hidden_turned), tile_spec(3, length, columns)]
        + [tile_spec(3, share, columns) for part in arrays],
        (bf16(length, width), bf16(tiles, half, columns), bf16(tiles, half, columns)),
        (
            pl.BlockSpec((length, width), lambda step: (0, 0)),
            tile_spec(3, half, columns),
            tile_spec(3, half, columns),
        ),
        [pltpu.VMEM((width, columns), jnp.bfloat16), pltpu.VMEM((length, width), jnp.float32)],
        4 * length * width * columns * tiles,
        4 * width * columns * tiles,
    )


def feed_forward(spot, hidden, hidden_turned, grad, grad_turned, entries):
    arrays = weight_list(entries, None)
    count = len(entries)
    share, units = arrays[0].shape
    columns = 512
    tiles = units // columns
    length, width = hidden.shape

    def kernel(spot_ref, hid_ref, hid_turned_ref, grad_ref, grad_turned_ref, *rest):
        refs, rest = rest[: len(arrays)], rest[len(arrays) :]
        out_ref, back_ref, up_keep, up_send, down_keep, down_send = rest[:6]
        up, down, out_sum, back_sum = rest[6:]
        step = pl.program_id(0)
        fill_both(up, down, spot_ref, refs, share, count)
        upward = product(hid_ref[...], up[...])
        squared = upward * upward
        bent = jnp.tanh(0.7978845608028654 * (upward + 0.044715 * (upward * squared)))
        activ = (0.5 * upward * (1.0 + bent)).astype(jnp.bfloat16)
        slope = 0.5 * (1.0 + bent) + 0.5 * upward * (1.0 - bent * bent) * (
            0.7978845608028654 * (1.0 + 3 * 0.044715 * squared)
        )
        activ_grad = product(grad_ref[...], down[...])
        upward_grad = (activ_grad * slope).astype(jnp.bfloat16)
        out_part = product_back(activ, down[...])
        back_part = product_back(upward_grad, up[...])

        @pl.when(step == 0)
        def begin():
            out_sum[...] = out_part
            back_sum[...] = back_part

        @pl.when(step > 0)
        def add():
            out_sum[...] += out_part
            back_sum[...] += back_part

        @pl.when(step == tiles - 1)
        def finish():
            out_ref[...] = out_sum[...].astype(jnp.bfloat16)
            back_ref[...] = back_sum[...].astype(jnp.bfloat16)

        put_grad(spot_ref, grad_turned_ref, activ, down_keep, down_send, share, count)
        put_grad(spot_ref, hid_turned_ref, upward_grad, up_keep, up_send, share, count)

    half = width // 2
    grad_out = bf16(half, units)
    grad_spec = tile_spec(2, half, columns)
    rows_spec = pl.BlockSpec((length, width), lambda step: (0, 0))
    wholes = [hidden, hidden_turned, grad, grad_turned]
    return call(
        kernel,
        tiles,
        spot,
        wholes + arrays,
        [whole_spec(part) for part in wholes]
        + [tile_spec(2, share, columns) for part in arrays],
        (bf16(length, width), bf16(length, width)) + (grad_out,) * 4,
        (rows_spec, rows_spec) + (grad_spec,) * 4,
        [pltpu.VMEM((width, columns), jnp.bfloat16)] * 2
        + [pltpu.VMEM((length, width), jnp.float32)] * 2,
        12 * length * width * units,
        8 * width * units,
    )


def head_lanes(shape, head):
    lane = lax.broadcasted_iota(jnp.int32, shape, len(shape) - 1)
    return (lane >= head * HD) & (lane < (head + 1) * HD)


def padding(shape, axis, block, real, count):
    place = lax.broadcasted_iota(jnp.int32, shape, axis)
    hidden = (place >= real) & (place < block)
    for other in range(1, count):
        hidden = hidden | ((place >= other * block + real) & (place < (other + 1) * block))
    return hidden


def attend(query, blocks, real):
    seqs, rows, width = query.shape
    count = len(blocks)
    keys = rows * count

    def kernel(query_ref, *rest):
        refs, out_ref = rest[:-1], rest[-1]
        queries = query_ref[0]
        key_all = jnp.concatenate([ref[0, 0] for ref in refs], axis=0)
        value_all = jnp.concatenate([ref[1, 0] for ref in refs], axis=0)
        hidden = padding((1, keys), 1, rows, real, count)
        result = jnp.zeros((rows, LANES), jnp.float32)
        for head in range(LANES // HD):
            mine = head_lanes((rows, LANES), head)
            scores = product_back(jnp.where(mine, queries, jnp.zeros_like(queries)), key_all)
            scores = jnp.where(hidden, -1e30, scores * 0.125)
            expd = jnp.exp(scores - jnp.max(scores, axis=1, keepdims=True))
            share = 1.0 / jnp.sum(expd, axis=1, keepdims=True)
            mixed = product((expd * share).astype(jnp.bfloat16), value_all)
            result = jnp.where(mine, mixed, result)
        out_ref[0] = result.astype(jnp.bfloat16)

    row_spec = pl.BlockSpec((1, rows, LANES), lambda seq, part: (seq, 0, part))
    block_spec = pl.BlockSpec((2, 1, rows, LANES), lambda seq, part: (0, seq, 0, part))
    return pl.pallas_call(
        kernel,
        grid=(seqs, width // LANES),
        in_specs=[row_spec] + [block_spec] * count,
        out_specs=row_spec,
        out_shape=bf16(seqs, rows, width),
        compiler_params=pltpu.CompilerParams(
            dimension_semantics=("arbitrary", "arbitrary"), vmem_limit_bytes=VMEM_LIMIT
        ),
        cost_estimate=pl.CostEstimate(
            flops=4 * seqs * rows * keys * width * 4,
            bytes_accessed=4 * seqs * keys * width,
            transcendentals=seqs * rows * keys * width // HD,
        ),
    )(query, *blocks)


def attend_grads(query, grad, blocks, real):
    seqs, rows, width = query.shape
    count = len(blocks)
    keys = rows * count

    def kernel(query_ref, grad_ref, *rest):
        refs, (query_grad_ref, *block_grads) = rest[:count], rest[count:]
        queries, grads = query_ref[0], grad_ref[0]
        key_all = jnp.concatenate([ref[0, 0] for ref in refs], axis=0)
        value_all = jnp.concatenate([ref[1, 0] for ref in refs], axis=0)
        hidden = padding((keys, 1), 0, rows, real, count)
        query_grad = jnp.zeros((rows, LANES), jnp.float32)
        key_grad = jnp.zeros((keys, LANES), jnp.float32)
        value_grad = jnp.zeros((keys, LANES), jnp.float32)
        for head in range(LANES // HD):
            mine = head_lanes((rows, LANES), head)
            own_query = jnp.where(mine, queries, jnp.zeros_like(queries))
            own_grad = jnp.where(mine, grads, jnp.zeros_like(grads))
            scores = product_back(key_all, own_query)
            scores = jnp.where(hidden, -1e30, scores * 0.125)
            expd = jnp.exp(scores - jnp.max(scores, axis=0, keepdims=True))
            probs = expd * (1.0 / jnp.sum(expd, axis=0, keepdims=True))
            prob_grad = product_back(value_all, own_grad)
            delta = jnp.sum(probs * prob_grad, axis=0, keepdims=True)
            score_grad = (probs * (prob_grad - delta)).astype(jnp.bfloat16)
            value_grad += product(probs.astype(jnp.bfloat16), own_grad)
            key_grad += product(score_grad, own_query)
            back = lax.dot_general(
                score_grad, key_all, (((0,), (0,)), ((), ())), preferred_element_type=jnp.float32
            )
            query_grad = jnp.where(mine, back, query_grad)
        query_grad_ref[0] = (query_grad * 0.125).astype(jnp.bfloat16)
        for place, ref in enumerate(block_grads):
            at = slice(place * rows, (place + 1) * rows)
            ref[0, 0] = (key_grad[at] * 0.125).astype(jnp.bfloat16)
            ref[1, 0] = value_grad[at].astype(jnp.bfloat16)

    row_spec = pl.BlockSpec((1, rows, LANES), lambda seq, part: (seq, 0, part))
    block_spec = pl.BlockSpec((2, 1, rows, LANES), lambda seq, part: (0, seq, 0, part))
    query_grad, *block_grads = pl.pallas_call(
        kernel,
        grid=(seqs, width // LANES),
        in_specs=[row_spec] * 2 + [block_spec] * count,
        out_specs=[row_spec] + [block_spec] * count,
        out_shape=[bf16(seqs, rows, width)] + [bf16(2, seqs, rows, width)] * count,
        compiler_params=pltpu.CompilerParams(
            dimension_semantics=("arbitrary", "arbitrary"), vmem_limit_bytes=VMEM_LIMIT
        ),
        cost_estimate=pl.CostEstimate(
            flops=10 * seqs * rows * keys * width * 4,
            bytes_accessed=8 * seqs * keys * width,
            transcendentals=seqs * rows * keys * width // HD,
        ),
    )(query, grad, *blocks)
    return query_grad, block_grads


def on_device(
    image_tokens,
    text_tokens,
    text_owner,
    conditioning,
    slot_sequence,
    image_w_mod,
    image_b_mod,
    image_w_qkv,
    image_w_proj,
    image_w_up,
    image_w_down,
    text_w_mod,
    text_b_mod,
    text_w_qkv,
    text_w_proj,
    text_w_up,
    text_w_down,
    image_cotangent,
    text_cotangent,
):
    tok_rank = lax.axis_index("tok")
    rep_rank = lax.axis_index("rep")
    rep_count = lax.axis_size("rep")
    tok_count = lax.axis_size("tok")
    seqs, image_rows, width = image_tokens.shape
    text_real = text_cotangent.shape[1]
    text_rows = -(-text_real // 16) * 16
    slots = conditioning.shape[0]
    share = image_w_mod.shape[0]
    heads_width = image_w_qkv.shape[2]
    rows = image_rows + text_rows
    real = image_rows + text_real
    spot = jnp.stack([tok_rank, lax.rem(rep_rank, 2)]).astype(jnp.int32)

    turn = lambda weight: jnp.transpose(weight, (1, 0, 2))
    qkv_weights = gather_pair(turn(image_w_qkv), turn(text_w_qkv))

    picker = (slot_sequence[:, None] == jnp.arange(slots, dtype=jnp.int32)[None, :]).astype(
        jnp.float32
    )
    cond_slots = jnp.dot(picker, conditioning, precision=exact_mode)
    activ_all = jax.nn.silu(cond_slots).astype(jnp.bfloat16)
    activ_group = lax.dynamic_slice_in_dim(activ_all, rep_rank * seqs, seqs, axis=0)
    activ_share = lax.dynamic_slice_in_dim(activ_group, tok_rank * share, share, axis=1)
    both_mod = tok_total(
        jnp.stack(
            [
                jnp.einsum("sd,dke->ske", activ_share, weight, preferred_element_type=jnp.float32)
                for weight in (image_w_mod, text_w_mod)
            ]
        )
    )
    image_mod = both_mod[0] + image_b_mod.astype(jnp.float32)[None]
    text_mod = both_mod[1] + text_b_mod.astype(jnp.float32)[None]

    owned = (text_owner == tok_rank).astype(jnp.float32)
    total_text = text_owner.shape[1]
    before = jnp.dot(
        owned,
        jnp.triu(jnp.ones((total_text, total_text), jnp.float32), 1),
        precision=exact_mode,
    )
    chosen = (
        (before[:, None, :] == jnp.arange(text_rows, dtype=jnp.float32)[None, :, None])
        & (owned[:, None, :] > 0.5)
    ).astype(jnp.bfloat16)
    text_input = jnp.einsum("srt,std->srd", chosen, text_tokens, preferred_element_type=jnp.float32)
    image_input = image_tokens.astype(jnp.float32)
    image_cot = image_cotangent.astype(jnp.float32)
    text_cot = jnp.pad(
        text_cotangent.astype(jnp.float32), ((0, 0), (0, text_rows - text_real), (0, 0))
    )

    flat = lambda values: values.reshape(-1, values.shape[-1])
    image_hid_one = flat(modulate(image_input, image_mod[:, 0], image_mod[:, 1]).astype(jnp.bfloat16))
    text_hid_one = flat(modulate(text_input, text_mod[:, 0], text_mod[:, 1]).astype(jnp.bfloat16))
    image_qkv = project(spot, image_hid_one, qkv_weights, 0, 3)
    text_qkv = project(spot, text_hid_one, qkv_weights, 1, 3)
    by_seq = lambda values: values.reshape(values.shape[:-2] + (seqs, -1, values.shape[-1]))
    both = lambda image, text: jnp.concatenate([by_seq(image), by_seq(text)], axis=-2)
    query = both(image_qkv[0], text_qkv[0])
    blocks = gather_blocks(both(image_qkv[1:], text_qkv[1:]))
    proj_weights = gather_pair(image_w_proj, text_w_proj)
    text_ff = gather_pair(text_w_up, text_w_down)
    image_ff = gather_pair(image_w_up, image_w_down)
    mixed = attend(query, blocks, real)
    image_mixed = flat(mixed[:, :image_rows])
    text_mixed = flat(mixed[:, image_rows:])
    image_branch = by_seq(head_sum(project_back(spot, image_mixed, proj_weights, 0)))
    text_branch = by_seq(head_sum(project_back(spot, text_mixed, proj_weights, 1)))

    def middle_of(stream, modul, branch, cot):
        middle = stream + modul[:, 2][:, None, :] * branch
        hidden = flat(modulate(middle, modul[:, 3], modul[:, 4]).astype(jnp.bfloat16))
        grad = flat((modul[:, 5][:, None, :] * cot).astype(jnp.bfloat16))
        return middle, hidden, grad

    image_middle, image_hid_two, image_db_two = middle_of(
        image_input, image_mod, image_branch, image_cot
    )
    text_middle, text_hid_two, text_db_two = middle_of(text_input, text_mod, text_branch, text_cot)
    image_part, image_back, image_up_keep, image_up_send, image_down_keep, image_down_send = (
        feed_forward(
            spot, image_hid_two, image_hid_two.T, image_db_two, image_db_two.T, image_ff
        )
    )
    text_part, text_back, text_up_keep, text_up_send, text_down_keep, text_down_send = (
        feed_forward(spot, text_hid_two, text_hid_two.T, text_db_two, text_db_two.T, text_ff)
    )
    image_hid_grad = by_seq(head_sum(image_back))
    text_hid_grad = by_seq(head_sum(text_back))
    ff_shares = [
        scatter_grad(text_down_keep, text_down_send, share),
        scatter_grad(text_up_keep, text_up_send, share),
        scatter_grad(image_down_keep, image_down_send, share),
        scatter_grad(image_up_keep, image_up_send, share),
    ]
    image_branch_two = by_seq(head_sum(image_part))
    text_branch_two = by_seq(head_sum(text_part))

    image_ln_grad, image_shift_two, image_scale_two = modulate_back(
        image_middle, image_mod, image_hid_grad, 3, 4
    )
    text_ln_grad, text_shift_two, text_scale_two = modulate_back(
        text_middle, text_mod, text_hid_grad, 3, 4
    )
    image_mid_grad = image_cot + image_ln_grad
    text_mid_grad = text_cot + text_ln_grad
    image_gate_one = jnp.sum(image_mid_grad * image_branch, axis=1)
    text_gate_one = jnp.sum(text_mid_grad * text_branch, axis=1)
    image_db_one = flat((image_mod[:, 2][:, None, :] * image_mid_grad).astype(jnp.bfloat16))
    text_db_one = flat((text_mod[:, 2][:, None, :] * text_mid_grad).astype(jnp.bfloat16))
    image_mixed_grad, image_proj_keep, image_proj_send = proj_grads(
        spot, image_db_one, image_db_one.T, image_mixed, proj_weights, 0
    )
    text_mixed_grad, text_proj_keep, text_proj_send = proj_grads(
        spot, text_db_one, text_db_one.T, text_mixed, proj_weights, 1
    )
    query_grad, block_grads = attend_grads(
        query, both(image_mixed_grad, text_mixed_grad), blocks, real
    )
    block_grad = halve(dict(enumerate(block_grads)))
    image_qkv_grad = jnp.concatenate(
        [query_grad[None, :, :image_rows], block_grad[:, :, :image_rows]], axis=0
    ).reshape(3, -1, heads_width)
    text_qkv_grad = jnp.concatenate(
        [query_grad[None, :, image_rows:], block_grad[:, :, image_rows:]], axis=0
    ).reshape(3, -1, heads_width)
    image_in_part, image_qkv_keep, image_qkv_send = qkv_grads(
        spot, image_hid_one.T, image_qkv_grad, qkv_weights, 0
    )
    text_in_part, text_qkv_keep, text_qkv_send = qkv_grads(
        spot, text_hid_one.T, text_qkv_grad, qkv_weights, 1
    )
    image_in_grad = by_seq(head_sum(image_in_part))
    text_in_grad = by_seq(head_sum(text_in_part))
    image_ln_one, image_shift_one, image_scale_one = modulate_back(
        image_input, image_mod, image_in_grad, 0, 1
    )
    text_ln_one, text_shift_one, text_scale_one = modulate_back(
        text_input, text_mod, text_in_grad, 0, 1
    )
    image_grad = (image_mid_grad + image_ln_one).astype(jnp.bfloat16)
    text_grad = (text_mid_grad + text_ln_one).astype(jnp.bfloat16)[:, :text_real]

    image_gated_one = image_mod[:, 2][:, None, :] * image_branch
    text_gated_one = text_mod[:, 2][:, None, :] * text_branch
    image_gated_two = image_mod[:, 5][:, None, :] * image_branch_two
    text_gated_two = text_mod[:, 5][:, None, :] * text_branch_two
    image_result = image_middle + image_gated_two
    text_result = text_middle + text_gated_two
    image_gate_two = jnp.sum(image_cot * image_branch_two, axis=1)
    text_gate_two = jnp.sum(text_cot * text_branch_two, axis=1)
    squares = jnp.concatenate(
        [
            stream_squares(
                image_input, image_gated_one, image_middle, image_gated_two, image_result
            ),
            stream_squares(
                *[
                    member[:, :text_real]
                    for member in (
                        text_input,
                        text_gated_one,
                        text_middle,
                        text_gated_two,
                        text_result,
                    )
                ]
            ),
        ]
    )

    early = jnp.stack(
        [
            jnp.stack([image_gate_one, image_shift_two, image_scale_two, image_gate_two], axis=1),
            jnp.stack([text_gate_one, text_shift_two, text_scale_two, text_gate_two], axis=1),
        ]
    )
    late = jnp.stack(
        [
            jnp.stack([image_shift_one, image_scale_one], axis=1),
            jnp.stack([text_shift_one, text_scale_one], axis=1),
        ]
    )
    square_row = jnp.pad(squares, (0, width - 10))[None]
    early_flat = jnp.concatenate([early.reshape(-1, width), square_row], axis=0)
    early_all = rep_gather(tok_total(early_flat))
    late_all = rep_gather(tok_total(late))
    square_total = jnp.sum(early_all[:, -1, :10], axis=0)
    early_table = jnp.moveaxis(
        early_all[:, :-1].reshape(rep_count, 2, seqs, 4, width), 0, 1
    ).reshape(2, slots, 4, width)
    late_table = jnp.moveaxis(late_all, 0, 1).reshape(2, slots, 2, width)
    mod_sum = jnp.concatenate([late_table, early_table], axis=2)

    half = ff_shares[0].shape[1] // 2
    ff_sums = line_sum([part for whole in ff_shares for part in (whole[:, :half], whole[:, half:])])
    text_down_sum, text_up_sum, image_down_sum, image_up_sum = [
        jnp.concatenate(ff_sums[place : place + 2], axis=1) for place in (0, 2, 4, 6)
    ]
    text_proj_sum, image_proj_sum = line_sum(
        [
            scatter_grad(text_proj_keep, text_proj_send, share),
            scatter_grad(image_proj_keep, image_proj_send, share),
        ]
    )
    qkv_sums = line_sum(
        [
            part
            for whole in (
                scatter_grad(text_qkv_keep, text_qkv_send, share),
                scatter_grad(image_qkv_keep, image_qkv_send, share),
            )
            for part in whole
        ]
    )
    text_qkv_sum = jnp.stack(qkv_sums[:3], axis=1)
    image_qkv_sum = jnp.stack(qkv_sums[3:], axis=1)

    activ_rows = lax.dynamic_slice_in_dim(activ_all, tok_rank * share, share, axis=1).astype(
        jnp.float32
    )
    image_g_mod = jnp.einsum("sd,ske->dke", activ_rows, mod_sum[0], precision=exact_mode)
    text_g_mod = jnp.einsum("sd,ske->dke", activ_rows, mod_sum[1], precision=exact_mode)
    image_g_bmod = jnp.sum(mod_sum[0], axis=0)
    text_g_bmod = jnp.sum(mod_sum[1], axis=0)
    activ_grad = jnp.einsum(
        "ske,dke->sd", mod_sum[0], image_w_mod.astype(jnp.float32), precision=exact_mode
    ) + jnp.einsum("ske,dke->sd", mod_sum[1], text_w_mod.astype(jnp.float32), precision=exact_mode)
    cond_rows = lax.dynamic_slice_in_dim(cond_slots, tok_rank * share, share, axis=1)
    unused_value, silu_back = jax.vjp(jax.nn.silu, cond_rows)
    slot_grad = silu_back(activ_grad)[0]
    cond_grad = jnp.dot(jnp.transpose(picker), slot_grad, precision=exact_mode)
    image_count = float(slots * image_rows * tok_count * width)
    text_count = float(slots * text_real * tok_count * width)
    counts = jnp.concatenate(
        [jnp.full((5,), image_count, jnp.float32), jnp.full((5,), text_count, jnp.float32)]
    )
    stream_rms = jnp.sqrt(square_total / counts)
    return (
        image_result.astype(jnp.bfloat16),
        text_result[:, :text_real].astype(jnp.bfloat16),
        image_grad,
        text_grad,
        cond_grad,
        image_g_mod,
        image_g_bmod,
        image_qkv_sum,
        image_proj_sum,
        image_up_sum,
        image_down_sum,
        text_g_mod,
        text_g_bmod,
        text_qkv_sum,
        text_proj_sum,
        text_up_sum,
        text_down_sum,
        stream_rms,
    )


def solution(mesh):
    in_specs = (
        P("rep", "tok", None),
        P("rep", None, None),
        P("rep", None),
        P(),
        P(),
        P("tok", None, None),
        P(),
        P("tok", None, "head"),
        P("tok", "head"),
        P("tok", "head"),
        P("tok", "head"),
        P("tok", None, None),
        P(),
        P("tok", None, "head"),
        P("tok", "head"),
        P("tok", "head"),
        P("tok", "head"),
        P("rep", "tok", None),
        P("rep", "tok", None),
    )
    out_specs = (
        P("rep", "tok", None),
        P("rep", "tok", None),
        P("rep", "tok", None),
        P("rep", "tok", None),
        P(None, "tok"),
        P("tok", None, None),
        P(),
        P("tok", None, "head"),
        P("tok", "head"),
        P("tok", "head"),
        P("tok", "head"),
        P("tok", None, None),
        P(),
        P("tok", None, "head"),
        P("tok", "head"),
        P("tok", "head"),
        P("tok", "head"),
        P(),
    )
    return jax.shard_map(
        on_device, mesh=mesh, in_specs=in_specs, out_specs=out_specs, check_vma=False
    )
```

time: 1650 us -> 1400 us (0.85)
  matrix products: 300 us -> 43.4 us
  local copies, waits for them, and re-layouts: 255 us -> 49 us
  Pallas kernels: 0 us -> 203 us
  other arithmetic: 220 us -> 167 us
  waiting for transfers between devices: 648 us -> 694 us
    dot_general x38 -> x2, matrix products: 261 us -> 0.47 us  [the longest x1 0.35 us: on_device(): jnp.einsum('srt,std->srd', chosen, text_tokens, preferred_element_type=jn...]
    pallas_call x0 -> x12, Pallas kernels: none -> 203 us  [the longest x10 126 us: call(): pl.pallas_call(kernel, grid=(tiles,), in_specs=[pl.BlockSpec(memory_space...]
    dynamic_update_slice x34 -> x0, local copies, waits for them, and re-layouts: 64.2 us -> none  [the longest x32 64.2 us: gather_pair(): lax.dynamic_update_slice(whole, part[None], (which, jnp.bitwise_xor(rank,...]
    another operation x14 -> x1, other arithmetic: 41.9 us -> 0.62 us  [on_device(): spot = jnp.stack([tok_rank, lax.rem(rep_rank, 2)]).astype(jnp.int32)]
    convert_element_type x11 -> x0, local copies, waits for them, and re-layouts: 38.9 us -> none  [the longest x10 38.9 us: halve(): pieces[away | bit].astype(jnp.bfloat16)]
    ppermute x8 -> x0, local copies, waits for them, and re-layouts: 34.6 us -> none  [flip(): lax.ppermute(values, axis, [(place, place ^ bit) for place in range(lax.a...]
    ppermute x22, waiting for transfers between devices: 234 us -> 265 us  [line_sum(): moved[step] = lax.ppermute(load, 'rep', pairs)]
    another operation x6 -> x1, local copies, waits for them, and re-layouts: 16.7 us -> 0.08 us  [on_device(): qkv_sums = line_sum([part for whole in (scatter_grad(text_qkv_keep, text_...]
  transfers between devices with their start and end apart: 116 -> 102, of which waited for: 38 -> 34; matrix products, arithmetic and copies ran while one was open for 42% -> 17% of each run, Pallas kernels for 0% -> 15%
where the time goes in v2:
time: 1400 us; the launch traced here: 1390 us
  waiting for transfers between devices  694 us (50%)
  starting transfers between devices  227 us (16%)
  Pallas kernels  203 us (14%)
  other arithmetic  167 us (12%)
  local copies, waits for them, and re-layouts  49 us (4%)
  matrix products  43.4 us (3%)
    ppermute x64, waiting for transfers between devices, flip(): lax.ppermute(values, axis, [(place, place ^ bit) for place in range(lax.a...  428 us
    ppermute x22, waiting for transfers between devices, line_sum(): moved[step] = lax.ppermute(load, 'rep', pairs)  265 us
    ppermute x22, starting transfers between devices, line_sum(): moved[step] = lax.ppermute(load, 'rep', pairs)  159 us
    pallas_call x10, Pallas kernels, call(): pl.pallas_call(kernel, grid=(tiles,), in_specs=[pl.BlockSpec(memory_space...  126 us
    ppermute x64, starting transfers between devices, flip(): lax.ppermute(values, axis, [(place, place ^ bit) for place in range(lax.a...  52.7 us
    pallas_call x1, Pallas kernels, attend_grads(): pl.pallas_call(kernel, grid=(seqs, width // LANES), in_specs=[row_spec] *...  51.1 us
  transfers between devices with their start and end apart: 102, of which 34 were waited for; matrix products, arithmetic and copies ran while one was open for 17% of the time, Pallas kernels for 15%

profile of v2, /device:TPU:0, one launch (start us, length us, event | category | flops | bytes accessed | tf_op | source)
XLA Modules:
  0.0 1385.4 jit_solution(15351341421305664421)
XLA Ops:
  2.4 4.2 convolution_bitcast_fusion
  19.7 34.2 %collective-permute-done.3.rest_2_ = bf16[3,384,768]{2,1,0:T(8,128)(2,1)S(1)} collective-permute-done((bf16[3,384,768]{2,1,0:T(8,128)(2,1)S(1)}, bf16[3,384,768]{2,1,0:T(8,128)(2,1)S(1)}, u32[]{:S(2)}, u32[]{:S(2)}) %collective-permute-start.3) | collective-permute-done | bytes 1769504 | tf_op jit(solution)/shard_map/ppermute | solution.py:39
  59.5 47.5 %collective-permute-done.1 = f32[2,2,6,1536]{3,1,2,0:T(2,128)S(1)} collective-permute-done((f32[2,2,6,1536]{3,1,2,0:T(2,128)S(1)}, f32[2,2,6,1536]{3,1,2,0:T(2,128)S(1)}, u32[]{:S(2)}, u32[]{:S(2)}) %collective-permute-start.1) | collective-permute-done | bytes 147488 | tf_op jit(solution)/shard_map/ppermute | solution.py:39
  115.6 6.5 shard_map.323
  122.2 9.2 shard_map.322
  137.0 51.4 %collective-permute-done.12.rest_2_ = bf16[384,768]{1,0:T(8,128)(2,1)S(1)} collective-permute-done((bf16[384,768]{1,0:T(8,128)(2,1)S(1)}, bf16[384,768]{1,0:T(8,128)(2,1)S(1)}, u32[]{:S(2)}, u32[]{:S(2)}) %collective-permute-start.12) | collective-permute-done | bytes 589856 | tf_op jit(solution)/shard_map/ppermute | solution.py:39
  194.0 9.1 collective-permute-done.13.rest_3_
  210.3 25.4 %shard_map.324 = bf16[2,304,768]{2,1,0:T(8,128)(2,1)} custom-call(bf16[2,304,768]{2,1,0:T(8,128)(2,1)} %pad_maximum_fusion.2.query_ref, bf16[2,2,304,768]{3,2,1,0:T(8,128)(2,1)} %copy-done.52, bf16[2,2,304,768]{3,2,1,0:T(8,128)(2,1)} %copy-done.86, bf16[2,2,304,768]{3,2,1,0:T(8,128)(2,1)} %copy-done.85, bf16[2,2,304,768]{3,2,1,0:T(8,128)(2,1)} %copy-done.87), custom_call_target="tpu_custom_call" | custom-call | flops 9084862464 | bytes 7471104 | tf_op jit(solution)/shard_map/pallas_call | solution.py:509
  241.2 5.0 collective-permute-done.19.rest_4_
  247.8 7.1 collective-permute-done.25
  259.5 21.8 %shard_map.328 = (bf16[96,1536]{1,0:T(8,128)(2,1)}, bf16[96,1536]{1,0:T(8,128)(2,1)}, bf16[768,3072]{1,0:T(8,128)(2,1)}, bf16[768,3072]{1,0:T(8,128)(2,1)}, bf16...) custom-call(s32[2]{0:T(128)} %pad_add_fusion.spot_ref, bf16[96,1536]{1,0:T(8,128)(2,1)} %bitcast.263, ...), custom_call_target="tpu_custom_call" | custom-call | flops 5435817984 | bytes 37748736 | tf_op jit(solution)/shard_map/pallas_call | solution.py:259
  285.7 5.0 shard_map.325
  294.5 12.5 collective-permute-done.20.rest_5_
  307.0 26.7 %collective-permute-done.32 = bf16[96,1536]{1,0:T(8,128)(2,1)S(1)} collective-permute-done((bf16[96,1536]{1,0:T(8,128)(2,1)S(1)}, bf16[96,1536]{1,0:T(8,128)(2,1)S(1)}, u32[]{:S(2)}, u32[]{:S(2)}) %collective-permute-start.32) | collective-permute-done | bytes 294944 | tf_op jit(solution)/shard_map/ppermute | solution.py:39
  337.5 5.3 shard_map.330
  357.9 42.6 %shard_map.326 = (bf16[512,1536]{1,0:T(8,128)(2,1)}, bf16[512,1536]{1,0:T(8,128)(2,1)}, bf16[768,3072]{1,0:T(8,128)(2,1)}, bf16[768,3072]{1,0:T(8,128)(2,1)}, bf...) custom-call(s32[2]{0:T(128)} %pad_add_fusion.spot_ref, bf16[512,1536]{1,0:T(8,128)(2,1)} %bitcast.237, ...), custom_call_target="tpu_custom_call" | custom-call | flops 28991029248 | bytes 37748736 | tf_op jit(solution)/shard_map/pallas_call | solution.py:259
  407.8 12.3 collective-permute-done.99
  422.8 15.2 %collective-permute-done.33 = bf16[512,1536]{1,0:T(8,128)(2,1)S(1)} collective-permute-done((bf16[512,1536]{1,0:T(8,128)(2,1)}, bf16[512,1536]{1,0:T(8,128)(2,1)S(1)}, u32[]{:S(2)}, u32[]{:S(2)}) %collective-permute-start.33) | collective-permute-done | bytes 1572896 | tf_op jit(solution)/shard_map/ppermute | solution.py:39
  438.5 32.5 %collective-permute-done.23 = bf16[512,1536]{1,0:T(8,128)(2,1)S(1)} collective-permute-done((bf16[512,1536]{1,0:T(8,128)(2,1)}, bf16[512,1536]{1,0:T(8,128)(2,1)S(1)}, u32[]{:S(2)}, u32[]{:S(2)}) %collective-permute-start.23) | collective-permute-done | bytes 1572896 | tf_op jit(solution)/shard_map/ppermute | solution.py:39
  472.4 5.0 fusion.18
  482.3 4.7 multiply_convert_fusion
  489.6 7.1 shard_map.329
  512.8 4.1 collective-permute-done.101
  517.4 51.1 %shard_map.331 = (bf16[2,304,768]{2,1,0:T(8,128)(2,1)}, bf16[2,2,304,768]{3,2,1,0:T(8,128)(2,1)}, bf16[2,2,304,768]{3,2,1,0:T(8,128)(2,1)}, bf16[2,2,304,768]{3,2,1,0:T(8,128)(2,1)}, bf16[2,2,304,768]{3,2,1,0:T(8,128)(2,1)}) custom-call(bf16[2,304,768]{2,1,0:T(8,128)(2,1)} %pad_maximum_fusion.2.query_ref, bf16[2,304,768]{2,1,0:T(8,128)(2,1)} %pad_maximum_fusion.3.grad_ref, ...), custom_call_target="tpu_custom_call" | custom-call | flops 22712156160 | bytes 14942208 | tf_op jit(solution)/shard_map/pallas_call | solution.py:565
  577.9 4.9 add_convert_fusion.4
  583.5 7.6 collective-permute-done.68
  593.5 4.2 add_convert_fusion.1
  599.9 3.9 add_convert_fusion.10
  605.5 4.0 add_convert_fusion.7
  609.4 22.6 %collective-permute-done.70 = bf16[384,768]{1,0:T(8,128)(2,1)S(1)} collective-permute-done((bf16[384,768]{1,0:T(8,128)(2,1)S(1)}, bf16[384,768]{1,0:T(8,128)(2,1)S(1)}, u32[]{:S(2)}, u32[]{:S(2)}) %collective-permute-start.70) | collective-permute-done | bytes 589856 | tf_op jit(solution)/shard_map/ppermute | solution.py:134
  638.0 10.6 shard_map.333
  652.3 14.5 %shard_map.332 = (bf16[512,1536]{1,0:T(8,128)(2,1)}, bf16[3,768,768]{2,1,0:T(8,128)(2,1)}, bf16[3,768,768]{2,1,0:T(8,128)(2,1)}) custom-call(s32[2]{0:T(128)} %pad_add_fusion.spot_ref, bf16[1536,512]{1,0:T(8,128)(2,1)} %bitcast.268, bf16[3,512,768]{2,1,0:T(8,128)(2,1)} %pad_maximum_fusion.grad_ref, bf16[3,384,768]{2,1,0:T(8,128)(2,1)} %bitcast.10.rest_0_, ...), custom_call_target="tpu_custom_call" | custom-call | flops 7247757312 | bytes 14155776 | tf_op jit(solution)/shard_map/pallas_call | solution.py:259
  671.4 64.6 %collective-permute-done.78 = bf16[384,3072]{1,0:T(8,128)(2,1)} collective-permute-done((bf16[384,3072]{1,0:T(8,128)(2,1)}, bf16[384,3072]{1,0:T(8,128)(2,1)}, u32[]{:S(2)}, u32[]{:S(2)}) %collective-permute-start.78) | collective-permute-done | bytes 2359328 | tf_op jit(solution)/shard_map/ppermute | solution.py:39
  735.9 4.3 add_convert_fusion
  742.4 5.4 collective-permute-start.79
  750.7 5.0 add_convert_fusion.3
  761.6 5.4 multiply_reduce_fusion.2
  768.8 6.3 concatenate.83
  775.3 61.5 %collective-permute-done.41 = f32[2,2,2,1536]{3,1,2,0:T(2,128)S(1)} collective-permute-done((f32[2,2,2,1536]{3,1,2,0:T(2,128)S(1)}, f32[2,2,2,1536]{3,1,2,0:T(2,128)S(1)}, u32[]{:S(2)}, u32[]{:S(2)}) %collective-permute-start.41) | collective-permute-done | bytes 49184 | tf_op jit(solution)/shard_map/ppermute | solution.py:39
  839.9 4.0 add_convert_fusion.38
  847.7 4.3 add_convert_fusion.9
  853.6 5.0 add_convert_fusion.6
  858.6 6.5 collective-permute-start.43
  865.8 39.7 %collective-permute-done.43 = f32[2,2,2,2,1536]{4,2,0,3,1:T(2,128)S(1)} collective-permute-done((f32[2,2,2,2,1536]{4,2,0,3,1:T(2,128)S(1)}, f32[2,2,2,2,1536]{4,2,0,3,1:T(2,128)S(1)}, u32[]{:S(2)}, u32[]{:S(2)}) %collective-permute-start.43) | collective-permute-done | bytes 98336 | tf_op jit(solution)/shard_map/ppermute | solution.py:39
  915.0 12.1 collective-permute-done.47
  935.8 8.7 convolution_bitcast_fusion.3
  944.6 7.9 fusion.21
  954.1 8.9 fusion.30
  968.0 8.9 fusion.27
  983.1 11.7 collective-permute-done.81
  994.8 24.3 %collective-permute-done.90 = bf16[384,1536]{1,0:T(8,128)(2,1)S(1)} collective-permute-done((bf16[384,1536]{1,0:T(8,128)(2,1)S(1)}, bf16[384,1536]{1,0:T(8,128)(2,1)S(1)}, u32[]{:S(2)}, u32[]{:S(2)}) %collective-permute-start.90) | collective-permute-done | bytes 1179680 | tf_op jit(solution)/shard_map/ppermute | solution.py:134
  1026.5 49.0 %collective-permute-start.83 = (bf16[384,1536]{1,0:T(8,128)(2,1)S(1)}, bf16[384,1536]{1,0:T(8,128)(2,1)S(1)}, u32[]{:S(2)}, u32[]{:S(2)}) collective-permute-start(bf16[384,1536]{1,0:T(8,128)(2,1)S(1)} %get-tuple-element.156), channel_id=1, source_target_pairs={{0,8},{8,0},{16,24},{24,16},{1,9},{9,1},{17,25},{25,17},{2,10},{10... | collective-permute-start | bytes 3538952 | tf_op jit(solution)/shard_map/ppermute | solution.py:134
  1088.1 51.8 %collective-permute-done.57 = bf16[384,768]{1,0:T(8,128)(2,1)S(1)} collective-permute-done((bf16[384,768]{1,0:T(8,128)(2,1)S(1)}, bf16[384,768]{1,0:T(8,128)(2,1)S(1)}, u32[]{:S(2)}, u32[]{:S(2)}) %collective-permute-start.57) | collective-permute-done | bytes 589856 | tf_op jit(solution)/shard_map/ppermute | solution.py:134
  1143.6 17.4 %collective-permute-start.59 = (bf16[384,768]{1,0:T(8,128)(2,1)S(1)}, bf16[384,768]{1,0:T(8,128)(2,1)S(1)}, u32[]{:S(2)}, u32[]{:S(2)}) collective-permute-start(bf16[384,768]{1,0:T(8,128)(2,1)S(1)} %broadcast_select_fusion.18), channel_id=1, source_target_pairs={{0,8},{8,0},{16,24},{24,16},{1,9},{9,1},{17,25},{25,17},{2,10},{10... | collective-permute-start | bytes 1769480 | tf_op jit(solution)/shard_map/ppermute | solution.py:134
  1161.5 7.4 collective-permute-done.59
  1170.9 41.4 %collective-permute-start.85 = (bf16[384,1536]{1,0:T(8,128)(2,1)S(1)}, bf16[384,1536]{1,0:T(8,128)(2,1)S(1)}, u32[]{:S(2)}, u32[]{:S(2)}) collective-permute-start(bf16[384,1536]{1,0:T(8,128)(2,1)S(1)} %get-tuple-element.152), channel_id=1, source_target_pairs={{0,8},{8,0},{16,24},{24,16},{1,9},{9,1},{17,25},{25,17},{2,10},{10... | collective-permute-start | bytes 3538952 | tf_op jit(solution)/shard_map/ppermute | solution.py:134
  1212.6 5.7 collective-permute-start.54
  1221.9 42.6 %collective-permute-done.54 = bf16[384,768]{1,0:T(8,128)(2,1)S(1)} collective-permute-done((bf16[384,768]{1,0:T(8,128)(2,1)S(1)}, bf16[384,768]{1,0:T(8,128)(2,1)S(1)}, u32[]{:S(2)}, u32[]{:S(2)}) %collective-permute-start.54) | collective-permute-done | bytes 589856 | tf_op jit(solution)/shard_map/ppermute | solution.py:134
  1269.1 16.1 %collective-permute-start.61 = (bf16[384,768]{1,0:T(8,128)(2,1)S(1)}, bf16[384,768]{1,0:T(8,128)(2,1)S(1)}, u32[]{:S(2)}, u32[]{:S(2)}) collective-permute-start(bf16[384,768]{1,0:T(8,128)(2,1)S(1)} %get-tuple-element.168), channel_id=1, source_target_pairs={{0,8},{8,0},{16,24},{24,16},{1,9},{9,1},{17,25},{25,17},{2,10},{10... | collective-permute-start | bytes 1769480 | tf_op jit(solution)/shard_map/ppermute | solution.py:134
  1288.4 6.3 collective-permute-done.61
  1294.8 12.6 collective-permute-done.56
  1317.8 38.3 %collective-permute-done.65 = bf16[384,768]{1,0:T(8,128)(2,1)S(1)} collective-permute-done((bf16[384,768]{1,0:T(8,128)(2,1)S(1)}, bf16[384,768]{1,0:T(8,128)(2,1)S(1)}, u32[]{:S(2)}, u32[]{:S(2)}) %collective-permute-start.65) | collective-permute-done | bytes 589856 | tf_op jit(solution)/shard_map/ppermute | solution.py:134
  1356.2 12.6 collective-permute-done.63
  1371.0 11.0 collective-permute-done.87
  (571 shorter events, 258.0 us)
Async XLA Ops:
  9.2 47.0 %collective-permute-start = (f32[2,2,6,1536]{3,1,2,0:T(2,128)}, f32[2,2,6,1536]{3,1,2,0:T(2,128)}, u32[]{:S(2)}, u32[]{:S(2)}) collective-permute-start(f32[2,2,6,1536]{3,1,2,0:T(2,128)} %pad_maximum_fusion.9), channel_id=1, source_target_pairs={{0,2},{2,0},{4,6},{6,4},{1,3},{3,1},{5,7},{7,5},{8,10},{10,8},{12,... | collective-permute-start | bytes 442376 | tf_op jit(solution)/shard_map/ppermute | solution.py:39
  9.7 101.7 %collective-permute-start.7 = (bf16[3,384,768]{2,1,0:T(8,128)(2,1)S(1)}, bf16[3,384,768]{2,1,0:T(8,128)(2,1)}, u32[]{:S(2)}, u32[]{:S(2)}) collective-permute-start(bf16[3,384,768]{2,1,0:T(8,128)(2,1)S(1)} %bitcast.221), channel_id=1, source_target_pairs={{0,2},{2,0},{4,6},{6,4},{1,3},{3,1},{5,7},{7,5},{8,10},{10,8},{12,... | collective-permute-start | bytes 5308424 | tf_op jit(solution)/shard_map/ppermute | solution.py:39
  11.4 42.5 %collective-permute-start.3 = (bf16[3,384,768]{2,1,0:T(8,128)(2,1)S(1)}, bf16[3,384,768]{2,1,0:T(8,128)(2,1)S(1)}, u32[]{:S(2)}, u32[]{:S(2)}) collective-permute-start(bf16[3,384,768]{2,1,0:T(8,128)(2,1)S(1)} %broadcast_select_fusion.2), channel_id=1, source_target_pairs={{0,4},{2,6},{4,0},{6,2},{1,5},{3,7},{5,1},{7,3},{8,12},{10,14},{12... | collective-permute-start | bytes 5308424 | tf_op jit(solution)/shard_map/ppermute | solution.py:39
  14.5 107.7 %collective-permute-start.2 = (bf16[3,384,768]{2,1,0:T(8,128)(2,1)}, bf16[3,384,768]{2,1,0:T(8,128)(2,1)}, u32[]{:S(2)}, u32[]{:S(2)}) collective-permute-start(bf16[3,384,768]{2,1,0:T(8,128)(2,1)} %bitcast.10.rest_0_), channel_id=1, source_target_pairs={{0,2},{2,0},{4,6},{6,4},{1,3},{3,1},{5,7},{7,5},{8,10},{10,8},{12,... | collective-permute-start | bytes 5308424 | tf_op jit(solution)/shard_map/ppermute | solution.py:39
  17.9 117.3 %collective-permute-start.28 = (bf16[384,3072]{1,0:T(8,128)(2,1)}, bf16[384,3072]{1,0:T(8,128)(2,1)}, u32[]{:S(2)}, u32[]{:S(2)}) collective-permute-start(bf16[384,3072]{1,0:T(8,128)(2,1)} %broadcast_select_fusion), channel_id=1, source_target_pairs={{0,4},{2,6},{4,0},{6,2},{1,5},{3,7},{5,1},{7,3},{8,12},{10,14},{12... | collective-permute-start | bytes 7077896 | tf_op jit(solution)/shard_map/ppermute | solution.py:39
  53.9 54.3 %collective-permute-start.4 = (bf16[3,384,768]{2,1,0:T(8,128)(2,1)S(1)}, bf16[3,384,768]{2,1,0:T(8,128)(2,1)S(1)}, u32[]{:S(2)}, u32[]{:S(2)}) collective-permute-start(bf16[3,384,768]{2,1,0:T(8,128)(2,1)S(1)} %collective-permute-done.3.rest_2_), channel_id=1, source_target_pairs={{0,8},{8,0},{16,24},{24,16},{1,9},{9,1},{17,25},{25,17},{2,10},{10... | collective-permute-start | bytes 5308424 | tf_op jit(solution)/shard_map/ppermute | solution.py:39
  57.2 49.7 %collective-permute-start.1 = (f32[2,2,6,1536]{3,1,2,0:T(2,128)S(1)}, f32[2,2,6,1536]{3,1,2,0:T(2,128)S(1)}, u32[]{:S(2)}, u32[]{:S(2)}) collective-permute-start(f32[2,2,6,1536]{3,1,2,0:T(2,128)S(1)} %fusion.88), channel_id=1, source_target_pairs={{0,4},{2,6},{4,0},{6,2},{1,5},{3,7},{5,1},{7,3},{8,12},{10,14},{12... | collective-permute-start | bytes 442376 | tf_op jit(solution)/shard_map/ppermute | solution.py:39
  132.9 57.3 %collective-permute-start.9 = (bf16[2,2,304,768]{3,2,1,0:T(8,128)(2,1)S(1)}, bf16[2,2,304,768]{3,2,1,0:T(8,128)(2,1)S(1)}, u32[]{:S(2)}, u32[]{:S(2)}) collective-permute-start(bf16[2,2,304,768]{3,2,1,0:T(8,128)(2,1)S(1)} %pad_maximum_fusion.1.rest_0_), channel_id=1, source_target_pairs={{0,4},{2,6},{4,0},{6,2},{1,5},{3,7},{5,1},{7,3},{8,12},{10,14},{12... | collective-permute-start | bytes 5603336 | tf_op jit(solution)/shard_map/ppermute | solution.py:39
  134.8 53.6 %collective-permute-start.12 = (bf16[384,768]{1,0:T(8,128)(2,1)S(1)}, bf16[384,768]{1,0:T(8,128)(2,1)S(1)}, u32[]{:S(2)}, u32[]{:S(2)}) collective-permute-start(bf16[384,768]{1,0:T(8,128)(2,1)S(1)} %broadcast_select_fusion.21), channel_id=1, source_target_pairs={{0,4},{2,6},{4,0},{6,2},{1,5},{3,7},{5,1},{7,3},{8,12},{10,14},{12... | collective-permute-start | bytes 1769480 | tf_op jit(solution)/shard_map/ppermute | solution.py:39
  135.2 72.1 %collective-permute-start.29 = (bf16[384,3072]{1,0:T(8,128)(2,1)}, bf16[384,3072]{1,0:T(8,128)(2,1)}, u32[]{:S(2)}, u32[]{:S(2)}) collective-permute-start(bf16[384,3072]{1,0:T(8,128)(2,1)} %collective-permute-done.28.rest_4_), channel_id=1, source_target_pairs={{0,8},{8,0},{16,24},{24,16},{1,9},{9,1},{17,25},{25,17},{2,10},{10... | collective-permute-start | bytes 7077896 | tf_op jit(solution)/shard_map/ppermute | solution.py:39
  137.0 55.4 %collective-permute-start.24 = (bf16[384,768]{1,0:T(8,128)(2,1)S(1)}, bf16[384,768]{1,0:T(8,128)(2,1)S(1)}, u32[]{:S(2)}, u32[]{:S(2)}) collective-permute-start(bf16[384,768]{1,0:T(8,128)(2,1)S(1)} %copy-done.37), channel_id=1, source_target_pairs={{0,2},{2,0},{4,6},{6,4},{1,3},{3,1},{5,7},{7,5},{8,10},{10,8},{12,... | collective-permute-start | bytes 1769480 | tf_op jit(solution)/shard_map/ppermute | solution.py:39
  192.4 53.9 %collective-permute-start.19 = (bf16[384,3072]{1,0:T(8,128)(2,1)}, bf16[384,3072]{1,0:T(8,128)(2,1)}, u32[]{:S(2)}, u32[]{:S(2)}) collective-permute-start(bf16[384,3072]{1,0:T(8,128)(2,1)} %broadcast_select_fusion.1), channel_id=1, source_target_pairs={{0,4},{2,6},{4,0},{6,2},{1,5},{3,7},{5,1},{7,3},{8,12},{10,14},{12... | collective-permute-start | bytes 7077896 | tf_op jit(solution)/shard_map/ppermute | solution.py:39
  207.1 52.4 %collective-permute-start.26 = (bf16[384,3072]{1,0:T(8,128)(2,1)}, bf16[384,3072]{1,0:T(8,128)(2,1)}, u32[]{:S(2)}, u32[]{:S(2)}) collective-permute-start(bf16[384,3072]{1,0:T(8,128)(2,1)} %rest_0_.9), channel_id=1, source_target_pairs={{0,2},{2,0},{4,6},{6,4},{1,3},{3,1},{5,7},{7,5},{8,10},{10,8},{12,... | collective-permute-start | bytes 7077896 | tf_op jit(solution)/shard_map/ppermute | solution.py:39
  207.3 52.2 %collective-permute-start.27 = (bf16[384,3072]{1,0:T(8,128)(2,1)}, bf16[384,3072]{1,0:T(8,128)(2,1)}, u32[]{:S(2)}, u32[]{:S(2)}) collective-permute-start(bf16[384,3072]{1,0:T(8,128)(2,1)} %rest_1_.3), channel_id=1, source_target_pairs={{0,2},{2,0},{4,6},{6,4},{1,3},{3,1},{5,7},{7,5},{8,10},{10,8},{12,... | collective-permute-start | bytes 7077896 | tf_op jit(solution)/shard_map/ppermute | solution.py:39
  207.6 51.9 %collective-permute-start.30 = (bf16[384,3072]{1,0:T(8,128)(2,1)}, bf16[384,3072]{1,0:T(8,128)(2,1)}, u32[]{:S(2)}, u32[]{:S(2)}) collective-permute-start(bf16[384,3072]{1,0:T(8,128)(2,1)} %collective-permute-done.28.rest_4_), channel_id=1, source_target_pairs={{0,2},{2,0},{4,6},{6,4},{1,3},{3,1},{5,7},{7,5},{8,10},{10,8},{12,... | collective-permute-start | bytes 7077896 | tf_op jit(solution)/shard_map/ppermute | solution.py:39
  210.1 49.4 %collective-permute-start.31 = (bf16[384,3072]{1,0:T(8,128)(2,1)}, bf16[384,3072]{1,0:T(8,128)(2,1)}, u32[]{:S(2)}, u32[]{:S(2)}) collective-permute-start(bf16[384,3072]{1,0:T(8,128)(2,1)} %collective-permute-done.29.rest_5_), channel_id=1, source_target_pairs={{0,2},{2,0},{4,6},{6,4},{1,3},{3,1},{5,7},{7,5},{8,10},{10,8},{12,... | collective-permute-start | bytes 7077896 | tf_op jit(solution)/shard_map/ppermute | solution.py:39
  254.9 52.1 %collective-permute-start.20 = (bf16[384,3072]{1,0:T(8,128)(2,1)}, bf16[384,3072]{1,0:T(8,128)(2,1)}, u32[]{:S(2)}, u32[]{:S(2)}) collective-permute-start(bf16[384,3072]{1,0:T(8,128)(2,1)} %collective-permute-done.19.rest_4_), channel_id=1, source_target_pairs={{0,8},{8,0},{16,24},{24,16},{1,9},{9,1},{17,25},{25,17},{2,10},{10... | collective-permute-start | bytes 7077896 | tf_op jit(solution)/shard_map/ppermute | solution.py:39
  283.1 74.8 %collective-permute-start.17 = (bf16[384,3072]{1,0:T(8,128)(2,1)}, bf16[384,3072]{1,0:T(8,128)(2,1)}, u32[]{:S(2)}, u32[]{:S(2)}) collective-permute-start(bf16[384,3072]{1,0:T(8,128)(2,1)} %rest_0_.7), channel_id=1, source_target_pairs={{0,2},{2,0},{4,6},{6,4},{1,3},{3,1},{5,7},{7,5},{8,10},{10,8},{12,... | collective-permute-start | bytes 7077896 | tf_op jit(solution)/shard_map/ppermute | solution.py:39
  283.3 74.6 %collective-permute-start.18 = (bf16[384,3072]{1,0:T(8,128)(2,1)}, bf16[384,3072]{1,0:T(8,128)(2,1)}, u32[]{:S(2)}, u32[]{:S(2)}) collective-permute-start(bf16[384,3072]{1,0:T(8,128)(2,1)} %rest_1_.2), channel_id=1, source_target_pairs={{0,2},{2,0},{4,6},{6,4},{1,3},{3,1},{5,7},{7,5},{8,10},{10,8},{12,... | collective-permute-start | bytes 7077896 | tf_op jit(solution)/shard_map/ppermute | solution.py:39
  290.7 52.1 %collective-permute-start.16 = (bf16[512,1536]{1,0:T(8,128)(2,1)}, bf16[512,1536]{1,0:T(8,128)(2,1)S(1)}, u32[]{:S(2)}, u32[]{:S(2)}) collective-permute-start(bf16[512,1536]{1,0:T(8,128)(2,1)} %shard_map.325), channel_id=1, source_target_pairs={{0,1},{1,0},{2,3},{3,2},{4,5},{5,4},{6,7},{7,6},{8,9},{9,8},{10,11... | collective-permute-start | bytes 4718600 | tf_op jit(solution)/shard_map/ppermute | solution.py:39
  291.1 42.6 %collective-permute-start.32 = (bf16[96,1536]{1,0:T(8,128)(2,1)S(1)}, bf16[96,1536]{1,0:T(8,128)(2,1)S(1)}, u32[]{:S(2)}, u32[]{:S(2)}) collective-permute-start(bf16[96,1536]{1,0:T(8,128)(2,1)S(1)} %copy-done.59), channel_id=1, source_target_pairs={{0,1},{1,0},{2,3},{3,2},{4,5},{5,4},{6,7},{7,6},{8,9},{9,8},{10,11... | collective-permute-start | bytes 884744 | tf_op jit(solution)/shard_map/ppermute | solution.py:39
  307.0 51.0 %collective-permute-start.21 = (bf16[384,3072]{1,0:T(8,128)(2,1)}, bf16[384,3072]{1,0:T(8,128)(2,1)}, u32[]{:S(2)}, u32[]{:S(2)}) collective-permute-start(bf16[384,3072]{1,0:T(8,128)(2,1)} %collective-permute-done.19.rest_4_), channel_id=1, source_target_pairs={{0,2},{2,0},{4,6},{6,4},{1,3},{3,1},{5,7},{7,5},{8,10},{10,8},{12,... | collective-permute-start | bytes 7077896 | tf_op jit(solution)/shard_map/ppermute | solution.py:39
  356.4 46.2 %collective-permute-start.98 = (bf16[384,768]{1,0:T(8,128)(2,1)}, bf16[384,768]{1,0:T(8,128)(2,1)}, u32[]{:S(2)}, u32[]{:S(2)}) collective-permute-start(bf16[384,768]{1,0:T(8,128)(2,1)} %add_convert_fusion.42), channel_id=1, source_target_pairs={{0,4},{2,6},{4,0},{6,2},{1,5},{3,7},{5,1},{7,3},{8,12},{10,14},{12... | collective-permute-start | bytes 1769480 | tf_op jit(solution)/shard_map/ppermute | solution.py:39
  400.5 37.5 %collective-permute-start.33 = (bf16[512,1536]{1,0:T(8,128)(2,1)}, bf16[512,1536]{1,0:T(8,128)(2,1)S(1)}, u32[]{:S(2)}, u32[]{:S(2)}) collective-permute-start(bf16[512,1536]{1,0:T(8,128)(2,1)} %get-tuple-element.49), channel_id=1, source_target_pairs={{0,1},{1,0},{2,3},{3,2},{4,5},{5,4},{6,7},{7,6},{8,9},{9,8},{10,11... | collective-permute-start | bytes 4718600 | tf_op jit(solution)/shard_map/ppermute | solution.py:39
  401.1 69.9 %collective-permute-start.23 = (bf16[512,1536]{1,0:T(8,128)(2,1)}, bf16[512,1536]{1,0:T(8,128)(2,1)S(1)}, u32[]{:S(2)}, u32[]{:S(2)}) collective-permute-start(bf16[512,1536]{1,0:T(8,128)(2,1)} %get-tuple-element.47), channel_id=1, source_target_pairs={{0,1},{1,0},{2,3},{3,2},{4,5},{5,4},{6,7},{7,6},{8,9},{9,8},{10,11... | collective-permute-start | bytes 4718600 | tf_op jit(solution)/shard_map/ppermute | solution.py:39
  407.7 168.6 %collective-permute-start.75 = (bf16[768,3072]{1,0:T(8,128)(2,1)}, bf16[768,3072]{1,0:T(8,128)(2,1)}, u32[]{:S(2)}, u32[]{:S(2)}) collective-permute-start(bf16[768,3072]{1,0:T(8,128)(2,1)} %get-tuple-element.71), channel_id=1, source_target_pairs={{0,2},{2,0},{4,6},{6,4},{1,3},{3,1},{5,7},{7,5},{8,10},{10,8},{12,... | collective-permute-start | bytes 14155784 | tf_op jit(solution)/shard_map/ppermute | solution.py:39
  421.0 75.7 %collective-permute-start.100 = (bf16[384,768]{1,0:T(8,128)(2,1)}, bf16[384,768]{1,0:T(8,128)(2,1)}, u32[]{:S(2)}, u32[]{:S(2)}) collective-permute-start(bf16[384,768]{1,0:T(8,128)(2,1)} %add_convert_fusion.40), channel_id=1, source_target_pairs={{8,16},{16,8},{9,17},{17,9},{10,18},{18,10},{11,19},{19,11},{12,20... | collective-permute-start | bytes 1769480 | tf_op jit(solution)/shard_map/ppermute | solution.py:138
  505.8 87.0 %collective-permute-start.77 = (bf16[768,3072]{1,0:T(8,128)(2,1)}, bf16[768,3072]{1,0:T(8,128)(2,1)}, u32[]{:S(2)}, u32[]{:S(2)}) collective-permute-start(bf16[768,3072]{1,0:T(8,128)(2,1)} %get-tuple-element.73), channel_id=1, source_target_pairs={{0,2},{2,0},{4,6},{6,4},{1,3},{3,1},{5,7},{7,5},{8,10},{10,8},{12,... | collective-permute-start | bytes 14155784 | tf_op jit(solution)/shard_map/ppermute | solution.py:39
  508.0 90.3 %collective-permute-start.71 = (bf16[768,3072]{1,0:T(8,128)(2,1)}, bf16[768,3072]{1,0:T(8,128)(2,1)}, u32[]{:S(2)}, u32[]{:S(2)}) collective-permute-start(bf16[768,3072]{1,0:T(8,128)(2,1)} %get-tuple-element.67), channel_id=1, source_target_pairs={{0,2},{2,0},{4,6},{6,4},{1,3},{3,1},{5,7},{7,5},{8,10},{10,8},{12,... | collective-permute-start | bytes 14155784 | tf_op jit(solution)/shard_map/ppermute | solution.py:39
  510.4 93.5 %collective-permute-start.73 = (bf16[768,3072]{1,0:T(8,128)(2,1)}, bf16[768,3072]{1,0:T(8,128)(2,1)}, u32[]{:S(2)}, u32[]{:S(2)}) collective-permute-start(bf16[768,3072]{1,0:T(8,128)(2,1)} %get-tuple-element.69), channel_id=1, source_target_pairs={{0,2},{2,0},{4,6},{6,4},{1,3},{3,1},{5,7},{7,5},{8,10},{10,8},{12,... | collective-permute-start | bytes 14155784 | tf_op jit(solution)/shard_map/ppermute | solution.py:39
  516.9 51.6 %collective-permute-start.67 = (bf16[384,768]{1,0:T(8,128)(2,1)}, bf16[384,768]{1,0:T(8,128)(2,1)}, u32[]{:S(2)}, u32[]{:S(2)}) collective-permute-start(bf16[384,768]{1,0:T(8,128)(2,1)} %add_convert_fusion.47), channel_id=1, source_target_pairs={{0,4},{2,6},{4,0},{6,2},{1,5},{3,7},{5,1},{7,3},{8,12},{10,14},{12... | collective-permute-start | bytes 1769480 | tf_op jit(solution)/shard_map/ppermute | solution.py:39
  582.8 50.9 %collective-permute-start.35 = (bf16[2,2,304,768]{3,2,1,0:T(8,128)(2,1)S(1)}, bf16[2,2,304,768]{3,2,1,0:T(8,128)(2,1)S(1)}, u32[]{:S(2)}, u32[]{:S(2)}) collective-permute-start(bf16[2,2,304,768]{3,2,1,0:T(8,128)(2,1)S(1)} %copy-done.88), channel_id=1, source_target_pairs={{0,2},{2,0},{4,6},{6,4},{1,3},{3,1},{5,7},{7,5},{8,10},{10,8},{12,... | collective-permute-start | bytes 5603336 | tf_op jit(solution)/shard_map/ppermute | solution.py:39
  591.1 44.1 %collective-permute-start.37 = (bf16[2,2,304,768]{3,2,1,0:T(8,128)(2,1)S(1)}, bf16[2,2,304,768]{3,2,1,0:T(8,128)(2,1)S(1)}, u32[]{:S(2)}, u32[]{:S(2)}) collective-permute-start(bf16[2,2,304,768]{3,2,1,0:T(8,128)(2,1)S(1)} %add_convert_fusion.13), channel_id=1, source_target_pairs={{0,4},{2,6},{4,0},{6,2},{1,5},{3,7},{5,1},{7,3},{8,12},{10,14},{12... | collective-permute-start | bytes 5603336 | tf_op jit(solution)/shard_map/ppermute | solution.py:39
  597.7 150.1 %collective-permute-start.76 = (bf16[384,3072]{1,0:T(8,128)(2,1)}, bf16[384,3072]{1,0:T(8,128)(2,1)}, u32[]{:S(2)}, u32[]{:S(2)}) collective-permute-start(bf16[384,3072]{1,0:T(8,128)(2,1)} %add_convert_fusion.4), channel_id=1, source_target_pairs={{0,4},{2,6},{4,0},{6,2},{1,5},{3,7},{5,1},{7,3},{8,12},{10,14},{12... | collective-permute-start | bytes 7077896 | tf_op jit(solution)/shard_map/ppermute | solution.py:39
  598.3 137.6 %collective-permute-start.78 = (bf16[384,3072]{1,0:T(8,128)(2,1)}, bf16[384,3072]{1,0:T(8,128)(2,1)}, u32[]{:S(2)}, u32[]{:S(2)}) collective-permute-start(bf16[384,3072]{1,0:T(8,128)(2,1)} %add_convert_fusion.1), channel_id=1, source_target_pairs={{0,4},{2,6},{4,0},{6,2},{1,5},{3,7},{5,1},{7,3},{8,12},{10,14},{12... | collective-permute-start | bytes 7077896 | tf_op jit(solution)/shard_map/ppermute | solution.py:39
  632.1 213.6 %collective-permute-start.72 = (bf16[384,3072]{1,0:T(8,128)(2,1)}, bf16[384,3072]{1,0:T(8,128)(2,1)}, u32[]{:S(2)}, u32[]{:S(2)}) collective-permute-start(bf16[384,3072]{1,0:T(8,128)(2,1)} %add_convert_fusion.10), channel_id=1, source_target_pairs={{0,4},{2,6},{4,0},{6,2},{1,5},{3,7},{5,1},{7,3},{8,12},{10,14},{12... | collective-permute-start | bytes 7077896 | tf_op jit(solution)/shard_map/ppermute | solution.py:39
  633.7 218.3 %collective-permute-start.74 = (bf16[384,3072]{1,0:T(8,128)(2,1)}, bf16[384,3072]{1,0:T(8,128)(2,1)}, u32[]{:S(2)}, u32[]{:S(2)}) collective-permute-start(bf16[384,3072]{1,0:T(8,128)(2,1)} %add_convert_fusion.7), channel_id=1, source_target_pairs={{0,4},{2,6},{4,0},{6,2},{1,5},{3,7},{5,1},{7,3},{8,12},{10,14},{12... | collective-permute-start | bytes 7077896 | tf_op jit(solution)/shard_map/ppermute | solution.py:39
  666.8 89.0 %collective-permute-start.38 = (bf16[512,1536]{1,0:T(8,128)(2,1)}, bf16[512,1536]{1,0:T(8,128)(2,1)S(1)}, u32[]{:S(2)}, u32[]{:S(2)}) collective-permute-start(bf16[512,1536]{1,0:T(8,128)(2,1)} %get-tuple-element.58), channel_id=1, source_target_pairs={{0,1},{1,0},{2,3},{3,2},{4,5},{5,4},{6,7},{7,6},{8,9},{9,8},{10,11... | collective-permute-start | bytes 4718600 | tf_op jit(solution)/shard_map/ppermute | solution.py:39
  742.4 94.4 %collective-permute-start.79 = (bf16[384,1536]{1,0:T(8,128)(2,1)}, bf16[384,1536]{1,0:T(8,128)(2,1)}, u32[]{:S(2)}, u32[]{:S(2)}) collective-permute-start(bf16[384,1536]{1,0:T(8,128)(2,1)} %get-tuple-element.164), channel_id=1, source_target_pairs={{0,8},{24,16},{1,9},{25,17},{2,10},{26,18},{3,11},{27,19},{4,12},{... | collective-permute-start | bytes 3538952 | tf_op jit(solution)/shard_map/ppermute | solution.py:134
  747.8 89.6 %collective-permute-start.88 = (bf16[384,1536]{1,0:T(8,128)(2,1)}, bf16[384,1536]{1,0:T(8,128)(2,1)}, u32[]{:S(2)}, u32[]{:S(2)}) collective-permute-start(bf16[384,1536]{1,0:T(8,128)(2,1)} %get-tuple-element.165), channel_id=1, source_target_pairs={{0,8},{24,16},{1,9},{25,17},{2,10},{26,18},{3,11},{27,19},{4,12},{... | collective-permute-start | bytes 3538952 | tf_op jit(solution)/shard_map/ppermute | solution.py:134
  767.2 69.6 %collective-permute-start.41 = (f32[2,2,2,1536]{3,1,2,0:T(2,128)S(1)}, f32[2,2,2,1536]{3,1,2,0:T(2,128)S(1)}, u32[]{:S(2)}, u32[]{:S(2)}) collective-permute-start(f32[2,2,2,1536]{3,1,2,0:T(2,128)S(1)} %fusion.87), channel_id=1, source_target_pairs={{0,4},{2,6},{4,0},{6,2},{1,5},{3,7},{5,1},{7,3},{8,12},{10,14},{12... | collective-permute-start | bytes 147464 | tf_op jit(solution)/shard_map/ppermute | solution.py:39
  836.8 140.0 %collective-permute-start.48 = (bf16[3,768,768]{2,1,0:T(8,128)(2,1)}, bf16[3,768,768]{2,1,0:T(8,128)(2,1)}, u32[]{:S(2)}, u32[]{:S(2)}) collective-permute-start(bf16[3,768,768]{2,1,0:T(8,128)(2,1)} %get-tuple-element.61), channel_id=1, source_target_pairs={{0,2},{2,0},{4,6},{6,4},{1,3},{3,1},{5,7},{7,5},{8,10},{10,8},{12,... | collective-permute-start | bytes 10616840 | tf_op jit(solution)/shard_map/ppermute | solution.py:39
  843.9 136.6 %collective-permute-start.50 = (bf16[3,768,768]{2,1,0:T(8,128)(2,1)}, bf16[3,768,768]{2,1,0:T(8,128)(2,1)}, u32[]{:S(2)}, u32[]{:S(2)}) collective-permute-start(bf16[3,768,768]{2,1,0:T(8,128)(2,1)} %get-tuple-element.63), channel_id=1, source_target_pairs={{0,2},{2,0},{4,6},{6,4},{1,3},{3,1},{5,7},{7,5},{8,10},{10,8},{12,... | collective-permute-start | bytes 10616840 | tf_op jit(solution)/shard_map/ppermute | solution.py:39
  843.9 119.0 %collective-permute-start.80 = (bf16[384,1536]{1,0:T(8,128)(2,1)S(1)}, bf16[384,1536]{1,0:T(8,128)(2,1)}, u32[]{:S(2)}, u32[]{:S(2)}) collective-permute-start(bf16[384,1536]{1,0:T(8,128)(2,1)S(1)} %get-tuple-element.162), channel_id=1, source_target_pairs={{8,16},{16,8},{9,17},{17,9},{10,18},{18,10},{11,19},{19,11},{12,20... | collective-permute-start | bytes 3538952 | tf_op jit(solution)/shard_map/ppermute | solution.py:138
  845.7 117.2 %collective-permute-start.89 = (bf16[384,1536]{1,0:T(8,128)(2,1)}, bf16[384,1536]{1,0:T(8,128)(2,1)}, u32[]{:S(2)}, u32[]{:S(2)}) collective-permute-start(bf16[384,1536]{1,0:T(8,128)(2,1)} %get-tuple-element.163), channel_id=1, source_target_pairs={{8,16},{16,8},{9,17},{17,9},{10,18},{18,10},{11,19},{19,11},{12,20... | collective-permute-start | bytes 3538952 | tf_op jit(solution)/shard_map/ppermute | solution.py:138
  858.6 46.8 %collective-permute-start.43 = (f32[2,2,2,2,1536]{4,2,0,3,1:T(2,128)S(1)}, f32[2,2,2,2,1536]{4,2,0,3,1:T(2,128)S(1)}, u32[]{:S(2)}, u32[]{:S(2)}) collective-permute-start(f32[2,2,2,2,1536]{4,2,0,3,1:T(2,128)S(1)} %pad_maximum_fusion.10), channel_id=1, source_target_pairs={{0,16},{8,24},{16,0},{24,8},{1,17},{9,25},{17,1},{25,9},{2,18},{10... | collective-permute-start | bytes 294920 | tf_op jit(solution)/shard_map/ppermute | solution.py:39
  965.9 53.1 %collective-permute-start.90 = (bf16[384,1536]{1,0:T(8,128)(2,1)S(1)}, bf16[384,1536]{1,0:T(8,128)(2,1)S(1)}, u32[]{:S(2)}, u32[]{:S(2)}) collective-permute-start(bf16[384,1536]{1,0:T(8,128)(2,1)S(1)} %get-tuple-element.161), channel_id=1, source_target_pairs={{0,8},{8,0},{16,24},{24,16},{1,9},{9,1},{17,25},{25,17},{2,10},{10... | collective-permute-start | bytes 3538952 | tf_op jit(solution)/shard_map/ppermute | solution.py:134
  978.9 107.0 %collective-permute-start.49 = (bf16[3,384,768]{2,1,0:T(8,128)(2,1)S(1)}, bf16[3,384,768]{2,1,0:T(8,128)(2,1)S(1)}, u32[]{:S(2)}, u32[]{:S(2)}) collective-permute-start(bf16[3,384,768]{2,1,0:T(8,128)(2,1)S(1)} %add_convert_fusion.19), channel_id=1, source_target_pairs={{0,4},{2,6},{4,0},{6,2},{1,5},{3,7},{5,1},{7,3},{8,12},{10,14},{12... | collective-permute-start | bytes 5308424 | tf_op jit(solution)/shard_map/ppermute | solution.py:39
  982.5 93.2 %collective-permute-start.51 = (bf16[3,384,768]{2,1,0:T(8,128)(2,1)S(1)}, bf16[3,384,768]{2,1,0:T(8,128)(2,1)S(1)}, u32[]{:S(2)}, u32[]{:S(2)}) collective-permute-start(bf16[3,384,768]{2,1,0:T(8,128)(2,1)S(1)} %add_convert_fusion.16), channel_id=1, source_target_pairs={{0,4},{2,6},{4,0},{6,2},{1,5},{3,7},{5,1},{7,3},{8,12},{10,14},{12... | collective-permute-start | bytes 5308424 | tf_op jit(solution)/shard_map/ppermute | solution.py:39
  1026.5 114.2 %collective-permute-start.83 = (bf16[384,1536]{1,0:T(8,128)(2,1)S(1)}, bf16[384,1536]{1,0:T(8,128)(2,1)S(1)}, u32[]{:S(2)}, u32[]{:S(2)}) collective-permute-start(bf16[384,1536]{1,0:T(8,128)(2,1)S(1)} %get-tuple-element.156), channel_id=1, source_target_pairs={{0,8},{8,0},{16,24},{24,16},{1,9},{9,1},{17,25},{25,17},{2,10},{10... | collective-permute-start | bytes 3538952 | tf_op jit(solution)/shard_map/ppermute | solution.py:134
  1075.6 65.2 %collective-permute-start.92 = (bf16[384,1536]{1,0:T(8,128)(2,1)S(1)}, bf16[384,1536]{1,0:T(8,128)(2,1)S(1)}, u32[]{:S(2)}, u32[]{:S(2)}) collective-permute-start(bf16[384,1536]{1,0:T(8,128)(2,1)S(1)} %get-tuple-element.157), channel_id=1, source_target_pairs={{0,8},{8,0},{16,24},{24,16},{1,9},{9,1},{17,25},{25,17},{2,10},{10... | collective-permute-start | bytes 3538952 | tf_op jit(solution)/shard_map/ppermute | solution.py:134
  1077.9 62.0 %collective-permute-start.57 = (bf16[384,768]{1,0:T(8,128)(2,1)S(1)}, bf16[384,768]{1,0:T(8,128)(2,1)S(1)}, u32[]{:S(2)}, u32[]{:S(2)}) collective-permute-start(bf16[384,768]{1,0:T(8,128)(2,1)S(1)} %get-tuple-element.172), channel_id=1, source_target_pairs={{0,8},{24,16},{1,9},{25,17},{2,10},{26,18},{3,11},{27,19},{4,12},{... | collective-permute-start | bytes 1769480 | tf_op jit(solution)/shard_map/ppermute | solution.py:134
  1084.6 76.9 %collective-permute-start.52 = (bf16[384,768]{1,0:T(8,128)(2,1)S(1)}, bf16[384,768]{1,0:T(8,128)(2,1)S(1)}, u32[]{:S(2)}, u32[]{:S(2)}) collective-permute-start(bf16[384,768]{1,0:T(8,128)(2,1)S(1)} %get-tuple-element.173), channel_id=1, source_target_pairs={{0,8},{24,16},{1,9},{25,17},{2,10},{26,18},{3,11},{27,19},{4,12},{... | collective-permute-start | bytes 1769480 | tf_op jit(solution)/shard_map/ppermute | solution.py:134
  1169.2 43.2 %collective-permute-start.53 = (bf16[384,768]{1,0:T(8,128)(2,1)S(1)}, bf16[384,768]{1,0:T(8,128)(2,1)S(1)}, u32[]{:S(2)}, u32[]{:S(2)}) collective-permute-start(bf16[384,768]{1,0:T(8,128)(2,1)S(1)} %get-tuple-element.171), channel_id=1, source_target_pairs={{8,16},{16,8},{9,17},{17,9},{10,18},{18,10},{11,19},{19,11},{12,20... | collective-permute-start | bytes 1769480 | tf_op jit(solution)/shard_map/ppermute | solution.py:138
  1170.9 94.8 %collective-permute-start.85 = (bf16[384,1536]{1,0:T(8,128)(2,1)S(1)}, bf16[384,1536]{1,0:T(8,128)(2,1)S(1)}, u32[]{:S(2)}, u32[]{:S(2)}) collective-permute-start(bf16[384,1536]{1,0:T(8,128)(2,1)S(1)} %get-tuple-element.152), channel_id=1, source_target_pairs={{0,8},{8,0},{16,24},{24,16},{1,9},{9,1},{17,25},{25,17},{2,10},{10... | collective-permute-start | bytes 3538952 | tf_op jit(solution)/shard_map/ppermute | solution.py:134
  1212.3 53.4 %collective-permute-start.94 = (bf16[384,1536]{1,0:T(8,128)(2,1)S(1)}, bf16[384,1536]{1,0:T(8,128)(2,1)S(1)}, u32[]{:S(2)}, u32[]{:S(2)}) collective-permute-start(bf16[384,1536]{1,0:T(8,128)(2,1)S(1)} %get-tuple-element.153), channel_id=1, source_target_pairs={{0,8},{8,0},{16,24},{24,16},{1,9},{9,1},{17,25},{25,17},{2,10},{10... | collective-permute-start | bytes 3538952 | tf_op jit(solution)/shard_map/ppermute | solution.py:134
  1212.6 52.0 %collective-permute-start.54 = (bf16[384,768]{1,0:T(8,128)(2,1)S(1)}, bf16[384,768]{1,0:T(8,128)(2,1)S(1)}, u32[]{:S(2)}, u32[]{:S(2)}) collective-permute-start(bf16[384,768]{1,0:T(8,128)(2,1)S(1)} %broadcast_select_fusion.20), channel_id=1, source_target_pairs={{0,8},{8,0},{16,24},{24,16},{1,9},{9,1},{17,25},{25,17},{2,10},{10... | collective-permute-start | bytes 1769480 | tf_op jit(solution)/shard_map/ppermute | solution.py:134
  1221.0 47.6 %collective-permute-start.60 = (bf16[384,768]{1,0:T(8,128)(2,1)S(1)}, bf16[384,768]{1,0:T(8,128)(2,1)S(1)}, u32[]{:S(2)}, u32[]{:S(2)}) collective-permute-start(bf16[384,768]{1,0:T(8,128)(2,1)S(1)} %get-tuple-element.170), channel_id=1, source_target_pairs={{8,16},{16,8},{9,17},{17,9},{10,18},{18,10},{11,19},{19,11},{12,20... | collective-permute-start | bytes 1769480 | tf_op jit(solution)/shard_map/ppermute | solution.py:138
  1266.4 45.4 %collective-permute-start.95 = (bf16[384,1536]{1,0:T(8,128)(2,1)S(1)}, bf16[384,1536]{1,0:T(8,128)(2,1)S(1)}, u32[]{:S(2)}, u32[]{:S(2)}) collective-permute-start(bf16[384,1536]{1,0:T(8,128)(2,1)S(1)} %get-tuple-element.151), channel_id=1, source_target_pairs={{8,16},{16,8},{9,17},{17,9},{10,18},{18,10},{11,19},{19,11},{12,20... | collective-permute-start | bytes 3538952 | tf_op jit(solution)/shard_map/ppermute | solution.py:138
  1267.1 49.1 %collective-permute-start.86 = (bf16[384,1536]{1,0:T(8,128)(2,1)S(1)}, bf16[384,1536]{1,0:T(8,128)(2,1)S(1)}, u32[]{:S(2)}, u32[]{:S(2)}) collective-permute-start(bf16[384,1536]{1,0:T(8,128)(2,1)S(1)} %get-tuple-element.150), channel_id=1, source_target_pairs={{8,16},{16,8},{9,17},{17,9},{10,18},{18,10},{11,19},{19,11},{12,20... | collective-permute-start | bytes 3538952 | tf_op jit(solution)/shard_map/ppermute | solution.py:138
  1312.0 58.9 %collective-permute-start.96 = (bf16[384,1536]{1,0:T(8,128)(2,1)S(1)}, bf16[384,1536]{1,0:T(8,128)(2,1)S(1)}, u32[]{:S(2)}, u32[]{:S(2)}) collective-permute-start(bf16[384,1536]{1,0:T(8,128)(2,1)S(1)} %add_convert_fusion.23), channel_id=1, source_target_pairs={{8,0},{16,24},{9,1},{17,25},{10,2},{18,26},{11,3},{19,27},{12,4},{... | collective-permute-start | bytes 3538952 | tf_op jit(solution)/shard_map/ppermute | solution.py:134
  1313.5 42.6 %collective-permute-start.65 = (bf16[384,768]{1,0:T(8,128)(2,1)S(1)}, bf16[384,768]{1,0:T(8,128)(2,1)S(1)}, u32[]{:S(2)}, u32[]{:S(2)}) collective-permute-start(bf16[384,768]{1,0:T(8,128)(2,1)S(1)} %add_convert_fusion.49), channel_id=1, source_target_pairs={{8,0},{16,24},{9,1},{17,25},{10,2},{18,26},{11,3},{19,27},{12,4},{... | collective-permute-start | bytes 1769480 | tf_op jit(solution)/shard_map/ppermute | solution.py:134
  1314.9 53.8 %collective-permute-start.63 = (bf16[384,768]{1,0:T(8,128)(2,1)S(1)}, bf16[384,768]{1,0:T(8,128)(2,1)S(1)}, u32[]{:S(2)}, u32[]{:S(2)}) collective-permute-start(bf16[384,768]{1,0:T(8,128)(2,1)S(1)} %add_convert_fusion.51), channel_id=1, source_target_pairs={{8,0},{16,24},{9,1},{17,25},{10,2},{18,26},{11,3},{19,27},{12,4},{... | collective-permute-start | bytes 1769480 | tf_op jit(solution)/shard_map/ppermute | solution.py:134
  1316.5 65.5 %collective-permute-start.87 = (bf16[384,1536]{1,0:T(8,128)(2,1)S(1)}, bf16[384,1536]{1,0:T(8,128)(2,1)S(1)}, u32[]{:S(2)}, u32[]{:S(2)}) collective-permute-start(bf16[384,1536]{1,0:T(8,128)(2,1)S(1)} %add_convert_fusion.31), channel_id=1, source_target_pairs={{8,0},{16,24},{9,1},{17,25},{10,2},{18,26},{11,3},{19,27},{12,4},{... | collective-permute-start | bytes 3538952 | tf_op jit(solution)/shard_map/ppermute | solution.py:134
  (143 other events, 2512.9 us)

commit v3 on v2

v3 whole, which is shorter than its diff:
```python
import functools

import jax
import jax.numpy as jnp
from jax import lax
from jax.experimental import pallas as pl
from jax.experimental.pallas import tpu as pltpu
from jax.sharding import PartitionSpec as P

HD = 64
LANES = 128
VMEM_LIMIT = 60 * 1024 * 1024
SMALL_COST = pl.CostEstimate(flops=1024, bytes_accessed=1024, transcendentals=0)

exact_mode = lax.Precision.HIGHEST


def normed(values):
    centered = values - jnp.mean(values, axis=-1, keepdims=True)
    scale = lax.rsqrt(jnp.mean(centered * centered, axis=-1, keepdims=True) + 1e-06)
    return centered * scale, scale


def flip(values, axis, bit):
    return lax.ppermute(
        values, axis, [(place, place ^ bit) for place in range(lax.axis_size(axis))]
    )


def head_pair(partial):
    if lax.axis_size("head") != 2:
        return lax.psum(partial, "head"), jnp.zeros_like(partial)
    return partial, flip(partial, "head", 1)


def after(values, *needed):
    return lax.optimization_barrier((values, *needed))[0]


class Sequence:
    def __init__(self):
        self.last = None

    def then(self, values):
        return values if self.last is None else after(values, self.last)

    def mark(self, output):
        self.last = output
        return output


class Lane:
    def __init__(self, axis, depth):
        self.axis, self.depth, self.over = axis, depth, []

    def flip(self, values, bit):
        if len(self.over) >= self.depth:
            values = after(values, self.over[-self.depth])
        moved = flip(values, self.axis, bit)
        self.over.append(moved)
        return moved


class Part:
    def __init__(self, away, half, array):
        self.away, self.half, self.array = away, half, array


def gather_weight(weight, axis, lane, needed=()):
    parity = lax.rem(lax.axis_index("rep"), 2)
    size = weight.shape[axis] // 2
    held = {0: lax.dynamic_slice_in_dim(weight, parity * size, size, axis=axis)}
    if needed:
        held[0] = after(held[0], *needed)
    bit = lax.axis_size("tok") // 2
    while bit > 1:
        for away, array in list(held.items()):
            held[away ^ bit] = lane.flip(array, bit)
        bit //= 2
    parts = [Part(0, None, weight)]
    for away, array in held.items():
        if away:
            parts += [Part(away, 0, array), Part(away, 1, flip(array, "rep", 1))]
    return parts + [Part(part.away ^ 1, part.half, flip(part.array, "tok", 1)) for part in parts]


def gather_blocks(values, lane):
    pieces = {0: values}
    bit = lax.axis_size("tok") // 2
    while bit > 0:
        for away, part in list(pieces.items()):
            pieces[away ^ bit] = lane.flip(part, bit) if bit > 1 else flip(part, "tok", bit)
        bit //= 2
    return [pieces[away] for away in range(len(pieces))]


def add_blocks(seq, first, second, outputs, kind=jnp.bfloat16):
    width = first.shape[-1]
    flat = lambda values: values.reshape(outputs, -1, width)
    first, second = flat(seq.then(first)), flat(second)
    rows = first.shape[1]
    tile = rows // 2

    def kernel(first_ref, second_ref, *out_refs):
        for place, out_ref in enumerate(out_refs):
            out_ref[...] = (
                first_ref[place].astype(jnp.float32) + second_ref[place].astype(jnp.float32)
            ).astype(kind)

    in_spec = pl.BlockSpec((outputs, tile, width), lambda step: (0, step, 0))
    sums = pl.pallas_call(
        kernel,
        grid=(2,),
        in_specs=[in_spec, in_spec],
        out_specs=[pl.BlockSpec((tile, width), lambda step: (step, 0))] * outputs,
        out_shape=[jax.ShapeDtypeStruct((rows, width), kind)] * outputs,
        compiler_params=pltpu.CompilerParams(
            dimension_semantics=("arbitrary",), vmem_limit_bytes=VMEM_LIMIT
        ),
        cost_estimate=SMALL_COST,
    )(first, second)
    seq.mark(sums[0])
    return sums


def core_sums(seq, keep, moved):
    sums = add_blocks(seq, keep, moved, keep.shape[0])
    return {2 * place: part for place, part in enumerate(sums)}


def chip_moves(seq, pieces, lane):
    bit = 2
    while 2 * bit < lax.axis_size("tok"):
        pieces = {
            away: add_blocks(seq, part, lane.flip(pieces[away | bit], bit), 1)[0]
            for away, part in pieces.items()
            if not away & bit
        }
        bit *= 2
    if bit >= lax.axis_size("tok"):
        return pieces[0], jnp.zeros_like(pieces[0])
    return pieces[0], lane.flip(pieces[bit], bit)


def exchange(pieces, lane):
    count = lax.axis_size("tok")
    rank = lax.axis_index("tok")
    held = {away: [(0, part)] for away, part in pieces.items()}
    bit = count // 2
    while bit > 0:
        leaving = jnp.stack([part for away in held if away & bit for source, part in held[away]])
        moved = lane.flip(leaving, bit) if bit > 1 else flip(leaving, "tok", bit)
        place, kept = 0, {}
        for away in [away for away in held if not away & bit]:
            kept[away] = list(held[away])
            for source, part in held[away | bit]:
                kept[away].append((source ^ bit, moved[place]))
                place += 1
        held = kept
        bit //= 2
    came = jnp.stack([part for source, part in sorted(held[0], key=lambda pair: pair[0])])
    return [
        lax.dynamic_index_in_dim(came, jnp.bitwise_xor(rank, place), 0, keepdims=False)
        for place in range(count)
    ]


class Line:
    def __init__(self, seq):
        self.seq = seq
        self.on_line = lax.axis_size("rep") == 4
        rank = lax.axis_index("rep")
        self.inner = ((rank == 1) | (rank == 2)).astype(jnp.int32).reshape(1)
        self.chunks, self.totals, self.outward = [], {}, {}
        self.place = 0
        self.came, self.pair, self.over = None, None, None

    def outer(self, load, pairs):
        return lax.ppermute(load, "rep", pairs)

    def add(self, chunk):
        self.chunks.append(chunk)
        if self.on_line and len(self.chunks) == 1:
            self.came = self.outer(chunk, [(0, 1), (3, 2)])

    def step(self, final=False):
        if not self.on_line:
            return
        k, seq = self.place, self.seq
        count = len(self.chunks)
        has_pair, has_total, has_next = k < count, 1 <= k <= count, k + 1 < count
        shape = self.chunks[0].shape
        ins, names = [], []
        if has_pair:
            ins += [self.chunks[k], self.came]
        if has_total:
            ins += [self.pair, self.over]
        if has_total and has_next:
            ins += [self.chunks[k + 1]]
        ins[0] = seq.then(ins[0])
        outs = int(has_pair) + int(has_total) * (2 if has_next else 1)
        tile = shape[0] // 2

        def kernel(inner_ref, *refs):
            ins_left, outs_left = list(refs[: len(ins)]), list(refs[len(ins) :])

            def plus(one, two):
                return (one[...].astype(jnp.float32) + two[...].astype(jnp.float32)).astype(
                    jnp.bfloat16
                )

            if has_pair:
                outs_left.pop(0)[...] = plus(ins_left.pop(0), ins_left.pop(0))
            if has_total:
                total = plus(ins_left.pop(0), ins_left.pop(0))
                outs_left.pop(0)[...] = total
                if has_next:
                    load_ref, next_ref = outs_left.pop(0), ins_left.pop(0)

                    @pl.when(inner_ref[0] == 1)
                    def send_total():
                        load_ref[...] = total

                    @pl.when(inner_ref[0] != 1)
                    def send_chunk():
                        load_ref[...] = next_ref[...]

        spec = pl.BlockSpec((tile, shape[1]), lambda step: (step, 0))
        made = list(
            pl.pallas_call(
                kernel,
                grid=(2,),
                in_specs=[pl.BlockSpec(memory_space=pltpu.SMEM)] + [spec] * len(ins),
                out_specs=[spec] * outs,
                out_shape=[bf16(*shape)] * outs,
                compiler_params=pltpu.CompilerParams(
                    dimension_semantics=("arbitrary",), vmem_limit_bytes=VMEM_LIMIT
                ),
                cost_estimate=SMALL_COST,
            )(self.inner, *ins)
        )
        seq.mark(made[0])
        if has_pair:
            self.pair = made.pop(0)
            self.over = lax.ppermute(self.pair, "rep", [(1, 2), (2, 1)])
        if has_total:
            self.totals[k - 1] = made.pop(0)
            if has_next:
                self.came = self.outer(made.pop(0), [(0, 1), (1, 0), (2, 3), (3, 2)])
                self.outward[k - 1] = self.came
            else:
                self.outward[k - 1] = self.outer(self.totals[k - 1], [(1, 0), (2, 3)])
        elif has_next:
            self.came = self.outer(self.chunks[k + 1], [(0, 1), (3, 2)])
        self.place += 1

    def finish(self):
        if not self.on_line:
            return [lax.psum(chunk, "rep").astype(jnp.float32) for chunk in self.chunks]
        while self.place <= len(self.chunks):
            self.step()
        return [
            jnp.where(self.inner[0] == 1, self.totals[k], self.outward[k]).astype(jnp.float32)
            for k in range(len(self.chunks))
        ]


def tok_total(values):
    bit = 1
    while bit < lax.axis_size("tok"):
        values = values + flip(values, "tok", bit)
        bit *= 2
    return values


def rep_gather(values):
    count = lax.axis_size("rep")
    rank = lax.axis_index("rep")
    pieces = values[None]
    bit = 1
    while bit < count:
        pieces = jnp.concatenate([pieces, flip(pieces, "rep", bit)], axis=0)
        bit *= 2
    return jnp.stack(
        [
            lax.dynamic_index_in_dim(pieces, jnp.bitwise_xor(rank, place), 0, keepdims=False)
            for place in range(count)
        ]
    )


def product(left, right):
    return jnp.dot(left, right, preferred_element_type=jnp.float32)


def product_back(left, right):
    return lax.dot_general(
        left, right, (((1,), (1,)), ((), ())), preferred_element_type=jnp.float32
    )


def tile_spec(rank, rows, columns):
    if rank == 3:
        return pl.BlockSpec((1, rows, columns), lambda step: (step, 0, 0))
    return pl.BlockSpec((rows, columns), lambda step: (0, step))


def whole_spec(array):
    zeros = (0,) * array.ndim
    return pl.BlockSpec(array.shape, lambda step: zeros, pipeline_mode=pl.Buffered(1))


def tile_of(ref):
    return ref[0] if len(ref.shape) == 3 else ref[...]


def fill(scratch, spot, parts, refs):
    rank, parity = spot[0], spot[1]
    share = parts[0].array.shape[-2]
    for part, ref in zip(parts, refs, strict=True):
        rows = part.array.shape[-2]
        start = jnp.bitwise_xor(rank, part.away) * share
        if part.half is not None:
            start = start + jnp.bitwise_xor(parity, part.half) * rows
        scratch[pl.ds(pl.multiple_of(start, rows), rows), :] = tile_of(ref)


def fill_one(scratch, spot, parts, refs, which):
    rank, parity = spot[0], spot[1]
    share = parts[0].array.shape[-2]
    for part, ref in zip(parts, refs, strict=True):
        start = pl.multiple_of(jnp.bitwise_xor(rank, part.away) * share, share)

        def lay(start=start, ref=ref):
            scratch[pl.ds(start, share), :] = tile_of(ref)

        if part.half is None:
            lay()
        else:
            pl.when(jnp.bitwise_xor(parity, part.half) == which)(lay)


def one_specs(parts, which):
    return [
        pl.BlockSpec(
            (1,) + part.array.shape[1:],
            functools.partial(lambda at, step: (at, 0, 0), which if part.half is None else 0),
        )
        for part in parts
    ]


def put_grad(spot, left_ref, right, keep_ref, send_ref, rows, count):
    rank = spot[0]
    for away in range(count):
        at = pl.ds(pl.multiple_of(jnp.bitwise_xor(rank, away) * rows, rows), rows)
        block = product(left_ref[at, :], right).astype(jnp.bfloat16)
        to = send_ref if away & 1 else keep_ref
        to[away // 2, 0] = block


def grad_specs(count, rows, columns):
    return pl.BlockSpec((count // 2, 1, rows, columns), lambda step: (0, step, 0, 0))


def call(kernel, tiles, spot, arrays, specs, outs, out_specs, scratch):
    return pl.pallas_call(
        kernel,
        grid=(tiles,),
        in_specs=[pl.BlockSpec(memory_space=pltpu.SMEM)] + specs,
        out_specs=out_specs,
        out_shape=outs,
        scratch_shapes=scratch,
        compiler_params=pltpu.CompilerParams(
            dimension_semantics=("arbitrary",), vmem_limit_bytes=VMEM_LIMIT
        ),
        cost_estimate=SMALL_COST,
    )(spot, *arrays)


def bf16(*shape):
    return jax.ShapeDtypeStruct(shape, jnp.bfloat16)


def project(spot, rows_in, parts):
    arrays = [part.array for part in parts]
    tiles, share, columns = arrays[0].shape
    length, width = rows_in.shape

    def kernel(spot_ref, in_ref, *rest):
        refs, out_ref, scratch = rest[:-2], rest[-2], rest[-1]
        fill(scratch, spot_ref, parts, refs)
        out_ref[0] = product(in_ref[...], scratch[...]).astype(jnp.bfloat16)

    return call(
        kernel,
        tiles,
        spot,
        [rows_in] + arrays,
        [whole_spec(rows_in)] + [tile_spec(3, part.shape[1], columns) for part in arrays],
        bf16(tiles, length, columns),
        pl.BlockSpec((1, length, columns), lambda step: (step, 0, 0)),
        [pltpu.VMEM((width, columns), jnp.bfloat16)],
    )


def project_back(spot, rows_in, parts, which, width):
    arrays = [part.array for part in parts]
    columns = arrays[0].shape[-1]
    length = rows_in.shape[0]

    def kernel(spot_ref, in_ref, *rest):
        refs, out_ref, scratch = rest[:-2], rest[-2], rest[-1]
        fill_one(scratch, spot_ref, parts, refs, which)
        out_ref[...] = product_back(in_ref[...], scratch[...]).astype(jnp.bfloat16)

    return call(
        kernel,
        1,
        spot,
        [rows_in] + arrays,
        [whole_spec(rows_in)] + one_specs(parts, which),
        bf16(length, width),
        pl.BlockSpec((length, width), lambda step: (0, 0)),
        [pltpu.VMEM((width, columns), jnp.bfloat16)],
    )


def proj_grads(spot, grad_rows, mixed_rows, parts, which):
    arrays = [part.array for part in parts]
    share, columns = arrays[0].shape[-2:]
    length, width = grad_rows.shape
    count = width // share

    def kernel(spot_ref, grad_ref, mixed_ref, *rest):
        refs, (out_ref, keep_ref, send_ref, scratch, turned) = rest[:-5], rest[-5:]
        fill_one(scratch, spot_ref, parts, refs, which)
        turned[...] = jnp.transpose(grad_ref[...])
        out_ref[...] = product(grad_ref[...], scratch[...]).astype(jnp.bfloat16)
        put_grad(spot_ref, turned, mixed_ref[...], keep_ref, send_ref, share, count)

    half = bf16(count // 2, 1, share, columns)
    return call(
        kernel,
        1,
        spot,
        [grad_rows, mixed_rows] + arrays,
        [whole_spec(grad_rows), whole_spec(mixed_rows)] + one_specs(parts, which),
        (bf16(length, columns), half, half),
        (pl.BlockSpec((length, columns), lambda step: (0, 0)),)
        + (grad_specs(count, share, columns),) * 2,
        [pltpu.VMEM((width, columns), jnp.bfloat16), pltpu.VMEM((width, length), jnp.bfloat16)],
    )


def qkv_grads(spot, hidden, query_grad, block_grads, parts):
    arrays = [part.array for part in parts]
    tiles, share, columns = arrays[0].shape
    length, width = hidden.shape
    count = width // share

    def kernel(spot_ref, hid_ref, query_ref, block_ref, *rest):
        refs, (out_ref, keep_ref, send_ref, scratch, total, turned, grad) = rest[:-7], rest[-7:]
        step = pl.program_id(0)
        fill(scratch, spot_ref, parts, refs)

        @pl.when(step == 0)
        def first():
            turned[...] = jnp.transpose(hid_ref[...])
            total[...] = jnp.zeros_like(total)
            grad[...] = query_ref[...]

        @pl.when(step > 0)
        def later():
            grad[...] = block_ref[0]

        total[...] += product_back(grad[...], scratch[...])
        put_grad(spot_ref, turned, grad[...], keep_ref, send_ref, share, count)

        @pl.when(step == tiles - 1)
        def finish():
            out_ref[...] = total[...].astype(jnp.bfloat16)

    half = bf16(count // 2, tiles, share, columns)
    return call(
        kernel,
        tiles,
        spot,
        [hidden, query_grad, block_grads] + arrays,
        [
            whole_spec(hidden),
            whole_spec(query_grad),
            pl.BlockSpec((1, length, columns), lambda step: (jnp.maximum(step - 1, 0), 0, 0)),
        ]
        + [tile_spec(3, part.shape[1], columns) for part in arrays],
        (bf16(length, width), half, half),
        (pl.BlockSpec((length, width), lambda step: (0, 0)),)
        + (grad_specs(count, share, columns),) * 2,
        [
            pltpu.VMEM((width, columns), jnp.bfloat16),
            pltpu.VMEM((length, width), jnp.float32),
            pltpu.VMEM((width, length), jnp.bfloat16),
            pltpu.VMEM((length, columns), jnp.bfloat16),
        ],
    )


def gelu_parts(upward):
    squared = upward * upward
    bent = jnp.tanh(0.7978845608028654 * (upward + 0.044715 * (upward * squared)))
    activ = 0.5 * upward * (1.0 + bent)
    slope = 0.5 * (1.0 + bent) + 0.5 * upward * (1.0 - bent * bent) * (
        0.7978845608028654 * (1.0 + 3 * 0.044715 * squared)
    )
    return activ, slope


def feed_forward(spot, hidden, grad, up_parts, down_parts, columns):
    arrays = [part.array for part in up_parts + down_parts]
    share, units = arrays[0].shape
    tiles = units // columns
    length, width = hidden.shape
    count = width // share

    def kernel(spot_ref, hid_ref, grad_ref, *rest):
        refs, rest = rest[: len(arrays)], rest[len(arrays) :]
        out_ref, back_ref, up_keep, up_send, down_keep, down_send = rest[:6]
        up, down, out_sum, back_sum, hid_turned, grad_turned = rest[6:]
        step = pl.program_id(0)

        @pl.when(step == 0)
        def begin():
            hid_turned[...] = jnp.transpose(hid_ref[...])
            grad_turned[...] = jnp.transpose(grad_ref[...])
            out_sum[...] = jnp.zeros_like(out_sum)
            back_sum[...] = jnp.zeros_like(back_sum)

        fill(up, spot_ref, up_parts, refs[: len(up_parts)])
        fill(down, spot_ref, down_parts, refs[len(up_parts) :])
        activ, slope = gelu_parts(product(hid_ref[...], up[...]))
        activ = activ.astype(jnp.bfloat16)
        upward_grad = (product(grad_ref[...], down[...]) * slope).astype(jnp.bfloat16)
        out_sum[...] += product_back(activ, down[...])
        back_sum[...] += product_back(upward_grad, up[...])
        put_grad(spot_ref, grad_turned, activ, down_keep, down_send, share, count)
        put_grad(spot_ref, hid_turned, upward_grad, up_keep, up_send, share, count)

        @pl.when(step == tiles - 1)
        def finish():
            out_ref[...] = out_sum[...].astype(jnp.bfloat16)
            back_ref[...] = back_sum[...].astype(jnp.bfloat16)

    rows_spec = pl.BlockSpec((length, width), lambda step: (0, 0))
    wholes = [hidden, grad]
    return call(
        kernel,
        tiles,
        spot,
        wholes + arrays,
        [whole_spec(part) for part in wholes]
        + [tile_spec(2, part.shape[0], columns) for part in arrays],
        (bf16(length, width), bf16(length, width))
        + (bf16(count // 2, tiles, share, columns),) * 4,
        (rows_spec, rows_spec) + (grad_specs(count, share, columns),) * 4,
        [pltpu.VMEM((width, columns), jnp.bfloat16)] * 2
        + [pltpu.VMEM((length, width), jnp.float32)] * 2
        + [pltpu.VMEM((width, length), jnp.bfloat16)] * 2,
    )


def activate(seq, first, second):
    shape = first.shape
    tile = shape[1] // 2

    def kernel(first_ref, second_ref, out_ref):
        upward = first_ref[0].astype(jnp.float32) + second_ref[0].astype(jnp.float32)
        activ_grad = first_ref[1].astype(jnp.float32) + second_ref[1].astype(jnp.float32)
        activ, slope = gelu_parts(upward)
        out_ref[0] = activ.astype(jnp.bfloat16)
        out_ref[1] = (activ_grad * slope).astype(jnp.bfloat16)

    spec = pl.BlockSpec((2, tile, shape[2]), lambda step: (0, step, 0))
    return seq.mark(
        pl.pallas_call(
            kernel,
            grid=(2,),
            in_specs=[spec, spec],
            out_specs=spec,
            out_shape=bf16(*shape),
            compiler_params=pltpu.CompilerParams(
                dimension_semantics=("arbitrary",), vmem_limit_bytes=VMEM_LIMIT
            ),
            cost_estimate=SMALL_COST,
        )(seq.then(first), second)
    )


def spread_up(spot, rows_in, up_shard, down_shard, count):
    length, share = rows_in.shape[1:]
    columns = up_shard.shape[1] // count

    def kernel(spot_ref, in_ref, up_ref, down_ref, keep_ref, send_ref):
        upward = product(in_ref[0], up_ref[...]).astype(jnp.bfloat16)
        activ_grad = product(in_ref[1], down_ref[...]).astype(jnp.bfloat16)
        odd = pl.program_id(0) % 2

        @pl.when(odd == 0)
        def keep():
            keep_ref[0, 0], keep_ref[0, 1] = upward, activ_grad

        @pl.when(odd != 0)
        def send():
            send_ref[0, 0], send_ref[0, 1] = upward, activ_grad

    shard_spec = pl.BlockSpec(
        (share, columns), lambda step, spot_ref: (0, jnp.bitwise_xor(spot_ref[0], step))
    )
    out_spec = pl.BlockSpec((1, 2, length, columns), lambda step, spot_ref: (step // 2, 0, 0, 0))
    out = bf16(count // 2, 2, length, columns)
    return pl.pallas_call(
        kernel,
        grid_spec=pltpu.PrefetchScalarGridSpec(
            num_scalar_prefetch=1,
            grid=(count,),
            in_specs=[
                pl.BlockSpec(rows_in.shape, lambda step, spot_ref: (0, 0, 0)),
                shard_spec,
                shard_spec,
            ],
            out_specs=[out_spec, out_spec],
        ),
        out_shape=[out, out],
        compiler_params=pltpu.CompilerParams(
            dimension_semantics=("arbitrary",), vmem_limit_bytes=VMEM_LIMIT
        ),
        cost_estimate=SMALL_COST,
    )(spot, rows_in, up_shard, down_shard)


def spread_down(spot, rows_in, blocks, up_shard, down_shard):
    count = len(blocks)
    length, columns = blocks[0].shape[1:]
    share, units = up_shard.shape

    def kernel(spot_ref, in_ref, up_ref, down_ref, *rest):
        refs, (out_ref, up_grad_ref, down_grad_ref) = rest[:count], rest[count:]
        hid_turned, grad_turned = jnp.transpose(in_ref[0]), jnp.transpose(in_ref[1])
        out_sum = jnp.zeros((length, share), jnp.float32)
        back_sum = jnp.zeros((length, share), jnp.float32)
        for away, ref in enumerate(refs):
            place = jnp.bitwise_xor(spot_ref[0], away)
            at = pl.ds(pl.multiple_of(place * columns, columns), columns)
            activ, upward_grad = ref[0], ref[1]
            out_sum += product_back(activ, down_ref[:, at])
            back_sum += product_back(upward_grad, up_ref[:, at])
            up_grad_ref[place] = product(hid_turned, upward_grad).astype(jnp.bfloat16)
            down_grad_ref[place] = product(grad_turned, activ).astype(jnp.bfloat16)
        out_ref[0] = back_sum.astype(jnp.bfloat16)
        out_ref[1] = out_sum.astype(jnp.bfloat16)

    zeros = lambda step: (0, 0, 0)
    arrays = [rows_in, up_shard, down_shard] + list(blocks)
    return call(
        kernel,
        1,
        spot,
        arrays,
        [whole_spec(part) for part in arrays],
        (bf16(2, length, share),) + (bf16(count, share, columns),) * 2,
        (pl.BlockSpec((2, length, share), zeros),)
        + (pl.BlockSpec((count, share, columns), zeros),) * 2,
        [],
    )


def spread_begin(seq, spot, hidden, grad, up_shard, down_shard, lane):
    count = lax.axis_size("tok")
    rank = lax.axis_index("tok")
    share = up_shard.shape[0]
    both = jnp.stack([hidden, grad])
    features = exchange(
        {
            away: lax.dynamic_slice_in_dim(
                both, jnp.bitwise_xor(rank, away) * share, share, axis=2
            )
            for away in range(count)
        },
        lane,
    )
    rows_in = seq.then(jnp.concatenate(features, axis=1))
    keep, send = spread_up(spot, rows_in, up_shard, down_shard, count)
    seq.mark(keep)
    pieces = core_sums(seq, keep, flip(send, "tok", 1))
    shape = (2,) + keep.shape[2:]
    stays, came = chip_moves(seq, pieces, lane)
    active = activate(seq, stays.reshape(shape), came.reshape(shape))
    return rows_in, gather_blocks(active, lane)


def spread_back(both, rows, lane):
    rank = lax.axis_index("tok")
    features = exchange(
        {
            away: lax.dynamic_slice_in_dim(both, jnp.bitwise_xor(rank, away) * rows, rows, axis=1)
            for away in range(lax.axis_size("tok"))
        },
        lane,
    )
    return jnp.concatenate(features, axis=2)


def row_kernel(seq, kernel, modul, rows_in, outs):
    seqs, length, width = rows_in[0].shape
    row_spec = pl.BlockSpec((1, length, width), lambda at: (at, 0, 0))
    sum_spec = pl.BlockSpec((1, 8, width), lambda at: (at, 0, 0))
    made = pl.pallas_call(
        kernel,
        grid=(seqs,),
        in_specs=[pl.BlockSpec((1,) + modul.shape[1:], lambda at: (at, 0, 0))]
        + [row_spec] * len(rows_in),
        out_specs=[sum_spec if kind is None else row_spec for kind in outs],
        out_shape=[
            jax.ShapeDtypeStruct((seqs, 8, width), jnp.float32)
            if kind is None
            else jax.ShapeDtypeStruct((seqs, length, width), kind)
            for kind in outs
        ],
        compiler_params=pltpu.CompilerParams(
            dimension_semantics=("arbitrary",), vmem_limit_bytes=VMEM_LIMIT
        ),
        cost_estimate=SMALL_COST,
    )(modul, seq.then(rows_in[0]), *rows_in[1:])
    seq.mark(made[0])
    return made


def wide(ref):
    return ref[0].astype(jnp.float32)


def put_sums(ref, rows):
    ref[0] = jnp.zeros_like(ref[0])
    for place, row in enumerate(rows):
        ref[0, place : place + 1] = jnp.sum(row, axis=0, keepdims=True)


def back_through(values, grad, scale_part):
    norm, factor = normed(values)
    inner = grad * (1.0 + scale_part)
    own = jnp.mean(inner, axis=-1, keepdims=True)
    along = jnp.mean(inner * norm, axis=-1, keepdims=True)
    return (inner - own - norm * along) * factor, norm


def first_hidden(seq, modul, stream):
    def kernel(mod_ref, x_ref, out_ref):
        norm, factor = normed(wide(x_ref))
        out_ref[0] = (norm * (1.0 + mod_ref[0, 1:2]) + mod_ref[0, 0:1]).astype(jnp.bfloat16)

    return row_kernel(seq, kernel, modul, [stream], [jnp.bfloat16])[0]


def middle_hidden(seq, modul, stream, branch, cot):
    def kernel(mod_ref, x_ref, one_ref, two_ref, cot_ref, hid_ref, grad_ref):
        middle = wide(x_ref) + mod_ref[0, 2:3] * (wide(one_ref) + wide(two_ref))
        norm, factor = normed(middle)
        hid_ref[0] = (norm * (1.0 + mod_ref[0, 4:5]) + mod_ref[0, 3:4]).astype(jnp.bfloat16)
        grad_ref[0] = (mod_ref[0, 5:6] * wide(cot_ref)).astype(jnp.bfloat16)

    return row_kernel(seq, kernel, modul, [stream, *branch, cot], [jnp.bfloat16, jnp.bfloat16])


def middle_grads(seq, modul, stream, branch, cot, hidden_grad):
    def kernel(mod_ref, x_ref, one_ref, two_ref, cot_ref, hid_ref, other_ref, mid_out, out, sums):
        branch_sum = wide(one_ref) + wide(two_ref)
        middle = wide(x_ref) + mod_ref[0, 2:3] * branch_sum
        grad = wide(hid_ref) + wide(other_ref)
        through, norm = back_through(middle, grad, mod_ref[0, 4:5])
        mid_grad = wide(cot_ref) + through
        mid_out[0] = mid_grad
        out[0] = (mod_ref[0, 2:3] * mid_grad).astype(jnp.bfloat16)
        put_sums(sums, [mid_grad * branch_sum, grad, grad * norm])

    return row_kernel(
        seq,
        kernel,
        modul,
        [stream, *branch, cot, *hidden_grad],
        [jnp.float32, jnp.bfloat16, None],
    )


def input_grads(seq, modul, stream, mid_grad, hidden_grad):
    def kernel(mod_ref, x_ref, mid_ref, hid_ref, other_ref, out, sums):
        grad = wide(hid_ref) + wide(other_ref)
        through, norm = back_through(wide(x_ref), grad, mod_ref[0, 1:2])
        out[0] = (mid_ref[0] + through).astype(jnp.bfloat16)
        put_sums(sums, [grad, grad * norm])

    return row_kernel(
        seq, kernel, modul, [stream, mid_grad, *hidden_grad], [jnp.bfloat16, None]
    )


def results(seq, modul, stream, branch, second, cot, real):
    def kernel(mod_ref, x_ref, one_ref, two_ref, three_ref, four_ref, cot_ref, out, sums):
        start = wide(x_ref)
        gated_one = mod_ref[0, 2:3] * (wide(one_ref) + wide(two_ref))
        middle = start + gated_one
        branch_two = wide(three_ref) + wide(four_ref)
        gated_two = mod_ref[0, 5:6] * branch_two
        result = middle + gated_two
        out[0] = result.astype(jnp.bfloat16)
        shown = lax.broadcasted_iota(jnp.int32, start.shape, 0) < real
        put_sums(
            sums,
            [wide(cot_ref) * branch_two]
            + [
                jnp.where(shown, member * member, 0.0)
                for member in (start, gated_one, middle, gated_two, result)
            ],
        )

    return row_kernel(
        seq, kernel, modul, [stream, *branch, *second, cot], [jnp.bfloat16, None]
    )


def head_lanes(shape, head):
    lane = lax.broadcasted_iota(jnp.int32, shape, len(shape) - 1)
    return (lane >= head * HD) & (lane < (head + 1) * HD)


def padding(shape, axis, image_rows, text_rows, real, count):
    place = lax.broadcasted_iota(jnp.int32, shape, axis) - image_rows * count
    hidden = (place >= real) & (place < text_rows)
    for other in range(1, count):
        hidden = hidden | (
            (place >= other * text_rows + real) & (place < (other + 1) * text_rows)
        )
    return hidden


def attention_specs(image, text):
    row = [
        pl.BlockSpec((1, rows, LANES), lambda seq, part: (seq, 0, part))
        for rows in (image.shape[1], text.shape[1])
    ]
    block = [
        pl.BlockSpec((2, 1, rows, LANES), lambda seq, part: (0, seq, 0, part))
        for rows in (image.shape[1], text.shape[1])
    ]
    return row, block


def joint(refs, index):
    return jnp.concatenate([ref[index] for ref in refs], axis=0)


def attend(image, text, image_blocks, text_blocks, real):
    seqs, image_rows, width = image.shape
    text_rows = text.shape[1]
    rows = image_rows + text_rows
    count = len(image_blocks)
    keys = rows * count

    def kernel(*rest):
        refs, (image_out, text_out) = rest[:-2], rest[-2:]
        queries = joint(refs[:2], 0)
        key_all = joint(refs[2:], (0, 0))
        value_all = joint(refs[2:], (1, 0))
        hidden = padding((1, keys), 1, image_rows, text_rows, real, count)
        result = jnp.zeros((rows, LANES), jnp.float32)
        for head in range(LANES // HD):
            mine = head_lanes((rows, LANES), head)
            scores = product_back(jnp.where(mine, queries, jnp.zeros_like(queries)), key_all)
            scores = jnp.where(hidden, -1e30, scores * 0.125)
            expd = jnp.exp(scores - jnp.max(scores, axis=1, keepdims=True))
            share = 1.0 / jnp.sum(expd, axis=1, keepdims=True)
            mixed = product((expd * share).astype(jnp.bfloat16), value_all)
            result = jnp.where(mine, mixed, result)
        image_out[0] = result[:image_rows].astype(jnp.bfloat16)
        text_out[0] = result[image_rows:].astype(jnp.bfloat16)

    row, block = attention_specs(image, text)
    return pl.pallas_call(
        kernel,
        grid=(seqs, width // LANES),
        in_specs=row + [block[0]] * count + [block[1]] * count,
        out_specs=row,
        out_shape=[bf16(*image.shape), bf16(*text.shape)],
        compiler_params=pltpu.CompilerParams(
            dimension_semantics=("arbitrary", "arbitrary"), vmem_limit_bytes=VMEM_LIMIT
        ),
        cost_estimate=SMALL_COST,
    )(image, text, *image_blocks, *text_blocks)


def attend_grads(queries_in, grads_in, image_blocks, text_blocks, real, seq):
    image, text = queries_in
    image_rows, width = image.shape[1:]
    text_rows = text.shape[1]
    rows = image_rows + text_rows
    count = len(image_blocks)
    keys = rows * count

    def kernel(*rest):
        refs, (image_out, text_out, image_keep, image_send, text_keep, text_send) = (
            rest[:-6],
            rest[-6:],
        )
        queries = joint(refs[:2], 0)
        grads = joint(refs[2:4], 0)
        key_all = joint(refs[4:], (0, 0))
        value_all = joint(refs[4:], (1, 0))
        hidden = padding((keys, 1), 0, image_rows, text_rows, real, count)
        query_grad = jnp.zeros((rows, LANES), jnp.float32)
        key_grad = jnp.zeros((keys, LANES), jnp.float32)
        value_grad = jnp.zeros((keys, LANES), jnp.float32)
        for head in range(LANES // HD):
            mine = head_lanes((rows, LANES), head)
            own_query = jnp.where(mine, queries, jnp.zeros_like(queries))
            own_grad = jnp.where(mine, grads, jnp.zeros_like(grads))
            scores = product_back(key_all, own_query)
            scores = jnp.where(hidden, -1e30, scores * 0.125)
            expd = jnp.exp(scores - jnp.max(scores, axis=0, keepdims=True))
            probs = expd * (1.0 / jnp.sum(expd, axis=0, keepdims=True))
            prob_grad = product_back(value_all, own_grad)
            delta = jnp.sum(probs * prob_grad, axis=0, keepdims=True)
            score_grad = (probs * (prob_grad - delta)).astype(jnp.bfloat16)
            value_grad += product(probs.astype(jnp.bfloat16), own_grad)
            key_grad += product(score_grad, own_query)
            back = lax.dot_general(
                score_grad, key_all, (((0,), (0,)), ((), ())), preferred_element_type=jnp.float32
            )
            query_grad = jnp.where(mine, back, query_grad)
        query_grad = (query_grad * 0.125).astype(jnp.bfloat16)
        image_out[0] = query_grad[:image_rows]
        text_out[0] = query_grad[image_rows:]
        key_grad = (key_grad * 0.125).astype(jnp.bfloat16)
        value_grad = value_grad.astype(jnp.bfloat16)
        for away in range(count):
            at = slice(away * image_rows, (away + 1) * image_rows)
            to = image_send if away & 1 else image_keep
            to[away // 2, 0], to[away // 2, 1] = key_grad[at], value_grad[at]
            first = count * image_rows + away * text_rows
            at = slice(first, first + text_rows)
            to = text_send if away & 1 else text_keep
            to[away // 2, 0], to[away // 2, 1] = key_grad[at], value_grad[at]

    def row_spec(length, at):
        return pl.BlockSpec((1, length, LANES), lambda part: (at, 0, part))

    def block_spec(length):
        return pl.BlockSpec((2, 1, length, LANES), lambda part: (0, seq, 0, part))

    def owner_spec(length):
        return pl.BlockSpec((count // 2, 2, length, LANES), lambda part: (0, 0, 0, part))

    sizes = (image_rows, text_rows)
    owners = [length for length in sizes for side in range(2)]
    return pl.pallas_call(
        kernel,
        grid=(width // LANES,),
        in_specs=[row_spec(length, seq) for length in sizes] * 2
        + [block_spec(image_rows)] * count
        + [block_spec(text_rows)] * count,
        out_specs=[row_spec(length, 0) for length in sizes]
        + [owner_spec(length) for length in owners],
        out_shape=[bf16(1, length, width) for length in sizes]
        + [bf16(count // 2, 2, length, width) for length in owners],
        compiler_params=pltpu.CompilerParams(
            dimension_semantics=("arbitrary",), vmem_limit_bytes=VMEM_LIMIT
        ),
        cost_estimate=SMALL_COST,
    )(image, text, *grads_in, *image_blocks, *text_blocks)


def on_device(
    image_tokens,
    text_tokens,
    text_owner,
    conditioning,
    slot_sequence,
    image_w_mod,
    image_b_mod,
    image_w_qkv,
    image_w_proj,
    image_w_up,
    image_w_down,
    text_w_mod,
    text_b_mod,
    text_w_qkv,
    text_w_proj,
    text_w_up,
    text_w_down,
    image_cotangent,
    text_cotangent,
):
    tok_rank = lax.axis_index("tok")
    rep_rank = lax.axis_index("rep")
    rep_count = lax.axis_size("rep")
    tok_count = lax.axis_size("tok")
    seqs, image_rows, width = image_tokens.shape
    text_real = text_cotangent.shape[1]
    text_rows = -(-text_real // 16) * 16
    slots = conditioning.shape[0]
    share = image_w_mod.shape[0]
    heads_width = image_w_qkv.shape[2]
    spot = jnp.stack([tok_rank, lax.rem(rep_rank, 2)]).astype(jnp.int32)

    turn = lambda weight: jnp.transpose(weight, (1, 0, 2))
    chips = Lane("tok", 2)
    image_qkv_parts = gather_weight(turn(image_w_qkv), 1, chips)

    picker = (slot_sequence[:, None] == jnp.arange(slots, dtype=jnp.int32)[None, :]).astype(
        jnp.float32
    )
    cond_slots = jnp.dot(picker, conditioning, precision=exact_mode)
    activ_all = jax.nn.silu(cond_slots).astype(jnp.bfloat16)
    activ_group = lax.dynamic_slice_in_dim(activ_all, rep_rank * seqs, seqs, axis=0)
    activ_share = lax.dynamic_slice_in_dim(activ_group, tok_rank * share, share, axis=1)
    both_mod = tok_total(
        jnp.stack(
            [
                jnp.einsum("sd,dke->ske", activ_share, weight, preferred_element_type=jnp.float32)
                for weight in (image_w_mod, text_w_mod)
            ]
        )
    )
    image_mod = both_mod[0] + image_b_mod.astype(jnp.float32)[None]
    text_mod = both_mod[1] + text_b_mod.astype(jnp.float32)[None]

    text_qkv_parts = gather_weight(turn(text_w_qkv), 1, chips, (both_mod,))
    proj_parts = gather_weight(jnp.stack([image_w_proj, text_w_proj]), 0, chips)

    owned = (text_owner == tok_rank).astype(jnp.float32)
    total_text = text_owner.shape[1]
    before = jnp.dot(
        owned,
        jnp.triu(jnp.ones((total_text, total_text), jnp.float32), 1),
        precision=exact_mode,
    )
    chosen = (
        (before[:, None, :] == jnp.arange(text_rows, dtype=jnp.float32)[None, :, None])
        & (owned[:, None, :] > 0.5)
    ).astype(jnp.bfloat16)
    text_input = jnp.einsum(
        "srt,std->srd", chosen, text_tokens, preferred_element_type=jnp.float32
    ).astype(jnp.bfloat16)
    text_cot = jnp.pad(text_cotangent, ((0, 0), (0, text_rows - text_real), (0, 0)))

    seq = Sequence()
    flat = lambda values: values.reshape(-1, values.shape[-1])
    by_seq = lambda values: values.reshape(values.shape[:-2] + (seqs, -1, values.shape[-1]))
    both = lambda pair: tuple(by_seq(part) for part in pair)
    heads = lambda partial: both(head_pair(partial))

    image_hid_one = flat(first_hidden(seq, image_mod, image_tokens))
    image_qkv = seq.mark(project(spot, image_hid_one, image_qkv_parts))
    image_blocks = gather_blocks(by_seq(image_qkv[1:]), chips)
    text_hid_one = flat(first_hidden(seq, text_mod, text_input))
    text_qkv = seq.mark(project(spot, text_hid_one, text_qkv_parts))
    text_blocks = gather_blocks(by_seq(text_qkv[1:]), chips)
    image_up_parts = gather_weight(image_w_up, 0, chips)
    image_down_parts = gather_weight(image_w_down, 0, chips)
    image_query, text_query = by_seq(image_qkv[0]), by_seq(text_qkv[0])
    image_mix, text_mix = attend(image_query, text_query, image_blocks, text_blocks, text_real)
    image_mixed, text_mixed = flat(image_mix), flat(text_mix)
    text_out = seq.mark(project_back(spot, text_mixed, proj_parts, 1, width))
    text_branch = heads(text_out)
    image_out = seq.mark(project_back(spot, seq.then(image_mixed), proj_parts, 0, width))
    image_branch = heads(image_out)

    text_hid_two, text_db_two = middle_hidden(seq, text_mod, text_input, text_branch, text_cot)
    text_in, text_active = spread_begin(
        seq, spot, flat(text_hid_two), flat(text_db_two), text_w_up, text_w_down, chips
    )
    image_hid_two, image_db_two = middle_hidden(
        seq, image_mod, image_tokens, image_branch, image_cotangent
    )
    image_part, image_back, image_up_keep, image_up_send, image_down_keep, image_down_send = (
        feed_forward(
            spot,
            flat(image_hid_two),
            flat(image_db_two),
            image_up_parts,
            image_down_parts,
            heads_width,
        )
    )
    seq.mark(image_back)
    image_hid_grad = heads(image_back)
    down_moved = flip(image_down_send, "tok", 1)
    up_moved = flip(image_up_send, "tok", 1)
    text_sums, text_up_grad, text_down_grad = spread_down(
        spot, seq.then(text_in), text_active, text_w_up, text_w_down
    )
    seq.mark(text_sums)
    line = Line(seq)
    for whole in (text_down_grad, text_up_grad):
        for place in range(2):
            line.add(flat(whole.reshape(2, -1, share, whole.shape[-1])[place]))
    image_down_pieces = core_sums(seq, image_down_keep, down_moved)
    image_down_pair = chip_moves(seq, image_down_pieces, chips)
    text_back, text_part = spread_back(text_sums, flat(text_input).shape[0], chips)
    text_hid_grad = heads(text_back)
    image_up_pieces = core_sums(seq, image_up_keep, up_moved)
    image_up_pair = chip_moves(seq, image_up_pieces, chips)

    image_mid_grad, image_db_one, image_mid_sums = middle_grads(
        seq, image_mod, image_tokens, image_branch, image_cotangent, image_hid_grad
    )
    image_mixed_grad, image_proj_keep, image_proj_send = proj_grads(
        spot, flat(image_db_one), image_mixed, proj_parts, 0
    )
    seq.mark(image_mixed_grad)
    line.step()
    text_mid_grad, text_db_one, text_mid_sums = middle_grads(
        seq, text_mod, text_input, text_branch, text_cot, text_hid_grad
    )
    text_mixed_grad, text_proj_keep, text_proj_send = proj_grads(
        spot, flat(text_db_one), text_mixed, proj_parts, 1
    )
    seq.mark(text_mixed_grad)
    grads_all = []
    mix_grads = (by_seq(image_mixed_grad), by_seq(text_mixed_grad))
    for at in range(seqs):
        made = attend_grads(
            (image_query, text_query),
            (seq.then(mix_grads[0]), mix_grads[1]),
            image_blocks,
            text_blocks,
            text_real,
            at,
        )
        seq.mark(made[0])
        grads_all.append(made)
        line.step()
        if at == 0:
            for part in add_blocks(seq, *image_down_pair, 2):
                line.add(part)
    image_query_grad, text_query_grad, *block_grads = [
        jnp.stack(parts, axis=-3) for parts in zip(*grads_all)
    ]
    text_pieces = core_sums(seq, block_grads[2], flip(block_grads[3], "tok", 1))
    text_moves = chip_moves(seq, text_pieces, chips)
    image_pieces = core_sums(seq, block_grads[0], flip(block_grads[1], "tok", 1))
    image_moves = chip_moves(seq, image_pieces, chips)
    for part in add_blocks(seq, *image_up_pair, 2):
        line.add(part)
    line.step()
    tail = Line(seq)
    proj_pairs = [
        chip_moves(seq, core_sums(seq, keep, flip(send, "tok", 1)), chips)
        for keep, send in ((image_proj_keep, image_proj_send), (text_proj_keep, text_proj_send))
    ]
    pair_of = lambda values: values.reshape(2, -1, heads_width)
    text_block_grad = pair_of(add_blocks(seq, *text_moves, 1)[0])
    text_in_part, text_qkv_keep, text_qkv_send = qkv_grads(
        spot, text_hid_one, flat(text_query_grad[0]), text_block_grad, text_qkv_parts
    )
    seq.mark(text_in_part)
    image_block_grad = pair_of(add_blocks(seq, *image_moves, 1)[0])
    image_in_part, image_qkv_keep, image_qkv_send = qkv_grads(
        spot, image_hid_one, flat(image_query_grad[0]), image_block_grad, image_qkv_parts
    )
    seq.mark(image_in_part)
    line.step()
    qkv_pairs = [
        chip_moves(seq, core_sums(seq, keep, flip(send, "tok", 1)), chips)
        for keep, send in ((image_qkv_keep, image_qkv_send), (text_qkv_keep, text_qkv_send))
    ]
    text_in_grad = heads(text_in_part)
    image_in_grad = heads(image_in_part)
    text_second = heads(after(text_part, image_in_part))
    image_second = heads(after(image_part, image_in_part))
    line.step()
    image_proj_share, text_proj_share = [add_blocks(seq, *pair, 1)[0] for pair in proj_pairs]
    line.step()
    text_grad, text_in_sums = input_grads(
        seq, text_mod, text_input, text_mid_grad, text_in_grad
    )
    image_grad, image_in_sums = input_grads(
        seq, image_mod, image_tokens, image_mid_grad, image_in_grad
    )
    line.step()
    ff_sums = line.finish()
    tail.add(image_proj_share)
    tail.add(text_proj_share)
    for part in add_blocks(seq, *qkv_pairs[0], 3):
        tail.add(part)
    tail.step()
    text_result, text_out_sums = results(
        seq, text_mod, text_input, text_branch, text_second, text_cot, text_real
    )
    image_result, image_out_sums = results(
        seq, image_mod, image_tokens, image_branch, image_second, image_cotangent, image_rows
    )
    tail.step()
    for part in add_blocks(seq, *qkv_pairs[1], 3):
        tail.add(part)
    tail_sums = tail.finish()
    columns_of = lambda place: jnp.concatenate(
        [
            column
            for part in ff_sums[place : place + 2]
            for column in part.reshape(-1, share, part.shape[-1])
        ],
        axis=1,
    )
    text_down_sum, text_up_sum, image_down_sum, image_up_sum = map(columns_of, (0, 2, 4, 6))
    image_proj_sum, text_proj_sum = tail_sums[:2]
    image_qkv_sum = jnp.stack(tail_sums[2:5], axis=1)
    text_qkv_sum = jnp.stack(tail_sums[5:], axis=1)

    early = jnp.stack(
        [
            jnp.concatenate([mid_sums[:, :3], out_sums[:, :1]], axis=1)
            for mid_sums, out_sums in (
                (image_mid_sums, image_out_sums),
                (text_mid_sums, text_out_sums),
            )
        ]
    )
    late = jnp.stack([image_in_sums[:, :2], text_in_sums[:, :2]])
    squares = jnp.concatenate(
        [jnp.sum(out_sums[:, 1:6], axis=(0, 2)) for out_sums in (image_out_sums, text_out_sums)]
    )
    square_row = jnp.pad(squares, (0, width - 10))[None]
    all_sums = jnp.concatenate(
        [early.reshape(-1, width), late.reshape(-1, width), square_row], axis=0
    )
    all_sums = rep_gather(tok_total(all_sums))
    square_total = jnp.sum(all_sums[:, -1, :10], axis=0)
    early_table = jnp.moveaxis(
        all_sums[:, : 8 * seqs].reshape(rep_count, 2, seqs, 4, width), 0, 1
    ).reshape(2, slots, 4, width)
    late_table = jnp.moveaxis(
        all_sums[:, 8 * seqs : -1].reshape(rep_count, 2, seqs, 2, width), 0, 1
    ).reshape(2, slots, 2, width)
    mod_sum = jnp.concatenate([late_table, early_table], axis=2)

    activ_rows = lax.dynamic_slice_in_dim(activ_all, tok_rank * share, share, axis=1).astype(
        jnp.float32
    )
    image_g_mod = jnp.einsum("sd,ske->dke", activ_rows, mod_sum[0], precision=exact_mode)
    text_g_mod = jnp.einsum("sd,ske->dke", activ_rows, mod_sum[1], precision=exact_mode)
    image_g_bmod = jnp.sum(mod_sum[0], axis=0)
    text_g_bmod = jnp.sum(mod_sum[1], axis=0)
    activ_grad = jnp.einsum(
        "ske,dke->sd", mod_sum[0], image_w_mod.astype(jnp.float32), precision=exact_mode
    ) + jnp.einsum("ske,dke->sd", mod_sum[1], text_w_mod.astype(jnp.float32), precision=exact_mode)
    cond_rows = lax.dynamic_slice_in_dim(cond_slots, tok_rank * share, share, axis=1)
    unused_value, silu_back = jax.vjp(jax.nn.silu, cond_rows)
    slot_grad = silu_back(activ_grad)[0]
    cond_grad = jnp.dot(jnp.transpose(picker), slot_grad, precision=exact_mode)
    image_count = float(slots * image_rows * tok_count * width)
    text_count = float(slots * text_real * tok_count * width)
    counts = jnp.concatenate(
        [jnp.full((5,), image_count, jnp.float32), jnp.full((5,), text_count, jnp.float32)]
    )
    stream_rms = jnp.sqrt(square_total / counts)
    return (
        image_result,
        text_result[:, :text_real],
        image_grad,
        text_grad[:, :text_real],
        cond_grad,
        image_g_mod,
        image_g_bmod,
        image_qkv_sum,
        image_proj_sum,
        image_up_sum,
        image_down_sum,
        text_g_mod,
        text_g_bmod,
        text_qkv_sum,
        text_proj_sum,
        text_up_sum,
        text_down_sum,
        stream_rms,
    )


def solution(mesh):
    in_specs = (
        P("rep", "tok", None),
        P("rep", None, None),
        P("rep", None),
        P(),
        P(),
        P("tok", None, None),
        P(),
        P("tok", None, "head"),
        P("tok", "head"),
        P("tok", "head"),
        P("tok", "head"),
        P("tok", None, None),
        P(),
        P("tok", None, "head"),
        P("tok", "head"),
        P("tok", "head"),
        P("tok", "head"),
        P("rep", "tok", None),
        P("rep", "tok", None),
    )
    out_specs = (
        P("rep", "tok", None),
        P("rep", "tok", None),
        P("rep", "tok", None),
        P("rep", "tok", None),
        P(None, "tok"),
        P("tok", None, None),
        P(),
        P("tok", None, "head"),
        P("tok", "head"),
        P("tok", "head"),
        P("tok", "head"),
        P("tok", None, None),
        P(),
        P("tok", None, "head"),
        P("tok", "head"),
        P("tok", "head"),
        P("tok", "head"),
        P(),
    )
    return jax.shard_map(
        on_device, mesh=mesh, in_specs=in_specs, out_specs=out_specs, check_vma=False
    )
```

time: 1400 us -> 1050 us (0.75)
  waiting for transfers between devices: 694 us -> 375 us
  Pallas kernels: 203 us -> 368 us
  other arithmetic: 167 us -> 53 us
  starting transfers between devices: 227 us -> 140 us
  local copies, waits for them, and re-layouts: 49 us -> 63.2 us
    pallas_call x2 -> x50, Pallas kernels: 76.4 us -> 247 us  [the longest x17 58.1 us: add_blocks(): pl.pallas_call(kernel, grid=(2,), in_specs=[in_spec, in_spec], out_specs=...]
    ppermute x64 -> x70, waiting for transfers between devices: 428 us -> 260 us  [flip(): lax.ppermute(values, axis, [(place, place ^ bit) for place in range(lax.a...]
    ppermute x38 -> x36, waiting for transfers between devices: 265 us -> 115 us  [the longest x20 115 us: outer(): return lax.ppermute(load, 'rep', pairs)]
    ppermute x38 -> x36, starting transfers between devices: 174 us -> 93.1 us  [the longest x20 69.6 us: outer(): return lax.ppermute(load, 'rep', pairs)]
    convert_element_type x43 -> x10, other arithmetic: 77.2 us -> 12.4 us  [finish(): jnp.where(self.inner[0] == 1, self.totals[k], self.outward[k])]
    reduce_sum x23 -> x3, other arithmetic: 32 us -> 2.08 us  [the longest x2 2.06 us: on_device(): jnp.sum(out_sums[:, 1:6], axis=(0, 2))]
    select_n x18 -> x0, other arithmetic: 18.5 us -> none  [the longest x4 6.81 us: gather_pair(): fetched = {0: jnp.where(parity == 0, first, second)}]
    ppermute x64 -> x70, starting transfers between devices: 52.7 us -> 47.3 us  [flip(): lax.ppermute(values, axis, [(place, place ^ bit) for place in range(lax.a...]
  transfers between devices with their start and end apart: 102 -> 106, of which waited for: 34 -> 36; matrix products, arithmetic and copies ran while one was open for 17% -> 13% of each run, Pallas kernels for 15% -> 26%
where the time goes in v3:
time: 1050 us; the launch traced here: 1040 us
  waiting for transfers between devices  375 us (36%)
  Pallas kernels  368 us (35%)
  starting transfers between devices  140 us (13%)
  local copies, waits for them, and re-layouts  63.2 us (6%)
  other arithmetic  53 us (5%)
  matrix products  42.1 us (4%)
    ppermute x70, waiting for transfers between devices, flip(): lax.ppermute(values, axis, [(place, place ^ bit) for place in range(lax.a...  260 us
    pallas_call x10, Pallas kernels, call(): pl.pallas_call(kernel, grid=(tiles,), in_specs=[pl.BlockSpec(memory_space...  122 us
    ppermute x20, waiting for transfers between devices, outer(): return lax.ppermute(load, 'rep', pairs)  115 us
    ppermute x20, starting transfers between devices, outer(): return lax.ppermute(load, 'rep', pairs)  69.6 us
    pallas_call x17, Pallas kernels, add_blocks(): pl.pallas_call(kernel, grid=(2,), in_specs=[in_spec, in_spec], out_specs=...  58.1 us
    pallas_call x18, Pallas kernels, step(): pl.pallas_call(kernel, grid=(2,), in_specs=[pl.BlockSpec(memory_space=plt...  57.5 us
    pallas_call x2, Pallas kernels, attend_grads(): pl.pallas_call(kernel, grid=(width // LANES,), in_specs=[row_spec(length,...  53.6 us
    ppermute x70, starting transfers between devices, flip(): lax.ppermute(values, axis, [(place, place ^ bit) for place in range(lax.a...  47.3 us
  transfers between devices with their start and end apart: 106, of which 36 were waited for; matrix products, arithmetic and copies ran while one was open for 13% of the time, Pallas kernels for 26%

profile of v3, /device:TPU:0, one launch (start us, length us, event | category | flops | bytes accessed | tf_op | source)
XLA Modules:
  0.0 1044.5 jit_solution(11995409903893074299)
XLA Ops:
  6.7 4.2 fusion.49
  13.5 12.2 %collective-permute-done.2.rest_1_ = bf16[3,192,768]{2,1,0:T(8,128)(2,1)S(1)} collective-permute-done((bf16[3,192,768]{2,1,0:T(8,128)(2,1)}, bf16[3,192,768]{2,1,0:T(8,128)(2,1)S(1)}, u32[]{:S(2)}, u32[]{:S(2)}) %collective-permute-start.2) | collective-permute-done | bytes 884768 | tf_op jit(solution)/shard_map/ppermute | solution.py:25
  33.5 13.2 %collective-permute-done.3.rest_2_ = bf16[3,192,768]{2,1,0:T(8,128)(2,1)} collective-permute-done((bf16[3,192,768]{2,1,0:T(8,128)(2,1)S(1)}, bf16[3,192,768]{2,1,0:T(8,128)(2,1)}, u32[]{:S(2)}, u32[]{:S(2)}) %collective-permute-start.3) | collective-permute-done | bytes 884768 | tf_op jit(solution)/shard_map/ppermute | solution.py:25
  52.9 8.3 shard_map.323
  62.8 6.3 collective-permute-done.7.rest_1_
  73.9 17.9 %collective-permute-done.8.rest_2_ = bf16[3,192,768]{2,1,0:T(8,128)(2,1)} collective-permute-done((bf16[3,192,768]{2,1,0:T(8,128)(2,1)}, bf16[3,192,768]{2,1,0:T(8,128)(2,1)}, u32[]{:S(2)}, u32[]{:S(2)}) %collective-permute-start.8) | collective-permute-done | bytes 884768 | tf_op jit(solution)/shard_map/ppermute | solution.py:25
  91.8 26.0 %collective-permute-done.16.rest_1_ = bf16[1,384,768]{2,1,0:T(8,128)(2,1)} collective-permute-done((bf16[1,384,768]{2,1,0:T(8,128)(2,1)S(1)}, bf16[1,384,768]{2,1,0:T(8,128)(2,1)}, u32[]{:S(2)}, u32[]{:S(2)}) %collective-permute-start.16) | collective-permute-done | bytes 589856 | tf_op jit(solution)/shard_map/ppermute | solution.py:25
  123.8 5.7 shard_map.325
  134.1 5.9 collective-permute-done.17.rest_8_.rest_10_
  146.9 25.8 %shard_map.326 = (bf16[2,256,768]{2,1,0:T(8,128)(2,1)}, bf16[2,48,768]{2,1,0:T(8,128)(2,1)}) custom-call(bf16[2,256,768]{2,1,0:T(8,128)(2,1)} %bitcast.222, bf16[2,48,768]{2,1,0:T(8,128)(2,1)} %bitcast.270, bf16[2,2,256,768]{3,2,1,0:T(8,128)(2,1)} %bitcast.214, bf16[2,2,256,768]{3,2,1,0:T(8,128)(2,1)} %collective-permute-done.12.rest_3_.rest_5_, ...), custom_call_target="tpu_custom_call" | custom-call | flops 1024 | bytes 1024 | tf_op jit(solution)/shard_map/pallas_call | solution.py:886
  179.8 17.5 %shard_map.328 = bf16[512,1536]{1,0:T(8,128)(2,1)} custom-call(s32[2]{0:T(128)} %pad_add_fusion.spot_ref, bf16[512,768]{1,0:T(8,128)(2,1)} %bitcast.251, bf16[2,384,768]{2,1,0:T(8,128)(2,1)} %copy-done.2, bf16[1,384,768]{2,1,0:T(8,128)(2,1)} %collective-permute-done.16.rest_1_, bf16[1,384,768]{2,1,0:T(8,128)(2,1)} %collective-permute-done.19.rest_2_, ...), custom_call_target="tpu_custom_call" | custom-call | flops 1024 | bytes 1024 | tf_op jit(solution)/shard_map/pallas_call | solution.py:367
  202.4 8.2 collective-permute-done.25
  213.4 8.4 shard_map.330
  225.2 26.7 %collective-permute-done.28.rest_7_ = bf16[192,3072]{1,0:T(8,128)(2,1)} collective-permute-done((bf16[192,3072]{1,0:T(8,128)(2,1)S(1)}, bf16[192,3072]{1,0:T(8,128)(2,1)}, u32[]{:S(2)}, u32[]{:S(2)}) %collective-permute-start.28) | collective-permute-done | bytes 1179680 | tf_op jit(solution)/shard_map/ppermute | solution.py:25
  258.4 22.7 %collective-permute-done.35.rest_8_ = bf16[192,3072]{1,0:T(8,128)(2,1)} collective-permute-done((bf16[192,3072]{1,0:T(8,128)(2,1)}, bf16[192,3072]{1,0:T(8,128)(2,1)}, u32[]{:S(2)}, u32[]{:S(2)}) %collective-permute-start.35) | collective-permute-done | bytes 1179680 | tf_op jit(solution)/shard_map/ppermute | solution.py:25
  281.1 23.5 %collective-permute-done.31.rest_2_ = bf16[192,3072]{1,0:T(8,128)(2,1)} collective-permute-done((bf16[192,3072]{1,0:T(8,128)(2,1)}, bf16[192,3072]{1,0:T(8,128)(2,1)}, u32[]{:S(2)}, u32[]{:S(2)}) %collective-permute-start.31) | collective-permute-done | bytes 1179680 | tf_op jit(solution)/shard_map/ppermute | solution.py:25
  308.4 4.9 shard_map.333
  314.7 40.1 %shard_map.334 = (bf16[512,1536]{1,0:T(8,128)(2,1)}, bf16[512,1536]{1,0:T(8,128)(2,1)}, bf16[2,4,384,768]{3,2,1,0:T(8,128)(2,1)}, bf16[2,4,384,768]{3,2,1,0:T(8,...) custom-call(s32[2]{0:T(128)} %pad_add_fusion.spot_ref, bf16[512,1536]{1,0:T(8,128)(2,1)} %bitcast.276, ...), custom_call_target="tpu_custom_call" | custom-call | flops 1024 | bytes 1024 | tf_op jit(solution)/shard_map/pallas_call | solution.py:367
  356.5 27.2 %collective-permute-done.40.rest_2_ = bf16[2,384,768]{2,1,0:T(8,128)(2,1)S(1)} collective-permute-done((bf16[2,384,768]{2,1,0:T(8,128)(2,1)S(1)}, bf16[2,384,768]{2,1,0:T(8,128)(2,1)S(1)}, u32[]{:S(2)}, u32[]{:S(2)}) %collective-permute-start.40) | collective-permute-done | bytes 1179680 | tf_op jit(solution)/shard_map/ppermute | solution.py:25
  386.7 10.9 %shard_map.335 = (bf16[2,384,384]{2,1,0:T(8,128)(2,1)}, bf16[4,384,768]{2,1,0:T(8,128)(2,1)}, bf16[4,384,768]{2,1,0:T(8,128)(2,1)}) custom-call(s32[2]{0:T(128)} %pad_add_fusion.spot_ref, bf16[2,384,384]{2,1,0:T(8,128)(2,1)} %pad_maximum_fusion.11.in_ref, bf16[384,3072]{1,0:T(8,128)(2,1)} %up_ref.3, bf16[384,3072]{1,0:T(8,128)(2,1)} %down_ref.3, ...), custom_call_target="tpu_custom_call" | custom-call | flops 1024 | bytes 1024 | tf_op jit(solution)/shard_map/pallas_call | solution.py:367
  405.0 6.0 shard_map.336
  416.3 5.7 shard_map.337
  422.0 7.4 shard_map.338
  429.3 6.6 shard_map.339
  442.8 6.5 collective-permute-done.48
  453.0 4.7 shard_map.342
  457.7 26.8 %shard_map.343 = (bf16[1,256,768]{2,1,0:T(8,128)(2,1)}, bf16[1,48,768]{2,1,0:T(8,128)(2,1)}, bf16[2,2,256,768]{3,2,1,0:T(8,128)(2,1)}, bf16[2,2,256,768]{3,2,1,0...) custom-call(bf16[2,256,768]{2,1,0:T(8,128)(2,1)} %bitcast.223, ...), custom_call_target="tpu_custom_call" | custom-call | flops 1024 | bytes 1024 | tf_op jit(solution)/shard_map/pallas_call | solution.py:962
  485.6 4.2 shard_map.344
  493.4 26.8 %shard_map.346 = (bf16[1,256,768]{2,1,0:T(8,128)(2,1)}, bf16[1,48,768]{2,1,0:T(8,128)(2,1)}, bf16[2,2,256,768]{3,2,1,0:T(8,128)(2,1)}, bf16[2,2,256,768]{3,2,1,0...) custom-call(bf16[2,256,768]{2,1,0:T(8,128)(2,1)} %bitcast.224, ...), custom_call_target="tpu_custom_call" | custom-call | flops 1024 | bytes 1024 | tf_op jit(solution)/shard_map/pallas_call | solution.py:962
  529.2 24.4 %collective-permute-done.52.refs_1_ = bf16[768,768]{1,0:T(8,128)(2,1)} collective-permute-done((bf16[768,768]{1,0:T(8,128)(2,1)S(1)}, bf16[768,768]{1,0:T(8,128)(2,1)}, u32[]{:S(2)}, u32[]{:S(2)}) %collective-permute-start.52) | collective-permute-done | bytes 1179680 | tf_op jit(solution)/shard_map/ppermute | solution.py:179
  554.7 4.2 shard_map.347
  569.2 4.4 shard_map.349
  573.6 4.1 collective-permute-done.56
  583.4 23.6 %collective-permute-done.57.refs_1_ = bf16[768,768]{1,0:T(8,128)(2,1)S(1)} collective-permute-done((bf16[768,768]{1,0:T(8,128)(2,1)}, bf16[768,768]{1,0:T(8,128)(2,1)S(1)}, u32[]{:S(2)}, u32[]{:S(2)}) %collective-permute-start.57) | collective-permute-done | bytes 1179680 | tf_op jit(solution)/shard_map/ppermute | solution.py:179
  613.5 4.2 shard_map.351
  624.6 9.6 shard_map.355
  638.3 14.4 %shard_map.357 = (bf16[512,1536]{1,0:T(8,128)(2,1)}, bf16[2,3,384,768]{3,2,1,0:T(8,128)(2,1)}, bf16[2,3,384,768]{3,2,1,0:T(8,128)(2,1)}) custom-call(s32[2]{0:T(128)} %pad_add_fusion.spot_ref, bf16[512,1536]{1,0:T(8,128)(2,1)} %bitcast.221, bf16[512,768]{1,0:T(8,128)(2,1)} %bitcast.255, bf16[2,512,768]{2,1,0:T(8,128)(2,1)} %bitcast.234, ...), custom_call_target="tpu_custom_call" | custom-call | flops 1024 | bytes 1024 | tf_op jit(solution)/shard_map/pallas_call | solution.py:367
  658.2 23.4 %collective-permute-done.63.refs_1_ = bf16[768,768]{1,0:T(8,128)(2,1)} collective-permute-done((bf16[768,768]{1,0:T(8,128)(2,1)}, bf16[768,768]{1,0:T(8,128)(2,1)}, u32[]{:S(2)}, u32[]{:S(2)}) %collective-permute-start.63) | collective-permute-done | bytes 1179680 | tf_op jit(solution)/shard_map/ppermute | solution.py:179
  681.5 4.2 shard_map.358
  685.7 3.8 collective-permute-start.67
  695.5 4.6 shard_map.359
  700.1 4.6 shard_map.360
  704.8 10.3 collective-permute-done.67.refs_1_
  715.1 4.2 shard_map.361
  735.6 5.5 collective-permute-done.70
  748.7 4.2 shard_map.364
  757.3 4.7 pad_maximum_fusion.2
  762.0 8.2 collective-permute-done.73
  775.7 5.7 shard_map.366
  795.5 20.3 %collective-permute-start.86 = (bf16[384,768]{1,0:T(8,128)(2,1)S(1)}, bf16[384,768]{1,0:T(8,128)(2,1)}, u32[]{:S(2)}, u32[]{:S(2)}) collective-permute-start(bf16[384,768]{1,0:T(8,128)(2,1)S(1)} %copy-done.28), channel_id=1, source_target_pairs={{0,8},{24,16},{1,9},{25,17},{2,10},{26,18},{3,11},{27,19},{4,12},{... | collective-permute-start | bytes 1769480 | tf_op jit(solution)/shard_map/ppermute | solution.py:179
  830.2 5.9 shard_map.372
  845.4 11.0 %collective-permute-done.83 = f32[25,1536]{1,0:T(8,128)S(1)} collective-permute-done((f32[25,1536]{1,0:T(8,128)S(1)}, f32[25,1536]{1,0:T(8,128)S(1)}, u32[]{:S(2)}, u32[]{:S(2)}) %collective-permute-start.83) | collective-permute-done | bytes 153632 | tf_op jit(solution)/shard_map/ppermute | solution.py:25
  864.0 23.2 %collective-permute-done.84 = f32[1,25,1536]{2,1,0:T(8,128)S(1)} collective-permute-done((f32[1,25,1536]{2,1,0:T(8,128)S(1)}, f32[1,25,1536]{2,1,0:T(8,128)S(1)}, u32[]{:S(2)}, u32[]{:S(2)}) %collective-permute-start.84) | collective-permute-done | bytes 153632 | tf_op jit(solution)/shard_map/ppermute | solution.py:25
  895.6 3.8 collective-permute-start.89
  914.2 7.7 convolution_bitcast_fusion.1
  926.2 7.8 fusion
  935.7 4.5 collective-permute-done.91.refs_1_
  948.1 8.9 fusion.5
  967.0 8.9 fusion.2
  980.0 4.0 collective-permute-start.97
  988.5 6.5 collective-permute-done.97.refs_1_
  1003.1 4.5 pad_maximum_fusion
  1029.4 4.8 collective-permute-done.103
  1034.2 8.0 collective-permute-done.105
  (510 shorter events, 329.7 us)
Async XLA Ops:
  13.2 39.6 %collective-permute-start.4 = (bf16[3,384,768]{2,1,0:T(8,128)(2,1)S(1)}, bf16[3,384,768]{2,1,0:T(8,128)(2,1)}, u32[]{:S(2)}, u32[]{:S(2)}) collective-permute-start(bf16[3,384,768]{2,1,0:T(8,128)(2,1)S(1)} %bitcast.229), channel_id=1, source_target_pairs={{0,2},{2,0},{4,6},{6,4},{1,3},{3,1},{5,7},{7,5},{8,10},{10,8},{12,... | collective-permute-start | bytes 5308424 | tf_op jit(solution)/shard_map/ppermute | solution.py:25
  48.1 69.9 %collective-permute-start.9 = (bf16[3,384,768]{2,1,0:T(8,128)(2,1)}, bf16[3,384,768]{2,1,0:T(8,128)(2,1)}, u32[]{:S(2)}, u32[]{:S(2)}) collective-permute-start(bf16[3,384,768]{2,1,0:T(8,128)(2,1)} %bitcast.13.rest_0_), channel_id=1, source_target_pairs={{0,2},{2,0},{4,6},{6,4},{1,3},{3,1},{5,7},{7,5},{8,10},{10,8},{12,... | collective-permute-start | bytes 5308424 | tf_op jit(solution)/shard_map/ppermute | solution.py:25
  69.1 50.4 %collective-permute-start.13 = (bf16[2,2,256,768]{3,2,1,0:T(8,128)(2,1)S(1)}, bf16[2,2,256,768]{3,2,1,0:T(8,128)(2,1)}, u32[]{:S(2)}, u32[]{:S(2)}) collective-permute-start(bf16[2,2,256,768]{3,2,1,0:T(8,128)(2,1)S(1)} %bitcast.212), channel_id=1, source_target_pairs={{0,4},{2,6},{4,0},{6,2},{1,5},{3,7},{5,1},{7,3},{8,12},{10,14},{12... | collective-permute-start | bytes 4718600 | tf_op jit(solution)/shard_map/ppermute | solution.py:25
  73.4 44.5 %collective-permute-start.16 = (bf16[1,384,768]{2,1,0:T(8,128)(2,1)S(1)}, bf16[1,384,768]{2,1,0:T(8,128)(2,1)}, u32[]{:S(2)}, u32[]{:S(2)}) collective-permute-start(bf16[1,384,768]{2,1,0:T(8,128)(2,1)S(1)} %fusion.1), channel_id=1, source_target_pairs={{0,4},{2,6},{4,0},{6,2},{1,5},{3,7},{5,1},{7,3},{8,12},{10,14},{12... | collective-permute-start | bytes 1769480 | tf_op jit(solution)/shard_map/ppermute | solution.py:25
  73.9 48.9 %collective-permute-start.10 = (bf16[3,192,768]{2,1,0:T(8,128)(2,1)}, bf16[3,192,768]{2,1,0:T(8,128)(2,1)S(1)}, u32[]{:S(2)}, u32[]{:S(2)}) collective-permute-start(bf16[3,192,768]{2,1,0:T(8,128)(2,1)} %collective-permute-done.7.rest_1_), channel_id=1, source_target_pairs={{0,2},{2,0},{4,6},{6,4},{1,3},{3,1},{5,7},{7,5},{8,10},{10,8},{12,... | collective-permute-start | bytes 2654216 | tf_op jit(solution)/shard_map/ppermute | solution.py:25
  91.8 31.1 %collective-permute-start.11 = (bf16[3,192,768]{2,1,0:T(8,128)(2,1)}, bf16[3,192,768]{2,1,0:T(8,128)(2,1)}, u32[]{:S(2)}, u32[]{:S(2)}) collective-permute-start(bf16[3,192,768]{2,1,0:T(8,128)(2,1)} %collective-permute-done.8.rest_2_), channel_id=1, source_target_pairs={{0,2},{2,0},{4,6},{6,4},{1,3},{3,1},{5,7},{7,5},{8,10},{10,8},{12,... | collective-permute-start | bytes 2654216 | tf_op jit(solution)/shard_map/ppermute | solution.py:25
  117.8 25.0 %collective-permute-start.12 = (bf16[2,2,256,768]{3,2,1,0:T(8,128)(2,1)S(1)}, bf16[2,2,256,768]{3,2,1,0:T(8,128)(2,1)}, u32[]{:S(2)}, u32[]{:S(2)}) collective-permute-start(bf16[2,2,256,768]{3,2,1,0:T(8,128)(2,1)S(1)} %bitcast.213), channel_id=1, source_target_pairs={{0,2},{2,0},{4,6},{6,4},{1,3},{3,1},{5,7},{7,5},{8,10},{10,8},{12,... | collective-permute-start | bytes 4718600 | tf_op jit(solution)/shard_map/ppermute | solution.py:25
  119.5 27.4 %collective-permute-start.14 = (bf16[2,2,256,768]{3,2,1,0:T(8,128)(2,1)}, bf16[2,2,256,768]{3,2,1,0:T(8,128)(2,1)}, u32[]{:S(2)}, u32[]{:S(2)}) collective-permute-start(bf16[2,2,256,768]{3,2,1,0:T(8,128)(2,1)} %collective-permute-done.13.rest_4_.rest_6_), channel_id=1, source_target_pairs={{0,2},{2,0},{4,6},{6,4},{1,3},{3,1},{5,7},{7,5},{8,10},{10,8},{12,... | collective-permute-start | bytes 4718600 | tf_op jit(solution)/shard_map/ppermute | solution.py:25
  133.5 39.2 %collective-permute-start.20 = (bf16[2,384,768]{2,1,0:T(8,128)(2,1)S(1)}, bf16[2,384,768]{2,1,0:T(8,128)(2,1)}, u32[]{:S(2)}, u32[]{:S(2)}) collective-permute-start(bf16[2,384,768]{2,1,0:T(8,128)(2,1)S(1)} %pad_maximum_fusion.6.rest_0_), channel_id=1, source_target_pairs={{0,2},{2,0},{4,6},{6,4},{1,3},{3,1},{5,7},{7,5},{8,10},{10,8},{12,... | collective-permute-start | bytes 3538952 | tf_op jit(solution)/shard_map/ppermute | solution.py:25
  141.1 60.6 %collective-permute-start.24 = (bf16[192,3072]{1,0:T(8,128)(2,1)}, bf16[192,3072]{1,0:T(8,128)(2,1)}, u32[]{:S(2)}, u32[]{:S(2)}) collective-permute-start(bf16[192,3072]{1,0:T(8,128)(2,1)} %constant_dynamic-slice_fusion.6), channel_id=1, source_target_pairs={{0,4},{2,6},{4,0},{6,2},{1,5},{3,7},{5,1},{7,3},{8,12},{10,14},{12... | collective-permute-start | bytes 3538952 | tf_op jit(solution)/shard_map/ppermute | solution.py:25
  142.7 30.0 %collective-permute-start.21 = (bf16[1,384,768]{2,1,0:T(8,128)(2,1)}, bf16[1,384,768]{2,1,0:T(8,128)(2,1)S(1)}, u32[]{:S(2)}, u32[]{:S(2)}) collective-permute-start(bf16[1,384,768]{2,1,0:T(8,128)(2,1)} %collective-permute-done.16.rest_1_), channel_id=1, source_target_pairs={{0,2},{2,0},{4,6},{6,4},{1,3},{3,1},{5,7},{7,5},{8,10},{10,8},{12,... | collective-permute-start | bytes 1769480 | tf_op jit(solution)/shard_map/ppermute | solution.py:25
  142.9 29.8 %collective-permute-start.22 = (bf16[1,384,768]{2,1,0:T(8,128)(2,1)}, bf16[1,384,768]{2,1,0:T(8,128)(2,1)S(1)}, u32[]{:S(2)}, u32[]{:S(2)}) collective-permute-start(bf16[1,384,768]{2,1,0:T(8,128)(2,1)} %collective-permute-done.19.rest_2_), channel_id=1, source_target_pairs={{0,2},{2,0},{4,6},{6,4},{1,3},{3,1},{5,7},{7,5},{8,10},{10,8},{12,... | collective-permute-start | bytes 1769480 | tf_op jit(solution)/shard_map/ppermute | solution.py:25
  221.8 30.5 %collective-permute-start.27 = (bf16[2,2,384,768]{3,2,1,0:T(8,128)(2,1)}, bf16[2,2,384,768]{3,2,1,0:T(8,128)(2,1)}, u32[]{:S(2)}, u32[]{:S(2)}) collective-permute-start(bf16[2,2,384,768]{3,2,1,0:T(8,128)(2,1)} %get-tuple-element.225), channel_id=1, source_target_pairs={{0,2},{2,0},{4,6},{6,4},{1,3},{3,1},{5,7},{7,5},{8,10},{10,8},{12,... | collective-permute-start | bytes 7077896 | tf_op jit(solution)/shard_map/ppermute | solution.py:25
  222.0 35.5 %collective-permute-start.32 = (bf16[384,3072]{1,0:T(8,128)(2,1)}, bf16[384,3072]{1,0:T(8,128)(2,1)}, u32[]{:S(2)}, u32[]{:S(2)}) collective-permute-start(bf16[384,3072]{1,0:T(8,128)(2,1)} %rest_0_.1), channel_id=1, source_target_pairs={{0,2},{2,0},{4,6},{6,4},{1,3},{3,1},{5,7},{7,5},{8,10},{10,8},{12,... | collective-permute-start | bytes 7077896 | tf_op jit(solution)/shard_map/ppermute | solution.py:25
  223.7 28.2 %collective-permute-start.28 = (bf16[192,3072]{1,0:T(8,128)(2,1)S(1)}, bf16[192,3072]{1,0:T(8,128)(2,1)}, u32[]{:S(2)}, u32[]{:S(2)}) collective-permute-start(bf16[192,3072]{1,0:T(8,128)(2,1)S(1)} %constant_dynamic-slice_fusion.5), channel_id=1, source_target_pairs={{0,4},{2,6},{4,0},{6,2},{1,5},{3,7},{5,1},{7,3},{8,12},{10,14},{12... | collective-permute-start | bytes 3538952 | tf_op jit(solution)/shard_map/ppermute | solution.py:25
  224.7 80.0 %collective-permute-start.30 = (bf16[512,1536]{1,0:T(8,128)(2,1)S(1)}, bf16[512,1536]{1,0:T(8,128)(2,1)}, u32[]{:S(2)}, u32[]{:S(2)}) collective-permute-start(bf16[512,1536]{1,0:T(8,128)(2,1)S(1)} %copy-done.5), channel_id=1, source_target_pairs={{0,1},{1,0},{2,3},{3,2},{4,5},{5,4},{6,7},{7,6},{8,9},{9,8},{10,11... | collective-permute-start | bytes 4718600 | tf_op jit(solution)/shard_map/ppermute | solution.py:25
  225.2 88.0 %collective-permute-start.36 = (bf16[384,3072]{1,0:T(8,128)(2,1)}, bf16[384,3072]{1,0:T(8,128)(2,1)}, u32[]{:S(2)}, u32[]{:S(2)}) collective-permute-start(bf16[384,3072]{1,0:T(8,128)(2,1)} %rest_6_.1), channel_id=1, source_target_pairs={{0,2},{2,0},{4,6},{6,4},{1,3},{3,1},{5,7},{7,5},{8,10},{10,8},{12,... | collective-permute-start | bytes 7077896 | tf_op jit(solution)/shard_map/ppermute | solution.py:25
  251.9 29.2 %collective-permute-start.35 = (bf16[192,3072]{1,0:T(8,128)(2,1)}, bf16[192,3072]{1,0:T(8,128)(2,1)}, u32[]{:S(2)}, u32[]{:S(2)}) collective-permute-start(bf16[192,3072]{1,0:T(8,128)(2,1)} %collective-permute-done.28.rest_7_), channel_id=1, source_target_pairs={{0,8},{8,0},{16,24},{24,16},{1,9},{9,1},{17,25},{25,17},{2,10},{10... | collective-permute-start | bytes 3538952 | tf_op jit(solution)/shard_map/ppermute | solution.py:25
  252.3 52.3 %collective-permute-start.31 = (bf16[192,3072]{1,0:T(8,128)(2,1)}, bf16[192,3072]{1,0:T(8,128)(2,1)}, u32[]{:S(2)}, u32[]{:S(2)}) collective-permute-start(bf16[192,3072]{1,0:T(8,128)(2,1)} %collective-permute-done.24.rest_1_), channel_id=1, source_target_pairs={{0,8},{8,0},{16,24},{24,16},{1,9},{9,1},{17,25},{25,17},{2,10},{10... | collective-permute-start | bytes 3538952 | tf_op jit(solution)/shard_map/ppermute | solution.py:25
  257.5 47.7 %collective-permute-start.29 = (bf16[768,768]{1,0:T(8,128)(2,1)}, bf16[768,768]{1,0:T(8,128)(2,1)}, u32[]{:S(2)}, u32[]{:S(2)}) collective-permute-start(bf16[768,768]{1,0:T(8,128)(2,1)} %get-tuple-element.230), channel_id=1, source_target_pairs={{0,4},{2,6},{4,0},{6,2},{1,5},{3,7},{5,1},{7,3},{8,12},{10,14},{12... | collective-permute-start | bytes 3538952 | tf_op jit(solution)/shard_map/ppermute | solution.py:25
  281.1 32.1 %collective-permute-start.37 = (bf16[192,3072]{1,0:T(8,128)(2,1)}, bf16[192,3072]{1,0:T(8,128)(2,1)}, u32[]{:S(2)}, u32[]{:S(2)}) collective-permute-start(bf16[192,3072]{1,0:T(8,128)(2,1)} %collective-permute-done.28.rest_7_), channel_id=1, source_target_pairs={{0,2},{2,0},{4,6},{6,4},{1,3},{3,1},{5,7},{7,5},{8,10},{10,8},{12,... | collective-permute-start | bytes 3538952 | tf_op jit(solution)/shard_map/ppermute | solution.py:25
  354.8 50.2 %collective-permute-start.42 = (bf16[2,4,384,768]{3,2,1,0:T(8,128)(2,1)}, bf16[2,4,384,768]{3,2,1,0:T(8,128)(2,1)}, u32[]{:S(2)}, u32[]{:S(2)}) collective-permute-start(bf16[2,4,384,768]{3,2,1,0:T(8,128)(2,1)} %get-tuple-element.241), channel_id=1, source_target_pairs={{0,2},{2,0},{4,6},{6,4},{1,3},{3,1},{5,7},{7,5},{8,10},{10,8},{12,... | collective-permute-start | bytes 14155784 | tf_op jit(solution)/shard_map/ppermute | solution.py:25
  355.3 61.0 %collective-permute-start.43 = (bf16[2,4,384,768]{3,2,1,0:T(8,128)(2,1)}, bf16[2,4,384,768]{3,2,1,0:T(8,128)(2,1)}, u32[]{:S(2)}, u32[]{:S(2)}) collective-permute-start(bf16[2,4,384,768]{3,2,1,0:T(8,128)(2,1)} %get-tuple-element.244), channel_id=1, source_target_pairs={{0,2},{2,0},{4,6},{6,4},{1,3},{3,1},{5,7},{7,5},{8,10},{10,8},{12,... | collective-permute-start | bytes 14155784 | tf_op jit(solution)/shard_map/ppermute | solution.py:25
  355.4 28.3 %collective-permute-start.40 = (bf16[2,384,768]{2,1,0:T(8,128)(2,1)S(1)}, bf16[2,384,768]{2,1,0:T(8,128)(2,1)S(1)}, u32[]{:S(2)}, u32[]{:S(2)}) collective-permute-start(bf16[2,384,768]{2,1,0:T(8,128)(2,1)S(1)} %copy-done.11), channel_id=1, source_target_pairs={{0,4},{2,6},{4,0},{6,2},{1,5},{3,7},{5,1},{7,3},{8,12},{10,14},{12... | collective-permute-start | bytes 3538952 | tf_op jit(solution)/shard_map/ppermute | solution.py:25
  356.3 27.9 %collective-permute-start.39 = (bf16[2,384,768]{2,1,0:T(8,128)(2,1)S(1)}, bf16[2,384,768]{2,1,0:T(8,128)(2,1)}, u32[]{:S(2)}, u32[]{:S(2)}) collective-permute-start(bf16[2,384,768]{2,1,0:T(8,128)(2,1)S(1)} %copy-done.11), channel_id=1, source_target_pairs={{0,2},{2,0},{4,6},{6,4},{1,3},{3,1},{5,7},{7,5},{8,10},{10,8},{12,... | collective-permute-start | bytes 3538952 | tf_op jit(solution)/shard_map/ppermute | solution.py:25
  383.7 38.2 %collective-permute-start.44 = (bf16[512,1536]{1,0:T(8,128)(2,1)}, bf16[512,1536]{1,0:T(8,128)(2,1)}, u32[]{:S(2)}, u32[]{:S(2)}) collective-permute-start(bf16[512,1536]{1,0:T(8,128)(2,1)} %get-tuple-element.236), channel_id=1, source_target_pairs={{0,1},{1,0},{2,3},{3,2},{4,5},{5,4},{6,7},{7,6},{8,9},{9,8},{10,11... | collective-permute-start | bytes 4718600 | tf_op jit(solution)/shard_map/ppermute | solution.py:25
  401.6 34.3 %collective-permute-start.45 = (bf16[768,768]{1,0:T(8,128)(2,1)S(1)}, bf16[768,768]{1,0:T(8,128)(2,1)}, u32[]{:S(2)}, u32[]{:S(2)}) collective-permute-start(bf16[768,768]{1,0:T(8,128)(2,1)S(1)} %bitcast.247), channel_id=1, source_target_pairs={{0,8},{24,16},{1,9},{25,17},{2,10},{26,18},{3,11},{27,19},{4,12},{... | collective-permute-start | bytes 3538952 | tf_op jit(solution)/shard_map/ppermute | solution.py:179
  411.1 78.7 %collective-permute-start.51 = (bf16[1536,768]{1,0:T(8,128)(2,1)}, bf16[1536,768]{1,0:T(8,128)(2,1)}, u32[]{:S(2)}, u32[]{:S(2)}) collective-permute-start(bf16[1536,768]{1,0:T(8,128)(2,1)} %get-tuple-element.264), channel_id=1, source_target_pairs={{0,4},{2,6},{4,0},{6,2},{1,5},{3,7},{5,1},{7,3},{8,12},{10,14},{12... | collective-permute-start | bytes 7077896 | tf_op jit(solution)/shard_map/ppermute | solution.py:25
  413.9 70.6 %collective-permute-start.49 = (bf16[768,768]{1,0:T(8,128)(2,1)S(1)}, bf16[768,768]{1,0:T(8,128)(2,1)}, u32[]{:S(2)}, u32[]{:S(2)}) collective-permute-start(bf16[768,768]{1,0:T(8,128)(2,1)S(1)} %bitcast.245), channel_id=1, source_target_pairs={{0,8},{24,16},{1,9},{25,17},{2,10},{26,18},{3,11},{27,19},{4,12},{... | collective-permute-start | bytes 3538952 | tf_op jit(solution)/shard_map/ppermute | solution.py:179
  438.5 46.0 %collective-permute-start.50 = (bf16[768,768]{1,0:T(8,128)(2,1)}, bf16[768,768]{1,0:T(8,128)(2,1)S(1)}, u32[]{:S(2)}, u32[]{:S(2)}) collective-permute-start(bf16[768,768]{1,0:T(8,128)(2,1)} %shard_map.340.refs_2_), channel_id=1, source_target_pairs={{8,16},{16,8},{9,17},{17,9},{10,18},{18,10},{11,19},{19,11},{12,20... | collective-permute-start | bytes 3538952 | tf_op jit(solution)/shard_map/ppermute | solution.py:245
  523.8 41.7 %collective-permute-start.55 = (bf16[2,2,2,256,768]{4,3,1,0,2:T(8,128)(2,1)}, bf16[2,2,2,256,768]{4,3,1,0,2:T(8,128)(2,1)}, u32[]{:S(2)}, u32[]{:S(2)}) collective-permute-start(bf16[2,2,2,256,768]{4,3,1,0,2:T(8,128)(2,1)} %pad_maximum_fusion.5), channel_id=1, source_target_pairs={{0,2},{2,0},{4,6},{6,4},{1,3},{3,1},{5,7},{7,5},{8,10},{10,8},{12,... | collective-permute-start | bytes 9437192 | tf_op jit(solution)/shard_map/ppermute | solution.py:25
  523.8 54.0 %collective-permute-start.56 = (bf16[1536,768]{1,0:T(8,128)(2,1)}, bf16[1536,768]{1,0:T(8,128)(2,1)}, u32[]{:S(2)}, u32[]{:S(2)}) collective-permute-start(bf16[1536,768]{1,0:T(8,128)(2,1)} %get-tuple-element.284), channel_id=1, source_target_pairs={{0,4},{2,6},{4,0},{6,2},{1,5},{3,7},{5,1},{7,3},{8,12},{10,14},{12... | collective-permute-start | bytes 7077896 | tf_op jit(solution)/shard_map/ppermute | solution.py:25
  524.7 29.0 %collective-permute-start.52 = (bf16[768,768]{1,0:T(8,128)(2,1)S(1)}, bf16[768,768]{1,0:T(8,128)(2,1)}, u32[]{:S(2)}, u32[]{:S(2)}) collective-permute-start(bf16[768,768]{1,0:T(8,128)(2,1)S(1)} %copy-done.81), channel_id=1, source_target_pairs={{0,8},{8,0},{16,24},{24,16},{1,9},{9,1},{17,25},{25,17},{2,10},{10... | collective-permute-start | bytes 3538952 | tf_op jit(solution)/shard_map/ppermute | solution.py:179
  527.2 26.5 %collective-permute-start.53 = (bf16[768,768]{1,0:T(8,128)(2,1)S(1)}, bf16[768,768]{1,0:T(8,128)(2,1)S(1)}, u32[]{:S(2)}, u32[]{:S(2)}) collective-permute-start(bf16[768,768]{1,0:T(8,128)(2,1)S(1)} %copy-done.51), channel_id=1, source_target_pairs={{8,16},{16,8},{9,17},{17,9},{10,18},{18,10},{11,19},{19,11},{12,20... | collective-permute-start | bytes 3538952 | tf_op jit(solution)/shard_map/ppermute | solution.py:245
  528.8 30.9 %collective-permute-start.54 = (bf16[2,2,2,48,768]{4,3,1,0,2:T(8,128)(2,1)}, bf16[2,2,2,48,768]{4,3,1,0,2:T(8,128)(2,1)}, u32[]{:S(2)}, u32[]{:S(2)}) collective-permute-start(bf16[2,2,2,48,768]{4,3,1,0,2:T(8,128)(2,1)} %pad_maximum_fusion.15), channel_id=1, source_target_pairs={{0,2},{2,0},{4,6},{6,4},{1,3},{3,1},{5,7},{7,5},{8,10},{10,8},{12,... | collective-permute-start | bytes 1769480 | tf_op jit(solution)/shard_map/ppermute | solution.py:25
  577.7 56.5 %collective-permute-start.62 = (bf16[1024,768]{1,0:T(8,128)(2,1)}, bf16[1024,768]{1,0:T(8,128)(2,1)S(1)}, u32[]{:S(2)}, u32[]{:S(2)}) collective-permute-start(bf16[1024,768]{1,0:T(8,128)(2,1)} %get-tuple-element.306), channel_id=1, source_target_pairs={{0,4},{2,6},{4,0},{6,2},{1,5},{3,7},{5,1},{7,3},{8,12},{10,14},{12... | collective-permute-start | bytes 4718600 | tf_op jit(solution)/shard_map/ppermute | solution.py:25
  578.7 28.3 %collective-permute-start.57 = (bf16[768,768]{1,0:T(8,128)(2,1)}, bf16[768,768]{1,0:T(8,128)(2,1)S(1)}, u32[]{:S(2)}, u32[]{:S(2)}) collective-permute-start(bf16[768,768]{1,0:T(8,128)(2,1)} %get-tuple-element.287), channel_id=1, source_target_pairs={{0,8},{8,0},{16,24},{24,16},{1,9},{9,1},{17,25},{25,17},{2,10},{10... | collective-permute-start | bytes 3538952 | tf_op jit(solution)/shard_map/ppermute | solution.py:179
  581.2 32.3 %collective-permute-start.58 = (bf16[768,768]{1,0:T(8,128)(2,1)}, bf16[768,768]{1,0:T(8,128)(2,1)}, u32[]{:S(2)}, u32[]{:S(2)}) collective-permute-start(bf16[768,768]{1,0:T(8,128)(2,1)} %get-tuple-element.273.refs_2_), channel_id=1, source_target_pairs={{8,16},{16,8},{9,17},{17,9},{10,18},{18,10},{11,19},{19,11},{12,20... | collective-permute-start | bytes 3538952 | tf_op jit(solution)/shard_map/ppermute | solution.py:245
  582.8 34.8 %collective-permute-start.59 = (bf16[2,1,384,768]{3,2,0,1:T(8,128)(2,1)}, bf16[2,1,384,768]{3,2,0,1:T(8,128)(2,1)}, u32[]{:S(2)}, u32[]{:S(2)}) collective-permute-start(bf16[2,1,384,768]{3,2,0,1:T(8,128)(2,1)} %bitcast.315), channel_id=1, source_target_pairs={{0,2},{2,0},{4,6},{6,4},{1,3},{3,1},{5,7},{7,5},{8,10},{10,8},{12,... | collective-permute-start | bytes 3538952 | tf_op jit(solution)/shard_map/ppermute | solution.py:25
  582.8 37.4 %collective-permute-start.60 = (bf16[2,1,384,768]{3,2,0,1:T(8,128)(2,1)}, bf16[2,1,384,768]{3,2,0,1:T(8,128)(2,1)}, u32[]{:S(2)}, u32[]{:S(2)}) collective-permute-start(bf16[2,1,384,768]{3,2,0,1:T(8,128)(2,1)} %bitcast.316), channel_id=1, source_target_pairs={{0,2},{2,0},{4,6},{6,4},{1,3},{3,1},{5,7},{7,5},{8,10},{10,8},{12,... | collective-permute-start | bytes 3538952 | tf_op jit(solution)/shard_map/ppermute | solution.py:25
  652.7 42.8 %collective-permute-start.65 = (bf16[2,3,384,768]{3,2,1,0:T(8,128)(2,1)}, bf16[2,3,384,768]{3,2,1,0:T(8,128)(2,1)}, u32[]{:S(2)}, u32[]{:S(2)}) collective-permute-start(bf16[2,3,384,768]{3,2,1,0:T(8,128)(2,1)} %get-tuple-element.313), channel_id=1, source_target_pairs={{0,2},{2,0},{4,6},{6,4},{1,3},{3,1},{5,7},{7,5},{8,10},{10,8},{12,... | collective-permute-start | bytes 10616840 | tf_op jit(solution)/shard_map/ppermute | solution.py:25
  652.8 47.4 %collective-permute-start.66 = (bf16[2,3,384,768]{3,2,1,0:T(8,128)(2,1)}, bf16[2,3,384,768]{3,2,1,0:T(8,128)(2,1)}, u32[]{:S(2)}, u32[]{:S(2)}) collective-permute-start(bf16[2,3,384,768]{3,2,1,0:T(8,128)(2,1)} %get-tuple-element.316), channel_id=1, source_target_pairs={{0,2},{2,0},{4,6},{6,4},{1,3},{3,1},{5,7},{7,5},{8,10},{10,8},{12,... | collective-permute-start | bytes 10616840 | tf_op jit(solution)/shard_map/ppermute | solution.py:25
  653.2 28.3 %collective-permute-start.63 = (bf16[768,768]{1,0:T(8,128)(2,1)}, bf16[768,768]{1,0:T(8,128)(2,1)}, u32[]{:S(2)}, u32[]{:S(2)}) collective-permute-start(bf16[768,768]{1,0:T(8,128)(2,1)} %get-tuple-element.310), channel_id=1, source_target_pairs={{0,8},{8,0},{16,24},{24,16},{1,9},{9,1},{17,25},{25,17},{2,10},{10... | collective-permute-start | bytes 3538952 | tf_op jit(solution)/shard_map/ppermute | solution.py:179
  655.0 26.5 %collective-permute-start.64 = (bf16[768,768]{1,0:T(8,128)(2,1)}, bf16[768,768]{1,0:T(8,128)(2,1)}, u32[]{:S(2)}, u32[]{:S(2)}) collective-permute-start(bf16[768,768]{1,0:T(8,128)(2,1)} %get-tuple-element.288.refs_2_), channel_id=1, source_target_pairs={{8,16},{16,8},{9,17},{17,9},{10,18},{18,10},{11,19},{19,11},{12,20... | collective-permute-start | bytes 3538952 | tf_op jit(solution)/shard_map/ppermute | solution.py:245
  685.7 29.4 %collective-permute-start.67 = (bf16[768,768]{1,0:T(8,128)(2,1)}, bf16[768,768]{1,0:T(8,128)(2,1)}, u32[]{:S(2)}, u32[]{:S(2)}) collective-permute-start(bf16[768,768]{1,0:T(8,128)(2,1)} %get-tuple-element.319), channel_id=1, source_target_pairs={{0,8},{8,0},{16,24},{24,16},{1,9},{9,1},{17,25},{25,17},{2,10},{10... | collective-permute-start | bytes 3538952 | tf_op jit(solution)/shard_map/ppermute | solution.py:179
  689.5 25.6 %collective-permute-start.68 = (bf16[768,768]{1,0:T(8,128)(2,1)}, bf16[768,768]{1,0:T(8,128)(2,1)}, u32[]{:S(2)}, u32[]{:S(2)}) collective-permute-start(bf16[768,768]{1,0:T(8,128)(2,1)} %get-tuple-element.311.refs_2_), channel_id=1, source_target_pairs={{8,16},{16,8},{9,17},{17,9},{10,18},{18,10},{11,19},{19,11},{12,20... | collective-permute-start | bytes 3538952 | tf_op jit(solution)/shard_map/ppermute | solution.py:245
  694.6 37.5 %collective-permute-start.69 = (bf16[384,768]{1,0:T(8,128)(2,1)}, bf16[384,768]{1,0:T(8,128)(2,1)S(1)}, u32[]{:S(2)}, u32[]{:S(2)}) collective-permute-start(bf16[384,768]{1,0:T(8,128)(2,1)} %get-tuple-element.323), channel_id=1, source_target_pairs={{0,4},{2,6},{4,0},{6,2},{1,5},{3,7},{5,1},{7,3},{8,12},{10,14},{12... | collective-permute-start | bytes 1769480 | tf_op jit(solution)/shard_map/ppermute | solution.py:25
  719.3 28.3 %collective-permute-start.71 = (bf16[768,768]{1,0:T(8,128)(2,1)}, bf16[768,768]{1,0:T(8,128)(2,1)S(1)}, u32[]{:S(2)}, u32[]{:S(2)}) collective-permute-start(bf16[768,768]{1,0:T(8,128)(2,1)} %get-tuple-element.329), channel_id=1, source_target_pairs={{0,8},{8,0},{16,24},{24,16},{1,9},{9,1},{17,25},{25,17},{2,10},{10... | collective-permute-start | bytes 3538952 | tf_op jit(solution)/shard_map/ppermute | solution.py:179
  726.2 48.8 %collective-permute-start.74 = (bf16[512,1536]{1,0:T(8,128)(2,1)}, bf16[512,1536]{1,0:T(8,128)(2,1)}, u32[]{:S(2)}, u32[]{:S(2)}) collective-permute-start(bf16[512,1536]{1,0:T(8,128)(2,1)} %get-tuple-element.308), channel_id=1, source_target_pairs={{0,1},{1,0},{2,3},{3,2},{4,5},{5,4},{6,7},{7,6},{8,9},{9,8},{10,11... | collective-permute-start | bytes 4718600 | tf_op jit(solution)/shard_map/ppermute | solution.py:25
  732.1 38.1 %collective-permute-start.73 = (bf16[96,1536]{1,0:T(8,128)(2,1)}, bf16[96,1536]{1,0:T(8,128)(2,1)}, u32[]{:S(2)}, u32[]{:S(2)}) collective-permute-start(bf16[96,1536]{1,0:T(8,128)(2,1)} %get-tuple-element.303), channel_id=1, source_target_pairs={{0,1},{1,0},{2,3},{3,2},{4,5},{5,4},{6,7},{7,6},{8,9},{9,8},{10,11... | collective-permute-start | bytes 884744 | tf_op jit(solution)/shard_map/ppermute | solution.py:25
  741.1 84.5 %collective-permute-start.80 = (bf16[96,1536]{1,0:T(8,128)(2,1)S(1)}, bf16[96,1536]{1,0:T(8,128)(2,1)}, u32[]{:S(2)}, u32[]{:S(2)}) collective-permute-start(bf16[96,1536]{1,0:T(8,128)(2,1)S(1)} %get-tuple-element.347), channel_id=1, source_target_pairs={{0,1},{1,0},{2,3},{3,2},{4,5},{5,4},{6,7},{7,6},{8,9},{9,8},{10,11... | collective-permute-start | bytes 884744 | tf_op jit(solution)/shard_map/ppermute | solution.py:25
  752.9 30.3 %collective-permute-start.75 = (bf16[768,768]{1,0:T(8,128)(2,1)}, bf16[768,768]{1,0:T(8,128)(2,1)S(1)}, u32[]{:S(2)}, u32[]{:S(2)}) collective-permute-start(bf16[768,768]{1,0:T(8,128)(2,1)} %get-tuple-element.338), channel_id=1, source_target_pairs={{0,8},{8,0},{16,24},{24,16},{1,9},{9,1},{17,25},{25,17},{2,10},{10... | collective-permute-start | bytes 3538952 | tf_op jit(solution)/shard_map/ppermute | solution.py:179
  755.6 30.8 %collective-permute-start.76 = (bf16[768,768]{1,0:T(8,128)(2,1)}, bf16[768,768]{1,0:T(8,128)(2,1)}, u32[]{:S(2)}, u32[]{:S(2)}) collective-permute-start(bf16[768,768]{1,0:T(8,128)(2,1)} %get-tuple-element.330.refs_2_), channel_id=1, source_target_pairs={{8,16},{16,8},{9,17},{17,9},{10,18},{18,10},{11,19},{19,11},{12,20... | collective-permute-start | bytes 3538952 | tf_op jit(solution)/shard_map/ppermute | solution.py:245
  770.2 48.0 %collective-permute-start.78 = (bf16[1152,768]{1,0:T(8,128)(2,1)}, bf16[1152,768]{1,0:T(8,128)(2,1)}, u32[]{:S(2)}, u32[]{:S(2)}) collective-permute-start(bf16[1152,768]{1,0:T(8,128)(2,1)} %get-tuple-element.343), channel_id=1, source_target_pairs={{0,4},{2,6},{4,0},{6,2},{1,5},{3,7},{5,1},{7,3},{8,12},{10,14},{12... | collective-permute-start | bytes 5308424 | tf_op jit(solution)/shard_map/ppermute | solution.py:25
  775.0 55.2 %collective-permute-start.81 = (bf16[512,1536]{1,0:T(8,128)(2,1)}, bf16[512,1536]{1,0:T(8,128)(2,1)}, u32[]{:S(2)}, u32[]{:S(2)}) collective-permute-start(bf16[512,1536]{1,0:T(8,128)(2,1)} %get-tuple-element.351), channel_id=1, source_target_pairs={{0,1},{1,0},{2,3},{3,2},{4,5},{5,4},{6,7},{7,6},{8,9},{9,8},{10,11... | collective-permute-start | bytes 4718600 | tf_op jit(solution)/shard_map/ppermute | solution.py:25
  783.2 39.0 %collective-permute-start.79 = (bf16[384,768]{1,0:T(8,128)(2,1)}, bf16[384,768]{1,0:T(8,128)(2,1)}, u32[]{:S(2)}, u32[]{:S(2)}) collective-permute-start(bf16[384,768]{1,0:T(8,128)(2,1)} %shard_map.362.refs_0_), channel_id=1, source_target_pairs={{0,8},{24,16},{1,9},{25,17},{2,10},{26,18},{3,11},{27,19},{4,12},{... | collective-permute-start | bytes 1769480 | tf_op jit(solution)/shard_map/ppermute | solution.py:179
  795.5 92.7 %collective-permute-start.86 = (bf16[384,768]{1,0:T(8,128)(2,1)S(1)}, bf16[384,768]{1,0:T(8,128)(2,1)}, u32[]{:S(2)}, u32[]{:S(2)}) collective-permute-start(bf16[384,768]{1,0:T(8,128)(2,1)S(1)} %copy-done.28), channel_id=1, source_target_pairs={{0,8},{24,16},{1,9},{25,17},{2,10},{26,18},{3,11},{27,19},{4,12},{... | collective-permute-start | bytes 1769480 | tf_op jit(solution)/shard_map/ppermute | solution.py:179
  818.3 74.3 %collective-permute-start.88 = (bf16[1152,768]{1,0:T(8,128)(2,1)}, bf16[1152,768]{1,0:T(8,128)(2,1)}, u32[]{:S(2)}, u32[]{:S(2)}) collective-permute-start(bf16[1152,768]{1,0:T(8,128)(2,1)} %get-tuple-element.364), channel_id=1, source_target_pairs={{0,4},{2,6},{4,0},{6,2},{1,5},{3,7},{5,1},{7,3},{8,12},{10,14},{12... | collective-permute-start | bytes 5308424 | tf_op jit(solution)/shard_map/ppermute | solution.py:25
  822.2 35.5 %collective-permute-start.98 = (bf16[768,768]{1,0:T(8,128)(2,1)}, bf16[768,768]{1,0:T(8,128)(2,1)}, u32[]{:S(2)}, u32[]{:S(2)}) collective-permute-start(bf16[768,768]{1,0:T(8,128)(2,1)} %get-tuple-element.384), channel_id=1, source_target_pairs={{8,0},{16,24},{9,1},{17,25},{10,2},{18,26},{11,3},{19,27},{12,4},{... | collective-permute-start | bytes 3538952 | tf_op jit(solution)/shard_map/ppermute | solution.py:179
  843.9 44.2 %collective-permute-start.87 = (bf16[384,768]{1,0:T(8,128)(2,1)S(1)}, bf16[384,768]{1,0:T(8,128)(2,1)}, u32[]{:S(2)}, u32[]{:S(2)}) collective-permute-start(bf16[384,768]{1,0:T(8,128)(2,1)S(1)} %copy-done.33), channel_id=1, source_target_pairs={{8,16},{16,8},{9,17},{17,9},{10,18},{18,10},{11,19},{19,11},{12,20... | collective-permute-start | bytes 1769480 | tf_op jit(solution)/shard_map/ppermute | solution.py:245
  856.4 129.1 %collective-permute-start.99 = (bf16[768,768]{1,0:T(8,128)(2,1)}, bf16[768,768]{1,0:T(8,128)(2,1)}, u32[]{:S(2)}, u32[]{:S(2)}) collective-permute-start(bf16[768,768]{1,0:T(8,128)(2,1)} %shard_map.368), channel_id=1, source_target_pairs={{8,0},{16,24},{9,1},{17,25},{10,2},{18,26},{11,3},{19,27},{12,4},{... | collective-permute-start | bytes 3538952 | tf_op jit(solution)/shard_map/ppermute | solution.py:179
  857.7 29.4 %collective-permute-start.84 = (f32[1,25,1536]{2,1,0:T(8,128)S(1)}, f32[1,25,1536]{2,1,0:T(8,128)S(1)}, u32[]{:S(2)}, u32[]{:S(2)}) collective-permute-start(f32[1,25,1536]{2,1,0:T(8,128)S(1)} %add_bitcast_fusion), channel_id=1, source_target_pairs={{0,8},{8,0},{16,24},{24,16},{1,9},{9,1},{17,25},{25,17},{2,10},{10... | collective-permute-start | bytes 460808 | tf_op jit(solution)/shard_map/ppermute | solution.py:25
  891.0 30.9 %collective-permute-start.90 = (bf16[384,768]{1,0:T(8,128)(2,1)}, bf16[384,768]{1,0:T(8,128)(2,1)}, u32[]{:S(2)}, u32[]{:S(2)}) collective-permute-start(bf16[384,768]{1,0:T(8,128)(2,1)} %get-tuple-element.361.refs_2_), channel_id=1, source_target_pairs={{8,16},{16,8},{9,17},{17,9},{10,18},{18,10},{11,19},{19,11},{12,20... | collective-permute-start | bytes 1769480 | tf_op jit(solution)/shard_map/ppermute | solution.py:245
  895.6 26.3 %collective-permute-start.89 = (bf16[384,768]{1,0:T(8,128)(2,1)}, bf16[384,768]{1,0:T(8,128)(2,1)}, u32[]{:S(2)}, u32[]{:S(2)}) collective-permute-start(bf16[384,768]{1,0:T(8,128)(2,1)} %get-tuple-element.367), channel_id=1, source_target_pairs={{0,8},{8,0},{16,24},{24,16},{1,9},{9,1},{17,25},{25,17},{2,10},{10... | collective-permute-start | bytes 1769480 | tf_op jit(solution)/shard_map/ppermute | solution.py:179
  (127 other events, 1745.3 us)

commit v4 on v3

--- a/solution.py
+++ b/solution.py
@@ -42,10 +42,10 @@
         self.last = None
 
     def then(self, values):
-        return values if self.last is None else after(values, self.last)
-
-    def mark(self, output):
-        self.last = output
+        return values if self.last is None else after(values, *self.last)
+
+    def mark(self, output, *moves):
+        self.last = (output, *moves)
         return output
 
 
@@ -66,7 +66,7 @@
         self.away, self.half, self.array = away, half, array
 
 
-def gather_weight(weight, axis, lane, needed=()):
+def fetch(weight, axis, lane, needed=()):
     parity = lax.rem(lax.axis_index("rep"), 2)
     size = weight.shape[axis] // 2
     held = {0: lax.dynamic_slice_in_dim(weight, parity * size, size, axis=axis)}
@@ -77,11 +77,24 @@
         for away, array in list(held.items()):
             held[away ^ bit] = lane.flip(array, bit)
         bit //= 2
-    parts = [Part(0, None, weight)]
+    del held[0]
+    return held
+
+
+def share_out(weight, own, held, needed=()):
+    parts = []
     for away, array in held.items():
-        if away:
-            parts += [Part(away, 0, array), Part(away, 1, flip(array, "rep", 1))]
-    return parts + [Part(part.away ^ 1, part.half, flip(part.array, "tok", 1)) for part in parts]
+        parts += [Part(away, 0, array), Part(away, 1, flip(array, "rep", 1))]
+    others = [
+        Part(
+            part.away ^ 1,
+            part.half,
+            flip(after(part.array, *needed) if needed else part.array, "tok", 1),
+        )
+        for part in parts
+    ]
+    swapped = [part.array for part in parts if part.half == 1]
+    return [Part(0, None, weight)] + parts + [Part(1, None, own)] + others, swapped
 
 
 def gather_blocks(values, lane):
@@ -126,6 +139,61 @@
 def core_sums(seq, keep, moved):
     sums = add_blocks(seq, keep, moved, keep.shape[0])
     return {2 * place: part for place, part in enumerate(sums)}
+
+
+def core_sums_joined(seq, keeps, moved):
+    pieces, pair, rows, width = keeps[0].shape
+    pairs = len(keeps)
+
+    def kernel(*refs):
+        for at in range(pairs):
+            for place in range(pieces):
+                refs[2 * pairs + place][at] = (
+                    refs[at][place].astype(jnp.float32)
+                    + refs[pairs + at][place].astype(jnp.float32)
+                ).astype(jnp.bfloat16)
+
+    spec = pl.BlockSpec((pieces, 1, rows, width), lambda step: (0, step, 0, 0))
+    sums = pl.pallas_call(
+        kernel,
+        grid=(pair,),
+        in_specs=[spec] * (2 * pairs),
+        out_specs=[pl.BlockSpec((pairs, 1, rows, width), lambda step: (0, step, 0, 0))] * pieces,
+        out_shape=[bf16(pairs, pair, rows, width)] * pieces,
+        compiler_params=pltpu.CompilerParams(
+            dimension_semantics=("arbitrary",), vmem_limit_bytes=VMEM_LIMIT
+        ),
+        cost_estimate=SMALL_COST,
+    )(seq.then(keeps[0]), *keeps[1:], *moved)
+    seq.mark(sums[0])
+    return {2 * place: part.reshape(-1, width) for place, part in enumerate(sums)}
+
+
+def add_split(seq, first, second, groups, top):
+    width = first.shape[-1]
+    first, second = seq.then(first).reshape(groups, -1, width), second.reshape(groups, -1, width)
+    rows = first.shape[1]
+
+    def kernel(first_ref, second_ref, top_ref, bottom_ref):
+        total = (first_ref[0].astype(jnp.float32) + second_ref[0].astype(jnp.float32)).astype(
+            jnp.bfloat16
+        )
+        top_ref[0], bottom_ref[0] = total[:top], total[top:]
+
+    spec = lambda length: pl.BlockSpec((1, length, width), lambda step: (step, 0, 0))
+    parts = pl.pallas_call(
+        kernel,
+        grid=(groups,),
+        in_specs=[spec(rows), spec(rows)],
+        out_specs=[spec(top), spec(rows - top)],
+        out_shape=[bf16(groups, top, width), bf16(groups, rows - top, width)],
+        compiler_params=pltpu.CompilerParams(
+            dimension_semantics=("arbitrary",), vmem_limit_bytes=VMEM_LIMIT
+        ),
+        cost_estimate=SMALL_COST,
+    )(first, second)
+    seq.mark(parts[0])
+    return parts
 
 
 def chip_moves(seq, pieces, lane):
@@ -142,27 +210,8 @@
     return pieces[0], lane.flip(pieces[bit], bit)
 
 
-def exchange(pieces, lane):
-    count = lax.axis_size("tok")
-    rank = lax.axis_index("tok")
-    held = {away: [(0, part)] for away, part in pieces.items()}
-    bit = count // 2
-    while bit > 0:
-        leaving = jnp.stack([part for away in held if away & bit for source, part in held[away]])
-        moved = lane.flip(leaving, bit) if bit > 1 else flip(leaving, "tok", bit)
-        place, kept = 0, {}
-        for away in [away for away in held if not away & bit]:
-            kept[away] = list(held[away])
-            for source, part in held[away | bit]:
-                kept[away].append((source ^ bit, moved[place]))
-                place += 1
-        held = kept
-        bit //= 2
-    came = jnp.stack([part for source, part in sorted(held[0], key=lambda pair: pair[0])])
-    return [
-        lax.dynamic_index_in_dim(came, jnp.bitwise_xor(rank, place), 0, keepdims=False)
-        for place in range(count)
-    ]
+def exchange(pieces):
+    return [pieces[0]] + [flip(part, "tok", 1 + place) for place, part in enumerate(pieces[1:])]
 
 
 class Line:
@@ -184,7 +233,7 @@
             self.came = self.outer(chunk, [(0, 1), (3, 2)])
 
     def step(self, final=False):
-        if not self.on_line:
+        if not self.on_line or not self.chunks or self.place > len(self.chunks):
             return
         k, seq = self.place, self.seq
         count = len(self.chunks)
@@ -265,9 +314,11 @@
         ]
 
 
-def tok_total(values):
+def tok_total(values, *needed):
     bit = 1
     while bit < lax.axis_size("tok"):
+        if bit == 2 and needed:
+            values = after(values, *needed)
         values = values + flip(values, "tok", bit)
         bit *= 2
     return values
@@ -453,13 +504,16 @@
     )
 
 
-def qkv_grads(spot, hidden, query_grad, block_grads, parts):
+def qkv_grads(spot, hidden, query_grads, block_grads, parts):
     arrays = [part.array for part in parts]
     tiles, share, columns = arrays[0].shape
     length, width = hidden.shape
     count = width // share
 
-    def kernel(spot_ref, hid_ref, query_ref, block_ref, *rest):
+    seqs, rows = len(query_grads), query_grads[0].shape[1]
+
+    def kernel(spot_ref, hid_ref, *rest):
+        query_refs, block_refs, rest = rest[:seqs], rest[seqs : 2 * seqs], rest[2 * seqs :]
         refs, (out_ref, keep_ref, send_ref, scratch, total, turned, grad) = rest[:-7], rest[-7:]
         step = pl.program_id(0)
         fill(scratch, spot_ref, parts, refs)
@@ -468,11 +522,13 @@
         def first():
             turned[...] = jnp.transpose(hid_ref[...])
             total[...] = jnp.zeros_like(total)
-            grad[...] = query_ref[...]
+            for at, ref in enumerate(query_refs):
+                grad[at * rows : (at + 1) * rows] = ref[0]
 
         @pl.when(step > 0)
         def later():
-            grad[...] = block_ref[0]
+            for at, ref in enumerate(block_refs):
+                grad[at * rows : (at + 1) * rows] = ref[0]
 
         total[...] += product_back(grad[...], scratch[...])
         put_grad(spot_ref, turned, grad[...], keep_ref, send_ref, share, count)
@@ -486,11 +542,15 @@
         kernel,
         tiles,
         spot,
-        [hidden, query_grad, block_grads] + arrays,
-        [
-            whole_spec(hidden),
-            whole_spec(query_grad),
-            pl.BlockSpec((1, length, columns), lambda step: (jnp.maximum(step - 1, 0), 0, 0)),
+        [hidden, *query_grads] + [block_grads] * seqs + arrays,
+        [whole_spec(hidden)]
+        + [whole_spec(part) for part in query_grads]
+        + [
+            pl.BlockSpec(
+                (1, rows, columns),
+                functools.partial(lambda at, step: (2 * at + jnp.maximum(step - 1, 0), 0, 0), at),
+            )
+            for at in range(seqs)
         ]
         + [tile_spec(3, part.shape[1], columns) for part in arrays],
         (bf16(length, width), half, half),
@@ -595,13 +655,64 @@
     )
 
 
-def spread_up(spot, rows_in, up_shard, down_shard, count):
-    length, share = rows_in.shape[1:]
+def middle_spread(seq, spot, modul, stream, branch, cot, count):
+    seqs, length, width = stream.shape
+    share = width // count
+
+    def kernel(spot_ref, mod_ref, x_ref, one_ref, two_ref, cot_ref, *rest):
+        outs, hid_all, grad_all = rest[:-2], rest[-2], rest[-1]
+        middle = wide(x_ref) + mod_ref[0, 2:3] * (wide(one_ref) + wide(two_ref))
+        norm, factor = normed(middle)
+        hid_all[...] = (norm * (1.0 + mod_ref[0, 4:5]) + mod_ref[0, 3:4]).astype(jnp.bfloat16)
+        grad_all[...] = (mod_ref[0, 5:6] * wide(cot_ref)).astype(jnp.bfloat16)
+        for away, out in enumerate(outs):
+            at = pl.multiple_of(jnp.bitwise_xor(spot_ref[0], away) * share, LANES)
+            out[0, 0] = hid_all[:, pl.ds(at, share)]
+            out[1, 0] = grad_all[:, pl.ds(at, share)]
+
+    row_spec = pl.BlockSpec((1, length, width), lambda at: (at, 0, 0))
+    made = pl.pallas_call(
+        kernel,
+        grid=(seqs,),
+        in_specs=[
+            pl.BlockSpec(memory_space=pltpu.SMEM),
+            pl.BlockSpec((1,) + modul.shape[1:], lambda at: (at, 0, 0)),
+        ]
+        + [row_spec] * 4,
+        out_specs=[pl.BlockSpec((2, 1, length, share), lambda at: (0, at, 0, 0))] * count,
+        out_shape=[bf16(2, seqs, length, share)] * count,
+        scratch_shapes=[pltpu.VMEM((length, width), jnp.bfloat16)] * 2,
+        compiler_params=pltpu.CompilerParams(
+            dimension_semantics=("arbitrary",), vmem_limit_bytes=VMEM_LIMIT
+        ),
+        cost_estimate=SMALL_COST,
+    )(spot, modul, seq.then(stream), *branch, cot)
+    seq.mark(made[0])
+    return [part.reshape(2, -1, share) for part in made]
+
+
+def lay_rows(spot, refs, scratch):
+    rows = refs[0].shape[1]
+    for away, ref in enumerate(refs):
+        at = pl.multiple_of(jnp.bitwise_xor(spot[0], away) * rows, rows)
+        scratch[:, pl.ds(at, rows), :] = ref[...]
+
+
+def spread_up(seq, spot, features, up_shard, down_shard):
+    count = len(features)
+    rows, share = features[0].shape[1:]
+    length = rows * count
     columns = up_shard.shape[1] // count
 
-    def kernel(spot_ref, in_ref, up_ref, down_ref, keep_ref, send_ref):
-        upward = product(in_ref[0], up_ref[...]).astype(jnp.bfloat16)
-        activ_grad = product(in_ref[1], down_ref[...]).astype(jnp.bfloat16)
+    def kernel(spot_ref, up_ref, down_ref, *rest):
+        refs, (keep_ref, send_ref, rows_in) = rest[:count], rest[count:]
+
+        @pl.when(pl.program_id(0) == 0)
+        def begin():
+            lay_rows(spot_ref, refs, rows_in)
+
+        upward = product(rows_in[0], up_ref[...]).astype(jnp.bfloat16)
+        activ_grad = product(rows_in[1], down_ref[...]).astype(jnp.bfloat16)
         odd = pl.program_id(0) % 2
 
         @pl.when(odd == 0)
@@ -617,34 +728,37 @@
     )
     out_spec = pl.BlockSpec((1, 2, length, columns), lambda step, spot_ref: (step // 2, 0, 0, 0))
     out = bf16(count // 2, 2, length, columns)
-    return pl.pallas_call(
+    keep, send = pl.pallas_call(
         kernel,
         grid_spec=pltpu.PrefetchScalarGridSpec(
             num_scalar_prefetch=1,
             grid=(count,),
-            in_specs=[
-                pl.BlockSpec(rows_in.shape, lambda step, spot_ref: (0, 0, 0)),
-                shard_spec,
-                shard_spec,
-            ],
+            in_specs=[shard_spec, shard_spec]
+            + [pl.BlockSpec(part.shape, lambda step, spot_ref: (0, 0, 0)) for part in features],
             out_specs=[out_spec, out_spec],
+            scratch_shapes=[pltpu.VMEM((2, length, share), jnp.bfloat16)],
         ),
         out_shape=[out, out],
         compiler_params=pltpu.CompilerParams(
             dimension_semantics=("arbitrary",), vmem_limit_bytes=VMEM_LIMIT
         ),
         cost_estimate=SMALL_COST,
-    )(spot, rows_in, up_shard, down_shard)
-
-
-def spread_down(spot, rows_in, blocks, up_shard, down_shard):
+    )(spot, up_shard, down_shard, seq.then(features[0]), *features[1:])
+    seq.mark(keep)
+    return keep, send
+
+
+def spread_down(spot, features, blocks, up_shard, down_shard):
     count = len(blocks)
     length, columns = blocks[0].shape[1:]
     share, units = up_shard.shape
-
-    def kernel(spot_ref, in_ref, up_ref, down_ref, *rest):
-        refs, (out_ref, up_grad_ref, down_grad_ref) = rest[:count], rest[count:]
-        hid_turned, grad_turned = jnp.transpose(in_ref[0]), jnp.transpose(in_ref[1])
+    rows = length // count
+
+    def kernel(spot_ref, up_ref, down_ref, *rest):
+        feature_refs, refs, rest = rest[:count], rest[count : 2 * count], rest[2 * count :]
+        outs, (up_grad_ref, down_grad_ref, rows_in, sums) = rest[:count], rest[count:]
+        lay_rows(spot_ref, feature_refs, rows_in)
+        hid_turned, grad_turned = jnp.transpose(rows_in[0]), jnp.transpose(rows_in[1])
         out_sum = jnp.zeros((length, share), jnp.float32)
         back_sum = jnp.zeros((length, share), jnp.float32)
         for away, ref in enumerate(refs):
@@ -655,58 +769,53 @@
             back_sum += product_back(upward_grad, up_ref[:, at])
             up_grad_ref[place] = product(hid_turned, upward_grad).astype(jnp.bfloat16)
             down_grad_ref[place] = product(grad_turned, activ).astype(jnp.bfloat16)
-        out_ref[0] = back_sum.astype(jnp.bfloat16)
-        out_ref[1] = out_sum.astype(jnp.bfloat16)
+        sums[0] = back_sum.astype(jnp.bfloat16)
+        sums[1] = out_sum.astype(jnp.bfloat16)
+        for away, out in enumerate(outs):
+            at = pl.multiple_of(jnp.bitwise_xor(spot_ref[0], away) * rows, rows)
+            out[...] = sums[:, pl.ds(at, rows), :]
 
     zeros = lambda step: (0, 0, 0)
-    arrays = [rows_in, up_shard, down_shard] + list(blocks)
-    return call(
+    arrays = [up_shard, down_shard] + list(features) + list(blocks)
+    *sums, up_grad, down_grad = call(
         kernel,
         1,
         spot,
         arrays,
         [whole_spec(part) for part in arrays],
-        (bf16(2, length, share),) + (bf16(count, share, columns),) * 2,
-        (pl.BlockSpec((2, length, share), zeros),)
+        (bf16(2, rows, share),) * count + (bf16(count, share, columns),) * 2,
+        (pl.BlockSpec((2, rows, share), zeros),) * count
         + (pl.BlockSpec((count, share, columns), zeros),) * 2,
+        [pltpu.VMEM((2, length, share), jnp.bfloat16)] * 2,
+    )
+    return sums, up_grad, down_grad
+
+
+def gather_features(seq, spot, pieces):
+    count = len(pieces)
+    rows, share = pieces[0].shape[1:]
+
+    def kernel(spot_ref, *rest):
+        refs, outs = rest[:count], rest[count:]
+        for away, ref in enumerate(refs):
+            at = pl.multiple_of(jnp.bitwise_xor(spot_ref[0], away) * share, LANES)
+            for place, out in enumerate(outs):
+                out[:, pl.ds(at, share)] = ref[place]
+
+    out_spec = pl.BlockSpec((rows, share * count), lambda step: (0, 0))
+    arrays = [seq.then(pieces[0])] + list(pieces[1:])
+    made = call(
+        kernel,
+        1,
+        spot,
+        arrays,
+        [whole_spec(part) for part in arrays],
+        (bf16(rows, share * count),) * 2,
+        (out_spec, out_spec),
         [],
     )
-
-
-def spread_begin(seq, spot, hidden, grad, up_shard, down_shard, lane):
-    count = lax.axis_size("tok")
-    rank = lax.axis_index("tok")
-    share = up_shard.shape[0]
-    both = jnp.stack([hidden, grad])
-    features = exchange(
-        {
-            away: lax.dynamic_slice_in_dim(
-                both, jnp.bitwise_xor(rank, away) * share, share, axis=2
-            )
-            for away in range(count)
-        },
-        lane,
-    )
-    rows_in = seq.then(jnp.concatenate(features, axis=1))
-    keep, send = spread_up(spot, rows_in, up_shard, down_shard, count)
-    seq.mark(keep)
-    pieces = core_sums(seq, keep, flip(send, "tok", 1))
-    shape = (2,) + keep.shape[2:]
-    stays, came = chip_moves(seq, pieces, lane)
-    active = activate(seq, stays.reshape(shape), came.reshape(shape))
-    return rows_in, gather_blocks(active, lane)
-
-
-def spread_back(both, rows, lane):
-    rank = lax.axis_index("tok")
-    features = exchange(
-        {
-            away: lax.dynamic_slice_in_dim(both, jnp.bitwise_xor(rank, away) * rows, rows, axis=1)
-            for away in range(lax.axis_size("tok"))
-        },
-        lane,
-    )
-    return jnp.concatenate(features, axis=2)
+    seq.mark(made[0])
+    return made
 
 
 def row_kernel(seq, kernel, modul, rows_in, outs):
@@ -905,10 +1014,7 @@
     keys = rows * count
 
     def kernel(*rest):
-        refs, (image_out, text_out, image_keep, image_send, text_keep, text_send) = (
-            rest[:-6],
-            rest[-6:],
-        )
+        refs, (image_out, text_out, keep_ref, send_ref) = rest[:-4], rest[-4:]
         queries = joint(refs[:2], 0)
         grads = joint(refs[2:4], 0)
         key_all = joint(refs[4:], (0, 0))
@@ -940,13 +1046,12 @@
         key_grad = (key_grad * 0.125).astype(jnp.bfloat16)
         value_grad = value_grad.astype(jnp.bfloat16)
         for away in range(count):
+            to, place = (send_ref if away & 1 else keep_ref), away // 2
             at = slice(away * image_rows, (away + 1) * image_rows)
-            to = image_send if away & 1 else image_keep
-            to[away // 2, 0], to[away // 2, 1] = key_grad[at], value_grad[at]
+            to[place, 0, :image_rows], to[place, 1, :image_rows] = key_grad[at], value_grad[at]
             first = count * image_rows + away * text_rows
             at = slice(first, first + text_rows)
-            to = text_send if away & 1 else text_keep
-            to[away // 2, 0], to[away // 2, 1] = key_grad[at], value_grad[at]
+            to[place, 0, image_rows:], to[place, 1, image_rows:] = key_grad[at], value_grad[at]
 
     def row_spec(length, at):
         return pl.BlockSpec((1, length, LANES), lambda part: (at, 0, part))
@@ -958,7 +1063,6 @@
         return pl.BlockSpec((count // 2, 2, length, LANES), lambda part: (0, 0, 0, part))
 
     sizes = (image_rows, text_rows)
-    owners = [length for length in sizes for side in range(2)]
     return pl.pallas_call(
         kernel,
         grid=(width // LANES,),
@@ -966,9 +1070,9 @@
         + [block_spec(image_rows)] * count
         + [block_spec(text_rows)] * count,
         out_specs=[row_spec(length, 0) for length in sizes]
-        + [owner_spec(length) for length in owners],
+        + [owner_spec(rows)] * 2,
         out_shape=[bf16(1, length, width) for length in sizes]
-        + [bf16(count // 2, 2, length, width) for length in owners],
+        + [bf16(count // 2, 2, rows, width)] * 2,
         compiler_params=pltpu.CompilerParams(
             dimension_semantics=("arbitrary",), vmem_limit_bytes=VMEM_LIMIT
         ),
@@ -1011,7 +1115,10 @@
 
     turn = lambda weight: jnp.transpose(weight, (1, 0, 2))
     chips = Lane("tok", 2)
-    image_qkv_parts = gather_weight(turn(image_w_qkv), 1, chips)
+    proj_stack = jnp.stack([image_w_proj, text_w_proj])
+    qkv_held = fetch(turn(image_w_qkv), 1, chips)
+    qkv_own, text_own = flip(turn(image_w_qkv), "tok", 1), flip(turn(text_w_qkv), "tok", 1)
+    image_qkv_parts, unused = share_out(turn(image_w_qkv), qkv_own, qkv_held)
 
     picker = (slot_sequence[:, None] == jnp.arange(slots, dtype=jnp.int32)[None, :]).astype(
         jnp.float32
@@ -1026,13 +1133,13 @@
                 jnp.einsum("sd,dke->ske", activ_share, weight, preferred_element_type=jnp.float32)
                 for weight in (image_w_mod, text_w_mod)
             ]
-        )
+        ),
+        *qkv_held.values(),
     )
     image_mod = both_mod[0] + image_b_mod.astype(jnp.float32)[None]
     text_mod = both_mod[1] + text_b_mod.astype(jnp.float32)[None]
 
-    text_qkv_parts = gather_weight(turn(text_w_qkv), 1, chips, (both_mod,))
-    proj_parts = gather_weight(jnp.stack([image_w_proj, text_w_proj]), 0, chips)
+    text_held = fetch(turn(text_w_qkv), 1, chips, (both_mod,))
 
     owned = (text_owner == tok_rank).astype(jnp.float32)
     total_text = text_owner.shape[1]
@@ -1057,32 +1164,52 @@
     heads = lambda partial: both(head_pair(partial))
 
     image_hid_one = flat(first_hidden(seq, image_mod, image_tokens))
-    image_qkv = seq.mark(project(spot, image_hid_one, image_qkv_parts))
+    image_qkv = seq.mark(
+        project(spot, after(seq.then(image_hid_one), *text_held.values()), image_qkv_parts)
+    )
     image_blocks = gather_blocks(by_seq(image_qkv[1:]), chips)
+    text_qkv_parts, unused = share_out(turn(text_w_qkv), text_own, text_held, (image_qkv,))
     text_hid_one = flat(first_hidden(seq, text_mod, text_input))
-    text_qkv = seq.mark(project(spot, text_hid_one, text_qkv_parts))
+    text_qkv = project(spot, seq.then(text_hid_one), text_qkv_parts)
     text_blocks = gather_blocks(by_seq(text_qkv[1:]), chips)
-    image_up_parts = gather_weight(image_w_up, 0, chips)
-    image_down_parts = gather_weight(image_w_down, 0, chips)
+    cores = Lane("tok", 1)
+    owned_shards = [
+        cores.flip(after(weight, image_qkv), 1)
+        for weight in (image_w_up, image_w_down, proj_stack)
+    ]
+    up_own, down_own, proj_own = owned_shards
+    seq.mark(text_qkv, *owned_shards)
+    proj_parts, unused = share_out(proj_stack, proj_own, fetch(proj_stack, 0, chips, (text_qkv,)))
+    up_held = fetch(image_w_up, 0, chips)
+    down_held = fetch(image_w_down, 0, chips)
+    image_up_parts, up_swapped = share_out(image_w_up, up_own, up_held)
+    image_down_parts, down_swapped = share_out(image_w_down, down_own, down_held)
     image_query, text_query = by_seq(image_qkv[0]), by_seq(text_qkv[0])
-    image_mix, text_mix = attend(image_query, text_query, image_blocks, text_blocks, text_real)
+    image_mix, text_mix = attend(
+        image_query, seq.then(text_query), image_blocks, text_blocks, text_real
+    )
+    seq.mark(image_mix, *up_held.values())
     image_mixed, text_mixed = flat(image_mix), flat(text_mix)
-    text_out = seq.mark(project_back(spot, text_mixed, proj_parts, 1, width))
+    text_out = seq.mark(project_back(spot, seq.then(text_mixed), proj_parts, 1, width))
     text_branch = heads(text_out)
-    image_out = seq.mark(project_back(spot, seq.then(image_mixed), proj_parts, 0, width))
+    image_out = project_back(spot, seq.then(image_mixed), proj_parts, 0, width)
+    seq.mark(image_out, *down_held.values())
     image_branch = heads(image_out)
 
-    text_hid_two, text_db_two = middle_hidden(seq, text_mod, text_input, text_branch, text_cot)
-    text_in, text_active = spread_begin(
-        seq, spot, flat(text_hid_two), flat(text_db_two), text_w_up, text_w_down, chips
+    text_features = exchange(
+        middle_spread(seq, spot, text_mod, text_input, text_branch, text_cot, tok_count)
     )
     image_hid_two, image_db_two = middle_hidden(
         seq, image_mod, image_tokens, image_branch, image_cotangent
     )
+    seq.mark(image_hid_two, *up_swapped, *down_swapped)
+    text_keep, text_send = spread_up(seq, spot, text_features, text_w_up, text_w_down)
+    text_pieces = core_sums(seq, text_keep, flip(text_send, "tok", 1))
+    text_stays, text_came = chip_moves(seq, text_pieces, chips)
     image_part, image_back, image_up_keep, image_up_send, image_down_keep, image_down_send = (
         feed_forward(
             spot,
-            flat(image_hid_two),
+            seq.then(flat(image_hid_two)),
             flat(image_db_two),
             image_up_parts,
             image_down_parts,
@@ -1090,40 +1217,57 @@
         )
     )
     seq.mark(image_back)
-    image_hid_grad = heads(image_back)
-    down_moved = flip(image_down_send, "tok", 1)
-    up_moved = flip(image_up_send, "tok", 1)
+    shape = (2,) + text_keep.shape[2:]
+    text_act = activate(seq, text_stays.reshape(shape), text_came.reshape(shape))
+    text_active = gather_blocks(text_act, chips)
+    image_hid_grad = heads(after(image_back, text_act))
+    image_down_send = after(image_down_send, text_act)
+    image_up_send = after(image_up_send, text_act)
+    chips = Lane("tok", 3)
+    image_down_pieces = core_sums(seq, image_down_keep, flip(image_down_send, "tok", 1))
+    image_down_pair = chip_moves(seq, image_down_pieces, chips)
+    image_up_pieces = core_sums(seq, image_up_keep, flip(image_up_send, "tok", 1))
+    image_up_pair = chip_moves(seq, image_up_pieces, chips)
     text_sums, text_up_grad, text_down_grad = spread_down(
-        spot, seq.then(text_in), text_active, text_w_up, text_w_down
-    )
-    seq.mark(text_sums)
+        spot,
+        [seq.then(text_features[0])] + text_features[1:],
+        text_active,
+        text_w_up,
+        text_w_down,
+    )
+    seq.mark(text_sums[0])
+    text_back_pieces = exchange(text_sums)
     line = Line(seq)
-    for whole in (text_down_grad, text_up_grad):
-        for place in range(2):
-            line.add(flat(whole.reshape(2, -1, share, whole.shape[-1])[place]))
-    image_down_pieces = core_sums(seq, image_down_keep, down_moved)
-    image_down_pair = chip_moves(seq, image_down_pieces, chips)
-    text_back, text_part = spread_back(text_sums, flat(text_input).shape[0], chips)
-    text_hid_grad = heads(text_back)
-    image_up_pieces = core_sums(seq, image_up_keep, up_moved)
-    image_up_pair = chip_moves(seq, image_up_pieces, chips)
+    if line.on_line:
+        for whole in (text_down_grad, text_up_grad):
+            for place in range(2):
+                line.add(flat(whole.reshape(2, -1, share, whole.shape[-1])[place]))
+        text_totals = None
+    else:
+        text_totals = [lax.psum(part, "rep") for part in (text_down_grad, text_up_grad)]
 
     image_mid_grad, image_db_one, image_mid_sums = middle_grads(
         seq, image_mod, image_tokens, image_branch, image_cotangent, image_hid_grad
     )
+    text_back, text_part = gather_features(seq, spot, text_back_pieces)
+    text_hid_grad = heads(text_back)
     image_mixed_grad, image_proj_keep, image_proj_send = proj_grads(
-        spot, flat(image_db_one), image_mixed, proj_parts, 0
+        spot, seq.then(flat(image_db_one)), image_mixed, proj_parts, 0
     )
     seq.mark(image_mixed_grad)
-    line.step()
     text_mid_grad, text_db_one, text_mid_sums = middle_grads(
         seq, text_mod, text_input, text_branch, text_cot, text_hid_grad
     )
     text_mixed_grad, text_proj_keep, text_proj_send = proj_grads(
-        spot, flat(text_db_one), text_mixed, proj_parts, 1
+        spot, seq.then(flat(text_db_one)), text_mixed, proj_parts, 1
     )
     seq.mark(text_mixed_grad)
-    grads_all = []
+    line.step()
+    proj_pieces = [
+        core_sums(seq, keep, flip(send, "tok", 1))
+        for keep, send in ((image_proj_keep, image_proj_send), (text_proj_keep, text_proj_send))
+    ]
+    made_grads, moved_grads = [], []
     mix_grads = (by_seq(image_mixed_grad), by_seq(text_mixed_grad))
     for at in range(seqs):
         made = attend_grads(
@@ -1134,82 +1278,85 @@
             text_real,
             at,
         )
+        made_grads.append(made)
         seq.mark(made[0])
-        grads_all.append(made)
+        if at == 0 or at == seqs - 1:
+            for part in add_blocks(seq, *(image_up_pair if at else image_down_pair), 2):
+                line.add(part)
+        if at == 0 and seqs == 1:
+            for part in add_blocks(seq, *image_up_pair, 2):
+                line.add(part)
         line.step()
-        if at == 0:
-            for part in add_blocks(seq, *image_down_pair, 2):
-                line.add(part)
-    image_query_grad, text_query_grad, *block_grads = [
-        jnp.stack(parts, axis=-3) for parts in zip(*grads_all)
-    ]
-    text_pieces = core_sums(seq, block_grads[2], flip(block_grads[3], "tok", 1))
-    text_moves = chip_moves(seq, text_pieces, chips)
-    image_pieces = core_sums(seq, block_grads[0], flip(block_grads[1], "tok", 1))
-    image_moves = chip_moves(seq, image_pieces, chips)
-    for part in add_blocks(seq, *image_up_pair, 2):
-        line.add(part)
+        moved_grads.append(flip(after(made[3], *seq.last), "tok", 1))
+    block_move = chip_moves(
+        seq, core_sums_joined(seq, [made[2] for made in made_grads], moved_grads), chips
+    )
     line.step()
     tail = Line(seq)
-    proj_pairs = [
-        chip_moves(seq, core_sums(seq, keep, flip(send, "tok", 1)), chips)
-        for keep, send in ((image_proj_keep, image_proj_send), (text_proj_keep, text_proj_send))
-    ]
-    pair_of = lambda values: values.reshape(2, -1, heads_width)
-    text_block_grad = pair_of(add_blocks(seq, *text_moves, 1)[0])
+    block_grads = add_split(seq, *block_move, 2 * seqs, image_rows)
+    proj_pairs = [chip_moves(seq, pieces, chips) for pieces in proj_pieces]
+    image_in_part, image_qkv_keep, image_qkv_send = qkv_grads(
+        spot,
+        seq.then(image_hid_one),
+        [made[0] for made in made_grads],
+        block_grads[0],
+        image_qkv_parts,
+    )
+    seq.mark(image_in_part)
     text_in_part, text_qkv_keep, text_qkv_send = qkv_grads(
-        spot, text_hid_one, flat(text_query_grad[0]), text_block_grad, text_qkv_parts
+        spot,
+        seq.then(text_hid_one),
+        [made[1] for made in made_grads],
+        block_grads[1],
+        text_qkv_parts,
     )
     seq.mark(text_in_part)
-    image_block_grad = pair_of(add_blocks(seq, *image_moves, 1)[0])
-    image_in_part, image_qkv_keep, image_qkv_send = qkv_grads(
-        spot, image_hid_one, flat(image_query_grad[0]), image_block_grad, image_qkv_parts
-    )
-    seq.mark(image_in_part)
-    line.step()
     qkv_pairs = [
         chip_moves(seq, core_sums(seq, keep, flip(send, "tok", 1)), chips)
         for keep, send in ((image_qkv_keep, image_qkv_send), (text_qkv_keep, text_qkv_send))
     ]
+    line.step()
+    image_in_grad = heads(image_in_part)
     text_in_grad = heads(text_in_part)
-    image_in_grad = heads(image_in_part)
-    text_second = heads(after(text_part, image_in_part))
-    image_second = heads(after(image_part, image_in_part))
-    line.step()
     image_proj_share, text_proj_share = [add_blocks(seq, *pair, 1)[0] for pair in proj_pairs]
     line.step()
+    image_grad, image_in_sums = input_grads(
+        seq, image_mod, image_tokens, image_mid_grad, image_in_grad
+    )
     text_grad, text_in_sums = input_grads(
         seq, text_mod, text_input, text_mid_grad, text_in_grad
     )
-    image_grad, image_in_sums = input_grads(
-        seq, image_mod, image_tokens, image_mid_grad, image_in_grad
-    )
+    text_second = heads(after(text_part, image_in_sums))
+    image_second = heads(after(image_part, image_in_sums))
+    image_qkv_shares = add_blocks(seq, *qkv_pairs[0], 3)
     line.step()
-    ff_sums = line.finish()
-    tail.add(image_proj_share)
-    tail.add(text_proj_share)
-    for part in add_blocks(seq, *qkv_pairs[0], 3):
+    text_qkv_shares = add_blocks(seq, *qkv_pairs[1], 3)
+    line.step()
+    for part in [image_proj_share, text_proj_share, *image_qkv_shares, *text_qkv_shares]:
         tail.add(part)
-    tail.step()
     text_result, text_out_sums = results(
         seq, text_mod, text_input, text_branch, text_second, text_cot, text_real
     )
     image_result, image_out_sums = results(
         seq, image_mod, image_tokens, image_branch, image_second, image_cotangent, image_rows
     )
-    tail.step()
-    for part in add_blocks(seq, *qkv_pairs[1], 3):
-        tail.add(part)
+    line.step()
+    line_sums = line.finish()
     tail_sums = tail.finish()
-    columns_of = lambda place: jnp.concatenate(
+    columns_of = lambda parts: jnp.concatenate(
         [
-            column
-            for part in ff_sums[place : place + 2]
+            column.astype(jnp.float32)
+            for part in parts
             for column in part.reshape(-1, share, part.shape[-1])
         ],
         axis=1,
     )
-    text_down_sum, text_up_sum, image_down_sum, image_up_sum = map(columns_of, (0, 2, 4, 6))
+    if text_totals is None:
+        text_totals = [jnp.concatenate(line_sums[at : at + 2]) for at in (0, 2)]
+        text_totals = [part.reshape(tok_count, share, -1) for part in text_totals]
+        line_sums = line_sums[4:]
+    text_down_sum, text_up_sum = [columns_of([part]) for part in text_totals]
+    image_down_sum, image_up_sum = columns_of(line_sums[:2]), columns_of(line_sums[2:])
     image_proj_sum, text_proj_sum = tail_sums[:2]
     image_qkv_sum = jnp.stack(tail_sums[2:5], axis=1)
     text_qkv_sum = jnp.stack(tail_sums[5:], axis=1)

time: 1050 us -> 984 us (0.937)
  waiting for transfers between devices: 375 us -> 344 us
  other arithmetic: 53 us -> 35.7 us
  Pallas kernels: 368 us -> 357 us
    ppermute x70 -> x71, waiting for transfers between devices: 260 us -> 206 us  [flip(): lax.ppermute(values, axis, [(place, place ^ bit) for place in range(lax.a...]
    ppermute x20, waiting for transfers between devices: 115 us -> 138 us  [outer(): return lax.ppermute(load, 'rep', pairs)]
    unnamed x176 -> x200, local copies, waits for them, and re-layouts: 15.9 us -> 33.1 us
    pallas_call x0 -> x3, Pallas kernels: none -> 11.9 us  [the longest x1 4.81 us: core_sums_joined(): pl.pallas_call(kernel, grid=(pair,), in_specs=[spec] * (2 * pairs), out_s...]
    pallas_call x17 -> x13, Pallas kernels: 58.1 us -> 46.9 us  [add_blocks(): pl.pallas_call(kernel, grid=(2,), in_specs=[in_spec, in_spec], out_specs=...]
    pallas_call x10 -> x11, Pallas kernels: 122 us -> 112 us  [call(): pl.pallas_call(kernel, grid=(tiles,), in_specs=[pl.BlockSpec(memory_space...]
    ppermute x70 -> x71, starting transfers between devices: 47.3 us -> 52.6 us  [flip(): lax.ppermute(values, axis, [(place, place ^ bit) for place in range(lax.a...]
    pallas_call x10 -> x9, Pallas kernels: 40.1 us -> 38.2 us  [row_kernel(): pl.pallas_call(kernel, grid=(seqs,), in_specs=[pl.BlockSpec((1,) + modul....]
  transfers between devices with their start and end apart: 106 -> 107, of which waited for: 36 -> 37; matrix products, arithmetic and copies ran while one was open for 13% -> 10% of each run, Pallas kernels for 26% -> 32%
where the time goes in v4:
time: 984 us; the launch traced here: 973 us
  Pallas kernels  357 us (36%)
  waiting for transfers between devices  344 us (35%)
  starting transfers between devices  132 us (13%)
  local copies, waits for them, and re-layouts  60.2 us (6%)
  matrix products  40.7 us (4%)
  other arithmetic  35.7 us (4%)
    ppermute x71, waiting for transfers between devices, flip(): lax.ppermute(values, axis, [(place, place ^ bit) for place in range(lax.a...  206 us
    ppermute x20, waiting for transfers between devices, outer(): return lax.ppermute(load, 'rep', pairs)  138 us
    pallas_call x11, Pallas kernels, call(): pl.pallas_call(kernel, grid=(tiles,), in_specs=[pl.BlockSpec(memory_space...  112 us
    ppermute x20, starting transfers between devices, outer(): return lax.ppermute(load, 'rep', pairs)  59.8 us
    pallas_call x18, Pallas kernels, step(): pl.pallas_call(kernel, grid=(2,), in_specs=[pl.BlockSpec(memory_space=plt...  57.6 us
    pallas_call x2, Pallas kernels, attend_grads(): pl.pallas_call(kernel, grid=(width // LANES,), in_specs=[row_spec(length,...  53.4 us
    ppermute x71, starting transfers between devices, flip(): lax.ppermute(values, axis, [(place, place ^ bit) for place in range(lax.a...  52.6 us
    pallas_call x13, Pallas kernels, add_blocks(): pl.pallas_call(kernel, grid=(2,), in_specs=[in_spec, in_spec], out_specs=...  46.9 us
  transfers between devices with their start and end apart: 107, of which 37 were waited for; matrix products, arithmetic and copies ran while one was open for 10% of the time, Pallas kernels for 32%

profile of v4, /device:TPU:0, one launch (start us, length us, event | category | flops | bytes accessed | tf_op | source)
XLA Modules:
  0.0 972.9 jit_solution(14121411675436137301)
XLA Ops:
  6.3 4.2 fusion.46
  12.4 13.6 %collective-permute-done.1.rest_1_.rest_5_ = bf16[3,192,768]{2,1,0:T(8,128)(2,1)} collective-permute-done((bf16[3,192,768]{2,1,0:T(8,128)(2,1)}, bf16[3,192,768]{2,1,0:T(8,128)(2,1)}, u32[]{:S(2)}, u32[]{:S(2)}) %collective-permute-start.1) | collective-permute-done | bytes 884768 | tf_op jit(solution)/shard_map/ppermute | solution.py:25
  31.9 4.5 collective-permute-done.2
  38.0 9.1 collective-permute-done.4.rest_2_.rest_6_
  51.6 6.1 collective-permute-done.3.rest_1_.rest_5_
  57.7 8.3 shard_map.323
  66.5 6.8 collective-permute-done.12.rest_3_
  78.3 18.4 %collective-permute-done.8.rest_2_.rest_6_ = bf16[3,192,768]{2,1,0:T(8,128)(2,1)} collective-permute-done((bf16[3,192,768]{2,1,0:T(8,128)(2,1)}, bf16[3,192,768]{2,1,0:T(8,128)(2,1)}, u32[]{:S(2)}, u32[]{:S(2)}) %collective-permute-start.8) | collective-permute-done | bytes 884768 | tf_op jit(solution)/shard_map/ppermute | solution.py:25
  101.9 5.7 shard_map.325
  123.5 9.3 collective-permute-done.22.rest_1_
  137.7 8.4 collective-permute-done.23.rest_2_
  151.3 25.8 %shard_map.326 = (bf16[2,256,768]{2,1,0:T(8,128)(2,1)}, bf16[2,48,768]{2,1,0:T(8,128)(2,1)}) custom-call(bf16[2,256,768]{2,1,0:T(8,128)(2,1)} %bitcast.172, bf16[2,48,768]{2,1,0:T(8,128)(2,1)} %bitcast.218, bf16[2,2,256,768]{3,2,1,0:T(8,128)(2,1)} %bitcast.161, bf16[2,2,256,768]{3,2,1,0:T(8,128)(2,1)} %collective-permute-done.15.rest_3_.rest_5_, ...), custom_call_target="tpu_custom_call" | custom-call | flops 1024 | bytes 1024 | tf_op jit(solution)/shard_map/pallas_call | solution.py:995
  182.5 5.0 shard_map.328
  192.4 38.0 %collective-permute-done.27 = bf16[96,1536]{1,0:T(8,128)(2,1)S(1)} collective-permute-done((bf16[96,1536]{1,0:T(8,128)(2,1)S(1)}, bf16[96,1536]{1,0:T(8,128)(2,1)S(1)}, u32[]{:S(2)}, u32[]{:S(2)}) %collective-permute-start.27) | collective-permute-done | bytes 294944 | tf_op jit(solution)/shard_map/ppermute | solution.py:25
  237.0 4.8 shard_map.330
  244.0 8.5 shard_map.331
  253.8 4.4 collective-permute-done.34
  264.8 40.1 %shard_map.333 = (bf16[512,1536]{1,0:T(8,128)(2,1)}, bf16[512,1536]{1,0:T(8,128)(2,1)}, bf16[2,4,384,768]{3,2,1,0:T(8,128)(2,1)}, bf16[2,4,384,768]{3,2,1,0:T(8,...) custom-call(s32[2]{0:T(128)} %pad_add_fusion.spot_ref, bf16[512,1536]{1,0:T(8,128)(2,1)} %bitcast.225, ...), custom_call_target="tpu_custom_call" | custom-call | flops 1024 | bytes 1024 | tf_op jit(solution)/shard_map/pallas_call | solution.py:418
  312.2 25.8 %collective-permute-done.43.rest_6_ = bf16[2,384,768]{2,1,0:T(8,128)(2,1)S(1)} collective-permute-done((bf16[2,384,768]{2,1,0:T(8,128)(2,1)}, bf16[2,384,768]{2,1,0:T(8,128)(2,1)S(1)}, u32[]{:S(2)}, u32[]{:S(2)}) %collective-permute-start.43) | collective-permute-done | bytes 1179680 | tf_op jit(solution)/shard_map/ppermute | solution.py:25
  338.0 6.1 shard_map.335
  344.1 5.7 shard_map.336
  350.7 11.0 %shard_map.337 = (bf16[2,96,384]{2,1,0:T(8,128)(2,1)}, bf16[2,96,384]{2,1,0:T(8,128)(2,1)}, bf16[2,96,384]{2,1,0:T(8,128)(2,1)}, bf16[2,96,384]{2,1,0:T(8,128)(2...) custom-call(s32[2]{0:T(128)} %pad_add_fusion.spot_ref, bf16[384,3072]{1,0:T(8,128)(2,1)} %up_ref.3, ...), custom_call_target="tpu_custom_call" | custom-call | flops 1024 | bytes 1024 | tf_op jit(solution)/shard_map/pallas_call | solution.py:418
  365.4 8.2 shard_map.338
  373.6 4.5 collective-permute-start.50
  382.6 6.7 shard_map.340
  390.9 7.9 collective-permute-done.49
  402.4 4.9 shard_map.342
  422.2 26.7 %shard_map.346 = (bf16[1,256,768]{2,1,0:T(8,128)(2,1)}, bf16[1,48,768]{2,1,0:T(8,128)(2,1)}, bf16[2,2,304,768]{3,2,1,0:T(8,128)(2,1)}, bf16[2,2,304,768]{3,2,1,0:T(8,128)(2,1)}) custom-call(bf16[2,256,768]{2,1,0:T(8,128)(2,1)} %bitcast.173, bf16[2,48,768]{2,1,0:T(8,128)(2,1)} %bitcast.219, bf16[2,256,768]{2,1,0:T(8,128)(2,1)} %bitcast.203, ...), custom_call_target="tpu_custom_call" | custom-call | flops 1024 | bytes 1024 | tf_op jit(solution)/shard_map/pallas_call | solution.py:1066
  453.5 4.2 shard_map.348
  459.0 26.7 %shard_map.349 = (bf16[1,256,768]{2,1,0:T(8,128)(2,1)}, bf16[1,48,768]{2,1,0:T(8,128)(2,1)}, bf16[2,2,304,768]{3,2,1,0:T(8,128)(2,1)}, bf16[2,2,304,768]{3,2,1,0:T(8,128)(2,1)}) custom-call(bf16[2,256,768]{2,1,0:T(8,128)(2,1)} %bitcast.174, bf16[2,48,768]{2,1,0:T(8,128)(2,1)} %bitcast.220, bf16[2,256,768]{2,1,0:T(8,128)(2,1)} %bitcast.204, ...), custom_call_target="tpu_custom_call" | custom-call | flops 1024 | bytes 1024 | tf_op jit(solution)/shard_map/pallas_call | solution.py:1066
  490.8 4.2 shard_map.351
  500.3 4.8 shard_map.352
  506.2 4.6 collective-permute-start.61
  512.5 24.7 %collective-permute-done.61.refs_1_ = bf16[768,768]{1,0:T(8,128)(2,1)S(1)} collective-permute-done((bf16[768,768]{1,0:T(8,128)(2,1)}, bf16[768,768]{1,0:T(8,128)(2,1)S(1)}, u32[]{:S(2)}, u32[]{:S(2)}) %collective-permute-start.61) | collective-permute-done | bytes 1179680 | tf_op jit(solution)/shard_map/ppermute | solution.py:228
  538.3 4.3 shard_map.353
  542.6 5.8 collective-permute-done.63
  553.7 14.4 %shard_map.355 = (bf16[512,1536]{1,0:T(8,128)(2,1)}, bf16[2,3,384,768]{3,2,1,0:T(8,128)(2,1)}, bf16[2,3,384,768]{3,2,1,0:T(8,128)(2,1)}) custom-call(s32[2]{0:T(128)} %pad_add_fusion.spot_ref, bf16[512,1536]{1,0:T(8,128)(2,1)} %bitcast.171, bf16[1,256,768]{2,1,0:T(8,128)(2,1)} %get-tuple-element.311.rest_0_, ...), custom_call_target="tpu_custom_call" | custom-call | flops 1024 | bytes 1024 | tf_op jit(solution)/shard_map/pallas_call | solution.py:418
  568.2 9.7 shard_map.356
  578.4 4.6 collective-permute-start.66
  589.6 4.6 shard_map.357
  595.1 4.6 shard_map.358
  599.8 9.8 %collective-permute-done.66.refs_1_ = bf16[768,768]{1,0:T(8,128)(2,1)} collective-permute-done((bf16[768,768]{1,0:T(8,128)(2,1)}, bf16[768,768]{1,0:T(8,128)(2,1)}, u32[]{:S(2)}, u32[]{:S(2)}) %collective-permute-start.66) | collective-permute-done | bytes 1179680 | tf_op jit(solution)/shard_map/ppermute | solution.py:228
  632.3 10.9 %collective-permute-done.70.refs_1_ = bf16[768,768]{1,0:T(8,128)(2,1)} collective-permute-done((bf16[768,768]{1,0:T(8,128)(2,1)}, bf16[768,768]{1,0:T(8,128)(2,1)}, u32[]{:S(2)}, u32[]{:S(2)}) %collective-permute-start.70) | collective-permute-done | bytes 1179680 | tf_op jit(solution)/shard_map/ppermute | solution.py:228
  644.2 4.2 shard_map.362
  650.2 5.7 shard_map.363
  673.1 17.7 %collective-permute-done.75.refs_1_ = bf16[768,768]{1,0:T(8,128)(2,1)} collective-permute-done((bf16[768,768]{1,0:T(8,128)(2,1)}, bf16[768,768]{1,0:T(8,128)(2,1)}, u32[]{:S(2)}, u32[]{:S(2)}) %collective-permute-start.75) | collective-permute-done | bytes 1179680 | tf_op jit(solution)/shard_map/ppermute | solution.py:228
  690.8 4.2 shard_map.366
  709.5 15.9 %collective-permute-done.78.refs_1_ = bf16[768,768]{1,0:T(8,128)(2,1)} collective-permute-done((bf16[768,768]{1,0:T(8,128)(2,1)}, bf16[768,768]{1,0:T(8,128)(2,1)}, u32[]{:S(2)}, u32[]{:S(2)}) %collective-permute-start.78) | collective-permute-done | bytes 1179680 | tf_op jit(solution)/shard_map/ppermute | solution.py:228
  725.4 5.2 collective-permute-start.88
  737.7 5.9 shard_map.370
  750.3 4.3 collective-permute-done.83
  765.5 26.3 %collective-permute-done.85 = f32[2,25,1536]{2,1,0:T(8,128)S(1)} collective-permute-done((f32[2,25,1536]{2,1,0:T(8,128)S(1)}, f32[2,25,1536]{2,1,0:T(8,128)S(1)}, u32[]{:S(2)}, u32[]{:S(2)}) %collective-permute-start.85) | collective-permute-done | bytes 307232 | tf_op jit(solution)/shard_map/ppermute | solution.py:25
  800.9 7.7 convolution_bitcast_fusion.1
  812.2 7.3 collective-permute-start.90
  820.2 7.7 fusion
  839.8 8.9 fusion.2
  858.8 8.9 fusion.5
  867.7 21.1 %collective-permute-done.94.refs_1_ = bf16[384,768]{1,0:T(8,128)(2,1)S(1)} collective-permute-done((bf16[384,768]{1,0:T(8,128)(2,1)}, bf16[384,768]{1,0:T(8,128)(2,1)S(1)}, u32[]{:S(2)}, u32[]{:S(2)}) %collective-permute-start.94) | collective-permute-done | bytes 589856 | tf_op jit(solution)/shard_map/ppermute | solution.py:228
  895.6 9.6 collective-permute-done.96.refs_1_
  909.8 5.9 collective-permute-start.98
  918.7 6.0 collective-permute-done.98.refs_1_
  931.6 4.5 pad_maximum_fusion
  951.9 9.6 collective-permute-done.104
  961.5 8.8 collective-permute-done.106
  (508 shorter events, 308.6 us)
Async XLA Ops:
  3.0 22.9 %collective-permute-start.1 = (bf16[3,192,768]{2,1,0:T(8,128)(2,1)}, bf16[3,192,768]{2,1,0:T(8,128)(2,1)}, u32[]{:S(2)}, u32[]{:S(2)}) collective-permute-start(bf16[3,192,768]{2,1,0:T(8,128)(2,1)} %dynamic-slice_bitcast_fusion.1), channel_id=1, source_target_pairs={{0,4},{2,6},{4,0},{6,2},{1,5},{3,7},{5,1},{7,3},{8,12},{10,14},{12... | collective-permute-start | bytes 2654216 | tf_op jit(solution)/shard_map/ppermute | solution.py:25
  6.0 51.7 %collective-permute-start.5 = (bf16[3,384,768]{2,1,0:T(8,128)(2,1)S(1)}, bf16[3,384,768]{2,1,0:T(8,128)(2,1)}, u32[]{:S(2)}, u32[]{:S(2)}) collective-permute-start(bf16[3,384,768]{2,1,0:T(8,128)(2,1)S(1)} %bitcast.177), channel_id=1, source_target_pairs={{0,2},{2,0},{4,6},{6,4},{1,3},{3,1},{5,7},{7,5},{8,10},{10,8},{12,... | collective-permute-start | bytes 5308424 | tf_op jit(solution)/shard_map/ppermute | solution.py:25
  25.9 21.2 %collective-permute-start.4 = (bf16[3,192,768]{2,1,0:T(8,128)(2,1)}, bf16[3,192,768]{2,1,0:T(8,128)(2,1)}, u32[]{:S(2)}, u32[]{:S(2)}) collective-permute-start(bf16[3,192,768]{2,1,0:T(8,128)(2,1)} %collective-permute-done.1.rest_1_.rest_5_), channel_id=1, source_target_pairs={{0,8},{8,0},{16,24},{24,16},{1,9},{9,1},{17,25},{25,17},{2,10},{10... | collective-permute-start | bytes 2654216 | tf_op jit(solution)/shard_map/ppermute | solution.py:25
  36.4 21.3 %collective-permute-start.3 = (bf16[3,192,768]{2,1,0:T(8,128)(2,1)}, bf16[3,192,768]{2,1,0:T(8,128)(2,1)}, u32[]{:S(2)}, u32[]{:S(2)}) collective-permute-start(bf16[3,192,768]{2,1,0:T(8,128)(2,1)} %dynamic-slice_bitcast_fusion), channel_id=1, source_target_pairs={{0,4},{2,6},{4,0},{6,2},{1,5},{3,7},{5,1},{7,3},{8,12},{10,14},{12... | collective-permute-start | bytes 2654216 | tf_op jit(solution)/shard_map/ppermute | solution.py:25
  38.0 19.8 %collective-permute-start.6 = (bf16[3,192,768]{2,1,0:T(8,128)(2,1)}, bf16[3,192,768]{2,1,0:T(8,128)(2,1)}, u32[]{:S(2)}, u32[]{:S(2)}) collective-permute-start(bf16[3,192,768]{2,1,0:T(8,128)(2,1)} %collective-permute-done.1.rest_1_.rest_5_), channel_id=1, source_target_pairs={{0,2},{2,0},{4,6},{6,4},{1,3},{3,1},{5,7},{7,5},{8,10},{10,8},{12,... | collective-permute-start | bytes 2654216 | tf_op jit(solution)/shard_map/ppermute | solution.py:25
  66.0 32.1 %collective-permute-start.9 = (bf16[3,384,768]{2,1,0:T(8,128)(2,1)}, bf16[3,384,768]{2,1,0:T(8,128)(2,1)}, u32[]{:S(2)}, u32[]{:S(2)}) collective-permute-start(bf16[3,384,768]{2,1,0:T(8,128)(2,1)} %bitcast.178), channel_id=1, source_target_pairs={{0,2},{2,0},{4,6},{6,4},{1,3},{3,1},{5,7},{7,5},{8,10},{10,8},{12,... | collective-permute-start | bytes 5308424 | tf_op jit(solution)/shard_map/ppermute | solution.py:25
  73.3 42.4 %collective-permute-start.13 = (bf16[384,3072]{1,0:T(8,128)(2,1)}, bf16[384,3072]{1,0:T(8,128)(2,1)}, u32[]{:S(2)}, u32[]{:S(2)}) collective-permute-start(bf16[384,3072]{1,0:T(8,128)(2,1)} %rest_6_.1), channel_id=1, source_target_pairs={{0,2},{2,0},{4,6},{6,4},{1,3},{3,1},{5,7},{7,5},{8,10},{10,8},{12,... | collective-permute-start | bytes 7077896 | tf_op jit(solution)/shard_map/ppermute | solution.py:25
  74.7 22.0 %collective-permute-start.8 = (bf16[3,192,768]{2,1,0:T(8,128)(2,1)}, bf16[3,192,768]{2,1,0:T(8,128)(2,1)}, u32[]{:S(2)}, u32[]{:S(2)}) collective-permute-start(bf16[3,192,768]{2,1,0:T(8,128)(2,1)} %collective-permute-done.3.rest_1_.rest_5_), channel_id=1, source_target_pairs={{0,8},{8,0},{16,24},{24,16},{1,9},{9,1},{17,25},{25,17},{2,10},{10... | collective-permute-start | bytes 2654216 | tf_op jit(solution)/shard_map/ppermute | solution.py:25
  76.5 37.4 %collective-permute-start.16 = (bf16[2,2,256,768]{3,2,1,0:T(8,128)(2,1)S(1)}, bf16[2,2,256,768]{3,2,1,0:T(8,128)(2,1)}, u32[]{:S(2)}, u32[]{:S(2)}) collective-permute-start(bf16[2,2,256,768]{3,2,1,0:T(8,128)(2,1)S(1)} %bitcast.159), channel_id=1, source_target_pairs={{0,4},{2,6},{4,0},{6,2},{1,5},{3,7},{5,1},{7,3},{8,12},{10,14},{12... | collective-permute-start | bytes 4718600 | tf_op jit(solution)/shard_map/ppermute | solution.py:25
  78.3 23.6 %collective-permute-start.10 = (bf16[3,192,768]{2,1,0:T(8,128)(2,1)}, bf16[3,192,768]{2,1,0:T(8,128)(2,1)}, u32[]{:S(2)}, u32[]{:S(2)}) collective-permute-start(bf16[3,192,768]{2,1,0:T(8,128)(2,1)} %collective-permute-done.3.rest_1_.rest_5_), channel_id=1, source_target_pairs={{0,2},{2,0},{4,6},{6,4},{1,3},{3,1},{5,7},{7,5},{8,10},{10,8},{12,... | collective-permute-start | bytes 2654216 | tf_op jit(solution)/shard_map/ppermute | solution.py:25
  98.1 36.5 %collective-permute-start.15 = (bf16[2,2,256,768]{3,2,1,0:T(8,128)(2,1)S(1)}, bf16[2,2,256,768]{3,2,1,0:T(8,128)(2,1)}, u32[]{:S(2)}, u32[]{:S(2)}) collective-permute-start(bf16[2,2,256,768]{3,2,1,0:T(8,128)(2,1)S(1)} %bitcast.160), channel_id=1, source_target_pairs={{0,2},{2,0},{4,6},{6,4},{1,3},{3,1},{5,7},{7,5},{8,10},{10,8},{12,... | collective-permute-start | bytes 4718600 | tf_op jit(solution)/shard_map/ppermute | solution.py:25
  115.7 30.4 %collective-permute-start.14 = (bf16[2,384,768]{2,1,0:T(8,128)(2,1)S(1)}, bf16[2,384,768]{2,1,0:T(8,128)(2,1)S(1)}, u32[]{:S(2)}, u32[]{:S(2)}) collective-permute-start(bf16[2,384,768]{2,1,0:T(8,128)(2,1)S(1)} %pad_maximum_fusion.4.rest_0_), channel_id=1, source_target_pairs={{0,2},{2,0},{4,6},{6,4},{1,3},{3,1},{5,7},{7,5},{8,10},{10,8},{12,... | collective-permute-start | bytes 3538952 | tf_op jit(solution)/shard_map/ppermute | solution.py:25
  115.7 35.6 %collective-permute-start.17 = (bf16[2,2,256,768]{3,2,1,0:T(8,128)(2,1)}, bf16[2,2,256,768]{3,2,1,0:T(8,128)(2,1)}, u32[]{:S(2)}, u32[]{:S(2)}) collective-permute-start(bf16[2,2,256,768]{3,2,1,0:T(8,128)(2,1)} %collective-permute-done.16.rest_4_.rest_6_), channel_id=1, source_target_pairs={{0,2},{2,0},{4,6},{6,4},{1,3},{3,1},{5,7},{7,5},{8,10},{10,8},{12,... | collective-permute-start | bytes 4718600 | tf_op jit(solution)/shard_map/ppermute | solution.py:25
  121.7 55.4 %collective-permute-start.21 = (bf16[192,3072]{1,0:T(8,128)(2,1)}, bf16[192,3072]{1,0:T(8,128)(2,1)}, u32[]{:S(2)}, u32[]{:S(2)}) collective-permute-start(bf16[192,3072]{1,0:T(8,128)(2,1)} %constant_dynamic-slice_fusion.5), channel_id=1, source_target_pairs={{0,4},{2,6},{4,0},{6,2},{1,5},{3,7},{5,1},{7,3},{8,12},{10,14},{12... | collective-permute-start | bytes 3538952 | tf_op jit(solution)/shard_map/ppermute | solution.py:25
  136.2 54.6 %collective-permute-start.26 = (bf16[192,3072]{1,0:T(8,128)(2,1)}, bf16[192,3072]{1,0:T(8,128)(2,1)}, u32[]{:S(2)}, u32[]{:S(2)}) collective-permute-start(bf16[192,3072]{1,0:T(8,128)(2,1)} %constant_dynamic-slice_fusion.4), channel_id=1, source_target_pairs={{0,4},{2,6},{4,0},{6,2},{1,5},{3,7},{5,1},{7,3},{8,12},{10,14},{12... | collective-permute-start | bytes 3538952 | tf_op jit(solution)/shard_map/ppermute | solution.py:25
  146.1 31.0 %collective-permute-start.24 = (bf16[1,384,768]{2,1,0:T(8,128)(2,1)S(1)}, bf16[1,384,768]{2,1,0:T(8,128)(2,1)S(1)}, u32[]{:S(2)}, u32[]{:S(2)}) collective-permute-start(bf16[1,384,768]{2,1,0:T(8,128)(2,1)S(1)} %collective-permute-done.22.rest_1_), channel_id=1, source_target_pairs={{0,2},{2,0},{4,6},{6,4},{1,3},{3,1},{5,7},{7,5},{8,10},{10,8},{12,... | collective-permute-start | bytes 1769480 | tf_op jit(solution)/shard_map/ppermute | solution.py:25
  147.1 30.0 %collective-permute-start.25 = (bf16[1,384,768]{2,1,0:T(8,128)(2,1)}, bf16[1,384,768]{2,1,0:T(8,128)(2,1)S(1)}, u32[]{:S(2)}, u32[]{:S(2)}) collective-permute-start(bf16[1,384,768]{2,1,0:T(8,128)(2,1)} %collective-permute-done.23.rest_2_), channel_id=1, source_target_pairs={{0,2},{2,0},{4,6},{6,4},{1,3},{3,1},{5,7},{7,5},{8,10},{10,8},{12,... | collective-permute-start | bytes 1769480 | tf_op jit(solution)/shard_map/ppermute | solution.py:25
  187.6 48.3 %collective-permute-start.28 = (bf16[512,1536]{1,0:T(8,128)(2,1)}, bf16[512,1536]{1,0:T(8,128)(2,1)S(1)}, u32[]{:S(2)}, u32[]{:S(2)}) collective-permute-start(bf16[512,1536]{1,0:T(8,128)(2,1)} %shard_map.328), channel_id=1, source_target_pairs={{0,1},{1,0},{2,3},{3,2},{4,5},{5,4},{6,7},{7,6},{8,9},{9,8},{10,11... | collective-permute-start | bytes 4718600 | tf_op jit(solution)/shard_map/ppermute | solution.py:25
  189.2 52.7 %collective-permute-start.29 = (bf16[192,3072]{1,0:T(8,128)(2,1)}, bf16[192,3072]{1,0:T(8,128)(2,1)}, u32[]{:S(2)}, u32[]{:S(2)}) collective-permute-start(bf16[192,3072]{1,0:T(8,128)(2,1)} %collective-permute-done.21.rest_1_), channel_id=1, source_target_pairs={{0,8},{8,0},{16,24},{24,16},{1,9},{9,1},{17,25},{25,17},{2,10},{10... | collective-permute-start | bytes 3538952 | tf_op jit(solution)/shard_map/ppermute | solution.py:25
  190.8 51.6 %collective-permute-start.30 = (bf16[192,3072]{1,0:T(8,128)(2,1)}, bf16[192,3072]{1,0:T(8,128)(2,1)}, u32[]{:S(2)}, u32[]{:S(2)}) collective-permute-start(bf16[192,3072]{1,0:T(8,128)(2,1)} %collective-permute-done.26.rest_7_), channel_id=1, source_target_pairs={{0,8},{8,0},{16,24},{24,16},{1,9},{9,1},{17,25},{25,17},{2,10},{10... | collective-permute-start | bytes 3538952 | tf_op jit(solution)/shard_map/ppermute | solution.py:25
  191.2 39.2 %collective-permute-start.27 = (bf16[96,1536]{1,0:T(8,128)(2,1)S(1)}, bf16[96,1536]{1,0:T(8,128)(2,1)S(1)}, u32[]{:S(2)}, u32[]{:S(2)}) collective-permute-start(bf16[96,1536]{1,0:T(8,128)(2,1)S(1)} %copy-done.25), channel_id=1, source_target_pairs={{0,1},{1,0},{2,3},{3,2},{4,5},{5,4},{6,7},{7,6},{8,9},{9,8},{10,11... | collective-permute-start | bytes 884744 | tf_op jit(solution)/shard_map/ppermute | solution.py:25
  263.1 41.7 %collective-permute-start.39 = (bf16[768,768]{1,0:T(8,128)(2,1)}, bf16[768,768]{1,0:T(8,128)(2,1)S(1)}, u32[]{:S(2)}, u32[]{:S(2)}) collective-permute-start(bf16[768,768]{1,0:T(8,128)(2,1)} %get-tuple-element.272), channel_id=1, source_target_pairs={{0,4},{2,6},{4,0},{6,2},{1,5},{3,7},{5,1},{7,3},{8,12},{10,14},{12... | collective-permute-start | bytes 3538952 | tf_op jit(solution)/shard_map/ppermute | solution.py:25
  309.2 28.7 %collective-permute-start.40 = (bf16[2,4,384,768]{3,2,1,0:T(8,128)(2,1)}, bf16[2,4,384,768]{3,2,1,0:T(8,128)(2,1)}, u32[]{:S(2)}, u32[]{:S(2)}) collective-permute-start(bf16[2,4,384,768]{3,2,1,0:T(8,128)(2,1)} %get-tuple-element.275), channel_id=1, source_target_pairs={{0,2},{2,0},{4,6},{6,4},{1,3},{3,1},{5,7},{7,5},{8,10},{10,8},{12,... | collective-permute-start | bytes 14155784 | tf_op jit(solution)/shard_map/ppermute | solution.py:25
  309.4 34.7 %collective-permute-start.41 = (bf16[2,4,384,768]{3,2,1,0:T(8,128)(2,1)}, bf16[2,4,384,768]{3,2,1,0:T(8,128)(2,1)}, u32[]{:S(2)}, u32[]{:S(2)}) collective-permute-start(bf16[2,4,384,768]{3,2,1,0:T(8,128)(2,1)} %get-tuple-element.279), channel_id=1, source_target_pairs={{0,2},{2,0},{4,6},{6,4},{1,3},{3,1},{5,7},{7,5},{8,10},{10,8},{12,... | collective-permute-start | bytes 14155784 | tf_op jit(solution)/shard_map/ppermute | solution.py:25
  309.8 28.2 %collective-permute-start.43 = (bf16[2,384,768]{2,1,0:T(8,128)(2,1)}, bf16[2,384,768]{2,1,0:T(8,128)(2,1)S(1)}, u32[]{:S(2)}, u32[]{:S(2)}) collective-permute-start(bf16[2,384,768]{2,1,0:T(8,128)(2,1)} %shard_map.334.rest_4_), channel_id=1, source_target_pairs={{0,4},{2,6},{4,0},{6,2},{1,5},{3,7},{5,1},{7,3},{8,12},{10,14},{12... | collective-permute-start | bytes 3538952 | tf_op jit(solution)/shard_map/ppermute | solution.py:25
  310.7 54.7 %collective-permute-start.45 = (bf16[512,1536]{1,0:T(8,128)(2,1)}, bf16[512,1536]{1,0:T(8,128)(2,1)}, u32[]{:S(2)}, u32[]{:S(2)}) collective-permute-start(bf16[512,1536]{1,0:T(8,128)(2,1)} %get-tuple-element.285), channel_id=1, source_target_pairs={{0,1},{1,0},{2,3},{3,2},{4,5},{5,4},{6,7},{7,6},{8,9},{9,8},{10,11... | collective-permute-start | bytes 4718600 | tf_op jit(solution)/shard_map/ppermute | solution.py:25
  312.2 37.5 %collective-permute-start.42 = (bf16[2,384,768]{2,1,0:T(8,128)(2,1)}, bf16[2,384,768]{2,1,0:T(8,128)(2,1)S(1)}, u32[]{:S(2)}, u32[]{:S(2)}) collective-permute-start(bf16[2,384,768]{2,1,0:T(8,128)(2,1)} %shard_map.334.rest_4_), channel_id=1, source_target_pairs={{0,2},{2,0},{4,6},{6,4},{1,3},{3,1},{5,7},{7,5},{8,10},{10,8},{12,... | collective-permute-start | bytes 3538952 | tf_op jit(solution)/shard_map/ppermute | solution.py:25
  373.6 34.7 %collective-permute-start.50 = (bf16[768,768]{1,0:T(8,128)(2,1)S(1)}, bf16[768,768]{1,0:T(8,128)(2,1)}, u32[]{:S(2)}, u32[]{:S(2)}) collective-permute-start(bf16[768,768]{1,0:T(8,128)(2,1)S(1)} %bitcast.194), channel_id=1, source_target_pairs={{0,8},{24,16},{1,9},{25,17},{2,10},{26,18},{3,11},{27,19},{4,12},{... | collective-permute-start | bytes 3538952 | tf_op jit(solution)/shard_map/ppermute | solution.py:228
  378.2 70.7 %collective-permute-start.53 = (bf16[1536,768]{1,0:T(8,128)(2,1)}, bf16[1536,768]{1,0:T(8,128)(2,1)}, u32[]{:S(2)}, u32[]{:S(2)}) collective-permute-start(bf16[1536,768]{1,0:T(8,128)(2,1)} %get-tuple-element.313), channel_id=1, source_target_pairs={{0,4},{2,6},{4,0},{6,2},{1,5},{3,7},{5,1},{7,3},{8,12},{10,14},{12... | collective-permute-start | bytes 7077896 | tf_op jit(solution)/shard_map/ppermute | solution.py:25
  389.4 22.9 %collective-permute-start.51 = (bf16[2,1,384,768]{3,2,0,1:T(8,128)(2,1)}, bf16[2,1,384,768]{3,2,0,1:T(8,128)(2,1)}, u32[]{:S(2)}, u32[]{:S(2)}) collective-permute-start(bf16[2,1,384,768]{3,2,0,1:T(8,128)(2,1)} %bitcast.252), channel_id=1, source_target_pairs={{0,2},{2,0},{4,6},{6,4},{1,3},{3,1},{5,7},{7,5},{8,10},{10,8},{12,... | collective-permute-start | bytes 3538952 | tf_op jit(solution)/shard_map/ppermute | solution.py:25
  407.4 78.3 %collective-permute-start.56 = (bf16[1536,768]{1,0:T(8,128)(2,1)}, bf16[1536,768]{1,0:T(8,128)(2,1)}, u32[]{:S(2)}, u32[]{:S(2)}) collective-permute-start(bf16[1536,768]{1,0:T(8,128)(2,1)} %get-tuple-element.321), channel_id=1, source_target_pairs={{0,4},{2,6},{4,0},{6,2},{1,5},{3,7},{5,1},{7,3},{8,12},{10,14},{12... | collective-permute-start | bytes 7077896 | tf_op jit(solution)/shard_map/ppermute | solution.py:25
  408.3 44.2 %collective-permute-start.54 = (bf16[768,768]{1,0:T(8,128)(2,1)S(1)}, bf16[768,768]{1,0:T(8,128)(2,1)S(1)}, u32[]{:S(2)}, u32[]{:S(2)}) collective-permute-start(bf16[768,768]{1,0:T(8,128)(2,1)S(1)} %bitcast.192), channel_id=1, source_target_pairs={{0,8},{24,16},{1,9},{25,17},{2,10},{26,18},{3,11},{27,19},{4,12},{... | collective-permute-start | bytes 3538952 | tf_op jit(solution)/shard_map/ppermute | solution.py:228
  412.3 40.2 %collective-permute-start.55 = (bf16[768,768]{1,0:T(8,128)(2,1)}, bf16[768,768]{1,0:T(8,128)(2,1)}, u32[]{:S(2)}, u32[]{:S(2)}) collective-permute-start(bf16[768,768]{1,0:T(8,128)(2,1)} %shard_map.343.refs_2_), channel_id=1, source_target_pairs={{8,16},{16,8},{9,17},{17,9},{10,18},{18,10},{11,19},{19,11},{12,20... | collective-permute-start | bytes 3538952 | tf_op jit(solution)/shard_map/ppermute | solution.py:294
  457.7 31.7 %collective-permute-start.57 = (bf16[768,768]{1,0:T(8,128)(2,1)}, bf16[768,768]{1,0:T(8,128)(2,1)S(1)}, u32[]{:S(2)}, u32[]{:S(2)}) collective-permute-start(bf16[768,768]{1,0:T(8,128)(2,1)} %get-tuple-element.326), channel_id=1, source_target_pairs={{0,8},{8,0},{16,24},{24,16},{1,9},{9,1},{17,25},{25,17},{2,10},{10... | collective-permute-start | bytes 3538952 | tf_op jit(solution)/shard_map/ppermute | solution.py:228
  457.9 31.5 %collective-permute-start.58 = (bf16[768,768]{1,0:T(8,128)(2,1)}, bf16[768,768]{1,0:T(8,128)(2,1)S(1)}, u32[]{:S(2)}, u32[]{:S(2)}) collective-permute-start(bf16[768,768]{1,0:T(8,128)(2,1)} %get-tuple-element.317.refs_2_), channel_id=1, source_target_pairs={{8,16},{16,8},{9,17},{17,9},{10,18},{18,10},{11,19},{19,11},{12,20... | collective-permute-start | bytes 3538952 | tf_op jit(solution)/shard_map/ppermute | solution.py:294
  505.1 43.2 %collective-permute-start.63 = (bf16[1216,768]{1,0:T(8,128)(2,1)}, bf16[1216,768]{1,0:T(8,128)(2,1)S(1)}, u32[]{:S(2)}, u32[]{:S(2)}) collective-permute-start(bf16[1216,768]{1,0:T(8,128)(2,1)} %bitcast.251), channel_id=1, source_target_pairs={{0,4},{2,6},{4,0},{6,2},{1,5},{3,7},{5,1},{7,3},{8,12},{10,14},{12... | collective-permute-start | bytes 5603336 | tf_op jit(solution)/shard_map/ppermute | solution.py:25
  506.2 31.0 %collective-permute-start.61 = (bf16[768,768]{1,0:T(8,128)(2,1)}, bf16[768,768]{1,0:T(8,128)(2,1)S(1)}, u32[]{:S(2)}, u32[]{:S(2)}) collective-permute-start(bf16[768,768]{1,0:T(8,128)(2,1)} %get-tuple-element.336), channel_id=1, source_target_pairs={{0,8},{8,0},{16,24},{24,16},{1,9},{9,1},{17,25},{25,17},{2,10},{10... | collective-permute-start | bytes 3538952 | tf_op jit(solution)/shard_map/ppermute | solution.py:228
  510.9 26.4 %collective-permute-start.62 = (bf16[768,768]{1,0:T(8,128)(2,1)}, bf16[768,768]{1,0:T(8,128)(2,1)}, u32[]{:S(2)}, u32[]{:S(2)}) collective-permute-start(bf16[768,768]{1,0:T(8,128)(2,1)} %get-tuple-element.327.refs_2_), channel_id=1, source_target_pairs={{8,16},{16,8},{9,17},{17,9},{10,18},{18,10},{11,19},{19,11},{12,20... | collective-permute-start | bytes 3538952 | tf_op jit(solution)/shard_map/ppermute | solution.py:294
  568.1 20.4 %collective-permute-start.64 = (bf16[2,3,384,768]{3,2,1,0:T(8,128)(2,1)}, bf16[2,3,384,768]{3,2,1,0:T(8,128)(2,1)}, u32[]{:S(2)}, u32[]{:S(2)}) collective-permute-start(bf16[2,3,384,768]{3,2,1,0:T(8,128)(2,1)} %get-tuple-element.351), channel_id=1, source_target_pairs={{0,2},{2,0},{4,6},{6,4},{1,3},{3,1},{5,7},{7,5},{8,10},{10,8},{12,... | collective-permute-start | bytes 10616840 | tf_op jit(solution)/shard_map/ppermute | solution.py:25
  578.4 31.1 %collective-permute-start.66 = (bf16[768,768]{1,0:T(8,128)(2,1)}, bf16[768,768]{1,0:T(8,128)(2,1)}, u32[]{:S(2)}, u32[]{:S(2)}) collective-permute-start(bf16[768,768]{1,0:T(8,128)(2,1)} %get-tuple-element.358), channel_id=1, source_target_pairs={{0,8},{8,0},{16,24},{24,16},{1,9},{9,1},{17,25},{25,17},{2,10},{10... | collective-permute-start | bytes 3538952 | tf_op jit(solution)/shard_map/ppermute | solution.py:228
  583.1 26.5 %collective-permute-start.67 = (bf16[768,768]{1,0:T(8,128)(2,1)}, bf16[768,768]{1,0:T(8,128)(2,1)}, u32[]{:S(2)}, u32[]{:S(2)}) collective-permute-start(bf16[768,768]{1,0:T(8,128)(2,1)} %get-tuple-element.337.refs_2_), channel_id=1, source_target_pairs={{8,16},{16,8},{9,17},{17,9},{10,18},{18,10},{11,19},{19,11},{12,20... | collective-permute-start | bytes 3538952 | tf_op jit(solution)/shard_map/ppermute | solution.py:294
  586.8 63.4 %collective-permute-start.72 = (bf16[512,1536]{1,0:T(8,128)(2,1)}, bf16[512,1536]{1,0:T(8,128)(2,1)}, u32[]{:S(2)}, u32[]{:S(2)}) collective-permute-start(bf16[512,1536]{1,0:T(8,128)(2,1)} %get-tuple-element.342), channel_id=1, source_target_pairs={{0,1},{1,0},{2,3},{3,2},{4,5},{5,4},{6,7},{7,6},{8,9},{9,8},{10,11... | collective-permute-start | bytes 4718600 | tf_op jit(solution)/shard_map/ppermute | solution.py:25
  588.4 33.8 %collective-permute-start.69 = (bf16[384,768]{1,0:T(8,128)(2,1)}, bf16[384,768]{1,0:T(8,128)(2,1)S(1)}, u32[]{:S(2)}, u32[]{:S(2)}) collective-permute-start(bf16[384,768]{1,0:T(8,128)(2,1)} %get-tuple-element.365), channel_id=1, source_target_pairs={{0,4},{2,6},{4,0},{6,2},{1,5},{3,7},{5,1},{7,3},{8,12},{10,14},{12... | collective-permute-start | bytes 1769480 | tf_op jit(solution)/shard_map/ppermute | solution.py:25
  594.2 30.8 %collective-permute-start.68 = (bf16[384,768]{1,0:T(8,128)(2,1)}, bf16[384,768]{1,0:T(8,128)(2,1)S(1)}, u32[]{:S(2)}, u32[]{:S(2)}) collective-permute-start(bf16[384,768]{1,0:T(8,128)(2,1)} %get-tuple-element.362), channel_id=1, source_target_pairs={{0,4},{2,6},{4,0},{6,2},{1,5},{3,7},{5,1},{7,3},{8,12},{10,14},{12... | collective-permute-start | bytes 1769480 | tf_op jit(solution)/shard_map/ppermute | solution.py:25
  613.8 29.3 %collective-permute-start.70 = (bf16[768,768]{1,0:T(8,128)(2,1)}, bf16[768,768]{1,0:T(8,128)(2,1)}, u32[]{:S(2)}, u32[]{:S(2)}) collective-permute-start(bf16[768,768]{1,0:T(8,128)(2,1)} %get-tuple-element.367), channel_id=1, source_target_pairs={{0,8},{8,0},{16,24},{24,16},{1,9},{9,1},{17,25},{25,17},{2,10},{10... | collective-permute-start | bytes 3538952 | tf_op jit(solution)/shard_map/ppermute | solution.py:228
  617.4 26.8 %collective-permute-start.71 = (bf16[768,768]{1,0:T(8,128)(2,1)}, bf16[768,768]{1,0:T(8,128)(2,1)}, u32[]{:S(2)}, u32[]{:S(2)}) collective-permute-start(bf16[768,768]{1,0:T(8,128)(2,1)} %get-tuple-element.359.refs_2_), channel_id=1, source_target_pairs={{8,16},{16,8},{9,17},{17,9},{10,18},{18,10},{11,19},{19,11},{12,20... | collective-permute-start | bytes 3538952 | tf_op jit(solution)/shard_map/ppermute | solution.py:294
  622.3 45.0 %collective-permute-start.74 = (bf16[1152,768]{1,0:T(8,128)(2,1)}, bf16[1152,768]{1,0:T(8,128)(2,1)}, u32[]{:S(2)}, u32[]{:S(2)}) collective-permute-start(bf16[1152,768]{1,0:T(8,128)(2,1)} %get-tuple-element.375), channel_id=1, source_target_pairs={{0,4},{2,6},{4,0},{6,2},{1,5},{3,7},{5,1},{7,3},{8,12},{10,14},{12... | collective-permute-start | bytes 5308424 | tf_op jit(solution)/shard_map/ppermute | solution.py:25
  625.1 32.3 %collective-permute-start.73 = (bf16[96,1536]{1,0:T(8,128)(2,1)S(1)}, bf16[96,1536]{1,0:T(8,128)(2,1)S(1)}, u32[]{:S(2)}, u32[]{:S(2)}) collective-permute-start(bf16[96,1536]{1,0:T(8,128)(2,1)S(1)} %copy-done.80), channel_id=1, source_target_pairs={{0,1},{1,0},{2,3},{3,2},{4,5},{5,4},{6,7},{7,6},{8,9},{9,8},{10,11... | collective-permute-start | bytes 884744 | tf_op jit(solution)/shard_map/ppermute | solution.py:25
  643.1 61.4 %collective-permute-start.77 = (bf16[1152,768]{1,0:T(8,128)(2,1)}, bf16[1152,768]{1,0:T(8,128)(2,1)}, u32[]{:S(2)}, u32[]{:S(2)}) collective-permute-start(bf16[1152,768]{1,0:T(8,128)(2,1)} %get-tuple-element.382), channel_id=1, source_target_pairs={{0,4},{2,6},{4,0},{6,2},{1,5},{3,7},{5,1},{7,3},{8,12},{10,14},{12... | collective-permute-start | bytes 5308424 | tf_op jit(solution)/shard_map/ppermute | solution.py:25
  648.5 42.3 %collective-permute-start.76 = (bf16[768,768]{1,0:T(8,128)(2,1)}, bf16[768,768]{1,0:T(8,128)(2,1)}, u32[]{:S(2)}, u32[]{:S(2)}) collective-permute-start(bf16[768,768]{1,0:T(8,128)(2,1)} %get-tuple-element.368.refs_2_), channel_id=1, source_target_pairs={{8,16},{16,8},{9,17},{17,9},{10,18},{18,10},{11,19},{19,11},{12,20... | collective-permute-start | bytes 3538952 | tf_op jit(solution)/shard_map/ppermute | solution.py:294
  655.9 81.8 %collective-permute-start.81 = (bf16[512,1536]{1,0:T(8,128)(2,1)}, bf16[512,1536]{1,0:T(8,128)(2,1)}, u32[]{:S(2)}, u32[]{:S(2)}) collective-permute-start(bf16[512,1536]{1,0:T(8,128)(2,1)} %get-tuple-element.394), channel_id=1, source_target_pairs={{0,1},{1,0},{2,3},{3,2},{4,5},{5,4},{6,7},{7,6},{8,9},{9,8},{10,11... | collective-permute-start | bytes 4718600 | tf_op jit(solution)/shard_map/ppermute | solution.py:25
  660.7 30.1 %collective-permute-start.75 = (bf16[768,768]{1,0:T(8,128)(2,1)}, bf16[768,768]{1,0:T(8,128)(2,1)}, u32[]{:S(2)}, u32[]{:S(2)}) collective-permute-start(bf16[768,768]{1,0:T(8,128)(2,1)} %get-tuple-element.378), channel_id=1, source_target_pairs={{0,8},{8,0},{16,24},{24,16},{1,9},{9,1},{17,25},{25,17},{2,10},{10... | collective-permute-start | bytes 3538952 | tf_op jit(solution)/shard_map/ppermute | solution.py:228
  667.3 130.1 %collective-permute-start.87 = (bf16[384,768]{1,0:T(8,128)(2,1)}, bf16[384,768]{1,0:T(8,128)(2,1)}, u32[]{:S(2)}, u32[]{:S(2)}) collective-permute-start(bf16[384,768]{1,0:T(8,128)(2,1)} %shard_map.360.refs_0_), channel_id=1, source_target_pairs={{0,8},{24,16},{1,9},{25,17},{2,10},{26,18},{3,11},{27,19},{4,12},{... | collective-permute-start | bytes 1769480 | tf_op jit(solution)/shard_map/ppermute | solution.py:228
  695.0 30.4 %collective-permute-start.78 = (bf16[768,768]{1,0:T(8,128)(2,1)}, bf16[768,768]{1,0:T(8,128)(2,1)}, u32[]{:S(2)}, u32[]{:S(2)}) collective-permute-start(bf16[768,768]{1,0:T(8,128)(2,1)} %get-tuple-element.385), channel_id=1, source_target_pairs={{0,8},{8,0},{16,24},{24,16},{1,9},{9,1},{17,25},{25,17},{2,10},{10... | collective-permute-start | bytes 3538952 | tf_op jit(solution)/shard_map/ppermute | solution.py:228
  697.5 33.2 %collective-permute-start.79 = (bf16[768,768]{1,0:T(8,128)(2,1)}, bf16[768,768]{1,0:T(8,128)(2,1)}, u32[]{:S(2)}, u32[]{:S(2)}) collective-permute-start(bf16[768,768]{1,0:T(8,128)(2,1)} %get-tuple-element.379.refs_2_), channel_id=1, source_target_pairs={{8,16},{16,8},{9,17},{17,9},{10,18},{18,10},{11,19},{19,11},{12,20... | collective-permute-start | bytes 3538952 | tf_op jit(solution)/shard_map/ppermute | solution.py:294
  704.5 29.7 %collective-permute-start.80 = (bf16[96,1536]{1,0:T(8,128)(2,1)S(1)}, bf16[96,1536]{1,0:T(8,128)(2,1)S(1)}, u32[]{:S(2)}, u32[]{:S(2)}) collective-permute-start(bf16[96,1536]{1,0:T(8,128)(2,1)S(1)} %copy-done.76), channel_id=1, source_target_pairs={{0,1},{1,0},{2,3},{3,2},{4,5},{5,4},{6,7},{7,6},{8,9},{9,8},{10,11... | collective-permute-start | bytes 884744 | tf_op jit(solution)/shard_map/ppermute | solution.py:25
  725.4 83.1 %collective-permute-start.88 = (bf16[384,768]{1,0:T(8,128)(2,1)}, bf16[384,768]{1,0:T(8,128)(2,1)}, u32[]{:S(2)}, u32[]{:S(2)}) collective-permute-start(bf16[384,768]{1,0:T(8,128)(2,1)} %shard_map.361.refs_0_), channel_id=1, source_target_pairs={{0,8},{24,16},{1,9},{25,17},{2,10},{26,18},{3,11},{27,19},{4,12},{... | collective-permute-start | bytes 1769480 | tf_op jit(solution)/shard_map/ppermute | solution.py:228
  746.3 47.5 %collective-permute-start.86 = (bf16[768,768]{1,0:T(8,128)(2,1)}, bf16[768,768]{1,0:T(8,128)(2,1)S(1)}, u32[]{:S(2)}, u32[]{:S(2)}) collective-permute-start(bf16[768,768]{1,0:T(8,128)(2,1)} %get-tuple-element.402.refs_0_), channel_id=1, source_target_pairs={{8,16},{16,8},{9,17},{17,9},{10,18},{18,10},{11,19},{19,11},{12,20... | collective-permute-start | bytes 3538952 | tf_op jit(solution)/shard_map/ppermute | solution.py:294
  756.0 138.0 %collective-permute-start.99 = (bf16[768,768]{1,0:T(8,128)(2,1)}, bf16[768,768]{1,0:T(8,128)(2,1)}, u32[]{:S(2)}, u32[]{:S(2)}) collective-permute-start(bf16[768,768]{1,0:T(8,128)(2,1)} %get-tuple-element.424), channel_id=1, source_target_pairs={{8,0},{16,24},{9,1},{17,25},{10,2},{18,26},{11,3},{19,27},{12,4},{... | collective-permute-start | bytes 3538952 | tf_op jit(solution)/shard_map/ppermute | solution.py:228
  762.1 29.6 %collective-permute-start.85 = (f32[2,25,1536]{2,1,0:T(8,128)S(1)}, f32[2,25,1536]{2,1,0:T(8,128)S(1)}, u32[]{:S(2)}, u32[]{:S(2)}) collective-permute-start(f32[2,25,1536]{2,1,0:T(8,128)S(1)} %pad_maximum_fusion.7), channel_id=1, source_target_pairs={{0,16},{8,24},{16,0},{24,8},{1,17},{9,25},{17,1},{25,9},{2,18},{10... | collective-permute-start | bytes 921608 | tf_op jit(solution)/shard_map/ppermute | solution.py:25
  848.8 66.9 %collective-permute-start.100 = (bf16[768,768]{1,0:T(8,128)(2,1)}, bf16[768,768]{1,0:T(8,128)(2,1)}, u32[]{:S(2)}, u32[]{:S(2)}) collective-permute-start(bf16[768,768]{1,0:T(8,128)(2,1)} %shard_map.371), channel_id=1, source_target_pairs={{8,0},{16,24},{9,1},{17,25},{10,2},{18,26},{11,3},{19,27},{12,4},{... | collective-permute-start | bytes 3538952 | tf_op jit(solution)/shard_map/ppermute | solution.py:228
  854.4 34.4 %collective-permute-start.94 = (bf16[384,768]{1,0:T(8,128)(2,1)}, bf16[384,768]{1,0:T(8,128)(2,1)S(1)}, u32[]{:S(2)}, u32[]{:S(2)}) collective-permute-start(bf16[384,768]{1,0:T(8,128)(2,1)} %get-tuple-element.413), channel_id=1, source_target_pairs={{0,8},{8,0},{16,24},{24,16},{1,9},{9,1},{17,25},{25,17},{2,10},{10... | collective-permute-start | bytes 1769480 | tf_op jit(solution)/shard_map/ppermute | solution.py:228
  857.9 30.9 %collective-permute-start.95 = (bf16[384,768]{1,0:T(8,128)(2,1)}, bf16[384,768]{1,0:T(8,128)(2,1)S(1)}, u32[]{:S(2)}, u32[]{:S(2)}) collective-permute-start(bf16[384,768]{1,0:T(8,128)(2,1)} %get-tuple-element.414.refs_2_), channel_id=1, source_target_pairs={{8,16},{16,8},{9,17},{17,9},{10,18},{18,10},{11,19},{19,11},{12,20... | collective-permute-start | bytes 1769480 | tf_op jit(solution)/shard_map/ppermute | solution.py:294
  948.3 22.0 %collective-permute-start.106 = (bf16[384,768]{1,0:T(8,128)(2,1)}, bf16[384,768]{1,0:T(8,128)(2,1)S(1)}, u32[]{:S(2)}, u32[]{:S(2)}) collective-permute-start(bf16[384,768]{1,0:T(8,128)(2,1)} %shard_map.380), channel_id=1, source_target_pairs={{8,0},{16,24},{9,1},{17,25},{10,2},{18,26},{11,3},{19,27},{12,4},{... | collective-permute-start | bytes 1769480 | tf_op jit(solution)/shard_map/ppermute | solution.py:228
  (140 other events, 1111.9 us)

commit v5 on v4

--- a/solution.py
+++ b/solution.py
@@ -81,10 +81,11 @@
     return held
 
 
-def share_out(weight, own, held, needed=()):
+def share_out(weight, own, held, needed=(), first=()):
     parts = []
     for away, array in held.items():
-        parts += [Part(away, 0, array), Part(away, 1, flip(array, "rep", 1))]
+        leaving = after(array, *first) if first else array
+        parts += [Part(away, 0, array), Part(away, 1, flip(leaving, "rep", 1))]
     others = [
         Part(
             part.away ^ 1,
@@ -97,12 +98,16 @@
     return [Part(0, None, weight)] + parts + [Part(1, None, own)] + others, swapped
 
 
-def gather_blocks(values, lane):
+def gather_blocks(values, lane, needed=()):
     pieces = {0: values}
     bit = lax.axis_size("tok") // 2
     while bit > 0:
         for away, part in list(pieces.items()):
-            pieces[away ^ bit] = lane.flip(part, bit) if bit > 1 else flip(part, "tok", bit)
+            if bit > 1:
+                pieces[away ^ bit] = lane.flip(part, bit)
+            else:
+                part = after(part, *needed) if away and needed else part
+                pieces[away ^ bit] = flip(part, "tok", bit)
         bit //= 2
     return [pieces[away] for away in range(len(pieces))]
 
@@ -324,13 +329,16 @@
     return values
 
 
-def rep_gather(values):
+def rep_gather(values, needed):
     count = lax.axis_size("rep")
     rank = lax.axis_index("rep")
     pieces = values[None]
     bit = 1
     while bit < count:
-        pieces = jnp.concatenate([pieces, flip(pieces, "rep", bit)], axis=0)
+        moved = flip(pieces, "rep", bit)
+        if needed:
+            moved = after(moved, needed.pop(0))
+        pieces = jnp.concatenate([pieces, moved], axis=0)
         bit *= 2
     return jnp.stack(
         [
@@ -1140,6 +1148,10 @@
     text_mod = both_mod[1] + text_b_mod.astype(jnp.float32)[None]
 
     text_held = fetch(turn(text_w_qkv), 1, chips, (both_mod,))
+    cores = Lane("tok", 1)
+    up_own = cores.flip(after(image_w_up, both_mod), 1)
+    down_own = cores.flip(after(image_w_down, both_mod), 1)
+    proj_held = fetch(proj_stack, 0, chips, tuple(text_held.values()))
 
     owned = (text_owner == tok_rank).astype(jnp.float32)
     total_text = text_owner.shape[1]
@@ -1165,25 +1177,26 @@
 
     image_hid_one = flat(first_hidden(seq, image_mod, image_tokens))
     image_qkv = seq.mark(
-        project(spot, after(seq.then(image_hid_one), *text_held.values()), image_qkv_parts)
-    )
-    image_blocks = gather_blocks(by_seq(image_qkv[1:]), chips)
-    text_qkv_parts, unused = share_out(turn(text_w_qkv), text_own, text_held, (image_qkv,))
-    text_hid_one = flat(first_hidden(seq, text_mod, text_input))
+        project(
+            spot,
+            after(seq.then(image_hid_one), *text_held.values(), up_own, down_own),
+            image_qkv_parts,
+        )
+    )
+    image_blocks = gather_blocks(after(by_seq(image_qkv[1:]), *proj_held.values()), chips)
+    text_qkv_parts, text_swapped = share_out(
+        turn(text_w_qkv), text_own, text_held, (image_qkv,)
+    )
+    text_hid_one = flat(first_hidden(seq, text_mod, after(text_input, *proj_held.values())))
     text_qkv = project(spot, seq.then(text_hid_one), text_qkv_parts)
     text_blocks = gather_blocks(by_seq(text_qkv[1:]), chips)
-    cores = Lane("tok", 1)
-    owned_shards = [
-        cores.flip(after(weight, image_qkv), 1)
-        for weight in (image_w_up, image_w_down, proj_stack)
-    ]
-    up_own, down_own, proj_own = owned_shards
-    seq.mark(text_qkv, *owned_shards)
-    proj_parts, unused = share_out(proj_stack, proj_own, fetch(proj_stack, 0, chips, (text_qkv,)))
+    proj_own = flip(after(proj_stack, image_qkv), "tok", 1)
+    seq.mark(text_qkv, proj_own)
+    proj_parts, unused = share_out(
+        proj_stack, proj_own, proj_held, (text_qkv,), (image_qkv,)
+    )
     up_held = fetch(image_w_up, 0, chips)
     down_held = fetch(image_w_down, 0, chips)
-    image_up_parts, up_swapped = share_out(image_w_up, up_own, up_held)
-    image_down_parts, down_swapped = share_out(image_w_down, down_own, down_held)
     image_query, text_query = by_seq(image_qkv[0]), by_seq(text_qkv[0])
     image_mix, text_mix = attend(
         image_query, seq.then(text_query), image_blocks, text_blocks, text_real
@@ -1192,9 +1205,14 @@
     image_mixed, text_mixed = flat(image_mix), flat(text_mix)
     text_out = seq.mark(project_back(spot, seq.then(text_mixed), proj_parts, 1, width))
     text_branch = heads(text_out)
+    image_up_parts, up_swapped = share_out(image_w_up, up_own, up_held)
+    image_down_parts, down_swapped = share_out(image_w_down, down_own, down_held)
     image_out = project_back(spot, seq.then(image_mixed), proj_parts, 0, width)
     seq.mark(image_out, *down_held.values())
-    image_branch = heads(image_out)
+    if lax.axis_size("head") == 2:
+        image_branch = both((image_out, flip(after(image_out, text_branch[1]), "head", 1)))
+    else:
+        image_branch = heads(image_out)
 
     text_features = exchange(
         middle_spread(seq, spot, text_mod, text_input, text_branch, text_cot, tok_count)
@@ -1219,15 +1237,14 @@
     seq.mark(image_back)
     shape = (2,) + text_keep.shape[2:]
     text_act = activate(seq, text_stays.reshape(shape), text_came.reshape(shape))
-    text_active = gather_blocks(text_act, chips)
+    text_lane = chips
     image_hid_grad = heads(after(image_back, text_act))
     image_down_send = after(image_down_send, text_act)
     image_up_send = after(image_up_send, text_act)
     chips = Lane("tok", 3)
     image_down_pieces = core_sums(seq, image_down_keep, flip(image_down_send, "tok", 1))
-    image_down_pair = chip_moves(seq, image_down_pieces, chips)
     image_up_pieces = core_sums(seq, image_up_keep, flip(image_up_send, "tok", 1))
-    image_up_pair = chip_moves(seq, image_up_pieces, chips)
+    text_active = gather_blocks(text_act, text_lane, (image_up_pieces[0],))
     text_sums, text_up_grad, text_down_grad = spread_down(
         spot,
         [seq.then(text_features[0])] + text_features[1:],
@@ -1237,6 +1254,11 @@
     )
     seq.mark(text_sums[0])
     text_back_pieces = exchange(text_sums)
+    behind = lambda pieces: {
+        away: after(part, text_sums[0]) if away else part for away, part in pieces.items()
+    }
+    image_down_pair = chip_moves(seq, behind(image_down_pieces), chips)
+    image_up_pair = chip_moves(seq, behind(image_up_pieces), chips)
     line = Line(seq)
     if line.on_line:
         for whole in (text_down_grad, text_up_grad):
@@ -1303,6 +1325,7 @@
         image_qkv_parts,
     )
     seq.mark(image_in_part)
+    line.step()
     text_in_part, text_qkv_keep, text_qkv_send = qkv_grads(
         spot,
         seq.then(text_hid_one),
@@ -1378,7 +1401,10 @@
     all_sums = jnp.concatenate(
         [early.reshape(-1, width), late.reshape(-1, width), square_row], axis=0
     )
-    all_sums = rep_gather(tok_total(all_sums))
+    waits = []
+    if line.on_line:
+        waits = [tail.totals[1], tail.totals[3]]
+    all_sums = rep_gather(tok_total(all_sums), waits)
     square_total = jnp.sum(all_sums[:, -1, :10], axis=0)
     early_table = jnp.moveaxis(
         all_sums[:, : 8 * seqs].reshape(rep_count, 2, seqs, 4, width), 0, 1
@@ -1391,8 +1417,8 @@
     activ_rows = lax.dynamic_slice_in_dim(activ_all, tok_rank * share, share, axis=1).astype(
         jnp.float32
     )
-    image_g_mod = jnp.einsum("sd,ske->dke", activ_rows, mod_sum[0], precision=exact_mode)
-    text_g_mod = jnp.einsum("sd,ske->dke", activ_rows, mod_sum[1], precision=exact_mode)
+    image_g_mod = jnp.einsum("sd,ske->dke", activ_rows, mod_sum[0], precision=lax.Precision.HIGH)
+    text_g_mod = jnp.einsum("sd,ske->dke", activ_rows, mod_sum[1], precision=lax.Precision.HIGH)
     image_g_bmod = jnp.sum(mod_sum[0], axis=0)
     text_g_bmod = jnp.sum(mod_sum[1], axis=0)
     activ_grad = jnp.einsum(

time: 984 us -> 933 us (0.948)
  waiting for transfers between devices: 344 us -> 296 us
    ppermute x71, waiting for transfers between devices: 206 us -> 178 us  [flip(): lax.ppermute(values, axis, [(place, place ^ bit) for place in range(lax.a...]
    ppermute x20, waiting for transfers between devices: 138 us -> 118 us  [outer(): return lax.ppermute(load, 'rep', pairs)]
    unnamed x200 -> x208, local copies, waits for them, and re-layouts: 33.1 us -> 27.9 us
  transfers between devices with their start and end apart: 107 -> 107, of which waited for: 37 -> 34; matrix products, arithmetic and copies ran while one was open for 10% -> 12% of each run, Pallas kernels for 32% -> 37%
where the time goes in v5:
time: 933 us; the launch traced here: 922 us
  Pallas kernels  357 us (38%)
  waiting for transfers between devices  296 us (32%)
  starting transfers between devices  126 us (14%)
  local copies, waits for them, and re-layouts  63.4 us (7%)
  matrix products  38.9 us (4%)
  other arithmetic  38.5 us (4%)
    ppermute x71, waiting for transfers between devices, flip(): lax.ppermute(values, axis, [(place, place ^ bit) for place in range(lax.a...  178 us
    ppermute x20, waiting for transfers between devices, outer(): return lax.ppermute(load, 'rep', pairs)  118 us
    pallas_call x11, Pallas kernels, call(): pl.pallas_call(kernel, grid=(tiles,), in_specs=[pl.BlockSpec(memory_space...  112 us
    pallas_call x18, Pallas kernels, step(): pl.pallas_call(kernel, grid=(2,), in_specs=[pl.BlockSpec(memory_space=plt...  57.8 us
    ppermute x20, starting transfers between devices, outer(): return lax.ppermute(load, 'rep', pairs)  56.9 us
    pallas_call x2, Pallas kernels, attend_grads(): pl.pallas_call(kernel, grid=(width // LANES,), in_specs=[row_spec(length,...  53.4 us
    ppermute x71, starting transfers between devices, flip(): lax.ppermute(values, axis, [(place, place ^ bit) for place in range(lax.a...  49 us
    pallas_call x13, Pallas kernels, add_blocks(): pl.pallas_call(kernel, grid=(2,), in_specs=[in_spec, in_spec], out_specs=...  46.5 us
  transfers between devices with their start and end apart: 107, of which 34 were waited for; matrix products, arithmetic and copies ran while one was open for 12% of the time, Pallas kernels for 37%

profile of v5, /device:TPU:0, one launch (start us, length us, event | category | flops | bytes accessed | tf_op | source)
XLA Modules:
  0.0 922.3 jit_solution(10408630202458651635)
XLA Ops:
  6.7 4.2 fusion.46
  14.5 11.4 %collective-permute-done.1.rest_1_.rest_5_ = bf16[3,192,768]{2,1,0:T(8,128)(2,1)} collective-permute-done((bf16[3,192,768]{2,1,0:T(8,128)(2,1)}, bf16[3,192,768]{2,1,0:T(8,128)(2,1)}, u32[]{:S(2)}, u32[]{:S(2)}) %collective-permute-start.1) | collective-permute-done | bytes 884768 | tf_op jit(solution)/shard_map/ppermute | solution.py:25
  27.6 4.3 collective-permute-done.2
  32.1 4.5 collective-permute-done.4.rest_3_
  42.2 16.8 %collective-permute-done.6.rest_2_.rest_6_ = bf16[3,192,768]{2,1,0:T(8,128)(2,1)} collective-permute-done((bf16[3,192,768]{2,1,0:T(8,128)(2,1)}, bf16[3,192,768]{2,1,0:T(8,128)(2,1)}, u32[]{:S(2)}, u32[]{:S(2)}) %collective-permute-start.6) | collective-permute-done | bytes 884768 | tf_op jit(solution)/shard_map/ppermute | solution.py:25
  70.2 8.3 shard_map.323
  80.7 6.7 collective-permute-done.11.rest_2_.rest_6_
  92.5 24.3 %collective-permute-done.17.rest_4_.rest_6_ = bf16[2,2,256,768]{3,2,1,0:T(8,128)(2,1)} collective-permute-done((bf16[2,2,256,768]{3,2,1,0:T(8,128)(2,1)S(1)}, bf16[2,2,256,768]{3,2,1,0:T(8,128)(2,1)}, u32[]{:S(2)}, u32[]{:S(2)}) %collective-permute-start.17) | collective-permute-done | bytes 1572896 | tf_op jit(solution)/shard_map/ppermute | solution.py:25
  119.9 5.7 shard_map.325
  131.0 5.4 collective-permute-done.20.rest_8_.rest_10_
  145.2 25.8 %shard_map.326 = (bf16[2,256,768]{2,1,0:T(8,128)(2,1)}, bf16[2,48,768]{2,1,0:T(8,128)(2,1)}) custom-call(bf16[2,256,768]{2,1,0:T(8,128)(2,1)} %bitcast.172, bf16[2,48,768]{2,1,0:T(8,128)(2,1)} %bitcast.215, bf16[2,2,256,768]{3,2,1,0:T(8,128)(2,1)} %bitcast.161, bf16[2,2,256,768]{3,2,1,0:T(8,128)(2,1)} %collective-permute-done.16.rest_3_.rest_5_, ...), custom_call_target="tpu_custom_call" | custom-call | flops 1024 | bytes 1024 | tf_op jit(solution)/shard_map/pallas_call | solution.py:1003
  177.9 5.0 shard_map.328
  194.2 27.1 %collective-permute-done.28 = bf16[512,1536]{1,0:T(8,128)(2,1)S(1)} collective-permute-done((bf16[512,1536]{1,0:T(8,128)(2,1)}, bf16[512,1536]{1,0:T(8,128)(2,1)S(1)}, u32[]{:S(2)}, u32[]{:S(2)}) %collective-permute-start.28) | collective-permute-done | bytes 1572896 | tf_op jit(solution)/shard_map/ppermute | solution.py:25
  222.5 4.8 shard_map.330
  227.4 12.5 %collective-permute-done.29.rest_2_ = bf16[192,3072]{1,0:T(8,128)(2,1)} collective-permute-done((bf16[192,3072]{1,0:T(8,128)(2,1)}, bf16[192,3072]{1,0:T(8,128)(2,1)}, u32[]{:S(2)}, u32[]{:S(2)}) %collective-permute-start.29) | collective-permute-done | bytes 1179680 | tf_op jit(solution)/shard_map/ppermute | solution.py:25
  241.3 8.5 shard_map.331
  250.9 6.2 collective-permute-done.34
  263.3 40.1 %shard_map.333 = (bf16[512,1536]{1,0:T(8,128)(2,1)}, bf16[512,1536]{1,0:T(8,128)(2,1)}, bf16[2,4,384,768]{3,2,1,0:T(8,128)(2,1)}, bf16[2,4,384,768]{3,2,1,0:T(8,...) custom-call(s32[2]{0:T(128)} %pad_add_fusion.spot_ref, bf16[512,1536]{1,0:T(8,128)(2,1)} %bitcast.222, ...), custom_call_target="tpu_custom_call" | custom-call | flops 1024 | bytes 1024 | tf_op jit(solution)/shard_map/pallas_call | solution.py:426
  310.7 5.4 collective-permute-done.40
  316.1 5.6 shard_map.335
  324.5 5.6 shard_map.336
  330.1 6.4 collective-permute-done.43.rest_6_
  339.5 11.0 %shard_map.337 = (bf16[2,96,384]{2,1,0:T(8,128)(2,1)}, bf16[2,96,384]{2,1,0:T(8,128)(2,1)}, bf16[2,96,384]{2,1,0:T(8,128)(2,1)}, bf16[2,96,384]{2,1,0:T(8,128)(2...) custom-call(s32[2]{0:T(128)} %pad_add_fusion.spot_ref, bf16[384,3072]{1,0:T(8,128)(2,1)} %up_ref.3, ...), custom_call_target="tpu_custom_call" | custom-call | flops 1024 | bytes 1024 | tf_op jit(solution)/shard_map/pallas_call | solution.py:426
  354.2 8.2 shard_map.338
  370.4 6.7 shard_map.340
  378.6 7.9 collective-permute-done.49
  390.2 5.2 shard_map.342
  410.3 26.7 %shard_map.346 = (bf16[1,256,768]{2,1,0:T(8,128)(2,1)}, bf16[1,48,768]{2,1,0:T(8,128)(2,1)}, bf16[2,2,304,768]{3,2,1,0:T(8,128)(2,1)}, bf16[2,2,304,768]{3,2,1,0:T(8,128)(2,1)}) custom-call(bf16[2,256,768]{2,1,0:T(8,128)(2,1)} %bitcast.173, bf16[2,48,768]{2,1,0:T(8,128)(2,1)} %bitcast.216, bf16[2,256,768]{2,1,0:T(8,128)(2,1)} %bitcast.200, ...), custom_call_target="tpu_custom_call" | custom-call | flops 1024 | bytes 1024 | tf_op jit(solution)/shard_map/pallas_call | solution.py:1074
  441.6 4.3 shard_map.348
  447.5 26.7 %shard_map.349 = (bf16[1,256,768]{2,1,0:T(8,128)(2,1)}, bf16[1,48,768]{2,1,0:T(8,128)(2,1)}, bf16[2,2,304,768]{3,2,1,0:T(8,128)(2,1)}, bf16[2,2,304,768]{3,2,1,0:T(8,128)(2,1)}) custom-call(bf16[2,256,768]{2,1,0:T(8,128)(2,1)} %bitcast.174, bf16[2,48,768]{2,1,0:T(8,128)(2,1)} %bitcast.217, bf16[2,256,768]{2,1,0:T(8,128)(2,1)} %bitcast.201, ...), custom_call_target="tpu_custom_call" | custom-call | flops 1024 | bytes 1024 | tf_op jit(solution)/shard_map/pallas_call | solution.py:1074
  479.2 4.2 shard_map.351
  483.9 4.6 collective-permute-start.61
  491.6 4.8 shard_map.352
  497.3 17.6 %collective-permute-done.61.refs_1_ = bf16[768,768]{1,0:T(8,128)(2,1)S(1)} collective-permute-done((bf16[768,768]{1,0:T(8,128)(2,1)}, bf16[768,768]{1,0:T(8,128)(2,1)S(1)}, u32[]{:S(2)}, u32[]{:S(2)}) %collective-permute-start.61) | collective-permute-done | bytes 1179680 | tf_op jit(solution)/shard_map/ppermute | solution.py:233
  515.9 4.2 shard_map.353
  523.6 15.5 %collective-permute-done.63 = bf16[1216,768]{1,0:T(8,128)(2,1)} collective-permute-done((bf16[1216,768]{1,0:T(8,128)(2,1)}, bf16[1216,768]{1,0:T(8,128)(2,1)}, u32[]{:S(2)}, u32[]{:S(2)}) %collective-permute-start.63) | collective-permute-done | bytes 1867808 | tf_op jit(solution)/shard_map/ppermute | solution.py:25
  543.2 14.5 %shard_map.355 = (bf16[512,1536]{1,0:T(8,128)(2,1)}, bf16[2,3,384,768]{3,2,1,0:T(8,128)(2,1)}, bf16[2,3,384,768]{3,2,1,0:T(8,128)(2,1)}) custom-call(s32[2]{0:T(128)} %pad_add_fusion.spot_ref, bf16[512,1536]{1,0:T(8,128)(2,1)} %bitcast.171, bf16[1,256,768]{2,1,0:T(8,128)(2,1)} %get-tuple-element.327.rest_0_, ...), custom_call_target="tpu_custom_call" | custom-call | flops 1024 | bytes 1024 | tf_op jit(solution)/shard_map/pallas_call | solution.py:426
  559.2 4.2 shard_map.356
  563.5 9.7 %shard_map.357 = (bf16[96,1536]{1,0:T(8,128)(2,1)}, bf16[2,3,384,768]{3,2,1,0:T(8,128)(2,1)}, bf16[2,3,384,768]{3,2,1,0:T(8,128)(2,1)}) custom-call(s32[2]{0:T(128)} %pad_add_fusion.spot_ref, bf16[96,1536]{1,0:T(8,128)(2,1)} %bitcast.203, bf16[1,48,768]{2,1,0:T(8,128)(2,1)} %get-tuple-element.367.rest_0_, bf16[1,48,768]{2,1,0:T(8,128)(2,1)} %get-tuple-element.368.rest_1_, ...), custom_call_target="tpu_custom_call" | custom-call | flops 1024 | bytes 1024 | tf_op jit(solution)/shard_map/pallas_call | solution.py:426
  583.7 4.6 shard_map.358
  589.2 4.6 shard_map.359
  593.8 11.6 %collective-permute-done.68.refs_1_ = bf16[768,768]{1,0:T(8,128)(2,1)S(1)} collective-permute-done((bf16[768,768]{1,0:T(8,128)(2,1)}, bf16[768,768]{1,0:T(8,128)(2,1)S(1)}, u32[]{:S(2)}, u32[]{:S(2)}) %collective-permute-start.68) | collective-permute-done | bytes 1179680 | tf_op jit(solution)/shard_map/ppermute | solution.py:233
  624.3 13.8 %collective-permute-done.72.refs_1_ = bf16[768,768]{1,0:T(8,128)(2,1)} collective-permute-done((bf16[768,768]{1,0:T(8,128)(2,1)}, bf16[768,768]{1,0:T(8,128)(2,1)}, u32[]{:S(2)}, u32[]{:S(2)}) %collective-permute-start.72) | collective-permute-done | bytes 1179680 | tf_op jit(solution)/shard_map/ppermute | solution.py:233
  638.2 4.2 shard_map.363
  647.9 4.7 pad_maximum_fusion.2
  653.8 5.7 shard_map.364
  666.7 4.4 collective-permute-start.86
  686.4 7.7 collective-permute-done.79
  707.5 5.9 shard_map.371
  719.6 4.4 pad_maximum_fusion.1
  732.6 6.8 collective-permute-start.89
  745.9 26.2 %collective-permute-done.89.refs_1_ = bf16[384,768]{1,0:T(8,128)(2,1)S(1)} collective-permute-done((bf16[384,768]{1,0:T(8,128)(2,1)}, bf16[384,768]{1,0:T(8,128)(2,1)S(1)}, u32[]{:S(2)}, u32[]{:S(2)}) %collective-permute-start.89) | collective-permute-done | bytes 589856 | tf_op jit(solution)/shard_map/ppermute | solution.py:233
  784.2 8.7 collective-permute-done.92.refs_1_
  800.8 4.5 pad_maximum_fusion
  808.1 9.0 collective-permute-done.94.refs_1_
  822.1 4.5 collective-permute-start.96
  828.6 7.7 convolution_bitcast_fusion.1
  836.3 7.8 fusion
  850.8 5.4 collective-permute-start.98
  856.2 7.3 fusion.2
  863.6 4.6 collective-permute-done.98.refs_1_
  874.3 7.4 fusion.5
  898.6 9.7 %collective-permute-done.104 = bf16[384,768]{1,0:T(8,128)(2,1)S(1)} collective-permute-done((bf16[384,768]{1,0:T(8,128)(2,1)}, bf16[384,768]{1,0:T(8,128)(2,1)S(1)}, u32[]{:S(2)}, u32[]{:S(2)}) %collective-permute-start.104) | collective-permute-done | bytes 589856 | tf_op jit(solution)/shard_map/ppermute | solution.py:233
  908.4 11.4 %collective-permute-done.106 = bf16[384,768]{1,0:T(8,128)(2,1)S(1)} collective-permute-done((bf16[384,768]{1,0:T(8,128)(2,1)}, bf16[384,768]{1,0:T(8,128)(2,1)S(1)}, u32[]{:S(2)}, u32[]{:S(2)}) %collective-permute-start.106) | collective-permute-done | bytes 589856 | tf_op jit(solution)/shard_map/ppermute | solution.py:233
  (516 shorter events, 306.4 us)
Async XLA Ops:
  2.9 22.9 %collective-permute-start.1 = (bf16[3,192,768]{2,1,0:T(8,128)(2,1)}, bf16[3,192,768]{2,1,0:T(8,128)(2,1)}, u32[]{:S(2)}, u32[]{:S(2)}) collective-permute-start(bf16[3,192,768]{2,1,0:T(8,128)(2,1)} %dynamic-slice_bitcast_fusion.1), channel_id=1, source_target_pairs={{0,4},{2,6},{4,0},{6,2},{1,5},{3,7},{5,1},{7,3},{8,12},{10,14},{12... | collective-permute-start | bytes 2654216 | tf_op jit(solution)/shard_map/ppermute | solution.py:25
  36.6 28.5 %collective-permute-start.5 = (bf16[384,3072]{1,0:T(8,128)(2,1)}, bf16[384,3072]{1,0:T(8,128)(2,1)}, u32[]{:S(2)}, u32[]{:S(2)}) collective-permute-start(bf16[384,3072]{1,0:T(8,128)(2,1)} %rest_6_.1), channel_id=1, source_target_pairs={{0,2},{2,0},{4,6},{6,4},{1,3},{3,1},{5,7},{7,5},{8,10},{10,8},{12,... | collective-permute-start | bytes 7077896 | tf_op jit(solution)/shard_map/ppermute | solution.py:25
  36.7 22.2 %collective-permute-start.6 = (bf16[3,192,768]{2,1,0:T(8,128)(2,1)}, bf16[3,192,768]{2,1,0:T(8,128)(2,1)}, u32[]{:S(2)}, u32[]{:S(2)}) collective-permute-start(bf16[3,192,768]{2,1,0:T(8,128)(2,1)} %collective-permute-done.1.rest_1_.rest_5_), channel_id=1, source_target_pairs={{0,8},{8,0},{16,24},{24,16},{1,9},{9,1},{17,25},{25,17},{2,10},{10... | collective-permute-start | bytes 2654216 | tf_op jit(solution)/shard_map/ppermute | solution.py:25
  38.2 32.0 %collective-permute-start.7 = (bf16[3,384,768]{2,1,0:T(8,128)(2,1)S(1)}, bf16[3,384,768]{2,1,0:T(8,128)(2,1)}, u32[]{:S(2)}, u32[]{:S(2)}) collective-permute-start(bf16[3,384,768]{2,1,0:T(8,128)(2,1)S(1)} %bitcast.177), channel_id=1, source_target_pairs={{0,2},{2,0},{4,6},{6,4},{1,3},{3,1},{5,7},{7,5},{8,10},{10,8},{12,... | collective-permute-start | bytes 5308424 | tf_op jit(solution)/shard_map/ppermute | solution.py:25
  40.5 22.3 %collective-permute-start.3 = (bf16[3,192,768]{2,1,0:T(8,128)(2,1)}, bf16[3,192,768]{2,1,0:T(8,128)(2,1)}, u32[]{:S(2)}, u32[]{:S(2)}) collective-permute-start(bf16[3,192,768]{2,1,0:T(8,128)(2,1)} %dynamic-slice_bitcast_fusion), channel_id=1, source_target_pairs={{0,4},{2,6},{4,0},{6,2},{1,5},{3,7},{5,1},{7,3},{8,12},{10,14},{12... | collective-permute-start | bytes 2654216 | tf_op jit(solution)/shard_map/ppermute | solution.py:25
  42.0 23.0 %collective-permute-start.8 = (bf16[3,192,768]{2,1,0:T(8,128)(2,1)}, bf16[3,192,768]{2,1,0:T(8,128)(2,1)}, u32[]{:S(2)}, u32[]{:S(2)}) collective-permute-start(bf16[3,192,768]{2,1,0:T(8,128)(2,1)} %collective-permute-done.1.rest_1_.rest_5_), channel_id=1, source_target_pairs={{0,2},{2,0},{4,6},{6,4},{1,3},{3,1},{5,7},{7,5},{8,10},{10,8},{12,... | collective-permute-start | bytes 2654216 | tf_op jit(solution)/shard_map/ppermute | solution.py:25
  65.1 23.2 %collective-permute-start.12 = (bf16[3,384,768]{2,1,0:T(8,128)(2,1)}, bf16[3,384,768]{2,1,0:T(8,128)(2,1)}, u32[]{:S(2)}, u32[]{:S(2)}) collective-permute-start(bf16[3,384,768]{2,1,0:T(8,128)(2,1)} %bitcast.16.rest_0_.rest_4_), channel_id=1, source_target_pairs={{0,2},{2,0},{4,6},{6,4},{1,3},{3,1},{5,7},{7,5},{8,10},{10,8},{12,... | collective-permute-start | bytes 5308424 | tf_op jit(solution)/shard_map/ppermute | solution.py:25
  65.1 22.4 %collective-permute-start.11 = (bf16[3,192,768]{2,1,0:T(8,128)(2,1)}, bf16[3,192,768]{2,1,0:T(8,128)(2,1)}, u32[]{:S(2)}, u32[]{:S(2)}) collective-permute-start(bf16[3,192,768]{2,1,0:T(8,128)(2,1)} %collective-permute-done.3.rest_1_.rest_5_), channel_id=1, source_target_pairs={{0,8},{8,0},{16,24},{24,16},{1,9},{9,1},{17,25},{25,17},{2,10},{10... | collective-permute-start | bytes 2654216 | tf_op jit(solution)/shard_map/ppermute | solution.py:25
  80.1 36.6 %collective-permute-start.17 = (bf16[2,2,256,768]{3,2,1,0:T(8,128)(2,1)S(1)}, bf16[2,2,256,768]{3,2,1,0:T(8,128)(2,1)}, u32[]{:S(2)}, u32[]{:S(2)}) collective-permute-start(bf16[2,2,256,768]{3,2,1,0:T(8,128)(2,1)S(1)} %bitcast.159), channel_id=1, source_target_pairs={{0,4},{2,6},{4,0},{6,2},{1,5},{3,7},{5,1},{7,3},{8,12},{10,14},{12... | collective-permute-start | bytes 4718600 | tf_op jit(solution)/shard_map/ppermute | solution.py:25
  87.4 32.4 %collective-permute-start.13 = (bf16[3,192,768]{2,1,0:T(8,128)(2,1)}, bf16[3,192,768]{2,1,0:T(8,128)(2,1)}, u32[]{:S(2)}, u32[]{:S(2)}) collective-permute-start(bf16[3,192,768]{2,1,0:T(8,128)(2,1)} %collective-permute-done.3.rest_1_.rest_5_), channel_id=1, source_target_pairs={{0,2},{2,0},{4,6},{6,4},{1,3},{3,1},{5,7},{7,5},{8,10},{10,8},{12,... | collective-permute-start | bytes 2654216 | tf_op jit(solution)/shard_map/ppermute | solution.py:25
  88.1 48.4 %collective-permute-start.15 = (bf16[2,384,768]{2,1,0:T(8,128)(2,1)S(1)}, bf16[2,384,768]{2,1,0:T(8,128)(2,1)}, u32[]{:S(2)}, u32[]{:S(2)}) collective-permute-start(bf16[2,384,768]{2,1,0:T(8,128)(2,1)S(1)} %pad_maximum_fusion.4.rest_0_), channel_id=1, source_target_pairs={{0,2},{2,0},{4,6},{6,4},{1,3},{3,1},{5,7},{7,5},{8,10},{10,8},{12,... | collective-permute-start | bytes 3538952 | tf_op jit(solution)/shard_map/ppermute | solution.py:25
  88.3 52.7 %collective-permute-start.16 = (bf16[2,2,256,768]{3,2,1,0:T(8,128)(2,1)S(1)}, bf16[2,2,256,768]{3,2,1,0:T(8,128)(2,1)}, u32[]{:S(2)}, u32[]{:S(2)}) collective-permute-start(bf16[2,2,256,768]{3,2,1,0:T(8,128)(2,1)S(1)} %bitcast.160), channel_id=1, source_target_pairs={{0,2},{2,0},{4,6},{6,4},{1,3},{3,1},{5,7},{7,5},{8,10},{10,8},{12,... | collective-permute-start | bytes 4718600 | tf_op jit(solution)/shard_map/ppermute | solution.py:25
  91.3 38.2 %collective-permute-start.23 = (bf16[1,384,768]{2,1,0:T(8,128)(2,1)}, bf16[1,384,768]{2,1,0:T(8,128)(2,1)}, u32[]{:S(2)}, u32[]{:S(2)}) collective-permute-start(bf16[1,384,768]{2,1,0:T(8,128)(2,1)} %collective-permute-done.10.rest_1_), channel_id=1, source_target_pairs={{0,8},{8,0},{16,24},{24,16},{1,9},{9,1},{17,25},{25,17},{2,10},{10... | collective-permute-start | bytes 1769480 | tf_op jit(solution)/shard_map/ppermute | solution.py:25
  116.8 28.4 %collective-permute-start.18 = (bf16[2,2,256,768]{3,2,1,0:T(8,128)(2,1)}, bf16[2,2,256,768]{3,2,1,0:T(8,128)(2,1)}, u32[]{:S(2)}, u32[]{:S(2)}) collective-permute-start(bf16[2,2,256,768]{3,2,1,0:T(8,128)(2,1)} %collective-permute-done.17.rest_4_.rest_6_), channel_id=1, source_target_pairs={{0,2},{2,0},{4,6},{6,4},{1,3},{3,1},{5,7},{7,5},{8,10},{10,8},{12,... | collective-permute-start | bytes 4718600 | tf_op jit(solution)/shard_map/ppermute | solution.py:25
  129.5 41.5 %collective-permute-start.22 = (bf16[192,3072]{1,0:T(8,128)(2,1)}, bf16[192,3072]{1,0:T(8,128)(2,1)}, u32[]{:S(2)}, u32[]{:S(2)}) collective-permute-start(bf16[192,3072]{1,0:T(8,128)(2,1)} %constant_dynamic-slice_fusion.5), channel_id=1, source_target_pairs={{0,4},{2,6},{4,0},{6,2},{1,5},{3,7},{5,1},{7,3},{8,12},{10,14},{12... | collective-permute-start | bytes 3538952 | tf_op jit(solution)/shard_map/ppermute | solution.py:25
  138.1 32.9 %collective-permute-start.25 = (bf16[1,384,768]{2,1,0:T(8,128)(2,1)}, bf16[1,384,768]{2,1,0:T(8,128)(2,1)S(1)}, u32[]{:S(2)}, u32[]{:S(2)}) collective-permute-start(bf16[1,384,768]{2,1,0:T(8,128)(2,1)} %collective-permute-done.23.rest_2_), channel_id=1, source_target_pairs={{0,2},{2,0},{4,6},{6,4},{1,3},{3,1},{5,7},{7,5},{8,10},{10,8},{12,... | collective-permute-start | bytes 1769480 | tf_op jit(solution)/shard_map/ppermute | solution.py:25
  138.4 32.6 %collective-permute-start.24 = (bf16[1,384,768]{2,1,0:T(8,128)(2,1)}, bf16[1,384,768]{2,1,0:T(8,128)(2,1)S(1)}, u32[]{:S(2)}, u32[]{:S(2)}) collective-permute-start(bf16[1,384,768]{2,1,0:T(8,128)(2,1)} %collective-permute-done.10.rest_1_), channel_id=1, source_target_pairs={{0,2},{2,0},{4,6},{6,4},{1,3},{3,1},{5,7},{7,5},{8,10},{10,8},{12,... | collective-permute-start | bytes 1769480 | tf_op jit(solution)/shard_map/ppermute | solution.py:25
  141.0 46.0 %collective-permute-start.26 = (bf16[192,3072]{1,0:T(8,128)(2,1)}, bf16[192,3072]{1,0:T(8,128)(2,1)}, u32[]{:S(2)}, u32[]{:S(2)}) collective-permute-start(bf16[192,3072]{1,0:T(8,128)(2,1)} %constant_dynamic-slice_fusion.4), channel_id=1, source_target_pairs={{0,4},{2,6},{4,0},{6,2},{1,5},{3,7},{5,1},{7,3},{8,12},{10,14},{12... | collective-permute-start | bytes 3538952 | tf_op jit(solution)/shard_map/ppermute | solution.py:25
  185.6 35.8 %collective-permute-start.28 = (bf16[512,1536]{1,0:T(8,128)(2,1)}, bf16[512,1536]{1,0:T(8,128)(2,1)S(1)}, u32[]{:S(2)}, u32[]{:S(2)}) collective-permute-start(bf16[512,1536]{1,0:T(8,128)(2,1)} %shard_map.328), channel_id=1, source_target_pairs={{0,1},{1,0},{2,3},{3,2},{4,5},{5,4},{6,7},{7,6},{8,9},{9,8},{10,11... | collective-permute-start | bytes 4718600 | tf_op jit(solution)/shard_map/ppermute | solution.py:25
  187.1 40.3 %collective-permute-start.30 = (bf16[192,3072]{1,0:T(8,128)(2,1)}, bf16[192,3072]{1,0:T(8,128)(2,1)S(1)}, u32[]{:S(2)}, u32[]{:S(2)}) collective-permute-start(bf16[192,3072]{1,0:T(8,128)(2,1)} %collective-permute-done.26.rest_7_), channel_id=1, source_target_pairs={{0,8},{8,0},{16,24},{24,16},{1,9},{9,1},{17,25},{25,17},{2,10},{10... | collective-permute-start | bytes 3538952 | tf_op jit(solution)/shard_map/ppermute | solution.py:25
  187.9 52.0 %collective-permute-start.29 = (bf16[192,3072]{1,0:T(8,128)(2,1)}, bf16[192,3072]{1,0:T(8,128)(2,1)}, u32[]{:S(2)}, u32[]{:S(2)}) collective-permute-start(bf16[192,3072]{1,0:T(8,128)(2,1)} %collective-permute-done.22.rest_1_), channel_id=1, source_target_pairs={{0,8},{8,0},{16,24},{24,16},{1,9},{9,1},{17,25},{25,17},{2,10},{10... | collective-permute-start | bytes 3538952 | tf_op jit(solution)/shard_map/ppermute | solution.py:25
  192.6 47.3 %collective-permute-start.31 = (bf16[2,96,384]{2,1,0:T(8,128)(2,1)}, bf16[2,96,384]{2,1,0:T(8,128)(2,1)S(1)}, u32[]{:S(2)}, u32[]{:S(2)}) collective-permute-start(bf16[2,96,384]{2,1,0:T(8,128)(2,1)} %bitcast.253), channel_id=1, source_target_pairs={{0,2},{2,0},{4,6},{6,4},{1,3},{3,1},{5,7},{7,5},{8,10},{10,8},{12,... | collective-permute-start | bytes 442376 | tf_op jit(solution)/shard_map/ppermute | solution.py:25
  192.6 47.3 %collective-permute-start.32 = (bf16[2,96,384]{2,1,0:T(8,128)(2,1)}, bf16[2,96,384]{2,1,0:T(8,128)(2,1)S(1)}, u32[]{:S(2)}, u32[]{:S(2)}) collective-permute-start(bf16[2,96,384]{2,1,0:T(8,128)(2,1)} %bitcast.252), channel_id=1, source_target_pairs={{0,4},{2,6},{4,0},{6,2},{1,5},{3,7},{5,1},{7,3},{8,12},{10,14},{12... | collective-permute-start | bytes 442376 | tf_op jit(solution)/shard_map/ppermute | solution.py:25
  262.2 41.2 %collective-permute-start.39 = (bf16[768,768]{1,0:T(8,128)(2,1)}, bf16[768,768]{1,0:T(8,128)(2,1)S(1)}, u32[]{:S(2)}, u32[]{:S(2)}) collective-permute-start(bf16[768,768]{1,0:T(8,128)(2,1)} %get-tuple-element.287), channel_id=1, source_target_pairs={{0,4},{2,6},{4,0},{6,2},{1,5},{3,7},{5,1},{7,3},{8,12},{10,14},{12... | collective-permute-start | bytes 3538952 | tf_op jit(solution)/shard_map/ppermute | solution.py:25
  308.3 28.2 %collective-permute-start.43 = (bf16[2,384,768]{2,1,0:T(8,128)(2,1)}, bf16[2,384,768]{2,1,0:T(8,128)(2,1)S(1)}, u32[]{:S(2)}, u32[]{:S(2)}) collective-permute-start(bf16[2,384,768]{2,1,0:T(8,128)(2,1)} %shard_map.334.rest_4_), channel_id=1, source_target_pairs={{0,4},{2,6},{4,0},{6,2},{1,5},{3,7},{5,1},{7,3},{8,12},{10,14},{12... | collective-permute-start | bytes 3538952 | tf_op jit(solution)/shard_map/ppermute | solution.py:25
  309.2 45.0 %collective-permute-start.45 = (bf16[512,1536]{1,0:T(8,128)(2,1)}, bf16[512,1536]{1,0:T(8,128)(2,1)}, u32[]{:S(2)}, u32[]{:S(2)}) collective-permute-start(bf16[512,1536]{1,0:T(8,128)(2,1)} %get-tuple-element.301), channel_id=1, source_target_pairs={{0,1},{1,0},{2,3},{3,2},{4,5},{5,4},{6,7},{7,6},{8,9},{9,8},{10,11... | collective-permute-start | bytes 4718600 | tf_op jit(solution)/shard_map/ppermute | solution.py:25
  310.7 25.8 %collective-permute-start.42 = (bf16[2,384,768]{2,1,0:T(8,128)(2,1)}, bf16[2,384,768]{2,1,0:T(8,128)(2,1)S(1)}, u32[]{:S(2)}, u32[]{:S(2)}) collective-permute-start(bf16[2,384,768]{2,1,0:T(8,128)(2,1)} %shard_map.334.rest_4_), channel_id=1, source_target_pairs={{0,2},{2,0},{4,6},{6,4},{1,3},{3,1},{5,7},{7,5},{8,10},{10,8},{12,... | collective-permute-start | bytes 3538952 | tf_op jit(solution)/shard_map/ppermute | solution.py:25
  362.4 34.1 %collective-permute-start.50 = (bf16[768,768]{1,0:T(8,128)(2,1)S(1)}, bf16[768,768]{1,0:T(8,128)(2,1)}, u32[]{:S(2)}, u32[]{:S(2)}) collective-permute-start(bf16[768,768]{1,0:T(8,128)(2,1)S(1)} %bitcast.191), channel_id=1, source_target_pairs={{0,8},{24,16},{1,9},{25,17},{2,10},{26,18},{3,11},{27,19},{4,12},{... | collective-permute-start | bytes 3538952 | tf_op jit(solution)/shard_map/ppermute | solution.py:233
  366.1 70.8 %collective-permute-start.53 = (bf16[1536,768]{1,0:T(8,128)(2,1)}, bf16[1536,768]{1,0:T(8,128)(2,1)}, u32[]{:S(2)}, u32[]{:S(2)}) collective-permute-start(bf16[1536,768]{1,0:T(8,128)(2,1)} %get-tuple-element.330), channel_id=1, source_target_pairs={{0,4},{2,6},{4,0},{6,2},{1,5},{3,7},{5,1},{7,3},{8,12},{10,14},{12... | collective-permute-start | bytes 7077896 | tf_op jit(solution)/shard_map/ppermute | solution.py:25
  377.1 23.3 %collective-permute-start.51 = (bf16[2,1,384,768]{3,2,0,1:T(8,128)(2,1)}, bf16[2,1,384,768]{3,2,0,1:T(8,128)(2,1)}, u32[]{:S(2)}, u32[]{:S(2)}) collective-permute-start(bf16[2,1,384,768]{3,2,0,1:T(8,128)(2,1)} %bitcast.249), channel_id=1, source_target_pairs={{0,2},{2,0},{4,6},{6,4},{1,3},{3,1},{5,7},{7,5},{8,10},{10,8},{12,... | collective-permute-start | bytes 3538952 | tf_op jit(solution)/shard_map/ppermute | solution.py:25
  395.3 78.9 %collective-permute-start.56 = (bf16[1536,768]{1,0:T(8,128)(2,1)}, bf16[1536,768]{1,0:T(8,128)(2,1)}, u32[]{:S(2)}, u32[]{:S(2)}) collective-permute-start(bf16[1536,768]{1,0:T(8,128)(2,1)} %get-tuple-element.339), channel_id=1, source_target_pairs={{0,4},{2,6},{4,0},{6,2},{1,5},{3,7},{5,1},{7,3},{8,12},{10,14},{12... | collective-permute-start | bytes 7077896 | tf_op jit(solution)/shard_map/ppermute | solution.py:25
  396.5 44.1 %collective-permute-start.54 = (bf16[768,768]{1,0:T(8,128)(2,1)S(1)}, bf16[768,768]{1,0:T(8,128)(2,1)S(1)}, u32[]{:S(2)}, u32[]{:S(2)}) collective-permute-start(bf16[768,768]{1,0:T(8,128)(2,1)S(1)} %bitcast.189), channel_id=1, source_target_pairs={{0,8},{24,16},{1,9},{25,17},{2,10},{26,18},{3,11},{27,19},{4,12},{... | collective-permute-start | bytes 3538952 | tf_op jit(solution)/shard_map/ppermute | solution.py:233
  400.4 40.2 %collective-permute-start.55 = (bf16[768,768]{1,0:T(8,128)(2,1)}, bf16[768,768]{1,0:T(8,128)(2,1)}, u32[]{:S(2)}, u32[]{:S(2)}) collective-permute-start(bf16[768,768]{1,0:T(8,128)(2,1)} %shard_map.343.refs_2_), channel_id=1, source_target_pairs={{8,16},{16,8},{9,17},{17,9},{10,18},{18,10},{11,19},{19,11},{12,20... | collective-permute-start | bytes 3538952 | tf_op jit(solution)/shard_map/ppermute | solution.py:299
  445.9 31.9 %collective-permute-start.57 = (bf16[768,768]{1,0:T(8,128)(2,1)}, bf16[768,768]{1,0:T(8,128)(2,1)S(1)}, u32[]{:S(2)}, u32[]{:S(2)}) collective-permute-start(bf16[768,768]{1,0:T(8,128)(2,1)} %get-tuple-element.344), channel_id=1, source_target_pairs={{0,8},{8,0},{16,24},{24,16},{1,9},{9,1},{17,25},{25,17},{2,10},{10... | collective-permute-start | bytes 3538952 | tf_op jit(solution)/shard_map/ppermute | solution.py:233
  446.8 31.0 %collective-permute-start.58 = (bf16[768,768]{1,0:T(8,128)(2,1)}, bf16[768,768]{1,0:T(8,128)(2,1)S(1)}, u32[]{:S(2)}, u32[]{:S(2)}) collective-permute-start(bf16[768,768]{1,0:T(8,128)(2,1)} %get-tuple-element.334.refs_2_), channel_id=1, source_target_pairs={{8,16},{16,8},{9,17},{17,9},{10,18},{18,10},{11,19},{19,11},{12,20... | collective-permute-start | bytes 3538952 | tf_op jit(solution)/shard_map/ppermute | solution.py:299
  483.9 31.0 %collective-permute-start.61 = (bf16[768,768]{1,0:T(8,128)(2,1)}, bf16[768,768]{1,0:T(8,128)(2,1)S(1)}, u32[]{:S(2)}, u32[]{:S(2)}) collective-permute-start(bf16[768,768]{1,0:T(8,128)(2,1)} %get-tuple-element.354), channel_id=1, source_target_pairs={{0,8},{8,0},{16,24},{24,16},{1,9},{9,1},{17,25},{25,17},{2,10},{10... | collective-permute-start | bytes 3538952 | tf_op jit(solution)/shard_map/ppermute | solution.py:233
  488.5 26.4 %collective-permute-start.62 = (bf16[768,768]{1,0:T(8,128)(2,1)}, bf16[768,768]{1,0:T(8,128)(2,1)}, u32[]{:S(2)}, u32[]{:S(2)}) collective-permute-start(bf16[768,768]{1,0:T(8,128)(2,1)} %get-tuple-element.345.refs_2_), channel_id=1, source_target_pairs={{8,16},{16,8},{9,17},{17,9},{10,18},{18,10},{11,19},{19,11},{12,20... | collective-permute-start | bytes 3538952 | tf_op jit(solution)/shard_map/ppermute | solution.py:299
  496.4 42.7 %collective-permute-start.63 = (bf16[1216,768]{1,0:T(8,128)(2,1)}, bf16[1216,768]{1,0:T(8,128)(2,1)}, u32[]{:S(2)}, u32[]{:S(2)}) collective-permute-start(bf16[1216,768]{1,0:T(8,128)(2,1)} %bitcast.248), channel_id=1, source_target_pairs={{0,4},{2,6},{4,0},{6,2},{1,5},{3,7},{5,1},{7,3},{8,12},{10,14},{12... | collective-permute-start | bytes 5603336 | tf_op jit(solution)/shard_map/ppermute | solution.py:25
  520.1 37.7 %collective-permute-start.64 = (bf16[768,768]{1,0:T(8,128)(2,1)}, bf16[768,768]{1,0:T(8,128)(2,1)S(1)}, u32[]{:S(2)}, u32[]{:S(2)}) collective-permute-start(bf16[768,768]{1,0:T(8,128)(2,1)} %get-tuple-element.363), channel_id=1, source_target_pairs={{0,8},{8,0},{16,24},{24,16},{1,9},{9,1},{17,25},{25,17},{2,10},{10... | collective-permute-start | bytes 3538952 | tf_op jit(solution)/shard_map/ppermute | solution.py:233
  522.9 34.9 %collective-permute-start.65 = (bf16[768,768]{1,0:T(8,128)(2,1)}, bf16[768,768]{1,0:T(8,128)(2,1)S(1)}, u32[]{:S(2)}, u32[]{:S(2)}) collective-permute-start(bf16[768,768]{1,0:T(8,128)(2,1)} %get-tuple-element.355.refs_2_), channel_id=1, source_target_pairs={{8,16},{16,8},{9,17},{17,9},{10,18},{18,10},{11,19},{19,11},{12,20... | collective-permute-start | bytes 3538952 | tf_op jit(solution)/shard_map/ppermute | solution.py:299
  557.7 24.9 %collective-permute-start.66 = (bf16[2,3,384,768]{3,2,1,0:T(8,128)(2,1)}, bf16[2,3,384,768]{3,2,1,0:T(8,128)(2,1)}, u32[]{:S(2)}, u32[]{:S(2)}) collective-permute-start(bf16[2,3,384,768]{3,2,1,0:T(8,128)(2,1)} %get-tuple-element.372), channel_id=1, source_target_pairs={{0,2},{2,0},{4,6},{6,4},{1,3},{3,1},{5,7},{7,5},{8,10},{10,8},{12,... | collective-permute-start | bytes 10616840 | tf_op jit(solution)/shard_map/ppermute | solution.py:25
  573.8 47.6 %collective-permute-start.71 = (bf16[384,768]{1,0:T(8,128)(2,1)}, bf16[384,768]{1,0:T(8,128)(2,1)S(1)}, u32[]{:S(2)}, u32[]{:S(2)}) collective-permute-start(bf16[384,768]{1,0:T(8,128)(2,1)} %get-tuple-element.386), channel_id=1, source_target_pairs={{0,4},{2,6},{4,0},{6,2},{1,5},{3,7},{5,1},{7,3},{8,12},{10,14},{12... | collective-permute-start | bytes 1769480 | tf_op jit(solution)/shard_map/ppermute | solution.py:25
  574.9 30.6 %collective-permute-start.69 = (bf16[768,768]{1,0:T(8,128)(2,1)}, bf16[768,768]{1,0:T(8,128)(2,1)}, u32[]{:S(2)}, u32[]{:S(2)}) collective-permute-start(bf16[768,768]{1,0:T(8,128)(2,1)} %get-tuple-element.365.refs_2_), channel_id=1, source_target_pairs={{8,16},{16,8},{9,17},{17,9},{10,18},{18,10},{11,19},{19,11},{12,20... | collective-permute-start | bytes 3538952 | tf_op jit(solution)/shard_map/ppermute | solution.py:299
  576.6 28.9 %collective-permute-start.68 = (bf16[768,768]{1,0:T(8,128)(2,1)}, bf16[768,768]{1,0:T(8,128)(2,1)S(1)}, u32[]{:S(2)}, u32[]{:S(2)}) collective-permute-start(bf16[768,768]{1,0:T(8,128)(2,1)} %get-tuple-element.379), channel_id=1, source_target_pairs={{0,8},{8,0},{16,24},{24,16},{1,9},{9,1},{17,25},{25,17},{2,10},{10... | collective-permute-start | bytes 3538952 | tf_op jit(solution)/shard_map/ppermute | solution.py:233
  582.6 33.9 %collective-permute-start.70 = (bf16[384,768]{1,0:T(8,128)(2,1)}, bf16[384,768]{1,0:T(8,128)(2,1)}, u32[]{:S(2)}, u32[]{:S(2)}) collective-permute-start(bf16[384,768]{1,0:T(8,128)(2,1)} %get-tuple-element.383), channel_id=1, source_target_pairs={{0,4},{2,6},{4,0},{6,2},{1,5},{3,7},{5,1},{7,3},{8,12},{10,14},{12... | collective-permute-start | bytes 1769480 | tf_op jit(solution)/shard_map/ppermute | solution.py:25
  588.4 64.3 %collective-permute-start.74 = (bf16[512,1536]{1,0:T(8,128)(2,1)}, bf16[512,1536]{1,0:T(8,128)(2,1)}, u32[]{:S(2)}, u32[]{:S(2)}) collective-permute-start(bf16[512,1536]{1,0:T(8,128)(2,1)} %get-tuple-element.361), channel_id=1, source_target_pairs={{0,1},{1,0},{2,3},{3,2},{4,5},{5,4},{6,7},{7,6},{8,9},{9,8},{10,11... | collective-permute-start | bytes 4718600 | tf_op jit(solution)/shard_map/ppermute | solution.py:25
  610.7 27.5 %collective-permute-start.72 = (bf16[768,768]{1,0:T(8,128)(2,1)}, bf16[768,768]{1,0:T(8,128)(2,1)}, u32[]{:S(2)}, u32[]{:S(2)}) collective-permute-start(bf16[768,768]{1,0:T(8,128)(2,1)} %get-tuple-element.388), channel_id=1, source_target_pairs={{0,8},{8,0},{16,24},{24,16},{1,9},{9,1},{17,25},{25,17},{2,10},{10... | collective-permute-start | bytes 3538952 | tf_op jit(solution)/shard_map/ppermute | solution.py:233
  612.4 25.8 %collective-permute-start.73 = (bf16[768,768]{1,0:T(8,128)(2,1)}, bf16[768,768]{1,0:T(8,128)(2,1)}, u32[]{:S(2)}, u32[]{:S(2)}) collective-permute-start(bf16[768,768]{1,0:T(8,128)(2,1)} %get-tuple-element.380.refs_2_), channel_id=1, source_target_pairs={{8,16},{16,8},{9,17},{17,9},{10,18},{18,10},{11,19},{19,11},{12,20... | collective-permute-start | bytes 3538952 | tf_op jit(solution)/shard_map/ppermute | solution.py:299
  616.5 50.2 %collective-permute-start.76 = (bf16[1152,768]{1,0:T(8,128)(2,1)}, bf16[1152,768]{1,0:T(8,128)(2,1)}, u32[]{:S(2)}, u32[]{:S(2)}) collective-permute-start(bf16[1152,768]{1,0:T(8,128)(2,1)} %get-tuple-element.396), channel_id=1, source_target_pairs={{0,4},{2,6},{4,0},{6,2},{1,5},{3,7},{5,1},{7,3},{8,12},{10,14},{12... | collective-permute-start | bytes 5308424 | tf_op jit(solution)/shard_map/ppermute | solution.py:25
  621.4 39.0 %collective-permute-start.75 = (bf16[96,1536]{1,0:T(8,128)(2,1)S(1)}, bf16[96,1536]{1,0:T(8,128)(2,1)S(1)}, u32[]{:S(2)}, u32[]{:S(2)}) collective-permute-start(bf16[96,1536]{1,0:T(8,128)(2,1)S(1)} %copy-done.83), channel_id=1, source_target_pairs={{0,1},{1,0},{2,3},{3,2},{4,5},{5,4},{6,7},{7,6},{8,9},{9,8},{10,11... | collective-permute-start | bytes 884744 | tf_op jit(solution)/shard_map/ppermute | solution.py:25
  642.4 31.8 %collective-permute-start.77 = (bf16[768,768]{1,0:T(8,128)(2,1)}, bf16[768,768]{1,0:T(8,128)(2,1)S(1)}, u32[]{:S(2)}, u32[]{:S(2)}) collective-permute-start(bf16[768,768]{1,0:T(8,128)(2,1)} %get-tuple-element.399), channel_id=1, source_target_pairs={{0,8},{8,0},{16,24},{24,16},{1,9},{9,1},{17,25},{25,17},{2,10},{10... | collective-permute-start | bytes 3538952 | tf_op jit(solution)/shard_map/ppermute | solution.py:233
  646.0 31.0 %collective-permute-start.78 = (bf16[768,768]{1,0:T(8,128)(2,1)}, bf16[768,768]{1,0:T(8,128)(2,1)}, u32[]{:S(2)}, u32[]{:S(2)}) collective-permute-start(bf16[768,768]{1,0:T(8,128)(2,1)} %get-tuple-element.389.refs_2_), channel_id=1, source_target_pairs={{8,16},{16,8},{9,17},{17,9},{10,18},{18,10},{11,19},{19,11},{12,20... | collective-permute-start | bytes 3538952 | tf_op jit(solution)/shard_map/ppermute | solution.py:299
  652.6 41.4 %collective-permute-start.79 = (bf16[1152,768]{1,0:T(8,128)(2,1)}, bf16[1152,768]{1,0:T(8,128)(2,1)}, u32[]{:S(2)}, u32[]{:S(2)}) collective-permute-start(bf16[1152,768]{1,0:T(8,128)(2,1)} %get-tuple-element.403), channel_id=1, source_target_pairs={{0,4},{2,6},{4,0},{6,2},{1,5},{3,7},{5,1},{7,3},{8,12},{10,14},{12... | collective-permute-start | bytes 5308424 | tf_op jit(solution)/shard_map/ppermute | solution.py:25
  660.4 47.1 %collective-permute-start.82 = (bf16[512,1536]{1,0:T(8,128)(2,1)}, bf16[512,1536]{1,0:T(8,128)(2,1)}, u32[]{:S(2)}, u32[]{:S(2)}) collective-permute-start(bf16[512,1536]{1,0:T(8,128)(2,1)} %get-tuple-element.413), channel_id=1, source_target_pairs={{0,1},{1,0},{2,3},{3,2},{4,5},{5,4},{6,7},{7,6},{8,9},{9,8},{10,11... | collective-permute-start | bytes 4718600 | tf_op jit(solution)/shard_map/ppermute | solution.py:25
  666.7 48.9 %collective-permute-start.86 = (bf16[384,768]{1,0:T(8,128)(2,1)}, bf16[384,768]{1,0:T(8,128)(2,1)}, u32[]{:S(2)}, u32[]{:S(2)}) collective-permute-start(bf16[384,768]{1,0:T(8,128)(2,1)} %shard_map.361.refs_0_), channel_id=1, source_target_pairs={{0,8},{24,16},{1,9},{25,17},{2,10},{26,18},{3,11},{27,19},{4,12},{... | collective-permute-start | bytes 1769480 | tf_op jit(solution)/shard_map/ppermute | solution.py:233
  674.2 55.5 %collective-permute-start.87 = (bf16[384,768]{1,0:T(8,128)(2,1)S(1)}, bf16[384,768]{1,0:T(8,128)(2,1)}, u32[]{:S(2)}, u32[]{:S(2)}) collective-permute-start(bf16[384,768]{1,0:T(8,128)(2,1)S(1)} %copy-done.33), channel_id=1, source_target_pairs={{0,8},{24,16},{1,9},{25,17},{2,10},{26,18},{3,11},{27,19},{4,12},{... | collective-permute-start | bytes 1769480 | tf_op jit(solution)/shard_map/ppermute | solution.py:233
  700.2 28.1 %collective-permute-start.99 = (bf16[768,768]{1,0:T(8,128)(2,1)}, bf16[768,768]{1,0:T(8,128)(2,1)}, u32[]{:S(2)}, u32[]{:S(2)}) collective-permute-start(bf16[768,768]{1,0:T(8,128)(2,1)} %get-tuple-element.445), channel_id=1, source_target_pairs={{8,0},{16,24},{9,1},{17,25},{10,2},{18,26},{11,3},{19,27},{12,4},{... | collective-permute-start | bytes 3538952 | tf_op jit(solution)/shard_map/ppermute | solution.py:233
  724.1 57.1 %collective-permute-start.100 = (bf16[768,768]{1,0:T(8,128)(2,1)}, bf16[768,768]{1,0:T(8,128)(2,1)}, u32[]{:S(2)}, u32[]{:S(2)}) collective-permute-start(bf16[768,768]{1,0:T(8,128)(2,1)} %shard_map.369), channel_id=1, source_target_pairs={{8,0},{16,24},{9,1},{17,25},{10,2},{18,26},{11,3},{19,27},{12,4},{... | collective-permute-start | bytes 3538952 | tf_op jit(solution)/shard_map/ppermute | solution.py:233
  732.6 39.5 %collective-permute-start.89 = (bf16[384,768]{1,0:T(8,128)(2,1)}, bf16[384,768]{1,0:T(8,128)(2,1)S(1)}, u32[]{:S(2)}, u32[]{:S(2)}) collective-permute-start(bf16[384,768]{1,0:T(8,128)(2,1)} %get-tuple-element.424), channel_id=1, source_target_pairs={{0,8},{8,0},{16,24},{24,16},{1,9},{9,1},{17,25},{25,17},{2,10},{10... | collective-permute-start | bytes 1769480 | tf_op jit(solution)/shard_map/ppermute | solution.py:233
  739.4 32.7 %collective-permute-start.90 = (bf16[384,768]{1,0:T(8,128)(2,1)}, bf16[384,768]{1,0:T(8,128)(2,1)S(1)}, u32[]{:S(2)}, u32[]{:S(2)}) collective-permute-start(bf16[384,768]{1,0:T(8,128)(2,1)} %get-tuple-element.422.refs_2_), channel_id=1, source_target_pairs={{8,16},{16,8},{9,17},{17,9},{10,18},{18,10},{11,19},{19,11},{12,20... | collective-permute-start | bytes 1769480 | tf_op jit(solution)/shard_map/ppermute | solution.py:299
  741.1 37.8 %collective-permute-start.85 = (f32[1,25,1536]{2,1,0:T(8,128)S(1)}, f32[1,25,1536]{2,1,0:T(8,128)}, u32[]{:S(2)}, u32[]{:S(2)}) collective-permute-start(f32[1,25,1536]{2,1,0:T(8,128)S(1)} %add_bitcast_fusion), channel_id=1, source_target_pairs={{0,8},{8,0},{16,24},{24,16},{1,9},{9,1},{17,25},{25,17},{2,10},{10... | collective-permute-start | bytes 460808 | tf_op jit(solution)/shard_map/ppermute | solution.py:25
  780.6 40.2 %collective-permute-start.91 = (f32[2,25,1536]{2,1,0:T(8,128)}, f32[2,25,1536]{2,1,0:T(8,128)}, u32[]{:S(2)}, u32[]{:S(2)}) collective-permute-start(f32[2,25,1536]{2,1,0:T(8,128)} %pad_maximum_fusion.7), channel_id=1, source_target_pairs={{0,16},{8,24},{16,0},{24,8},{1,17},{9,25},{17,1},{25,9},{2,18},{10... | collective-permute-start | bytes 921608 | tf_op jit(solution)/shard_map/ppermute | solution.py:25
  822.1 24.2 %collective-permute-start.96 = (bf16[384,768]{1,0:T(8,128)(2,1)}, bf16[384,768]{1,0:T(8,128)(2,1)S(1)}, u32[]{:S(2)}, u32[]{:S(2)}) collective-permute-start(bf16[384,768]{1,0:T(8,128)(2,1)} %get-tuple-element.438), channel_id=1, source_target_pairs={{0,8},{8,0},{16,24},{24,16},{1,9},{9,1},{17,25},{25,17},{2,10},{10... | collective-permute-start | bytes 1769480 | tf_op jit(solution)/shard_map/ppermute | solution.py:233
  895.0 24.7 %collective-permute-start.106 = (bf16[384,768]{1,0:T(8,128)(2,1)}, bf16[384,768]{1,0:T(8,128)(2,1)S(1)}, u32[]{:S(2)}, u32[]{:S(2)}) collective-permute-start(bf16[384,768]{1,0:T(8,128)(2,1)} %shard_map.380), channel_id=1, source_target_pairs={{8,0},{16,24},{9,1},{17,25},{10,2},{18,26},{11,3},{19,27},{12,4},{... | collective-permute-start | bytes 1769480 | tf_op jit(solution)/shard_map/ppermute | solution.py:233
  (144 other events, 1348.3 us)

commit v6 on v5

--- a/solution.py
+++ b/solution.py
@@ -1183,12 +1183,14 @@
             image_qkv_parts,
         )
     )
-    image_blocks = gather_blocks(after(by_seq(image_qkv[1:]), *proj_held.values()), chips)
     text_qkv_parts, text_swapped = share_out(
         turn(text_w_qkv), text_own, text_held, (image_qkv,)
     )
     text_hid_one = flat(first_hidden(seq, text_mod, after(text_input, *proj_held.values())))
     text_qkv = project(spot, seq.then(text_hid_one), text_qkv_parts)
+    image_blocks = gather_blocks(
+        after(by_seq(image_qkv[1:]), *proj_held.values()), chips, (text_qkv,)
+    )
     text_blocks = gather_blocks(by_seq(text_qkv[1:]), chips)
     proj_own = flip(after(proj_stack, image_qkv), "tok", 1)
     seq.mark(text_qkv, proj_own)
@@ -1314,7 +1316,7 @@
         seq, core_sums_joined(seq, [made[2] for made in made_grads], moved_grads), chips
     )
     line.step()
-    tail = Line(seq)
+    tail, text_tail = Line(seq), Line(seq)
     block_grads = add_split(seq, *block_move, 2 * seqs, image_rows)
     proj_pairs = [chip_moves(seq, pieces, chips) for pieces in proj_pieces]
     image_in_part, image_qkv_keep, image_qkv_send = qkv_grads(
@@ -1355,8 +1357,10 @@
     line.step()
     text_qkv_shares = add_blocks(seq, *qkv_pairs[1], 3)
     line.step()
-    for part in [image_proj_share, text_proj_share, *image_qkv_shares, *text_qkv_shares]:
+    for part in (image_proj_share, *image_qkv_shares):
         tail.add(part)
+    for part in (text_proj_share, *text_qkv_shares):
+        text_tail.add(part)
     text_result, text_out_sums = results(
         seq, text_mod, text_input, text_branch, text_second, text_cot, text_real
     )
@@ -1365,7 +1369,11 @@
     )
     line.step()
     line_sums = line.finish()
+    for at in range(len(tail.chunks) + 1):
+        tail.step()
+        text_tail.step()
     tail_sums = tail.finish()
+    text_tail_sums = text_tail.finish()
     columns_of = lambda parts: jnp.concatenate(
         [
             column.astype(jnp.float32)
@@ -1380,9 +1388,9 @@
         line_sums = line_sums[4:]
     text_down_sum, text_up_sum = [columns_of([part]) for part in text_totals]
     image_down_sum, image_up_sum = columns_of(line_sums[:2]), columns_of(line_sums[2:])
-    image_proj_sum, text_proj_sum = tail_sums[:2]
-    image_qkv_sum = jnp.stack(tail_sums[2:5], axis=1)
-    text_qkv_sum = jnp.stack(tail_sums[5:], axis=1)
+    image_proj_sum, text_proj_sum = tail_sums[0], text_tail_sums[0]
+    image_qkv_sum = jnp.stack(tail_sums[1:], axis=1)
+    text_qkv_sum = jnp.stack(text_tail_sums[1:], axis=1)
 
     early = jnp.stack(
         [
@@ -1403,7 +1411,7 @@
     )
     waits = []
     if line.on_line:
-        waits = [tail.totals[1], tail.totals[3]]
+        waits = [tail.totals[0], tail.totals[2]]
     all_sums = rep_gather(tok_total(all_sums), waits)
     square_total = jnp.sum(all_sums[:, -1, :10], axis=0)
     early_table = jnp.moveaxis(

time: 933 us -> 912 us (0.977)
  waiting for transfers between devices: 296 us -> 275 us
    ppermute x20 -> x22, waiting for transfers between devices: 118 us -> 81.9 us  [outer(): return lax.ppermute(load, 'rep', pairs)]
    ppermute x71, waiting for transfers between devices: 178 us -> 193 us  [flip(): lax.ppermute(values, axis, [(place, place ^ bit) for place in range(lax.a...]
    unnamed x208 -> x192, local copies, waits for them, and re-layouts: 27.9 us -> 24.9 us
    ppermute x20 -> x22, starting transfers between devices: 56.9 us -> 54.2 us  [outer(): return lax.ppermute(load, 'rep', pairs)]
    pallas_call x18 -> x19, Pallas kernels: 57.8 us -> 58.6 us  [step(): pl.pallas_call(kernel, grid=(2,), in_specs=[pl.BlockSpec(memory_space=plt...]
  transfers between devices with their start and end apart: 107 -> 109, of which waited for: 34 -> 33; matrix products, arithmetic and copies ran while one was open for 12% -> 12% of each run, Pallas kernels for 37% -> 38%
where the time goes in v6:
time: 912 us; the launch traced here: 901 us
  Pallas kernels  358 us (39%)
  waiting for transfers between devices  275 us (30%)
  starting transfers between devices  128 us (14%)
  local copies, waits for them, and re-layouts  56.6 us (6%)
  other arithmetic  42.6 us (5%)
  matrix products  38.8 us (4%)
    ppermute x71, waiting for transfers between devices, flip(): lax.ppermute(values, axis, [(place, place ^ bit) for place in range(lax.a...  193 us
    pallas_call x11, Pallas kernels, call(): pl.pallas_call(kernel, grid=(tiles,), in_specs=[pl.BlockSpec(memory_space...  112 us
    ppermute x22, waiting for transfers between devices, outer(): return lax.ppermute(load, 'rep', pairs)  81.9 us
    pallas_call x19, Pallas kernels, step(): pl.pallas_call(kernel, grid=(2,), in_specs=[pl.BlockSpec(memory_space=plt...  58.6 us
    ppermute x22, starting transfers between devices, outer(): return lax.ppermute(load, 'rep', pairs)  54.2 us
    pallas_call x2, Pallas kernels, attend_grads(): pl.pallas_call(kernel, grid=(width // LANES,), in_specs=[row_spec(length,...  53.4 us
    ppermute x71, starting transfers between devices, flip(): lax.ppermute(values, axis, [(place, place ^ bit) for place in range(lax.a...  48.5 us
    pallas_call x13, Pallas kernels, add_blocks(): pl.pallas_call(kernel, grid=(2,), in_specs=[in_spec, in_spec], out_specs=...  46.5 us
  transfers between devices with their start and end apart: 109, of which 33 were waited for; matrix products, arithmetic and copies ran while one was open for 12% of the time, Pallas kernels for 38%

profile of v6, /device:TPU:0, one launch (start us, length us, event | category | flops | bytes accessed | tf_op | source)
XLA Modules:
  0.0 901.1 jit_solution(10390722128210562001)
XLA Ops:
  6.7 4.2 fusion.46
  14.5 11.4 %collective-permute-done.1.rest_1_.rest_5_ = bf16[3,192,768]{2,1,0:T(8,128)(2,1)} collective-permute-done((bf16[3,192,768]{2,1,0:T(8,128)(2,1)}, bf16[3,192,768]{2,1,0:T(8,128)(2,1)}, u32[]{:S(2)}, u32[]{:S(2)}) %collective-permute-start.1) | collective-permute-done | bytes 884768 | tf_op jit(solution)/shard_map/ppermute | solution.py:25
  27.6 4.3 collective-permute-done.2
  32.1 4.5 collective-permute-done.4.rest_3_
  41.0 18.0 %collective-permute-done.6.rest_2_.rest_6_ = bf16[3,192,768]{2,1,0:T(8,128)(2,1)} collective-permute-done((bf16[3,192,768]{2,1,0:T(8,128)(2,1)}, bf16[3,192,768]{2,1,0:T(8,128)(2,1)}, u32[]{:S(2)}, u32[]{:S(2)}) %collective-permute-start.6) | collective-permute-done | bytes 884768 | tf_op jit(solution)/shard_map/ppermute | solution.py:25
  69.8 8.3 shard_map.323
  81.3 6.7 collective-permute-done.11.rest_2_.rest_6_
  94.1 5.7 shard_map.325
  99.8 16.7 %collective-permute-done.17.rest_4_.rest_6_ = bf16[2,2,256,768]{3,2,1,0:T(8,128)(2,1)} collective-permute-done((bf16[2,2,256,768]{3,2,1,0:T(8,128)(2,1)S(1)}, bf16[2,2,256,768]{3,2,1,0:T(8,128)(2,1)}, u32[]{:S(2)}, u32[]{:S(2)}) %collective-permute-start.17) | collective-permute-done | bytes 1572896 | tf_op jit(solution)/shard_map/ppermute | solution.py:25
  121.9 5.4 collective-permute-done.20.rest_8_.rest_10_
  136.5 25.8 %shard_map.326 = (bf16[2,256,768]{2,1,0:T(8,128)(2,1)}, bf16[2,48,768]{2,1,0:T(8,128)(2,1)}) custom-call(bf16[2,256,768]{2,1,0:T(8,128)(2,1)} %bitcast.172, bf16[2,48,768]{2,1,0:T(8,128)(2,1)} %bitcast.218, bf16[2,2,256,768]{3,2,1,0:T(8,128)(2,1)} %bitcast.161, bf16[2,2,256,768]{3,2,1,0:T(8,128)(2,1)} %collective-permute-done.16.rest_3_.rest_5_, ...), custom_call_target="tpu_custom_call" | custom-call | flops 1024 | bytes 1024 | tf_op jit(solution)/shard_map/pallas_call | solution.py:1003
  169.2 5.0 shard_map.328
  185.1 27.5 %collective-permute-done.28 = bf16[512,1536]{1,0:T(8,128)(2,1)S(1)} collective-permute-done((bf16[512,1536]{1,0:T(8,128)(2,1)}, bf16[512,1536]{1,0:T(8,128)(2,1)S(1)}, u32[]{:S(2)}, u32[]{:S(2)}) %collective-permute-start.28) | collective-permute-done | bytes 1572896 | tf_op jit(solution)/shard_map/ppermute | solution.py:25
  213.8 4.8 shard_map.330
  218.7 12.1 %collective-permute-done.29.rest_2_ = bf16[192,3072]{1,0:T(8,128)(2,1)} collective-permute-done((bf16[192,3072]{1,0:T(8,128)(2,1)}, bf16[192,3072]{1,0:T(8,128)(2,1)}, u32[]{:S(2)}, u32[]{:S(2)}) %collective-permute-start.29) | collective-permute-done | bytes 1179680 | tf_op jit(solution)/shard_map/ppermute | solution.py:25
  232.2 8.5 shard_map.331
  241.8 6.2 collective-permute-done.34
  254.1 40.1 %shard_map.333 = (bf16[512,1536]{1,0:T(8,128)(2,1)}, bf16[512,1536]{1,0:T(8,128)(2,1)}, bf16[2,4,384,768]{3,2,1,0:T(8,128)(2,1)}, bf16[2,4,384,768]{3,2,1,0:T(8,...) custom-call(s32[2]{0:T(128)} %pad_add_fusion.spot_ref, bf16[512,1536]{1,0:T(8,128)(2,1)} %bitcast.227, ...), custom_call_target="tpu_custom_call" | custom-call | flops 1024 | bytes 1024 | tf_op jit(solution)/shard_map/pallas_call | solution.py:426
  301.6 5.3 collective-permute-done.40
  306.9 5.6 shard_map.335
  315.3 5.6 shard_map.336
  321.0 6.4 collective-permute-done.43.rest_6_
  330.3 11.0 %shard_map.337 = (bf16[2,96,384]{2,1,0:T(8,128)(2,1)}, bf16[2,96,384]{2,1,0:T(8,128)(2,1)}, bf16[2,96,384]{2,1,0:T(8,128)(2,1)}, bf16[2,96,384]{2,1,0:T(8,128)(2...) custom-call(s32[2]{0:T(128)} %pad_add_fusion.spot_ref, bf16[384,3072]{1,0:T(8,128)(2,1)} %up_ref.3, ...), custom_call_target="tpu_custom_call" | custom-call | flops 1024 | bytes 1024 | tf_op jit(solution)/shard_map/pallas_call | solution.py:426
  345.0 8.2 shard_map.338
  353.2 4.7 collective-permute-start.50
  362.2 6.7 shard_map.340
  370.5 7.9 collective-permute-done.49
  382.0 5.1 shard_map.342
  402.1 26.7 %shard_map.346 = (bf16[1,256,768]{2,1,0:T(8,128)(2,1)}, bf16[1,48,768]{2,1,0:T(8,128)(2,1)}, bf16[2,2,304,768]{3,2,1,0:T(8,128)(2,1)}, bf16[2,2,304,768]{3,2,1,0:T(8,128)(2,1)}) custom-call(bf16[2,256,768]{2,1,0:T(8,128)(2,1)} %bitcast.173, bf16[2,48,768]{2,1,0:T(8,128)(2,1)} %bitcast.219, bf16[2,256,768]{2,1,0:T(8,128)(2,1)} %bitcast.203, ...), custom_call_target="tpu_custom_call" | custom-call | flops 1024 | bytes 1024 | tf_op jit(solution)/shard_map/pallas_call | solution.py:1074
  433.3 4.2 shard_map.348
  438.3 26.7 %shard_map.349 = (bf16[1,256,768]{2,1,0:T(8,128)(2,1)}, bf16[1,48,768]{2,1,0:T(8,128)(2,1)}, bf16[2,2,304,768]{3,2,1,0:T(8,128)(2,1)}, bf16[2,2,304,768]{3,2,1,0:T(8,128)(2,1)}) custom-call(bf16[2,256,768]{2,1,0:T(8,128)(2,1)} %bitcast.174, bf16[2,48,768]{2,1,0:T(8,128)(2,1)} %bitcast.220, bf16[2,256,768]{2,1,0:T(8,128)(2,1)} %bitcast.204, ...), custom_call_target="tpu_custom_call" | custom-call | flops 1024 | bytes 1024 | tf_op jit(solution)/shard_map/pallas_call | solution.py:1074
  470.2 4.2 shard_map.351
  474.7 4.6 collective-permute-start.61
  482.4 4.8 shard_map.352
  488.2 17.5 %collective-permute-done.61.refs_1_ = bf16[768,768]{1,0:T(8,128)(2,1)S(1)} collective-permute-done((bf16[768,768]{1,0:T(8,128)(2,1)}, bf16[768,768]{1,0:T(8,128)(2,1)S(1)}, u32[]{:S(2)}, u32[]{:S(2)}) %collective-permute-start.61) | collective-permute-done | bytes 1179680 | tf_op jit(solution)/shard_map/ppermute | solution.py:233
  506.7 4.2 shard_map.353
  515.4 14.4 %collective-permute-done.63 = bf16[1216,768]{1,0:T(8,128)(2,1)S(1)} collective-permute-done((bf16[1216,768]{1,0:T(8,128)(2,1)}, bf16[1216,768]{1,0:T(8,128)(2,1)S(1)}, u32[]{:S(2)}, u32[]{:S(2)}) %collective-permute-start.63) | collective-permute-done | bytes 1867808 | tf_op jit(solution)/shard_map/ppermute | solution.py:25
  535.2 14.4 %shard_map.355 = (bf16[512,1536]{1,0:T(8,128)(2,1)}, bf16[2,3,384,768]{3,2,1,0:T(8,128)(2,1)}, bf16[2,3,384,768]{3,2,1,0:T(8,128)(2,1)}) custom-call(s32[2]{0:T(128)} %pad_add_fusion.spot_ref, bf16[512,1536]{1,0:T(8,128)(2,1)} %bitcast.171, bf16[1,256,768]{2,1,0:T(8,128)(2,1)} %get-tuple-element.326.rest_0_, ...), custom_call_target="tpu_custom_call" | custom-call | flops 1024 | bytes 1024 | tf_op jit(solution)/shard_map/pallas_call | solution.py:426
  550.6 4.2 shard_map.356
  554.9 9.7 %shard_map.357 = (bf16[96,1536]{1,0:T(8,128)(2,1)}, bf16[2,3,384,768]{3,2,1,0:T(8,128)(2,1)}, bf16[2,3,384,768]{3,2,1,0:T(8,128)(2,1)}) custom-call(s32[2]{0:T(128)} %pad_add_fusion.spot_ref, bf16[96,1536]{1,0:T(8,128)(2,1)} %bitcast.206, bf16[1,48,768]{2,1,0:T(8,128)(2,1)} %get-tuple-element.366.rest_0_, bf16[1,48,768]{2,1,0:T(8,128)(2,1)} %get-tuple-element.367.rest_1_, ...), custom_call_target="tpu_custom_call" | custom-call | flops 1024 | bytes 1024 | tf_op jit(solution)/shard_map/pallas_call | solution.py:426
  575.8 4.6 shard_map.358
  580.4 4.6 shard_map.359
  585.0 12.1 %collective-permute-done.68.refs_1_ = bf16[768,768]{1,0:T(8,128)(2,1)} collective-permute-done((bf16[768,768]{1,0:T(8,128)(2,1)}, bf16[768,768]{1,0:T(8,128)(2,1)}, u32[]{:S(2)}, u32[]{:S(2)}) %collective-permute-start.68) | collective-permute-done | bytes 1179680 | tf_op jit(solution)/shard_map/ppermute | solution.py:233
  597.1 4.2 shard_map.360
  604.8 4.6 pad_maximum_fusion.3
  620.1 8.3 collective-permute-done.72.refs_1_
  628.4 4.3 shard_map.363
  641.3 5.7 collective-permute-done.74
  648.1 5.7 shard_map.364
  659.4 5.0 collective-permute-start.86
  678.3 9.5 %collective-permute-done.79 = bf16[1152,768]{1,0:T(8,128)(2,1)S(1)} collective-permute-done((bf16[1152,768]{1,0:T(8,128)(2,1)}, bf16[1152,768]{1,0:T(8,128)(2,1)S(1)}, u32[]{:S(2)}, u32[]{:S(2)}) %collective-permute-start.79) | collective-permute-done | bytes 1769504 | tf_op jit(solution)/shard_map/ppermute | solution.py:25
  687.8 4.7 collective-permute-start.87
  704.2 5.9 shard_map.371
  721.2 7.4 collective-permute-start.91
  738.7 4.4 pad_maximum_fusion.1
  753.4 15.6 %collective-permute-done.85 = f32[1,25,1536]{2,1,0:T(8,128)S(1)} collective-permute-done((f32[1,25,1536]{2,1,0:T(8,128)S(1)}, f32[1,25,1536]{2,1,0:T(8,128)S(1)}, u32[]{:S(2)}, u32[]{:S(2)}) %collective-permute-start.85) | collective-permute-done | bytes 153632 | tf_op jit(solution)/shard_map/ppermute | solution.py:25
  774.6 7.0 collective-permute-done.93.refs_1_
  786.8 14.6 %collective-permute-done.95.refs_1_ = bf16[384,768]{1,0:T(8,128)(2,1)S(1)} collective-permute-done((bf16[384,768]{1,0:T(8,128)(2,1)}, bf16[384,768]{1,0:T(8,128)(2,1)S(1)}, u32[]{:S(2)}, u32[]{:S(2)}) %collective-permute-start.95) | collective-permute-done | bytes 589856 | tf_op jit(solution)/shard_map/ppermute | solution.py:233
  827.0 7.3 fusion.2
  834.4 7.7 convolution_bitcast_fusion.1
  842.0 7.4 fusion.5
  854.8 7.7 fusion
  876.6 14.8 %collective-permute-done.108 = bf16[384,768]{1,0:T(8,128)(2,1)S(1)} collective-permute-done((bf16[384,768]{1,0:T(8,128)(2,1)}, bf16[384,768]{1,0:T(8,128)(2,1)S(1)}, u32[]{:S(2)}, u32[]{:S(2)}) %collective-permute-start.108) | collective-permute-done | bytes 589856 | tf_op jit(solution)/shard_map/ppermute | solution.py:233
  893.5 4.9 collective-permute-done.103
  (505 shorter events, 303.2 us)
Async XLA Ops:
  36.6 29.3 %collective-permute-start.5 = (bf16[384,3072]{1,0:T(8,128)(2,1)}, bf16[384,3072]{1,0:T(8,128)(2,1)}, u32[]{:S(2)}, u32[]{:S(2)}) collective-permute-start(bf16[384,3072]{1,0:T(8,128)(2,1)} %rest_6_.1), channel_id=1, source_target_pairs={{0,2},{2,0},{4,6},{6,4},{1,3},{3,1},{5,7},{7,5},{8,10},{10,8},{12,... | collective-permute-start | bytes 7077896 | tf_op jit(solution)/shard_map/ppermute | solution.py:25
  38.2 31.6 %collective-permute-start.7 = (bf16[3,384,768]{2,1,0:T(8,128)(2,1)S(1)}, bf16[3,384,768]{2,1,0:T(8,128)(2,1)}, u32[]{:S(2)}, u32[]{:S(2)}) collective-permute-start(bf16[3,384,768]{2,1,0:T(8,128)(2,1)S(1)} %bitcast.177), channel_id=1, source_target_pairs={{0,2},{2,0},{4,6},{6,4},{1,3},{3,1},{5,7},{7,5},{8,10},{10,8},{12,... | collective-permute-start | bytes 5308424 | tf_op jit(solution)/shard_map/ppermute | solution.py:25
  61.6 27.3 %collective-permute-start.12 = (bf16[3,384,768]{2,1,0:T(8,128)(2,1)}, bf16[3,384,768]{2,1,0:T(8,128)(2,1)}, u32[]{:S(2)}, u32[]{:S(2)}) collective-permute-start(bf16[3,384,768]{2,1,0:T(8,128)(2,1)} %bitcast.178), channel_id=1, source_target_pairs={{0,2},{2,0},{4,6},{6,4},{1,3},{3,1},{5,7},{7,5},{8,10},{10,8},{12,... | collective-permute-start | bytes 5308424 | tf_op jit(solution)/shard_map/ppermute | solution.py:25
  79.8 36.7 %collective-permute-start.17 = (bf16[2,2,256,768]{3,2,1,0:T(8,128)(2,1)S(1)}, bf16[2,2,256,768]{3,2,1,0:T(8,128)(2,1)}, u32[]{:S(2)}, u32[]{:S(2)}) collective-permute-start(bf16[2,2,256,768]{3,2,1,0:T(8,128)(2,1)S(1)} %bitcast.159), channel_id=1, source_target_pairs={{0,4},{2,6},{4,0},{6,2},{1,5},{3,7},{5,1},{7,3},{8,12},{10,14},{12... | collective-permute-start | bytes 4718600 | tf_op jit(solution)/shard_map/ppermute | solution.py:25
  88.6 38.7 %collective-permute-start.15 = (bf16[2,384,768]{2,1,0:T(8,128)(2,1)S(1)}, bf16[2,384,768]{2,1,0:T(8,128)(2,1)}, u32[]{:S(2)}, u32[]{:S(2)}) collective-permute-start(bf16[2,384,768]{2,1,0:T(8,128)(2,1)S(1)} %pad_maximum_fusion.4.rest_0_), channel_id=1, source_target_pairs={{0,2},{2,0},{4,6},{6,4},{1,3},{3,1},{5,7},{7,5},{8,10},{10,8},{12,... | collective-permute-start | bytes 3538952 | tf_op jit(solution)/shard_map/ppermute | solution.py:25
  88.9 43.1 %collective-permute-start.16 = (bf16[2,2,256,768]{3,2,1,0:T(8,128)(2,1)S(1)}, bf16[2,2,256,768]{3,2,1,0:T(8,128)(2,1)}, u32[]{:S(2)}, u32[]{:S(2)}) collective-permute-start(bf16[2,2,256,768]{3,2,1,0:T(8,128)(2,1)S(1)} %bitcast.160), channel_id=1, source_target_pairs={{0,2},{2,0},{4,6},{6,4},{1,3},{3,1},{5,7},{7,5},{8,10},{10,8},{12,... | collective-permute-start | bytes 4718600 | tf_op jit(solution)/shard_map/ppermute | solution.py:25
  90.8 30.1 %collective-permute-start.23 = (bf16[1,384,768]{2,1,0:T(8,128)(2,1)}, bf16[1,384,768]{2,1,0:T(8,128)(2,1)}, u32[]{:S(2)}, u32[]{:S(2)}) collective-permute-start(bf16[1,384,768]{2,1,0:T(8,128)(2,1)} %collective-permute-done.10.rest_1_), channel_id=1, source_target_pairs={{0,8},{8,0},{16,24},{24,16},{1,9},{9,1},{17,25},{25,17},{2,10},{10... | collective-permute-start | bytes 1769480 | tf_op jit(solution)/shard_map/ppermute | solution.py:25
  120.8 41.5 %collective-permute-start.22 = (bf16[192,3072]{1,0:T(8,128)(2,1)}, bf16[192,3072]{1,0:T(8,128)(2,1)}, u32[]{:S(2)}, u32[]{:S(2)}) collective-permute-start(bf16[192,3072]{1,0:T(8,128)(2,1)} %constant_dynamic-slice_fusion.5), channel_id=1, source_target_pairs={{0,4},{2,6},{4,0},{6,2},{1,5},{3,7},{5,1},{7,3},{8,12},{10,14},{12... | collective-permute-start | bytes 3538952 | tf_op jit(solution)/shard_map/ppermute | solution.py:25
  129.0 33.3 %collective-permute-start.25 = (bf16[1,384,768]{2,1,0:T(8,128)(2,1)}, bf16[1,384,768]{2,1,0:T(8,128)(2,1)S(1)}, u32[]{:S(2)}, u32[]{:S(2)}) collective-permute-start(bf16[1,384,768]{2,1,0:T(8,128)(2,1)} %collective-permute-done.23.rest_2_), channel_id=1, source_target_pairs={{0,2},{2,0},{4,6},{6,4},{1,3},{3,1},{5,7},{7,5},{8,10},{10,8},{12,... | collective-permute-start | bytes 1769480 | tf_op jit(solution)/shard_map/ppermute | solution.py:25
  129.3 33.0 %collective-permute-start.24 = (bf16[1,384,768]{2,1,0:T(8,128)(2,1)}, bf16[1,384,768]{2,1,0:T(8,128)(2,1)S(1)}, u32[]{:S(2)}, u32[]{:S(2)}) collective-permute-start(bf16[1,384,768]{2,1,0:T(8,128)(2,1)} %collective-permute-done.10.rest_1_), channel_id=1, source_target_pairs={{0,2},{2,0},{4,6},{6,4},{1,3},{3,1},{5,7},{7,5},{8,10},{10,8},{12,... | collective-permute-start | bytes 1769480 | tf_op jit(solution)/shard_map/ppermute | solution.py:25
  131.9 46.4 %collective-permute-start.26 = (bf16[192,3072]{1,0:T(8,128)(2,1)}, bf16[192,3072]{1,0:T(8,128)(2,1)}, u32[]{:S(2)}, u32[]{:S(2)}) collective-permute-start(bf16[192,3072]{1,0:T(8,128)(2,1)} %constant_dynamic-slice_fusion.4), channel_id=1, source_target_pairs={{0,4},{2,6},{4,0},{6,2},{1,5},{3,7},{5,1},{7,3},{8,12},{10,14},{12... | collective-permute-start | bytes 3538952 | tf_op jit(solution)/shard_map/ppermute | solution.py:25
  176.8 35.8 %collective-permute-start.28 = (bf16[512,1536]{1,0:T(8,128)(2,1)}, bf16[512,1536]{1,0:T(8,128)(2,1)S(1)}, u32[]{:S(2)}, u32[]{:S(2)}) collective-permute-start(bf16[512,1536]{1,0:T(8,128)(2,1)} %shard_map.328), channel_id=1, source_target_pairs={{0,1},{1,0},{2,3},{3,2},{4,5},{5,4},{6,7},{7,6},{8,9},{9,8},{10,11... | collective-permute-start | bytes 4718600 | tf_op jit(solution)/shard_map/ppermute | solution.py:25
  178.3 40.3 %collective-permute-start.30 = (bf16[192,3072]{1,0:T(8,128)(2,1)}, bf16[192,3072]{1,0:T(8,128)(2,1)S(1)}, u32[]{:S(2)}, u32[]{:S(2)}) collective-permute-start(bf16[192,3072]{1,0:T(8,128)(2,1)} %collective-permute-done.26.rest_7_), channel_id=1, source_target_pairs={{0,8},{8,0},{16,24},{24,16},{1,9},{9,1},{17,25},{25,17},{2,10},{10... | collective-permute-start | bytes 3538952 | tf_op jit(solution)/shard_map/ppermute | solution.py:25
  179.6 51.2 %collective-permute-start.29 = (bf16[192,3072]{1,0:T(8,128)(2,1)}, bf16[192,3072]{1,0:T(8,128)(2,1)}, u32[]{:S(2)}, u32[]{:S(2)}) collective-permute-start(bf16[192,3072]{1,0:T(8,128)(2,1)} %collective-permute-done.22.rest_1_), channel_id=1, source_target_pairs={{0,8},{8,0},{16,24},{24,16},{1,9},{9,1},{17,25},{25,17},{2,10},{10... | collective-permute-start | bytes 3538952 | tf_op jit(solution)/shard_map/ppermute | solution.py:25
  183.9 46.9 %collective-permute-start.31 = (bf16[2,96,384]{2,1,0:T(8,128)(2,1)}, bf16[2,96,384]{2,1,0:T(8,128)(2,1)S(1)}, u32[]{:S(2)}, u32[]{:S(2)}) collective-permute-start(bf16[2,96,384]{2,1,0:T(8,128)(2,1)} %bitcast.256), channel_id=1, source_target_pairs={{0,2},{2,0},{4,6},{6,4},{1,3},{3,1},{5,7},{7,5},{8,10},{10,8},{12,... | collective-permute-start | bytes 442376 | tf_op jit(solution)/shard_map/ppermute | solution.py:25
  183.9 46.9 %collective-permute-start.32 = (bf16[2,96,384]{2,1,0:T(8,128)(2,1)}, bf16[2,96,384]{2,1,0:T(8,128)(2,1)S(1)}, u32[]{:S(2)}, u32[]{:S(2)}) collective-permute-start(bf16[2,96,384]{2,1,0:T(8,128)(2,1)} %bitcast.255), channel_id=1, source_target_pairs={{0,4},{2,6},{4,0},{6,2},{1,5},{3,7},{5,1},{7,3},{8,12},{10,14},{12... | collective-permute-start | bytes 442376 | tf_op jit(solution)/shard_map/ppermute | solution.py:25
  253.0 41.2 %collective-permute-start.39 = (bf16[768,768]{1,0:T(8,128)(2,1)}, bf16[768,768]{1,0:T(8,128)(2,1)S(1)}, u32[]{:S(2)}, u32[]{:S(2)}) collective-permute-start(bf16[768,768]{1,0:T(8,128)(2,1)} %get-tuple-element.286), channel_id=1, source_target_pairs={{0,4},{2,6},{4,0},{6,2},{1,5},{3,7},{5,1},{7,3},{8,12},{10,14},{12... | collective-permute-start | bytes 3538952 | tf_op jit(solution)/shard_map/ppermute | solution.py:25
  299.1 28.2 %collective-permute-start.43 = (bf16[2,384,768]{2,1,0:T(8,128)(2,1)}, bf16[2,384,768]{2,1,0:T(8,128)(2,1)S(1)}, u32[]{:S(2)}, u32[]{:S(2)}) collective-permute-start(bf16[2,384,768]{2,1,0:T(8,128)(2,1)} %shard_map.334.rest_4_), channel_id=1, source_target_pairs={{0,4},{2,6},{4,0},{6,2},{1,5},{3,7},{5,1},{7,3},{8,12},{10,14},{12... | collective-permute-start | bytes 3538952 | tf_op jit(solution)/shard_map/ppermute | solution.py:25
  300.1 44.9 %collective-permute-start.45 = (bf16[512,1536]{1,0:T(8,128)(2,1)}, bf16[512,1536]{1,0:T(8,128)(2,1)}, u32[]{:S(2)}, u32[]{:S(2)}) collective-permute-start(bf16[512,1536]{1,0:T(8,128)(2,1)} %get-tuple-element.300), channel_id=1, source_target_pairs={{0,1},{1,0},{2,3},{3,2},{4,5},{5,4},{6,7},{7,6},{8,9},{9,8},{10,11... | collective-permute-start | bytes 4718600 | tf_op jit(solution)/shard_map/ppermute | solution.py:25
  301.6 25.7 %collective-permute-start.42 = (bf16[2,384,768]{2,1,0:T(8,128)(2,1)}, bf16[2,384,768]{2,1,0:T(8,128)(2,1)S(1)}, u32[]{:S(2)}, u32[]{:S(2)}) collective-permute-start(bf16[2,384,768]{2,1,0:T(8,128)(2,1)} %shard_map.334.rest_4_), channel_id=1, source_target_pairs={{0,2},{2,0},{4,6},{6,4},{1,3},{3,1},{5,7},{7,5},{8,10},{10,8},{12,... | collective-permute-start | bytes 3538952 | tf_op jit(solution)/shard_map/ppermute | solution.py:25
  353.2 35.0 %collective-permute-start.50 = (bf16[768,768]{1,0:T(8,128)(2,1)S(1)}, bf16[768,768]{1,0:T(8,128)(2,1)}, u32[]{:S(2)}, u32[]{:S(2)}) collective-permute-start(bf16[768,768]{1,0:T(8,128)(2,1)S(1)} %bitcast.194), channel_id=1, source_target_pairs={{0,8},{24,16},{1,9},{25,17},{2,10},{26,18},{3,11},{27,19},{4,12},{... | collective-permute-start | bytes 3538952 | tf_op jit(solution)/shard_map/ppermute | solution.py:233
  357.9 70.8 %collective-permute-start.53 = (bf16[1536,768]{1,0:T(8,128)(2,1)}, bf16[1536,768]{1,0:T(8,128)(2,1)}, u32[]{:S(2)}, u32[]{:S(2)}) collective-permute-start(bf16[1536,768]{1,0:T(8,128)(2,1)} %get-tuple-element.329), channel_id=1, source_target_pairs={{0,4},{2,6},{4,0},{6,2},{1,5},{3,7},{5,1},{7,3},{8,12},{10,14},{12... | collective-permute-start | bytes 7077896 | tf_op jit(solution)/shard_map/ppermute | solution.py:25
  387.1 77.9 %collective-permute-start.56 = (bf16[1536,768]{1,0:T(8,128)(2,1)}, bf16[1536,768]{1,0:T(8,128)(2,1)}, u32[]{:S(2)}, u32[]{:S(2)}) collective-permute-start(bf16[1536,768]{1,0:T(8,128)(2,1)} %get-tuple-element.338), channel_id=1, source_target_pairs={{0,4},{2,6},{4,0},{6,2},{1,5},{3,7},{5,1},{7,3},{8,12},{10,14},{12... | collective-permute-start | bytes 7077896 | tf_op jit(solution)/shard_map/ppermute | solution.py:25
  388.2 44.1 %collective-permute-start.54 = (bf16[768,768]{1,0:T(8,128)(2,1)S(1)}, bf16[768,768]{1,0:T(8,128)(2,1)S(1)}, u32[]{:S(2)}, u32[]{:S(2)}) collective-permute-start(bf16[768,768]{1,0:T(8,128)(2,1)S(1)} %bitcast.192), channel_id=1, source_target_pairs={{0,8},{24,16},{1,9},{25,17},{2,10},{26,18},{3,11},{27,19},{4,12},{... | collective-permute-start | bytes 3538952 | tf_op jit(solution)/shard_map/ppermute | solution.py:233
  392.1 40.2 %collective-permute-start.55 = (bf16[768,768]{1,0:T(8,128)(2,1)}, bf16[768,768]{1,0:T(8,128)(2,1)}, u32[]{:S(2)}, u32[]{:S(2)}) collective-permute-start(bf16[768,768]{1,0:T(8,128)(2,1)} %shard_map.343.refs_2_), channel_id=1, source_target_pairs={{8,16},{16,8},{9,17},{17,9},{10,18},{18,10},{11,19},{19,11},{12,20... | collective-permute-start | bytes 3538952 | tf_op jit(solution)/shard_map/ppermute | solution.py:299
  437.6 31.3 %collective-permute-start.57 = (bf16[768,768]{1,0:T(8,128)(2,1)}, bf16[768,768]{1,0:T(8,128)(2,1)S(1)}, u32[]{:S(2)}, u32[]{:S(2)}) collective-permute-start(bf16[768,768]{1,0:T(8,128)(2,1)} %get-tuple-element.343), channel_id=1, source_target_pairs={{0,8},{8,0},{16,24},{24,16},{1,9},{9,1},{17,25},{25,17},{2,10},{10... | collective-permute-start | bytes 3538952 | tf_op jit(solution)/shard_map/ppermute | solution.py:233
  437.6 31.3 %collective-permute-start.58 = (bf16[768,768]{1,0:T(8,128)(2,1)}, bf16[768,768]{1,0:T(8,128)(2,1)S(1)}, u32[]{:S(2)}, u32[]{:S(2)}) collective-permute-start(bf16[768,768]{1,0:T(8,128)(2,1)} %get-tuple-element.333.refs_2_), channel_id=1, source_target_pairs={{8,16},{16,8},{9,17},{17,9},{10,18},{18,10},{11,19},{19,11},{12,20... | collective-permute-start | bytes 3538952 | tf_op jit(solution)/shard_map/ppermute | solution.py:299
  474.7 31.0 %collective-permute-start.61 = (bf16[768,768]{1,0:T(8,128)(2,1)}, bf16[768,768]{1,0:T(8,128)(2,1)S(1)}, u32[]{:S(2)}, u32[]{:S(2)}) collective-permute-start(bf16[768,768]{1,0:T(8,128)(2,1)} %get-tuple-element.353), channel_id=1, source_target_pairs={{0,8},{8,0},{16,24},{24,16},{1,9},{9,1},{17,25},{25,17},{2,10},{10... | collective-permute-start | bytes 3538952 | tf_op jit(solution)/shard_map/ppermute | solution.py:233
  479.3 26.4 %collective-permute-start.62 = (bf16[768,768]{1,0:T(8,128)(2,1)}, bf16[768,768]{1,0:T(8,128)(2,1)}, u32[]{:S(2)}, u32[]{:S(2)}) collective-permute-start(bf16[768,768]{1,0:T(8,128)(2,1)} %get-tuple-element.344.refs_2_), channel_id=1, source_target_pairs={{8,16},{16,8},{9,17},{17,9},{10,18},{18,10},{11,19},{19,11},{12,20... | collective-permute-start | bytes 3538952 | tf_op jit(solution)/shard_map/ppermute | solution.py:299
  487.2 42.6 %collective-permute-start.63 = (bf16[1216,768]{1,0:T(8,128)(2,1)}, bf16[1216,768]{1,0:T(8,128)(2,1)S(1)}, u32[]{:S(2)}, u32[]{:S(2)}) collective-permute-start(bf16[1216,768]{1,0:T(8,128)(2,1)} %bitcast.251), channel_id=1, source_target_pairs={{0,4},{2,6},{4,0},{6,2},{1,5},{3,7},{5,1},{7,3},{8,12},{10,14},{12... | collective-permute-start | bytes 5603336 | tf_op jit(solution)/shard_map/ppermute | solution.py:25
  510.9 38.7 %collective-permute-start.64 = (bf16[768,768]{1,0:T(8,128)(2,1)}, bf16[768,768]{1,0:T(8,128)(2,1)S(1)}, u32[]{:S(2)}, u32[]{:S(2)}) collective-permute-start(bf16[768,768]{1,0:T(8,128)(2,1)} %get-tuple-element.362), channel_id=1, source_target_pairs={{0,8},{8,0},{16,24},{24,16},{1,9},{9,1},{17,25},{25,17},{2,10},{10... | collective-permute-start | bytes 3538952 | tf_op jit(solution)/shard_map/ppermute | solution.py:233
  513.7 36.0 %collective-permute-start.65 = (bf16[768,768]{1,0:T(8,128)(2,1)}, bf16[768,768]{1,0:T(8,128)(2,1)}, u32[]{:S(2)}, u32[]{:S(2)}) collective-permute-start(bf16[768,768]{1,0:T(8,128)(2,1)} %get-tuple-element.354.refs_2_), channel_id=1, source_target_pairs={{8,16},{16,8},{9,17},{17,9},{10,18},{18,10},{11,19},{19,11},{12,20... | collective-permute-start | bytes 3538952 | tf_op jit(solution)/shard_map/ppermute | solution.py:299
  549.5 25.2 %collective-permute-start.66 = (bf16[2,3,384,768]{3,2,1,0:T(8,128)(2,1)}, bf16[2,3,384,768]{3,2,1,0:T(8,128)(2,1)}, u32[]{:S(2)}, u32[]{:S(2)}) collective-permute-start(bf16[2,3,384,768]{3,2,1,0:T(8,128)(2,1)} %get-tuple-element.371), channel_id=1, source_target_pairs={{0,2},{2,0},{4,6},{6,4},{1,3},{3,1},{5,7},{7,5},{8,10},{10,8},{12,... | collective-permute-start | bytes 10616840 | tf_op jit(solution)/shard_map/ppermute | solution.py:25
  565.2 51.8 %collective-permute-start.71 = (bf16[384,768]{1,0:T(8,128)(2,1)}, bf16[384,768]{1,0:T(8,128)(2,1)S(1)}, u32[]{:S(2)}, u32[]{:S(2)}) collective-permute-start(bf16[384,768]{1,0:T(8,128)(2,1)} %get-tuple-element.385), channel_id=1, source_target_pairs={{0,4},{2,6},{4,0},{6,2},{1,5},{3,7},{5,1},{7,3},{8,12},{10,14},{12... | collective-permute-start | bytes 1769480 | tf_op jit(solution)/shard_map/ppermute | solution.py:25
  566.2 30.9 %collective-permute-start.69 = (bf16[768,768]{1,0:T(8,128)(2,1)}, bf16[768,768]{1,0:T(8,128)(2,1)}, u32[]{:S(2)}, u32[]{:S(2)}) collective-permute-start(bf16[768,768]{1,0:T(8,128)(2,1)} %get-tuple-element.364.refs_2_), channel_id=1, source_target_pairs={{8,16},{16,8},{9,17},{17,9},{10,18},{18,10},{11,19},{19,11},{12,20... | collective-permute-start | bytes 3538952 | tf_op jit(solution)/shard_map/ppermute | solution.py:299
  567.9 29.2 %collective-permute-start.68 = (bf16[768,768]{1,0:T(8,128)(2,1)}, bf16[768,768]{1,0:T(8,128)(2,1)}, u32[]{:S(2)}, u32[]{:S(2)}) collective-permute-start(bf16[768,768]{1,0:T(8,128)(2,1)} %get-tuple-element.378), channel_id=1, source_target_pairs={{0,8},{8,0},{16,24},{24,16},{1,9},{9,1},{17,25},{25,17},{2,10},{10... | collective-permute-start | bytes 3538952 | tf_op jit(solution)/shard_map/ppermute | solution.py:233
  574.7 36.3 %collective-permute-start.70 = (bf16[384,768]{1,0:T(8,128)(2,1)}, bf16[384,768]{1,0:T(8,128)(2,1)S(1)}, u32[]{:S(2)}, u32[]{:S(2)}) collective-permute-start(bf16[384,768]{1,0:T(8,128)(2,1)} %get-tuple-element.382), channel_id=1, source_target_pairs={{0,4},{2,6},{4,0},{6,2},{1,5},{3,7},{5,1},{7,3},{8,12},{10,14},{12... | collective-permute-start | bytes 1769480 | tf_op jit(solution)/shard_map/ppermute | solution.py:25
  601.3 27.1 %collective-permute-start.72 = (bf16[768,768]{1,0:T(8,128)(2,1)}, bf16[768,768]{1,0:T(8,128)(2,1)}, u32[]{:S(2)}, u32[]{:S(2)}) collective-permute-start(bf16[768,768]{1,0:T(8,128)(2,1)} %get-tuple-element.387), channel_id=1, source_target_pairs={{0,8},{8,0},{16,24},{24,16},{1,9},{9,1},{17,25},{25,17},{2,10},{10... | collective-permute-start | bytes 3538952 | tf_op jit(solution)/shard_map/ppermute | solution.py:233
  603.1 25.3 %collective-permute-start.73 = (bf16[768,768]{1,0:T(8,128)(2,1)}, bf16[768,768]{1,0:T(8,128)(2,1)}, u32[]{:S(2)}, u32[]{:S(2)}) collective-permute-start(bf16[768,768]{1,0:T(8,128)(2,1)} %get-tuple-element.379.refs_2_), channel_id=1, source_target_pairs={{8,16},{16,8},{9,17},{17,9},{10,18},{18,10},{11,19},{19,11},{12,20... | collective-permute-start | bytes 3538952 | tf_op jit(solution)/shard_map/ppermute | solution.py:299
  609.4 37.6 %collective-permute-start.74 = (bf16[512,1536]{1,0:T(8,128)(2,1)}, bf16[512,1536]{1,0:T(8,128)(2,1)}, u32[]{:S(2)}, u32[]{:S(2)}) collective-permute-start(bf16[512,1536]{1,0:T(8,128)(2,1)} %get-tuple-element.360), channel_id=1, source_target_pairs={{0,1},{1,0},{2,3},{3,2},{4,5},{5,4},{6,7},{7,6},{8,9},{9,8},{10,11... | collective-permute-start | bytes 4718600 | tf_op jit(solution)/shard_map/ppermute | solution.py:25
  611.1 48.4 %collective-permute-start.76 = (bf16[1152,768]{1,0:T(8,128)(2,1)}, bf16[1152,768]{1,0:T(8,128)(2,1)}, u32[]{:S(2)}, u32[]{:S(2)}) collective-permute-start(bf16[1152,768]{1,0:T(8,128)(2,1)} %get-tuple-element.395), channel_id=1, source_target_pairs={{0,4},{2,6},{4,0},{6,2},{1,5},{3,7},{5,1},{7,3},{8,12},{10,14},{12... | collective-permute-start | bytes 5308424 | tf_op jit(solution)/shard_map/ppermute | solution.py:25
  617.0 36.8 %collective-permute-start.75 = (bf16[96,1536]{1,0:T(8,128)(2,1)S(1)}, bf16[96,1536]{1,0:T(8,128)(2,1)}, u32[]{:S(2)}, u32[]{:S(2)}) collective-permute-start(bf16[96,1536]{1,0:T(8,128)(2,1)S(1)} %copy-done.74), channel_id=1, source_target_pairs={{0,1},{1,0},{2,3},{3,2},{4,5},{5,4},{6,7},{7,6},{8,9},{9,8},{10,11... | collective-permute-start | bytes 884744 | tf_op jit(solution)/shard_map/ppermute | solution.py:25
  632.7 34.8 %collective-permute-start.77 = (bf16[768,768]{1,0:T(8,128)(2,1)}, bf16[768,768]{1,0:T(8,128)(2,1)}, u32[]{:S(2)}, u32[]{:S(2)}) collective-permute-start(bf16[768,768]{1,0:T(8,128)(2,1)} %get-tuple-element.398), channel_id=1, source_target_pairs={{0,8},{8,0},{16,24},{24,16},{1,9},{9,1},{17,25},{25,17},{2,10},{10... | collective-permute-start | bytes 3538952 | tf_op jit(solution)/shard_map/ppermute | solution.py:233
  636.3 31.9 %collective-permute-start.78 = (bf16[768,768]{1,0:T(8,128)(2,1)}, bf16[768,768]{1,0:T(8,128)(2,1)}, u32[]{:S(2)}, u32[]{:S(2)}) collective-permute-start(bf16[768,768]{1,0:T(8,128)(2,1)} %get-tuple-element.388.refs_2_), channel_id=1, source_target_pairs={{8,16},{16,8},{9,17},{17,9},{10,18},{18,10},{11,19},{19,11},{12,20... | collective-permute-start | bytes 3538952 | tf_op jit(solution)/shard_map/ppermute | solution.py:299
  647.0 40.8 %collective-permute-start.79 = (bf16[1152,768]{1,0:T(8,128)(2,1)}, bf16[1152,768]{1,0:T(8,128)(2,1)S(1)}, u32[]{:S(2)}, u32[]{:S(2)}) collective-permute-start(bf16[1152,768]{1,0:T(8,128)(2,1)} %get-tuple-element.402), channel_id=1, source_target_pairs={{0,4},{2,6},{4,0},{6,2},{1,5},{3,7},{5,1},{7,3},{8,12},{10,14},{12... | collective-permute-start | bytes 5308424 | tf_op jit(solution)/shard_map/ppermute | solution.py:25
  657.4 46.8 %collective-permute-start.82 = (bf16[512,1536]{1,0:T(8,128)(2,1)}, bf16[512,1536]{1,0:T(8,128)(2,1)}, u32[]{:S(2)}, u32[]{:S(2)}) collective-permute-start(bf16[512,1536]{1,0:T(8,128)(2,1)} %get-tuple-element.412), channel_id=1, source_target_pairs={{0,1},{1,0},{2,3},{3,2},{4,5},{5,4},{6,7},{7,6},{8,9},{9,8},{10,11... | collective-permute-start | bytes 4718600 | tf_op jit(solution)/shard_map/ppermute | solution.py:25
  659.4 54.7 %collective-permute-start.86 = (bf16[384,768]{1,0:T(8,128)(2,1)S(1)}, bf16[384,768]{1,0:T(8,128)(2,1)}, u32[]{:S(2)}, u32[]{:S(2)}) collective-permute-start(bf16[384,768]{1,0:T(8,128)(2,1)S(1)} %copy-done.30), channel_id=1, source_target_pairs={{0,8},{24,16},{1,9},{25,17},{2,10},{26,18},{3,11},{27,19},{4,12},{... | collective-permute-start | bytes 1769480 | tf_op jit(solution)/shard_map/ppermute | solution.py:233
  667.5 32.6 %collective-permute-start.81 = (bf16[96,1536]{1,0:T(8,128)(2,1)S(1)}, bf16[96,1536]{1,0:T(8,128)(2,1)}, u32[]{:S(2)}, u32[]{:S(2)}) collective-permute-start(bf16[96,1536]{1,0:T(8,128)(2,1)S(1)} %copy-done.71), channel_id=1, source_target_pairs={{0,1},{1,0},{2,3},{3,2},{4,5},{5,4},{6,7},{7,6},{8,9},{9,8},{10,11... | collective-permute-start | bytes 884744 | tf_op jit(solution)/shard_map/ppermute | solution.py:25
  687.8 33.4 %collective-permute-start.87 = (bf16[384,768]{1,0:T(8,128)(2,1)S(1)}, bf16[384,768]{1,0:T(8,128)(2,1)}, u32[]{:S(2)}, u32[]{:S(2)}) collective-permute-start(bf16[384,768]{1,0:T(8,128)(2,1)S(1)} %copy-done.29), channel_id=1, source_target_pairs={{0,8},{24,16},{1,9},{25,17},{2,10},{26,18},{3,11},{27,19},{4,12},{... | collective-permute-start | bytes 1769480 | tf_op jit(solution)/shard_map/ppermute | solution.py:233
  695.5 38.3 %collective-permute-start.88 = (bf16[384,768]{1,0:T(8,128)(2,1)}, bf16[384,768]{1,0:T(8,128)(2,1)}, u32[]{:S(2)}, u32[]{:S(2)}) collective-permute-start(bf16[384,768]{1,0:T(8,128)(2,1)} %get-tuple-element.421.refs_0_), channel_id=1, source_target_pairs={{0,8},{24,16},{1,9},{25,17},{2,10},{26,18},{3,11},{27,19},{4,12},{... | collective-permute-start | bytes 1769480 | tf_op jit(solution)/shard_map/ppermute | solution.py:233
  700.2 53.2 %collective-permute-start.104 = (bf16[768,768]{1,0:T(8,128)(2,1)}, bf16[768,768]{1,0:T(8,128)(2,1)}, u32[]{:S(2)}, u32[]{:S(2)}) collective-permute-start(bf16[768,768]{1,0:T(8,128)(2,1)} %get-tuple-element.447), channel_id=1, source_target_pairs={{8,0},{16,24},{9,1},{17,25},{10,2},{18,26},{11,3},{19,27},{12,4},{... | collective-permute-start | bytes 3538952 | tf_op jit(solution)/shard_map/ppermute | solution.py:233
  733.8 73.2 %collective-permute-start.105 = (bf16[768,768]{1,0:T(8,128)(2,1)}, bf16[768,768]{1,0:T(8,128)(2,1)}, u32[]{:S(2)}, u32[]{:S(2)}) collective-permute-start(bf16[768,768]{1,0:T(8,128)(2,1)} %shard_map.369), channel_id=1, source_target_pairs={{8,0},{16,24},{9,1},{17,25},{10,2},{18,26},{11,3},{19,27},{12,4},{... | collective-permute-start | bytes 3538952 | tf_op jit(solution)/shard_map/ppermute | solution.py:233
  735.1 33.9 %collective-permute-start.85 = (f32[1,25,1536]{2,1,0:T(8,128)S(1)}, f32[1,25,1536]{2,1,0:T(8,128)S(1)}, u32[]{:S(2)}, u32[]{:S(2)}) collective-permute-start(f32[1,25,1536]{2,1,0:T(8,128)S(1)} %add_bitcast_fusion), channel_id=1, source_target_pairs={{0,8},{8,0},{16,24},{24,16},{1,9},{9,1},{17,25},{25,17},{2,10},{10... | collective-permute-start | bytes 460808 | tf_op jit(solution)/shard_map/ppermute | solution.py:25
  746.0 35.6 %collective-permute-start.94 = (bf16[384,768]{1,0:T(8,128)(2,1)}, bf16[384,768]{1,0:T(8,128)(2,1)}, u32[]{:S(2)}, u32[]{:S(2)}) collective-permute-start(bf16[384,768]{1,0:T(8,128)(2,1)} %get-tuple-element.427.refs_2_), channel_id=1, source_target_pairs={{8,16},{16,8},{9,17},{17,9},{10,18},{18,10},{11,19},{19,11},{12,20... | collective-permute-start | bytes 1769480 | tf_op jit(solution)/shard_map/ppermute | solution.py:299
  747.5 34.1 %collective-permute-start.93 = (bf16[384,768]{1,0:T(8,128)(2,1)}, bf16[384,768]{1,0:T(8,128)(2,1)S(1)}, u32[]{:S(2)}, u32[]{:S(2)}) collective-permute-start(bf16[384,768]{1,0:T(8,128)(2,1)} %get-tuple-element.431), channel_id=1, source_target_pairs={{0,8},{8,0},{16,24},{24,16},{1,9},{9,1},{17,25},{25,17},{2,10},{10... | collective-permute-start | bytes 1769480 | tf_op jit(solution)/shard_map/ppermute | solution.py:233
  753.3 48.0 %collective-permute-start.95 = (bf16[384,768]{1,0:T(8,128)(2,1)}, bf16[384,768]{1,0:T(8,128)(2,1)S(1)}, u32[]{:S(2)}, u32[]{:S(2)}) collective-permute-start(bf16[384,768]{1,0:T(8,128)(2,1)} %get-tuple-element.434), channel_id=1, source_target_pairs={{0,8},{8,0},{16,24},{24,16},{1,9},{9,1},{17,25},{25,17},{2,10},{10... | collective-permute-start | bytes 1769480 | tf_op jit(solution)/shard_map/ppermute | solution.py:233
  769.0 33.2 %collective-permute-start.96 = (bf16[384,768]{1,0:T(8,128)(2,1)}, bf16[384,768]{1,0:T(8,128)(2,1)}, u32[]{:S(2)}, u32[]{:S(2)}) collective-permute-start(bf16[384,768]{1,0:T(8,128)(2,1)} %get-tuple-element.429.refs_2_), channel_id=1, source_target_pairs={{8,16},{16,8},{9,17},{17,9},{10,18},{18,10},{11,19},{19,11},{12,20... | collective-permute-start | bytes 1769480 | tf_op jit(solution)/shard_map/ppermute | solution.py:299
  781.6 43.1 %collective-permute-start.90 = (f32[2,25,1536]{2,1,0:T(8,128)}, f32[2,25,1536]{2,1,0:T(8,128)}, u32[]{:S(2)}, u32[]{:S(2)}) collective-permute-start(f32[2,25,1536]{2,1,0:T(8,128)} %pad_maximum_fusion.7), channel_id=1, source_target_pairs={{0,16},{8,24},{16,0},{24,8},{1,17},{9,25},{17,1},{25,9},{2,18},{10... | collective-permute-start | bytes 921608 | tf_op jit(solution)/shard_map/ppermute | solution.py:25
  785.3 33.3 %collective-permute-start.98 = (bf16[384,768]{1,0:T(8,128)(2,1)}, bf16[384,768]{1,0:T(8,128)(2,1)}, u32[]{:S(2)}, u32[]{:S(2)}) collective-permute-start(bf16[384,768]{1,0:T(8,128)(2,1)} %get-tuple-element.432.refs_2_), channel_id=1, source_target_pairs={{8,16},{16,8},{9,17},{17,9},{10,18},{18,10},{11,19},{19,11},{12,20... | collective-permute-start | bytes 1769480 | tf_op jit(solution)/shard_map/ppermute | solution.py:299
  805.0 44.4 %collective-permute-start.100 = (bf16[384,768]{1,0:T(8,128)(2,1)}, bf16[384,768]{1,0:T(8,128)(2,1)}, u32[]{:S(2)}, u32[]{:S(2)}) collective-permute-start(bf16[384,768]{1,0:T(8,128)(2,1)} %get-tuple-element.444), channel_id=1, source_target_pairs={{0,8},{8,0},{16,24},{24,16},{1,9},{9,1},{17,25},{25,17},{2,10},{10... | collective-permute-start | bytes 1769480 | tf_op jit(solution)/shard_map/ppermute | solution.py:233
  807.0 42.4 %collective-permute-start.101 = (bf16[384,768]{1,0:T(8,128)(2,1)}, bf16[384,768]{1,0:T(8,128)(2,1)}, u32[]{:S(2)}, u32[]{:S(2)}) collective-permute-start(bf16[384,768]{1,0:T(8,128)(2,1)} %get-tuple-element.436.refs_2_), channel_id=1, source_target_pairs={{8,16},{16,8},{9,17},{17,9},{10,18},{18,10},{11,19},{19,11},{12,20... | collective-permute-start | bytes 1769480 | tf_op jit(solution)/shard_map/ppermute | solution.py:299
  821.9 44.7 %collective-permute-start.102 = (bf16[384,768]{1,0:T(8,128)(2,1)}, bf16[384,768]{1,0:T(8,128)(2,1)}, u32[]{:S(2)}, u32[]{:S(2)}) collective-permute-start(bf16[384,768]{1,0:T(8,128)(2,1)} %get-tuple-element.446.refs_0_), channel_id=1, source_target_pairs={{8,16},{16,8},{9,17},{17,9},{10,18},{18,10},{11,19},{19,11},{12,20... | collective-permute-start | bytes 1769480 | tf_op jit(solution)/shard_map/ppermute | solution.py:299
  823.4 52.1 %collective-permute-start.99 = (bf16[384,768]{1,0:T(8,128)(2,1)}, bf16[384,768]{1,0:T(8,128)(2,1)}, u32[]{:S(2)}, u32[]{:S(2)}) collective-permute-start(bf16[384,768]{1,0:T(8,128)(2,1)} %get-tuple-element.439), channel_id=1, source_target_pairs={{8,0},{16,24},{9,1},{17,25},{10,2},{18,26},{11,3},{19,27},{12,4},{... | collective-permute-start | bytes 1769480 | tf_op jit(solution)/shard_map/ppermute | solution.py:233
  872.9 25.6 %collective-permute-start.103 = (bf16[384,768]{1,0:T(8,128)(2,1)S(1)}, bf16[384,768]{1,0:T(8,128)(2,1)S(1)}, u32[]{:S(2)}, u32[]{:S(2)}) collective-permute-start(bf16[384,768]{1,0:T(8,128)(2,1)S(1)} %copy-done.40), channel_id=1, source_target_pairs={{8,0},{16,24},{9,1},{17,25},{10,2},{18,26},{11,3},{19,27},{12,4},{... | collective-permute-start | bytes 1769480 | tf_op jit(solution)/shard_map/ppermute | solution.py:233
  (138 other events, 1332.7 us)

commit v7 on v6

--- a/solution.py
+++ b/solution.py
@@ -760,11 +760,11 @@
     count = len(blocks)
     length, columns = blocks[0].shape[1:]
     share, units = up_shard.shape
-    rows = length // count
+    rows, half = length // count, count // 2
 
     def kernel(spot_ref, up_ref, down_ref, *rest):
         feature_refs, refs, rest = rest[:count], rest[count : 2 * count], rest[2 * count :]
-        outs, (up_grad_ref, down_grad_ref, rows_in, sums) = rest[:count], rest[count:]
+        outs, (up_low, up_high, down_low, down_high, rows_in, sums) = rest[:count], rest[count:]
         lay_rows(spot_ref, feature_refs, rows_in)
         hid_turned, grad_turned = jnp.transpose(rows_in[0]), jnp.transpose(rows_in[1])
         out_sum = jnp.zeros((length, share), jnp.float32)
@@ -775,8 +775,17 @@
             activ, upward_grad = ref[0], ref[1]
             out_sum += product_back(activ, down_ref[:, at])
             back_sum += product_back(upward_grad, up_ref[:, at])
-            up_grad_ref[place] = product(hid_turned, upward_grad).astype(jnp.bfloat16)
-            down_grad_ref[place] = product(grad_turned, activ).astype(jnp.bfloat16)
+            up_block = product(hid_turned, upward_grad).astype(jnp.bfloat16)
+            down_block = product(grad_turned, activ).astype(jnp.bfloat16)
+
+            def put_low(place=place, up_block=up_block, down_block=down_block):
+                up_low[place], down_low[place] = up_block, down_block
+
+            def put_high(place=place, up_block=up_block, down_block=down_block):
+                up_high[place - half], down_high[place - half] = up_block, down_block
+
+            pl.when(place < half)(put_low)
+            pl.when(place >= half)(put_high)
         sums[0] = back_sum.astype(jnp.bfloat16)
         sums[1] = out_sum.astype(jnp.bfloat16)
         for away, out in enumerate(outs):
@@ -785,18 +794,18 @@
 
     zeros = lambda step: (0, 0, 0)
     arrays = [up_shard, down_shard] + list(features) + list(blocks)
-    *sums, up_grad, down_grad = call(
+    *sums, up_low, up_high, down_low, down_high = call(
         kernel,
         1,
         spot,
         arrays,
         [whole_spec(part) for part in arrays],
-        (bf16(2, rows, share),) * count + (bf16(count, share, columns),) * 2,
+        (bf16(2, rows, share),) * count + (bf16(half, share, columns),) * 4,
         (pl.BlockSpec((2, rows, share), zeros),) * count
-        + (pl.BlockSpec((count, share, columns), zeros),) * 2,
+        + (pl.BlockSpec((half, share, columns), zeros),) * 4,
         [pltpu.VMEM((2, length, share), jnp.bfloat16)] * 2,
     )
-    return sums, up_grad, down_grad
+    return sums, (up_low, up_high), (down_low, down_high)
 
 
 def gather_features(seq, spot, pieces):
@@ -1264,11 +1273,13 @@
     line = Line(seq)
     if line.on_line:
         for whole in (text_down_grad, text_up_grad):
-            for place in range(2):
-                line.add(flat(whole.reshape(2, -1, share, whole.shape[-1])[place]))
+            for part in whole:
+                line.add(flat(part))
         text_totals = None
     else:
-        text_totals = [lax.psum(part, "rep") for part in (text_down_grad, text_up_grad)]
+        text_totals = [
+            lax.psum(jnp.concatenate(parts), "rep") for parts in (text_down_grad, text_up_grad)
+        ]
 
     image_mid_grad, image_db_one, image_mid_sums = middle_grads(
         seq, image_mod, image_tokens, image_branch, image_cotangent, image_hid_grad

time: 912 us -> 911 us (level)
    unnamed x192 -> x188, local copies, waits for them, and re-layouts: 24.9 us -> 26.4 us
where the time goes in v7:
time: 911 us; the launch traced here: 900 us
  Pallas kernels  358 us (39%)
  waiting for transfers between devices  275 us (30%)
  starting transfers between devices  130 us (14%)
  local copies, waits for them, and re-layouts  53.2 us (6%)
  other arithmetic  42.5 us (5%)
  matrix products  38.9 us (4%)
    ppermute x71, waiting for transfers between devices, flip(): lax.ppermute(values, axis, [(place, place ^ bit) for place in range(lax.a...  193 us
    pallas_call x11, Pallas kernels, call(): pl.pallas_call(kernel, grid=(tiles,), in_specs=[pl.BlockSpec(memory_space...  113 us
    ppermute x22, waiting for transfers between devices, outer(): return lax.ppermute(load, 'rep', pairs)  81.8 us
    pallas_call x19, Pallas kernels, step(): pl.pallas_call(kernel, grid=(2,), in_specs=[pl.BlockSpec(memory_space=plt...  58.6 us
    ppermute x22, starting transfers between devices, outer(): return lax.ppermute(load, 'rep', pairs)  54.8 us
    pallas_call x2, Pallas kernels, attend_grads(): pl.pallas_call(kernel, grid=(width // LANES,), in_specs=[row_spec(length,...  53.4 us
    ppermute x71, starting transfers between devices, flip(): lax.ppermute(values, axis, [(place, place ^ bit) for place in range(lax.a...  49 us
    pallas_call x13, Pallas kernels, add_blocks(): pl.pallas_call(kernel, grid=(2,), in_specs=[in_spec, in_spec], out_specs=...  46.4 us
  transfers between devices with their start and end apart: 109, of which 33 were waited for; matrix products, arithmetic and copies ran while one was open for 12% of the time, Pallas kernels for 38%

profile of v7, /device:TPU:0, one launch (start us, length us, event | category | flops | bytes accessed | tf_op | source)
XLA Modules:
  0.0 900.1 jit_solution(248215525408353683)
XLA Ops:
  6.7 4.2 fusion.46
  14.5 11.4 %collective-permute-done.1.rest_1_.rest_5_ = bf16[3,192,768]{2,1,0:T(8,128)(2,1)} collective-permute-done((bf16[3,192,768]{2,1,0:T(8,128)(2,1)}, bf16[3,192,768]{2,1,0:T(8,128)(2,1)}, u32[]{:S(2)}, u32[]{:S(2)}) %collective-permute-start.1) | collective-permute-done | bytes 884768 | tf_op jit(solution)/shard_map/ppermute | solution.py:25
  27.6 4.3 collective-permute-done.2
  32.1 4.5 collective-permute-done.4.rest_3_
  41.1 18.0 %collective-permute-done.6.rest_2_.rest_6_ = bf16[3,192,768]{2,1,0:T(8,128)(2,1)} collective-permute-done((bf16[3,192,768]{2,1,0:T(8,128)(2,1)}, bf16[3,192,768]{2,1,0:T(8,128)(2,1)}, u32[]{:S(2)}, u32[]{:S(2)}) %collective-permute-start.6) | collective-permute-done | bytes 884768 | tf_op jit(solution)/shard_map/ppermute | solution.py:25
  69.5 8.3 shard_map.323
  81.0 6.7 collective-permute-done.11.rest_2_.rest_6_
  93.8 5.7 shard_map.325
  99.5 16.6 %collective-permute-done.17.rest_4_.rest_6_ = bf16[2,2,256,768]{3,2,1,0:T(8,128)(2,1)} collective-permute-done((bf16[2,2,256,768]{3,2,1,0:T(8,128)(2,1)S(1)}, bf16[2,2,256,768]{3,2,1,0:T(8,128)(2,1)}, u32[]{:S(2)}, u32[]{:S(2)}) %collective-permute-start.17) | collective-permute-done | bytes 1572896 | tf_op jit(solution)/shard_map/ppermute | solution.py:25
  121.6 5.4 collective-permute-done.20.rest_8_.rest_10_
  136.2 25.8 %shard_map.326 = (bf16[2,256,768]{2,1,0:T(8,128)(2,1)}, bf16[2,48,768]{2,1,0:T(8,128)(2,1)}) custom-call(bf16[2,256,768]{2,1,0:T(8,128)(2,1)} %bitcast.172, bf16[2,48,768]{2,1,0:T(8,128)(2,1)} %bitcast.215, bf16[2,2,256,768]{3,2,1,0:T(8,128)(2,1)} %bitcast.161, bf16[2,2,256,768]{3,2,1,0:T(8,128)(2,1)} %collective-permute-done.16.rest_3_.rest_5_, ...), custom_call_target="tpu_custom_call" | custom-call | flops 1024 | bytes 1024 | tf_op jit(solution)/shard_map/pallas_call | solution.py:1012
  169.0 5.0 shard_map.328
  185.1 27.3 %collective-permute-done.28 = bf16[512,1536]{1,0:T(8,128)(2,1)S(1)} collective-permute-done((bf16[512,1536]{1,0:T(8,128)(2,1)}, bf16[512,1536]{1,0:T(8,128)(2,1)S(1)}, u32[]{:S(2)}, u32[]{:S(2)}) %collective-permute-start.28) | collective-permute-done | bytes 1572896 | tf_op jit(solution)/shard_map/ppermute | solution.py:25
  213.5 4.8 shard_map.330
  218.4 12.2 %collective-permute-done.29.rest_2_ = bf16[192,3072]{1,0:T(8,128)(2,1)} collective-permute-done((bf16[192,3072]{1,0:T(8,128)(2,1)}, bf16[192,3072]{1,0:T(8,128)(2,1)}, u32[]{:S(2)}, u32[]{:S(2)}) %collective-permute-start.29) | collective-permute-done | bytes 1179680 | tf_op jit(solution)/shard_map/ppermute | solution.py:25
  231.9 8.5 shard_map.331
  241.6 6.2 collective-permute-done.34
  253.8 40.1 %shard_map.333 = (bf16[512,1536]{1,0:T(8,128)(2,1)}, bf16[512,1536]{1,0:T(8,128)(2,1)}, bf16[2,4,384,768]{3,2,1,0:T(8,128)(2,1)}, bf16[2,4,384,768]{3,2,1,0:T(8,...) custom-call(s32[2]{0:T(128)} %pad_add_fusion.spot_ref, bf16[512,1536]{1,0:T(8,128)(2,1)} %bitcast.225, ...), custom_call_target="tpu_custom_call" | custom-call | flops 1024 | bytes 1024 | tf_op jit(solution)/shard_map/pallas_call | solution.py:426
  301.3 5.4 collective-permute-done.40
  306.7 5.6 shard_map.335
  313.4 5.6 shard_map.336
  319.1 8.1 collective-permute-done.43.rest_6_
  330.4 12.5 %shard_map.337 = (bf16[2,96,384]{2,1,0:T(8,128)(2,1)}, bf16[2,96,384]{2,1,0:T(8,128)(2,1)}, bf16[2,96,384]{2,1,0:T(8,128)(2,1)}, bf16[2,96,384]{2,1,0:T(8,128)(2...) custom-call(s32[2]{0:T(128)} %pad_add_fusion.spot_ref, ...), custom_call_target="tpu_custom_call" | custom-call | flops 1024 | bytes 1024 | tf_op jit(solution)/shard_map/pallas_call | solution.py:426
  346.0 7.4 shard_map.338
  353.3 4.7 collective-permute-start.50
  362.3 6.9 shard_map.340
  370.8 7.9 collective-permute-done.49
  382.2 4.8 shard_map.342
  399.8 26.7 %shard_map.346 = (bf16[1,256,768]{2,1,0:T(8,128)(2,1)}, bf16[1,48,768]{2,1,0:T(8,128)(2,1)}, bf16[2,2,304,768]{3,2,1,0:T(8,128)(2,1)}, bf16[2,2,304,768]{3,2,1,0:T(8,128)(2,1)}) custom-call(bf16[2,256,768]{2,1,0:T(8,128)(2,1)} %bitcast.173, bf16[2,48,768]{2,1,0:T(8,128)(2,1)} %bitcast.216, bf16[2,256,768]{2,1,0:T(8,128)(2,1)} %bitcast.199, ...), custom_call_target="tpu_custom_call" | custom-call | flops 1024 | bytes 1024 | tf_op jit(solution)/shard_map/pallas_call | solution.py:1083
  431.4 4.2 shard_map.348
  436.8 26.7 %shard_map.349 = (bf16[1,256,768]{2,1,0:T(8,128)(2,1)}, bf16[1,48,768]{2,1,0:T(8,128)(2,1)}, bf16[2,2,304,768]{3,2,1,0:T(8,128)(2,1)}, bf16[2,2,304,768]{3,2,1,0:T(8,128)(2,1)}) custom-call(bf16[2,256,768]{2,1,0:T(8,128)(2,1)} %bitcast.174, bf16[2,48,768]{2,1,0:T(8,128)(2,1)} %bitcast.217, bf16[2,256,768]{2,1,0:T(8,128)(2,1)} %bitcast.200, ...), custom_call_target="tpu_custom_call" | custom-call | flops 1024 | bytes 1024 | tf_op jit(solution)/shard_map/pallas_call | solution.py:1083
  468.7 4.3 shard_map.351
  473.3 4.6 collective-permute-start.61
  480.8 4.8 shard_map.352
  486.6 17.7 %collective-permute-done.61.refs_1_ = bf16[768,768]{1,0:T(8,128)(2,1)S(1)} collective-permute-done((bf16[768,768]{1,0:T(8,128)(2,1)}, bf16[768,768]{1,0:T(8,128)(2,1)S(1)}, u32[]{:S(2)}, u32[]{:S(2)}) %collective-permute-start.61) | collective-permute-done | bytes 1179680 | tf_op jit(solution)/shard_map/ppermute | solution.py:233
  505.3 4.2 shard_map.353
  514.0 14.3 %collective-permute-done.63 = bf16[1216,768]{1,0:T(8,128)(2,1)S(1)} collective-permute-done((bf16[1216,768]{1,0:T(8,128)(2,1)}, bf16[1216,768]{1,0:T(8,128)(2,1)S(1)}, u32[]{:S(2)}, u32[]{:S(2)}) %collective-permute-start.63) | collective-permute-done | bytes 1867808 | tf_op jit(solution)/shard_map/ppermute | solution.py:25
  533.6 14.4 %shard_map.355 = (bf16[512,1536]{1,0:T(8,128)(2,1)}, bf16[2,3,384,768]{3,2,1,0:T(8,128)(2,1)}, bf16[2,3,384,768]{3,2,1,0:T(8,128)(2,1)}) custom-call(s32[2]{0:T(128)} %pad_add_fusion.spot_ref, bf16[512,1536]{1,0:T(8,128)(2,1)} %bitcast.171, bf16[1,256,768]{2,1,0:T(8,128)(2,1)} %get-tuple-element.329.rest_0_, ...), custom_call_target="tpu_custom_call" | custom-call | flops 1024 | bytes 1024 | tf_op jit(solution)/shard_map/pallas_call | solution.py:426
  549.0 4.2 shard_map.356
  553.3 9.7 %shard_map.357 = (bf16[96,1536]{1,0:T(8,128)(2,1)}, bf16[2,3,384,768]{3,2,1,0:T(8,128)(2,1)}, bf16[2,3,384,768]{3,2,1,0:T(8,128)(2,1)}) custom-call(s32[2]{0:T(128)} %pad_add_fusion.spot_ref, bf16[96,1536]{1,0:T(8,128)(2,1)} %bitcast.202, bf16[1,48,768]{2,1,0:T(8,128)(2,1)} %get-tuple-element.370.rest_0_, bf16[1,48,768]{2,1,0:T(8,128)(2,1)} %get-tuple-element.371.rest_1_, ...), custom_call_target="tpu_custom_call" | custom-call | flops 1024 | bytes 1024 | tf_op jit(solution)/shard_map/pallas_call | solution.py:426
  574.6 4.6 shard_map.358
  579.2 4.6 shard_map.359
  583.9 12.0 %collective-permute-done.68.refs_1_ = bf16[768,768]{1,0:T(8,128)(2,1)} collective-permute-done((bf16[768,768]{1,0:T(8,128)(2,1)}, bf16[768,768]{1,0:T(8,128)(2,1)}, u32[]{:S(2)}, u32[]{:S(2)}) %collective-permute-start.68) | collective-permute-done | bytes 1179680 | tf_op jit(solution)/shard_map/ppermute | solution.py:233
  595.8 4.2 shard_map.360
  603.6 4.6 pad_maximum_fusion.3
  619.0 8.2 collective-permute-done.72.refs_1_
  627.2 4.2 shard_map.363
  639.8 6.1 collective-permute-done.74
  647.0 5.7 shard_map.364
  658.3 4.9 collective-permute-start.86
  677.1 9.5 %collective-permute-done.79 = bf16[1152,768]{1,0:T(8,128)(2,1)S(1)} collective-permute-done((bf16[1152,768]{1,0:T(8,128)(2,1)}, bf16[1152,768]{1,0:T(8,128)(2,1)S(1)}, u32[]{:S(2)}, u32[]{:S(2)}) %collective-permute-start.79) | collective-permute-done | bytes 1769504 | tf_op jit(solution)/shard_map/ppermute | solution.py:25
  686.6 4.6 collective-permute-start.87
  703.0 5.9 shard_map.371
  720.2 7.4 collective-permute-start.91
  737.7 4.4 pad_maximum_fusion.1
  752.1 15.8 %collective-permute-done.85 = f32[1,25,1536]{2,1,0:T(8,128)S(1)} collective-permute-done((f32[1,25,1536]{2,1,0:T(8,128)S(1)}, f32[1,25,1536]{2,1,0:T(8,128)S(1)}, u32[]{:S(2)}, u32[]{:S(2)}) %collective-permute-start.85) | collective-permute-done | bytes 153632 | tf_op jit(solution)/shard_map/ppermute | solution.py:25
  773.6 7.0 collective-permute-done.93.refs_1_
  785.7 14.5 %collective-permute-done.95.refs_1_ = bf16[384,768]{1,0:T(8,128)(2,1)S(1)} collective-permute-done((bf16[384,768]{1,0:T(8,128)(2,1)}, bf16[384,768]{1,0:T(8,128)(2,1)S(1)}, u32[]{:S(2)}, u32[]{:S(2)}) %collective-permute-start.95) | collective-permute-done | bytes 589856 | tf_op jit(solution)/shard_map/ppermute | solution.py:233
  826.0 7.3 fusion.2
  833.3 7.7 convolution_bitcast_fusion.1
  841.0 7.4 fusion.5
  854.0 7.7 fusion
  875.8 14.9 %collective-permute-done.108 = bf16[384,768]{1,0:T(8,128)(2,1)S(1)} collective-permute-done((bf16[384,768]{1,0:T(8,128)(2,1)}, bf16[384,768]{1,0:T(8,128)(2,1)S(1)}, u32[]{:S(2)}, u32[]{:S(2)}) %collective-permute-start.108) | collective-permute-done | bytes 589856 | tf_op jit(solution)/shard_map/ppermute | solution.py:233
  892.8 4.6 collective-permute-done.103
  (499 shorter events, 300.1 us)
Async XLA Ops:
  36.6 29.0 %collective-permute-start.5 = (bf16[384,3072]{1,0:T(8,128)(2,1)}, bf16[384,3072]{1,0:T(8,128)(2,1)}, u32[]{:S(2)}, u32[]{:S(2)}) collective-permute-start(bf16[384,3072]{1,0:T(8,128)(2,1)} %rest_6_.1), channel_id=1, source_target_pairs={{0,2},{2,0},{4,6},{6,4},{1,3},{3,1},{5,7},{7,5},{8,10},{10,8},{12,... | collective-permute-start | bytes 7077896 | tf_op jit(solution)/shard_map/ppermute | solution.py:25
  36.7 32.7 %collective-permute-start.7 = (bf16[3,384,768]{2,1,0:T(8,128)(2,1)S(1)}, bf16[3,384,768]{2,1,0:T(8,128)(2,1)}, u32[]{:S(2)}, u32[]{:S(2)}) collective-permute-start(bf16[3,384,768]{2,1,0:T(8,128)(2,1)S(1)} %bitcast.177), channel_id=1, source_target_pairs={{0,2},{2,0},{4,6},{6,4},{1,3},{3,1},{5,7},{7,5},{8,10},{10,8},{12,... | collective-permute-start | bytes 5308424 | tf_op jit(solution)/shard_map/ppermute | solution.py:25
  61.3 27.2 %collective-permute-start.12 = (bf16[3,384,768]{2,1,0:T(8,128)(2,1)}, bf16[3,384,768]{2,1,0:T(8,128)(2,1)}, u32[]{:S(2)}, u32[]{:S(2)}) collective-permute-start(bf16[3,384,768]{2,1,0:T(8,128)(2,1)} %bitcast.178), channel_id=1, source_target_pairs={{0,2},{2,0},{4,6},{6,4},{1,3},{3,1},{5,7},{7,5},{8,10},{10,8},{12,... | collective-permute-start | bytes 5308424 | tf_op jit(solution)/shard_map/ppermute | solution.py:25
  79.4 36.7 %collective-permute-start.17 = (bf16[2,2,256,768]{3,2,1,0:T(8,128)(2,1)S(1)}, bf16[2,2,256,768]{3,2,1,0:T(8,128)(2,1)}, u32[]{:S(2)}, u32[]{:S(2)}) collective-permute-start(bf16[2,2,256,768]{3,2,1,0:T(8,128)(2,1)S(1)} %bitcast.159), channel_id=1, source_target_pairs={{0,4},{2,6},{4,0},{6,2},{1,5},{3,7},{5,1},{7,3},{8,12},{10,14},{12... | collective-permute-start | bytes 4718600 | tf_op jit(solution)/shard_map/ppermute | solution.py:25
  88.3 38.7 %collective-permute-start.15 = (bf16[2,384,768]{2,1,0:T(8,128)(2,1)S(1)}, bf16[2,384,768]{2,1,0:T(8,128)(2,1)}, u32[]{:S(2)}, u32[]{:S(2)}) collective-permute-start(bf16[2,384,768]{2,1,0:T(8,128)(2,1)S(1)} %pad_maximum_fusion.4.rest_0_), channel_id=1, source_target_pairs={{0,2},{2,0},{4,6},{6,4},{1,3},{3,1},{5,7},{7,5},{8,10},{10,8},{12,... | collective-permute-start | bytes 3538952 | tf_op jit(solution)/shard_map/ppermute | solution.py:25
  88.5 43.1 %collective-permute-start.16 = (bf16[2,2,256,768]{3,2,1,0:T(8,128)(2,1)S(1)}, bf16[2,2,256,768]{3,2,1,0:T(8,128)(2,1)}, u32[]{:S(2)}, u32[]{:S(2)}) collective-permute-start(bf16[2,2,256,768]{3,2,1,0:T(8,128)(2,1)S(1)} %bitcast.160), channel_id=1, source_target_pairs={{0,2},{2,0},{4,6},{6,4},{1,3},{3,1},{5,7},{7,5},{8,10},{10,8},{12,... | collective-permute-start | bytes 4718600 | tf_op jit(solution)/shard_map/ppermute | solution.py:25
  90.4 30.1 %collective-permute-start.23 = (bf16[1,384,768]{2,1,0:T(8,128)(2,1)}, bf16[1,384,768]{2,1,0:T(8,128)(2,1)}, u32[]{:S(2)}, u32[]{:S(2)}) collective-permute-start(bf16[1,384,768]{2,1,0:T(8,128)(2,1)} %collective-permute-done.10.rest_1_), channel_id=1, source_target_pairs={{0,8},{8,0},{16,24},{24,16},{1,9},{9,1},{17,25},{25,17},{2,10},{10... | collective-permute-start | bytes 1769480 | tf_op jit(solution)/shard_map/ppermute | solution.py:25
  120.5 41.5 %collective-permute-start.22 = (bf16[192,3072]{1,0:T(8,128)(2,1)}, bf16[192,3072]{1,0:T(8,128)(2,1)}, u32[]{:S(2)}, u32[]{:S(2)}) collective-permute-start(bf16[192,3072]{1,0:T(8,128)(2,1)} %constant_dynamic-slice_fusion.5), channel_id=1, source_target_pairs={{0,4},{2,6},{4,0},{6,2},{1,5},{3,7},{5,1},{7,3},{8,12},{10,14},{12... | collective-permute-start | bytes 3538952 | tf_op jit(solution)/shard_map/ppermute | solution.py:25
  128.7 33.4 %collective-permute-start.25 = (bf16[1,384,768]{2,1,0:T(8,128)(2,1)}, bf16[1,384,768]{2,1,0:T(8,128)(2,1)S(1)}, u32[]{:S(2)}, u32[]{:S(2)}) collective-permute-start(bf16[1,384,768]{2,1,0:T(8,128)(2,1)} %collective-permute-done.23.rest_2_), channel_id=1, source_target_pairs={{0,2},{2,0},{4,6},{6,4},{1,3},{3,1},{5,7},{7,5},{8,10},{10,8},{12,... | collective-permute-start | bytes 1769480 | tf_op jit(solution)/shard_map/ppermute | solution.py:25
  129.0 33.1 %collective-permute-start.24 = (bf16[1,384,768]{2,1,0:T(8,128)(2,1)}, bf16[1,384,768]{2,1,0:T(8,128)(2,1)S(1)}, u32[]{:S(2)}, u32[]{:S(2)}) collective-permute-start(bf16[1,384,768]{2,1,0:T(8,128)(2,1)} %collective-permute-done.10.rest_1_), channel_id=1, source_target_pairs={{0,2},{2,0},{4,6},{6,4},{1,3},{3,1},{5,7},{7,5},{8,10},{10,8},{12,... | collective-permute-start | bytes 1769480 | tf_op jit(solution)/shard_map/ppermute | solution.py:25
  131.6 46.5 %collective-permute-start.26 = (bf16[192,3072]{1,0:T(8,128)(2,1)}, bf16[192,3072]{1,0:T(8,128)(2,1)}, u32[]{:S(2)}, u32[]{:S(2)}) collective-permute-start(bf16[192,3072]{1,0:T(8,128)(2,1)} %constant_dynamic-slice_fusion.4), channel_id=1, source_target_pairs={{0,4},{2,6},{4,0},{6,2},{1,5},{3,7},{5,1},{7,3},{8,12},{10,14},{12... | collective-permute-start | bytes 3538952 | tf_op jit(solution)/shard_map/ppermute | solution.py:25
  176.6 35.8 %collective-permute-start.28 = (bf16[512,1536]{1,0:T(8,128)(2,1)}, bf16[512,1536]{1,0:T(8,128)(2,1)S(1)}, u32[]{:S(2)}, u32[]{:S(2)}) collective-permute-start(bf16[512,1536]{1,0:T(8,128)(2,1)} %shard_map.328), channel_id=1, source_target_pairs={{0,1},{1,0},{2,3},{3,2},{4,5},{5,4},{6,7},{7,6},{8,9},{9,8},{10,11... | collective-permute-start | bytes 4718600 | tf_op jit(solution)/shard_map/ppermute | solution.py:25
  178.1 40.3 %collective-permute-start.30 = (bf16[192,3072]{1,0:T(8,128)(2,1)}, bf16[192,3072]{1,0:T(8,128)(2,1)S(1)}, u32[]{:S(2)}, u32[]{:S(2)}) collective-permute-start(bf16[192,3072]{1,0:T(8,128)(2,1)} %collective-permute-done.26.rest_7_), channel_id=1, source_target_pairs={{0,8},{8,0},{16,24},{24,16},{1,9},{9,1},{17,25},{25,17},{2,10},{10... | collective-permute-start | bytes 3538952 | tf_op jit(solution)/shard_map/ppermute | solution.py:25
  179.4 51.2 %collective-permute-start.29 = (bf16[192,3072]{1,0:T(8,128)(2,1)}, bf16[192,3072]{1,0:T(8,128)(2,1)}, u32[]{:S(2)}, u32[]{:S(2)}) collective-permute-start(bf16[192,3072]{1,0:T(8,128)(2,1)} %collective-permute-done.22.rest_1_), channel_id=1, source_target_pairs={{0,8},{8,0},{16,24},{24,16},{1,9},{9,1},{17,25},{25,17},{2,10},{10... | collective-permute-start | bytes 3538952 | tf_op jit(solution)/shard_map/ppermute | solution.py:25
  183.9 46.7 %collective-permute-start.31 = (bf16[2,96,384]{2,1,0:T(8,128)(2,1)}, bf16[2,96,384]{2,1,0:T(8,128)(2,1)S(1)}, u32[]{:S(2)}, u32[]{:S(2)}) collective-permute-start(bf16[2,96,384]{2,1,0:T(8,128)(2,1)} %bitcast.257), channel_id=1, source_target_pairs={{0,2},{2,0},{4,6},{6,4},{1,3},{3,1},{5,7},{7,5},{8,10},{10,8},{12,... | collective-permute-start | bytes 442376 | tf_op jit(solution)/shard_map/ppermute | solution.py:25
  184.0 46.6 %collective-permute-start.32 = (bf16[2,96,384]{2,1,0:T(8,128)(2,1)}, bf16[2,96,384]{2,1,0:T(8,128)(2,1)S(1)}, u32[]{:S(2)}, u32[]{:S(2)}) collective-permute-start(bf16[2,96,384]{2,1,0:T(8,128)(2,1)} %bitcast.256), channel_id=1, source_target_pairs={{0,4},{2,6},{4,0},{6,2},{1,5},{3,7},{5,1},{7,3},{8,12},{10,14},{12... | collective-permute-start | bytes 442376 | tf_op jit(solution)/shard_map/ppermute | solution.py:25
  252.8 41.1 %collective-permute-start.39 = (bf16[768,768]{1,0:T(8,128)(2,1)}, bf16[768,768]{1,0:T(8,128)(2,1)S(1)}, u32[]{:S(2)}, u32[]{:S(2)}) collective-permute-start(bf16[768,768]{1,0:T(8,128)(2,1)} %get-tuple-element.288), channel_id=1, source_target_pairs={{0,4},{2,6},{4,0},{6,2},{1,5},{3,7},{5,1},{7,3},{8,12},{10,14},{12... | collective-permute-start | bytes 3538952 | tf_op jit(solution)/shard_map/ppermute | solution.py:25
  298.9 28.3 %collective-permute-start.43 = (bf16[2,384,768]{2,1,0:T(8,128)(2,1)}, bf16[2,384,768]{2,1,0:T(8,128)(2,1)}, u32[]{:S(2)}, u32[]{:S(2)}) collective-permute-start(bf16[2,384,768]{2,1,0:T(8,128)(2,1)} %shard_map.334.rest_4_), channel_id=1, source_target_pairs={{0,4},{2,6},{4,0},{6,2},{1,5},{3,7},{5,1},{7,3},{8,12},{10,14},{12... | collective-permute-start | bytes 3538952 | tf_op jit(solution)/shard_map/ppermute | solution.py:25
  299.9 44.9 %collective-permute-start.45 = (bf16[512,1536]{1,0:T(8,128)(2,1)S(1)}, bf16[512,1536]{1,0:T(8,128)(2,1)S(1)}, u32[]{:S(2)}, u32[]{:S(2)}) collective-permute-start(bf16[512,1536]{1,0:T(8,128)(2,1)S(1)} %copy-done.44), channel_id=1, source_target_pairs={{0,1},{1,0},{2,3},{3,2},{4,5},{5,4},{6,7},{7,6},{8,9},{9,8},{10,11... | collective-permute-start | bytes 4718600 | tf_op jit(solution)/shard_map/ppermute | solution.py:25
  301.3 25.9 %collective-permute-start.42 = (bf16[2,384,768]{2,1,0:T(8,128)(2,1)}, bf16[2,384,768]{2,1,0:T(8,128)(2,1)}, u32[]{:S(2)}, u32[]{:S(2)}) collective-permute-start(bf16[2,384,768]{2,1,0:T(8,128)(2,1)} %shard_map.334.rest_4_), channel_id=1, source_target_pairs={{0,2},{2,0},{4,6},{6,4},{1,3},{3,1},{5,7},{7,5},{8,10},{10,8},{12,... | collective-permute-start | bytes 3538952 | tf_op jit(solution)/shard_map/ppermute | solution.py:25
  353.3 34.8 %collective-permute-start.50 = (bf16[768,768]{1,0:T(8,128)(2,1)}, bf16[768,768]{1,0:T(8,128)(2,1)}, u32[]{:S(2)}, u32[]{:S(2)}) collective-permute-start(bf16[768,768]{1,0:T(8,128)(2,1)} %bitcast.48.refs_0_), channel_id=1, source_target_pairs={{0,8},{24,16},{1,9},{25,17},{2,10},{26,18},{3,11},{27,19},{4,12},{... | collective-permute-start | bytes 3538952 | tf_op jit(solution)/shard_map/ppermute | solution.py:233
  358.0 68.4 %collective-permute-start.53 = (bf16[1536,768]{1,0:T(8,128)(2,1)}, bf16[1536,768]{1,0:T(8,128)(2,1)S(1)}, u32[]{:S(2)}, u32[]{:S(2)}) collective-permute-start(bf16[1536,768]{1,0:T(8,128)(2,1)} %get-tuple-element.332), channel_id=1, source_target_pairs={{0,4},{2,6},{4,0},{6,2},{1,5},{3,7},{5,1},{7,3},{8,12},{10,14},{12... | collective-permute-start | bytes 7077896 | tf_op jit(solution)/shard_map/ppermute | solution.py:25
  387.0 76.5 %collective-permute-start.56 = (bf16[1536,768]{1,0:T(8,128)(2,1)}, bf16[1536,768]{1,0:T(8,128)(2,1)}, u32[]{:S(2)}, u32[]{:S(2)}) collective-permute-start(bf16[1536,768]{1,0:T(8,128)(2,1)} %get-tuple-element.341), channel_id=1, source_target_pairs={{0,4},{2,6},{4,0},{6,2},{1,5},{3,7},{5,1},{7,3},{8,12},{10,14},{12... | collective-permute-start | bytes 7077896 | tf_op jit(solution)/shard_map/ppermute | solution.py:25
  388.2 43.2 %collective-permute-start.54 = (bf16[768,768]{1,0:T(8,128)(2,1)}, bf16[768,768]{1,0:T(8,128)(2,1)}, u32[]{:S(2)}, u32[]{:S(2)}) collective-permute-start(bf16[768,768]{1,0:T(8,128)(2,1)} %bitcast.234), channel_id=1, source_target_pairs={{0,8},{24,16},{1,9},{25,17},{2,10},{26,18},{3,11},{27,19},{4,12},{... | collective-permute-start | bytes 3538952 | tf_op jit(solution)/shard_map/ppermute | solution.py:233
  393.0 38.4 %collective-permute-start.55 = (bf16[768,768]{1,0:T(8,128)(2,1)}, bf16[768,768]{1,0:T(8,128)(2,1)}, u32[]{:S(2)}, u32[]{:S(2)}) collective-permute-start(bf16[768,768]{1,0:T(8,128)(2,1)} %shard_map.343.refs_2_), channel_id=1, source_target_pairs={{8,16},{16,8},{9,17},{17,9},{10,18},{18,10},{11,19},{19,11},{12,20... | collective-permute-start | bytes 3538952 | tf_op jit(solution)/shard_map/ppermute | solution.py:299
  435.6 31.7 %collective-permute-start.57 = (bf16[768,768]{1,0:T(8,128)(2,1)}, bf16[768,768]{1,0:T(8,128)(2,1)S(1)}, u32[]{:S(2)}, u32[]{:S(2)}) collective-permute-start(bf16[768,768]{1,0:T(8,128)(2,1)} %get-tuple-element.346), channel_id=1, source_target_pairs={{0,8},{8,0},{16,24},{24,16},{1,9},{9,1},{17,25},{25,17},{2,10},{10... | collective-permute-start | bytes 3538952 | tf_op jit(solution)/shard_map/ppermute | solution.py:233
  435.6 31.7 %collective-permute-start.58 = (bf16[768,768]{1,0:T(8,128)(2,1)}, bf16[768,768]{1,0:T(8,128)(2,1)S(1)}, u32[]{:S(2)}, u32[]{:S(2)}) collective-permute-start(bf16[768,768]{1,0:T(8,128)(2,1)} %get-tuple-element.336.refs_2_), channel_id=1, source_target_pairs={{8,16},{16,8},{9,17},{17,9},{10,18},{18,10},{11,19},{19,11},{12,20... | collective-permute-start | bytes 3538952 | tf_op jit(solution)/shard_map/ppermute | solution.py:299
  473.3 31.0 %collective-permute-start.61 = (bf16[768,768]{1,0:T(8,128)(2,1)}, bf16[768,768]{1,0:T(8,128)(2,1)S(1)}, u32[]{:S(2)}, u32[]{:S(2)}) collective-permute-start(bf16[768,768]{1,0:T(8,128)(2,1)} %get-tuple-element.357), channel_id=1, source_target_pairs={{0,8},{8,0},{16,24},{24,16},{1,9},{9,1},{17,25},{25,17},{2,10},{10... | collective-permute-start | bytes 3538952 | tf_op jit(solution)/shard_map/ppermute | solution.py:233
  477.9 26.4 %collective-permute-start.62 = (bf16[768,768]{1,0:T(8,128)(2,1)}, bf16[768,768]{1,0:T(8,128)(2,1)}, u32[]{:S(2)}, u32[]{:S(2)}) collective-permute-start(bf16[768,768]{1,0:T(8,128)(2,1)} %get-tuple-element.348.refs_2_), channel_id=1, source_target_pairs={{8,16},{16,8},{9,17},{17,9},{10,18},{18,10},{11,19},{19,11},{12,20... | collective-permute-start | bytes 3538952 | tf_op jit(solution)/shard_map/ppermute | solution.py:299
  485.6 42.6 %collective-permute-start.63 = (bf16[1216,768]{1,0:T(8,128)(2,1)}, bf16[1216,768]{1,0:T(8,128)(2,1)S(1)}, u32[]{:S(2)}, u32[]{:S(2)}) collective-permute-start(bf16[1216,768]{1,0:T(8,128)(2,1)} %bitcast.252), channel_id=1, source_target_pairs={{0,4},{2,6},{4,0},{6,2},{1,5},{3,7},{5,1},{7,3},{8,12},{10,14},{12... | collective-permute-start | bytes 5603336 | tf_op jit(solution)/shard_map/ppermute | solution.py:25
  509.5 38.6 %collective-permute-start.64 = (bf16[768,768]{1,0:T(8,128)(2,1)}, bf16[768,768]{1,0:T(8,128)(2,1)S(1)}, u32[]{:S(2)}, u32[]{:S(2)}) collective-permute-start(bf16[768,768]{1,0:T(8,128)(2,1)} %get-tuple-element.366), channel_id=1, source_target_pairs={{0,8},{8,0},{16,24},{24,16},{1,9},{9,1},{17,25},{25,17},{2,10},{10... | collective-permute-start | bytes 3538952 | tf_op jit(solution)/shard_map/ppermute | solution.py:233
  512.2 35.8 %collective-permute-start.65 = (bf16[768,768]{1,0:T(8,128)(2,1)}, bf16[768,768]{1,0:T(8,128)(2,1)}, u32[]{:S(2)}, u32[]{:S(2)}) collective-permute-start(bf16[768,768]{1,0:T(8,128)(2,1)} %get-tuple-element.358.refs_2_), channel_id=1, source_target_pairs={{8,16},{16,8},{9,17},{17,9},{10,18},{18,10},{11,19},{19,11},{12,20... | collective-permute-start | bytes 3538952 | tf_op jit(solution)/shard_map/ppermute | solution.py:299
  547.9 25.5 %collective-permute-start.66 = (bf16[2,3,384,768]{3,2,1,0:T(8,128)(2,1)}, bf16[2,3,384,768]{3,2,1,0:T(8,128)(2,1)}, u32[]{:S(2)}, u32[]{:S(2)}) collective-permute-start(bf16[2,3,384,768]{3,2,1,0:T(8,128)(2,1)} %get-tuple-element.375), channel_id=1, source_target_pairs={{0,2},{2,0},{4,6},{6,4},{1,3},{3,1},{5,7},{7,5},{8,10},{10,8},{12,... | collective-permute-start | bytes 10616840 | tf_op jit(solution)/shard_map/ppermute | solution.py:25
  563.6 52.2 %collective-permute-start.71 = (bf16[384,768]{1,0:T(8,128)(2,1)}, bf16[384,768]{1,0:T(8,128)(2,1)S(1)}, u32[]{:S(2)}, u32[]{:S(2)}) collective-permute-start(bf16[384,768]{1,0:T(8,128)(2,1)} %get-tuple-element.389), channel_id=1, source_target_pairs={{0,4},{2,6},{4,0},{6,2},{1,5},{3,7},{5,1},{7,3},{8,12},{10,14},{12... | collective-permute-start | bytes 1769480 | tf_op jit(solution)/shard_map/ppermute | solution.py:25
  564.7 31.2 %collective-permute-start.69 = (bf16[768,768]{1,0:T(8,128)(2,1)}, bf16[768,768]{1,0:T(8,128)(2,1)}, u32[]{:S(2)}, u32[]{:S(2)}) collective-permute-start(bf16[768,768]{1,0:T(8,128)(2,1)} %get-tuple-element.368.refs_2_), channel_id=1, source_target_pairs={{8,16},{16,8},{9,17},{17,9},{10,18},{18,10},{11,19},{19,11},{12,20... | collective-permute-start | bytes 3538952 | tf_op jit(solution)/shard_map/ppermute | solution.py:299
  566.5 29.3 %collective-permute-start.68 = (bf16[768,768]{1,0:T(8,128)(2,1)}, bf16[768,768]{1,0:T(8,128)(2,1)}, u32[]{:S(2)}, u32[]{:S(2)}) collective-permute-start(bf16[768,768]{1,0:T(8,128)(2,1)} %get-tuple-element.382), channel_id=1, source_target_pairs={{0,8},{8,0},{16,24},{24,16},{1,9},{9,1},{17,25},{25,17},{2,10},{10... | collective-permute-start | bytes 3538952 | tf_op jit(solution)/shard_map/ppermute | solution.py:233
  573.5 36.4 %collective-permute-start.70 = (bf16[384,768]{1,0:T(8,128)(2,1)}, bf16[384,768]{1,0:T(8,128)(2,1)S(1)}, u32[]{:S(2)}, u32[]{:S(2)}) collective-permute-start(bf16[384,768]{1,0:T(8,128)(2,1)} %get-tuple-element.386), channel_id=1, source_target_pairs={{0,4},{2,6},{4,0},{6,2},{1,5},{3,7},{5,1},{7,3},{8,12},{10,14},{12... | collective-permute-start | bytes 1769480 | tf_op jit(solution)/shard_map/ppermute | solution.py:25
  600.1 27.1 %collective-permute-start.72 = (bf16[768,768]{1,0:T(8,128)(2,1)}, bf16[768,768]{1,0:T(8,128)(2,1)}, u32[]{:S(2)}, u32[]{:S(2)}) collective-permute-start(bf16[768,768]{1,0:T(8,128)(2,1)} %get-tuple-element.391), channel_id=1, source_target_pairs={{0,8},{8,0},{16,24},{24,16},{1,9},{9,1},{17,25},{25,17},{2,10},{10... | collective-permute-start | bytes 3538952 | tf_op jit(solution)/shard_map/ppermute | solution.py:233
  601.8 25.3 %collective-permute-start.73 = (bf16[768,768]{1,0:T(8,128)(2,1)}, bf16[768,768]{1,0:T(8,128)(2,1)}, u32[]{:S(2)}, u32[]{:S(2)}) collective-permute-start(bf16[768,768]{1,0:T(8,128)(2,1)} %get-tuple-element.383.refs_2_), channel_id=1, source_target_pairs={{8,16},{16,8},{9,17},{17,9},{10,18},{18,10},{11,19},{19,11},{12,20... | collective-permute-start | bytes 3538952 | tf_op jit(solution)/shard_map/ppermute | solution.py:299
  608.2 37.6 %collective-permute-start.74 = (bf16[512,1536]{1,0:T(8,128)(2,1)}, bf16[512,1536]{1,0:T(8,128)(2,1)}, u32[]{:S(2)}, u32[]{:S(2)}) collective-permute-start(bf16[512,1536]{1,0:T(8,128)(2,1)} %get-tuple-element.364), channel_id=1, source_target_pairs={{0,1},{1,0},{2,3},{3,2},{4,5},{5,4},{6,7},{7,6},{8,9},{9,8},{10,11... | collective-permute-start | bytes 4718600 | tf_op jit(solution)/shard_map/ppermute | solution.py:25
  609.9 48.4 %collective-permute-start.76 = (bf16[1152,768]{1,0:T(8,128)(2,1)}, bf16[1152,768]{1,0:T(8,128)(2,1)}, u32[]{:S(2)}, u32[]{:S(2)}) collective-permute-start(bf16[1152,768]{1,0:T(8,128)(2,1)} %get-tuple-element.399), channel_id=1, source_target_pairs={{0,4},{2,6},{4,0},{6,2},{1,5},{3,7},{5,1},{7,3},{8,12},{10,14},{12... | collective-permute-start | bytes 5308424 | tf_op jit(solution)/shard_map/ppermute | solution.py:25
  615.9 36.8 %collective-permute-start.75 = (bf16[96,1536]{1,0:T(8,128)(2,1)S(1)}, bf16[96,1536]{1,0:T(8,128)(2,1)}, u32[]{:S(2)}, u32[]{:S(2)}) collective-permute-start(bf16[96,1536]{1,0:T(8,128)(2,1)S(1)} %copy-done.72), channel_id=1, source_target_pairs={{0,1},{1,0},{2,3},{3,2},{4,5},{5,4},{6,7},{7,6},{8,9},{9,8},{10,11... | collective-permute-start | bytes 884744 | tf_op jit(solution)/shard_map/ppermute | solution.py:25
  631.4 34.9 %collective-permute-start.77 = (bf16[768,768]{1,0:T(8,128)(2,1)}, bf16[768,768]{1,0:T(8,128)(2,1)}, u32[]{:S(2)}, u32[]{:S(2)}) collective-permute-start(bf16[768,768]{1,0:T(8,128)(2,1)} %get-tuple-element.402), channel_id=1, source_target_pairs={{0,8},{8,0},{16,24},{24,16},{1,9},{9,1},{17,25},{25,17},{2,10},{10... | collective-permute-start | bytes 3538952 | tf_op jit(solution)/shard_map/ppermute | solution.py:233
  635.0 32.0 %collective-permute-start.78 = (bf16[768,768]{1,0:T(8,128)(2,1)}, bf16[768,768]{1,0:T(8,128)(2,1)}, u32[]{:S(2)}, u32[]{:S(2)}) collective-permute-start(bf16[768,768]{1,0:T(8,128)(2,1)} %get-tuple-element.392.refs_2_), channel_id=1, source_target_pairs={{8,16},{16,8},{9,17},{17,9},{10,18},{18,10},{11,19},{19,11},{12,20... | collective-permute-start | bytes 3538952 | tf_op jit(solution)/shard_map/ppermute | solution.py:299
  645.8 40.8 %collective-permute-start.79 = (bf16[1152,768]{1,0:T(8,128)(2,1)}, bf16[1152,768]{1,0:T(8,128)(2,1)S(1)}, u32[]{:S(2)}, u32[]{:S(2)}) collective-permute-start(bf16[1152,768]{1,0:T(8,128)(2,1)} %get-tuple-element.406), channel_id=1, source_target_pairs={{0,4},{2,6},{4,0},{6,2},{1,5},{3,7},{5,1},{7,3},{8,12},{10,14},{12... | collective-permute-start | bytes 5308424 | tf_op jit(solution)/shard_map/ppermute | solution.py:25
  656.3 46.7 %collective-permute-start.82 = (bf16[512,1536]{1,0:T(8,128)(2,1)}, bf16[512,1536]{1,0:T(8,128)(2,1)}, u32[]{:S(2)}, u32[]{:S(2)}) collective-permute-start(bf16[512,1536]{1,0:T(8,128)(2,1)} %get-tuple-element.416), channel_id=1, source_target_pairs={{0,1},{1,0},{2,3},{3,2},{4,5},{5,4},{6,7},{7,6},{8,9},{9,8},{10,11... | collective-permute-start | bytes 4718600 | tf_op jit(solution)/shard_map/ppermute | solution.py:25
  658.3 54.6 %collective-permute-start.86 = (bf16[384,768]{1,0:T(8,128)(2,1)S(1)}, bf16[384,768]{1,0:T(8,128)(2,1)}, u32[]{:S(2)}, u32[]{:S(2)}) collective-permute-start(bf16[384,768]{1,0:T(8,128)(2,1)S(1)} %copy-done.29), channel_id=1, source_target_pairs={{0,8},{24,16},{1,9},{25,17},{2,10},{26,18},{3,11},{27,19},{4,12},{... | collective-permute-start | bytes 1769480 | tf_op jit(solution)/shard_map/ppermute | solution.py:233
  666.3 32.7 %collective-permute-start.81 = (bf16[96,1536]{1,0:T(8,128)(2,1)S(1)}, bf16[96,1536]{1,0:T(8,128)(2,1)}, u32[]{:S(2)}, u32[]{:S(2)}) collective-permute-start(bf16[96,1536]{1,0:T(8,128)(2,1)S(1)} %copy-done.69), channel_id=1, source_target_pairs={{0,1},{1,0},{2,3},{3,2},{4,5},{5,4},{6,7},{7,6},{8,9},{9,8},{10,11... | collective-permute-start | bytes 884744 | tf_op jit(solution)/shard_map/ppermute | solution.py:25
  686.6 33.6 %collective-permute-start.87 = (bf16[384,768]{1,0:T(8,128)(2,1)S(1)}, bf16[384,768]{1,0:T(8,128)(2,1)}, u32[]{:S(2)}, u32[]{:S(2)}) collective-permute-start(bf16[384,768]{1,0:T(8,128)(2,1)S(1)} %copy-done.28), channel_id=1, source_target_pairs={{0,8},{24,16},{1,9},{25,17},{2,10},{26,18},{3,11},{27,19},{4,12},{... | collective-permute-start | bytes 1769480 | tf_op jit(solution)/shard_map/ppermute | solution.py:233
  694.3 38.4 %collective-permute-start.88 = (bf16[384,768]{1,0:T(8,128)(2,1)}, bf16[384,768]{1,0:T(8,128)(2,1)}, u32[]{:S(2)}, u32[]{:S(2)}) collective-permute-start(bf16[384,768]{1,0:T(8,128)(2,1)} %get-tuple-element.425.refs_0_), channel_id=1, source_target_pairs={{0,8},{24,16},{1,9},{25,17},{2,10},{26,18},{3,11},{27,19},{4,12},{... | collective-permute-start | bytes 1769480 | tf_op jit(solution)/shard_map/ppermute | solution.py:233
  698.9 53.1 %collective-permute-start.104 = (bf16[768,768]{1,0:T(8,128)(2,1)}, bf16[768,768]{1,0:T(8,128)(2,1)}, u32[]{:S(2)}, u32[]{:S(2)}) collective-permute-start(bf16[768,768]{1,0:T(8,128)(2,1)} %get-tuple-element.451), channel_id=1, source_target_pairs={{8,0},{16,24},{9,1},{17,25},{10,2},{18,26},{11,3},{19,27},{12,4},{... | collective-permute-start | bytes 3538952 | tf_op jit(solution)/shard_map/ppermute | solution.py:233
  732.7 73.3 %collective-permute-start.105 = (bf16[768,768]{1,0:T(8,128)(2,1)}, bf16[768,768]{1,0:T(8,128)(2,1)}, u32[]{:S(2)}, u32[]{:S(2)}) collective-permute-start(bf16[768,768]{1,0:T(8,128)(2,1)} %shard_map.369), channel_id=1, source_target_pairs={{8,0},{16,24},{9,1},{17,25},{10,2},{18,26},{11,3},{19,27},{12,4},{... | collective-permute-start | bytes 3538952 | tf_op jit(solution)/shard_map/ppermute | solution.py:233
  734.0 33.9 %collective-permute-start.85 = (f32[1,25,1536]{2,1,0:T(8,128)S(1)}, f32[1,25,1536]{2,1,0:T(8,128)S(1)}, u32[]{:S(2)}, u32[]{:S(2)}) collective-permute-start(f32[1,25,1536]{2,1,0:T(8,128)S(1)} %add_bitcast_fusion), channel_id=1, source_target_pairs={{0,8},{8,0},{16,24},{24,16},{1,9},{9,1},{17,25},{25,17},{2,10},{10... | collective-permute-start | bytes 460808 | tf_op jit(solution)/shard_map/ppermute | solution.py:25
  745.0 35.6 %collective-permute-start.94 = (bf16[384,768]{1,0:T(8,128)(2,1)}, bf16[384,768]{1,0:T(8,128)(2,1)}, u32[]{:S(2)}, u32[]{:S(2)}) collective-permute-start(bf16[384,768]{1,0:T(8,128)(2,1)} %get-tuple-element.431.refs_2_), channel_id=1, source_target_pairs={{8,16},{16,8},{9,17},{17,9},{10,18},{18,10},{11,19},{19,11},{12,20... | collective-permute-start | bytes 1769480 | tf_op jit(solution)/shard_map/ppermute | solution.py:299
  746.5 34.1 %collective-permute-start.93 = (bf16[384,768]{1,0:T(8,128)(2,1)}, bf16[384,768]{1,0:T(8,128)(2,1)S(1)}, u32[]{:S(2)}, u32[]{:S(2)}) collective-permute-start(bf16[384,768]{1,0:T(8,128)(2,1)} %get-tuple-element.435), channel_id=1, source_target_pairs={{0,8},{8,0},{16,24},{24,16},{1,9},{9,1},{17,25},{25,17},{2,10},{10... | collective-permute-start | bytes 1769480 | tf_op jit(solution)/shard_map/ppermute | solution.py:233
  752.1 48.2 %collective-permute-start.95 = (bf16[384,768]{1,0:T(8,128)(2,1)}, bf16[384,768]{1,0:T(8,128)(2,1)S(1)}, u32[]{:S(2)}, u32[]{:S(2)}) collective-permute-start(bf16[384,768]{1,0:T(8,128)(2,1)} %get-tuple-element.438), channel_id=1, source_target_pairs={{0,8},{8,0},{16,24},{24,16},{1,9},{9,1},{17,25},{25,17},{2,10},{10... | collective-permute-start | bytes 1769480 | tf_op jit(solution)/shard_map/ppermute | solution.py:233
  767.9 33.2 %collective-permute-start.96 = (bf16[384,768]{1,0:T(8,128)(2,1)}, bf16[384,768]{1,0:T(8,128)(2,1)}, u32[]{:S(2)}, u32[]{:S(2)}) collective-permute-start(bf16[384,768]{1,0:T(8,128)(2,1)} %get-tuple-element.433.refs_2_), channel_id=1, source_target_pairs={{8,16},{16,8},{9,17},{17,9},{10,18},{18,10},{11,19},{19,11},{12,20... | collective-permute-start | bytes 1769480 | tf_op jit(solution)/shard_map/ppermute | solution.py:299
  780.6 43.0 %collective-permute-start.90 = (f32[2,25,1536]{2,1,0:T(8,128)}, f32[2,25,1536]{2,1,0:T(8,128)}, u32[]{:S(2)}, u32[]{:S(2)}) collective-permute-start(f32[2,25,1536]{2,1,0:T(8,128)} %pad_maximum_fusion.7), channel_id=1, source_target_pairs={{0,16},{8,24},{16,0},{24,8},{1,17},{9,25},{17,1},{25,9},{2,18},{10... | collective-permute-start | bytes 921608 | tf_op jit(solution)/shard_map/ppermute | solution.py:25
  784.2 33.3 %collective-permute-start.98 = (bf16[384,768]{1,0:T(8,128)(2,1)}, bf16[384,768]{1,0:T(8,128)(2,1)}, u32[]{:S(2)}, u32[]{:S(2)}) collective-permute-start(bf16[384,768]{1,0:T(8,128)(2,1)} %get-tuple-element.436.refs_2_), channel_id=1, source_target_pairs={{8,16},{16,8},{9,17},{17,9},{10,18},{18,10},{11,19},{19,11},{12,20... | collective-permute-start | bytes 1769480 | tf_op jit(solution)/shard_map/ppermute | solution.py:299
  804.0 44.4 %collective-permute-start.100 = (bf16[384,768]{1,0:T(8,128)(2,1)}, bf16[384,768]{1,0:T(8,128)(2,1)}, u32[]{:S(2)}, u32[]{:S(2)}) collective-permute-start(bf16[384,768]{1,0:T(8,128)(2,1)} %get-tuple-element.448), channel_id=1, source_target_pairs={{0,8},{8,0},{16,24},{24,16},{1,9},{9,1},{17,25},{25,17},{2,10},{10... | collective-permute-start | bytes 1769480 | tf_op jit(solution)/shard_map/ppermute | solution.py:233
  806.0 42.3 %collective-permute-start.101 = (bf16[384,768]{1,0:T(8,128)(2,1)}, bf16[384,768]{1,0:T(8,128)(2,1)}, u32[]{:S(2)}, u32[]{:S(2)}) collective-permute-start(bf16[384,768]{1,0:T(8,128)(2,1)} %get-tuple-element.440.refs_2_), channel_id=1, source_target_pairs={{8,16},{16,8},{9,17},{17,9},{10,18},{18,10},{11,19},{19,11},{12,20... | collective-permute-start | bytes 1769480 | tf_op jit(solution)/shard_map/ppermute | solution.py:299
  820.9 44.9 %collective-permute-start.102 = (bf16[384,768]{1,0:T(8,128)(2,1)}, bf16[384,768]{1,0:T(8,128)(2,1)}, u32[]{:S(2)}, u32[]{:S(2)}) collective-permute-start(bf16[384,768]{1,0:T(8,128)(2,1)} %get-tuple-element.450.refs_0_), channel_id=1, source_target_pairs={{8,16},{16,8},{9,17},{17,9},{10,18},{18,10},{11,19},{19,11},{12,20... | collective-permute-start | bytes 1769480 | tf_op jit(solution)/shard_map/ppermute | solution.py:299
  822.3 52.3 %collective-permute-start.99 = (bf16[384,768]{1,0:T(8,128)(2,1)}, bf16[384,768]{1,0:T(8,128)(2,1)}, u32[]{:S(2)}, u32[]{:S(2)}) collective-permute-start(bf16[384,768]{1,0:T(8,128)(2,1)} %get-tuple-element.443), channel_id=1, source_target_pairs={{8,0},{16,24},{9,1},{17,25},{10,2},{18,26},{11,3},{19,27},{12,4},{... | collective-permute-start | bytes 1769480 | tf_op jit(solution)/shard_map/ppermute | solution.py:233
  872.1 25.4 %collective-permute-start.103 = (bf16[384,768]{1,0:T(8,128)(2,1)S(1)}, bf16[384,768]{1,0:T(8,128)(2,1)S(1)}, u32[]{:S(2)}, u32[]{:S(2)}) collective-permute-start(bf16[384,768]{1,0:T(8,128)(2,1)S(1)} %copy-done.39), channel_id=1, source_target_pairs={{8,0},{16,24},{9,1},{17,25},{10,2},{18,26},{11,3},{19,27},{12,4},{... | collective-permute-start | bytes 1769480 | tf_op jit(solution)/shard_map/ppermute | solution.py:233
  (136 other events, 1275.0 us)
